TPU v7x, 32 devices: a whole 2x2x4 slice. The times are simulated.
32 devices in a mesh: row: 4 (over y, x), col: 4 (over z), layer: 2 (over core).
Axes of the slice: x: 2, y: 2, z: 4, core: 2. Of those that a mesh axis runs over, the one named last changes fastest.
Arguments:
- trailing: float32 [4, 4, 256, 4, 4, 256], P(None, 'row', None, None, 'col'), may hold values from -6 to 6
- panel: float32 [4, 4, 256, 256], P(None, 'row', 'col'), may hold values from -0.6 to 0.6
- inverse_factor: float32 [256, 256], replicated, may hold values from -1 to 2, as said below
Outputs:
- updated: float32 [4, 4, 256, 4, 4, 256], P('layer', 'row', None, None, 'col')
Inputs may be any that keep to these rules, and one draw needn't show every extreme that they name: inverse_factor is lower triangular; its diagonal lies between 1 and 2.
All inputs are finite; a program needn't handle non-finite values.
Results may differ from a plain program's by a relative error of at most 0.0025.
Values may be sent and summed in bfloat16 or wider, within the bound.
No kernel may reach another device: no remote copies, remote signals or barrier semaphores. Data moves between devices by JAX's collectives and lax.ppermute only.
A program may use at most 64 MiB of HBM per device.

v0:
```python
import jax
import jax.numpy as jnp
from jax import lax
from jax.sharding import PartitionSpec as P


def from_root(x, axis, root):
    mine = lax.axis_index(axis) == root
    return lax.psum(jnp.where(mine, x, jnp.zeros_like(x)), axis)


def apply_inverse(source, inverse_factor):
    panel_width = inverse_factor.shape[0]
    product = jnp.dot(
        source.reshape(-1, panel_width),
        inverse_factor.T,
        precision=lax.Precision.HIGHEST,
        preferred_element_type=jnp.float32,
    )
    return product.astype(jnp.bfloat16).reshape(source.shape)


def per_device(trailing, panel, inverse_factor):
    row_tiles = trailing.shape[0]
    tile_size = trailing.shape[2]
    col_tiles = trailing.shape[3]
    layer_count = lax.axis_size("layer")
    layer_index = lax.axis_index("layer")
    column_index = lax.axis_index("col")
    row_count = lax.axis_size("row")
    factor_rows = lax.all_gather(apply_inverse(panel, inverse_factor), "col", axis=2, tiled=True)
    picked = lax.dynamic_index_in_dim(factor_rows, column_index // row_count, 1, keepdims=False)
    factor_cols = from_root(picked, "row", column_index % row_count)
    row_factor = factor_rows.reshape(row_tiles * tile_size, tile_size)
    col_factor = factor_cols.reshape(col_tiles * tile_size, tile_size)
    matrix = trailing.reshape(row_tiles * tile_size, col_tiles * tile_size)
    share_rows = row_tiles * tile_size // layer_count
    own_rows = lax.dynamic_slice_in_dim(matrix, layer_index * share_rows, share_rows, 0)
    contract_dims = (((1,), (1,)), ((), ()))
    row_block = lax.dynamic_slice_in_dim(row_factor, layer_index * share_rows, share_rows, 0)
    update = lax.dot_general(
        row_block, col_factor, contract_dims, preferred_element_type=jnp.float32
    )
    result = own_rows - update
    return result.reshape(row_tiles // layer_count, 1, tile_size, col_tiles, 1, tile_size)


def solution(mesh):
    return jax.shard_map(
        per_device,
        mesh=mesh,
        in_specs=(P(None, "row", None, None, "col", None), P(None, "row", "col", None), P()),
        out_specs=P("layer", "row", None, None, "col", None),
        check_vma=False,
    )
```

profile of v0, /device:TPU:0, one launch (start us, length us, event | category | flops | bytes accessed | tf_op | source)
XLA Modules:
  0.0 86.9 jit_solution(3604971355798855397)
XLA Ops:
  6.5 0.0 copy-start
  6.5 0.0 all-reduce.2.cloned.1.call-start
  6.5 0.9 %copy-done = f32[4,1,64,256]{3,2,1,0:T(8,128)S(1)} copy-done((f32[4,1,64,256]{3,2,1,0:T(8,128)S(1)}, f32[4,1,64,256]{3,2,1,0:T(8,128)}, u32[]{:S(2)}) %copy-start) | copy-done | bytes 262168
  7.5 1.4 %convolution_convert_fusion = bf16[256,256]{1,0:T(8,128)(2,1)S(1)} fusion(f32[256,256]{1,0:T(8,128)S(1)} %bitcast.10, f32[256,256]{1,0:T(8,128)} %param.5), kind=kOutput, calls=%fused_computation.1 | convolution fusion | flops 201392128 | bytes 655360 | tf_op jit(solution)/shard_map/dot_general | solution.py:14
  8.9 17.4 %all_gather.3 = bf16[4,1,256,256]{3,2,0,1:T(8,128)(2,1)S(1)} all-gather(bf16[4,1,64,256]{3,2,0,1:T(8,128)(2,1)S(1)} %bitcast.15), channel_id=1, replica_groups=mesh['row'=4,'col'=4,'layer'=2] {'col'}, dimensions={2}, use_global_device_ids=true | all-gather | bytes 655360 | tf_op jit(solution)/shard_map/all_gather | solution.py:31
  26.2 0.8 broadcast_select_fusion
  27.0 0.0 all-reduce.2.cloned.1.call-update
  27.1 14.1 %reduce = f32[4,256,4,256]{3,2,1,0:T(4,128)} reduce(f32[4,1,256,4,1,256]{5,4,3,2,1,0:T(1,128)} %param.3, f32[]{:T(128)} %constant.45), dimensions={1,4}, to_apply=%param.3.reduce_sub_computation | reduce | bytes 8388612 | tf_op args[0]
  41.1 5.1 %copy.5 = f32[128,8,4,256]{3,1,2,0:T(8,128)} copy(f32[128,8,4,256]{3,2,1,0:T(4,128)} %bitcast.11) | data formatting | bytes 8388608
  46.3 28.1 %all-reduce.2.cloned.1.call-done = bf16[1024,256]{1,0:T(8,128)(2,1)} async-done(((bf16[1024,256]{1,0:T(8,128)(2,1)}), bf16[1024,256]{1,0:T(8,128)(2,1)}) %all-reduce.2.cloned.1.call-update) | async-done | bytes 524304 | tf_op jit(solution)/shard_map/psum | solution.py:9
  74.3 2.2 %dynamic-slice_subtract_fusion = f32[512,1024]{1,0:T(8,128)S(1)} fusion(f32[1024,1024]{1,0:T(8,128)} %bitcast.12, s32[]{:T(128)S(6)} %select_n.26, bf16[1024,256]{1,0:T(8,128)(2,1)} %all-reduce.2.cloned.1.call-done, bf16[1024,256]{1,0:T(8,128)(2,1)S(1)} %bitcast.13), kind=kOutput, calls=%fused_computation | convolution fusion | flops 268959744 | bytes 4981760 | tf_op jit(solution)/shard_map/dot_general | solution.py:41
  76.6 3.5 %reshape.28 = f32[2,1,256,4,1,256]{5,4,3,2,1,0:T(1,128)} reshape(f32[512,1024]{1,0:T(8,128)S(1)} %dynamic-slice_subtract_fusion) | data formatting | bytes 4194304 | tf_op jit(solution)/shard_map/reshape | solution.py:45
Async XLA Ops:
  6.5 1.0 %copy-start = (f32[4,1,64,256]{3,2,1,0:T(8,128)S(1)}, f32[4,1,64,256]{3,2,1,0:T(8,128)}, u32[]{:S(2)}) copy-start(f32[4,1,64,256]{3,2,1,0:T(8,128)} %param.4) | copy-start | bytes 786436
  6.5 67.8 %all-reduce.2.cloned.1.call-start = ((), (), s32[]{:S(2)}) async-start(), calls=%async_computation | async-start | bytes 1048576 | tf_op jit(solution)/shard_map/psum | solution.py:9
Sparse Core Ops, SparseCore 0:
  27.2 47.0 all-reduce.1
where the time goes:
time: 87.2 us; the launch traced here: 86.9 us
  waiting for transfers between devices  28.1 us (32%)
  blocking collectives  17.4 us (20%)
  other arithmetic  14.9 us (17%)
  between operations  13.4 us (15%)
  local copies, waits for them, and re-layouts  9.56 us (11%)
  matrix products  3.6 us (4%)
    psum x1, waiting for transfers between devices, from_root(): return lax.psum(jnp.where(mine, x, jnp.zeros_like(x)), axis)  28.1 us
    all_gather x1, blocking collectives, per_device(): lax.all_gather(apply_inverse(panel, inverse_factor), 'col', axis=2, tiled...  17.4 us
    unnamed x1, other arithmetic  14.1 us
    unnamed x3, local copies, waits for them, and re-layouts  6.06 us
    reshape x1, local copies, waits for them, and re-layouts, per_device(): result.reshape(row_tiles // layer_count, 1, tile_size, col_tiles, 1, tile...  3.5 us
    dot_general x1, matrix products, per_device(): lax.dot_general(row_block, col_factor, contract_dims, preferred_element_t...  2.23 us
  transfers between devices with their start and end apart: 1, of which 1 were waited for; matrix products, arithmetic and copies ran while one was open for 22% of the time, Pallas kernels for 0%

commit v1 on v0

v1 whole, which is shorter than its diff:
```python
import jax
import jax.numpy as jnp
from jax import lax
from jax.experimental import pallas as pl
from jax.experimental.pallas import tpu as pltpu
from jax.sharding import PartitionSpec as P

LANES = 128
VMEM_BYTES = 24 * 1024 * 1024
AXES = ("row", "col", "layer")


def factor_kernel(panel_ref, inverse_ref, factor_ref, panel_buf, inverse_buf, sems):
    half = factor_ref.shape[0]
    tile_rows = factor_ref.shape[1]
    width = factor_ref.shape[2]
    layer = lax.axis_index("layer")
    copies = [
        pltpu.make_async_copy(panel_ref.at[pl.ds(layer * half, half), 0], panel_buf, sems.at[0]),
        pltpu.make_async_copy(inverse_ref, inverse_buf, sems.at[1]),
    ]
    for copy in copies:
        copy.start()
    for copy in copies:
        copy.wait()
    product = lax.dot_general(
        panel_buf[...].reshape(half * tile_rows, width),
        inverse_buf[...],
        (((1,), (1,)), ((), ())),
        precision=lax.Precision.HIGHEST,
        preferred_element_type=jnp.float32,
    )
    factor_ref[...] = product.astype(jnp.bfloat16).reshape(factor_ref.shape)


def make_factor(panel, inverse_factor, half):
    _, _, tile_rows, width = panel.shape
    return pl.pallas_call(
        factor_kernel,
        out_shape=jax.ShapeDtypeStruct((half, tile_rows, width), jnp.bfloat16),
        in_specs=[pl.BlockSpec(memory_space=pl.ANY)] * 2,
        out_specs=pl.BlockSpec(memory_space=pltpu.VMEM),
        scratch_shapes=[
            pltpu.VMEM((half, tile_rows, width), jnp.float32),
            pltpu.VMEM((width, width), jnp.float32),
            pltpu.SemaphoreType.DMA((2,)),
        ],
        compiler_params=pltpu.CompilerParams(vmem_limit_bytes=VMEM_BYTES),
        name="factor",
    )(panel, inverse_factor)


def partner(index, step, count):
    return index ^ step if count & (count - 1) == 0 else (index + step) % count


def update_kernel(pieces, layers, half, tile, tile_rows, col_tiles, *refs):
    row_refs = refs[:pieces]
    col_refs = refs[pieces : pieces * (1 + layers)]
    trailing_ref, out_ref, row_buf, col_buf, in_buf, out_buf, in_sems, out_sems = refs[pieces * (1 + layers) :]
    r, c, layer = (lax.axis_index(axis) for axis in AXES)
    lines = tile * col_tiles * tile // LANES
    per_row = col_tiles * tile // LANES
    loads = [
        pltpu.make_async_copy(
            trailing_ref.at[pl.ds((layer * half + k) * lines, lines)], in_buf.at[k], in_sems.at[k]
        )
        for k in range(half)
    ]
    for load in loads:
        load.start()
    for step in range(pieces):
        row_at = pl.multiple_of(partner(c, step, pieces) * tile_rows, tile_rows)
        col_at = pl.multiple_of(partner(r, step, pieces) * tile_rows, tile_rows)
        for k in range(half):
            row_buf[k, pl.ds(row_at, tile_rows), :] = row_refs[step][k]
        for shift in range(layers):
            owner = lax.rem(layer + shift, layers)
            for k in range(half):
                col_buf[owner * half + k, pl.ds(col_at, tile_rows), :] = col_refs[shift * pieces + step][k]
    stores = []
    for k in range(half):
        loads[k].wait()
        for j in range(col_tiles):
            update = lax.dot_general(
                row_buf[k], col_buf[j], (((1,), (1,)), ((), ())), preferred_element_type=jnp.float32
            )
            for part in range(tile // LANES):
                lines_at = pl.ds(j * (tile // LANES) + part, tile, stride=per_row)
                out_buf[k, lines_at, :] = in_buf[k, lines_at, :] - update[:, part * LANES : (part + 1) * LANES]
        store = pltpu.make_async_copy(out_buf.at[k], out_ref.at[pl.ds(k * lines, lines)], out_sems.at[k])
        store.start()
        stores.append(store)
    for store in stores:
        store.wait()


def update_trailing(row_pieces, col_pieces, trailing, half, layers):
    row_tiles, _, tile, col_tiles, _, _ = trailing.shape
    pieces = len(row_pieces)
    tile_rows = row_pieces[0].shape[1]
    width = row_pieces[0].shape[2]
    lines = tile * col_tiles * tile // LANES

    def body(*refs):
        update_kernel(pieces, layers, half, tile, tile_rows, col_tiles, *refs)

    result = pl.pallas_call(
        body,
        out_shape=jax.ShapeDtypeStruct((half * lines, LANES), jnp.float32),
        in_specs=[pl.BlockSpec(memory_space=pltpu.VMEM)] * (pieces * (1 + layers))
        + [pl.BlockSpec(memory_space=pl.ANY)],
        out_specs=pl.BlockSpec(memory_space=pl.ANY),
        scratch_shapes=[
            pltpu.VMEM((half, tile, width), jnp.bfloat16),
            pltpu.VMEM((half * layers, tile, width), jnp.bfloat16),
            pltpu.VMEM((half, lines, LANES), jnp.float32),
            pltpu.VMEM((half, lines, LANES), jnp.float32),
            pltpu.SemaphoreType.DMA((half,)),
            pltpu.SemaphoreType.DMA((half,)),
        ],
        compiler_params=pltpu.CompilerParams(vmem_limit_bytes=VMEM_BYTES),
        name="update",
    )(*row_pieces, *col_pieces, trailing.reshape(row_tiles * lines, LANES))
    return result.reshape(half, 1, tile, col_tiles, 1, tile)


def per_device(trailing, panel, inverse_factor):
    layers = lax.axis_size("layer")
    count = lax.axis_size("row")
    half = trailing.shape[0] // layers
    factor = make_factor(panel, inverse_factor, half)
    swapped = lax.ppermute(
        factor, ("row", "col"), [(a * count + b, b * count + a) for a in range(count) for b in range(count)]
    )
    plane = [swapped]
    for step in range(1, count):
        plane.append(lax.ppermute(swapped, "row", [(a, partner(a, step, count)) for a in range(count)]))
    line = [factor]
    for step in range(1, count):
        line.append(lax.ppermute(factor, "col", [(partner(b, step, count), b) for b in range(count)]))
    others = []
    for shift in range(1, layers):
        pairs = [((l + shift) % layers, l) for l in range(layers)]
        others += [lax.ppermute(piece, "layer", pairs) for piece in plane]
    return update_trailing(line, plane + others, trailing, half, layers)


def solution(mesh):
    assert mesh.shape["row"] == mesh.shape["col"]
    return jax.shard_map(
        per_device,
        mesh=mesh,
        in_specs=(P(None, "row", None, None, "col", None), P(None, "row", "col", None), P()),
        out_specs=P("layer", "row", None, None, "col", None),
        check_vma=False,
    )
```

time: 87.2 us -> 28.6 us (0.33)
  waiting for transfers between devices: 28.1 us -> 1.9 us
  starting transfers between devices: 0.01 us -> 19.4 us
  blocking collectives: 17.4 us -> 0 us
  other arithmetic: 14.9 us -> 0 us
  between operations: 13.4 us -> 0.05 us
  local copies, waits for them, and re-layouts: 9.56 us -> 4.08 us
  matrix products: 3.6 us -> 0 us
  Pallas kernels: 0 us -> 2.77 us
    psum x1 -> x0, waiting for transfers between devices: 28.1 us -> none  [from_root(): return lax.psum(jnp.where(mine, x, jnp.zeros_like(x)), axis)]
    ppermute x0 -> x11, starting transfers between devices: none -> 19.4 us  [the longest x3 10.3 us: per_device(): lax.ppermute(factor, 'col', [(partner(b, step, count), b) for b in range(...]
    all_gather x1 -> x0, blocking collectives: 17.4 us -> none  [per_device(): lax.all_gather(apply_inverse(panel, inverse_factor), 'col', axis=2, tiled...]
    unnamed x1 -> x0, other arithmetic: 14.1 us -> none
    dot_general x2 -> x0, matrix products: 3.6 us -> none  [the longest x1 2.23 us: per_device(): lax.dot_general(row_block, col_factor, contract_dims, preferred_element_t...]
    reshape x1 -> x0, local copies, waits for them, and re-layouts: 3.5 us -> none  [per_device(): result.reshape(row_tiles // layer_count, 1, tile_size, col_tiles, 1, tile...]
    pallas_call x0 -> x2, Pallas kernels: none -> 2.77 us  [the longest x1 2.19 us: update_trailing(): pl.pallas_call(body, out_shape=jax.ShapeDtypeStruct((half * lines, LANES)...]
    unnamed x3 -> x6, local copies, waits for them, and re-layouts: 6.06 us -> 4.08 us
  transfers between devices with their start and end apart: 1 -> 11, of which waited for: 1 -> 2; matrix products, arithmetic and copies ran while one was open for 22% -> 0% of each run, Pallas kernels for 0% -> 0%
where the time goes in v1:
time: 28.6 us; the launch traced here: 28.2 us
  starting transfers between devices  19.4 us (68%)
  local copies, waits for them, and re-layouts  4.08 us (14%)
  Pallas kernels  2.77 us (10%)
  waiting for transfers between devices  1.9 us (7%)
    ppermute x3, starting transfers between devices, per_device(): lax.ppermute(factor, 'col', [(partner(b, step, count), b) for b in range(...  10.3 us
    ppermute x3, starting transfers between devices, per_device(): lax.ppermute(swapped, 'row', [(a, partner(a, step, count)) for a in range...  7.85 us
    unnamed x6, local copies, waits for them, and re-layouts  4.08 us
    pallas_call x1, Pallas kernels, update_trailing(): pl.pallas_call(body, out_shape=jax.ShapeDtypeStruct((half * lines, LANES)...  2.19 us
    ppermute x3, waiting for transfers between devices, per_device(): lax.ppermute(factor, 'col', [(partner(b, step, count), b) for b in range(...  1.33 us
    ppermute x1, starting transfers between devices, per_device(): lax.ppermute(factor, ('row', 'col'), [(a * count + b, b * count + a) for...  0.66 us
    ppermute x4, starting transfers between devices, per_device(): others += [lax.ppermute(piece, 'layer', pairs) for piece in plane]  0.58 us
    pallas_call x1, Pallas kernels, make_factor(): pl.pallas_call(factor_kernel, out_shape=jax.ShapeDtypeStruct((half, tile_...  0.57 us
  transfers between devices with their start and end apart: 11, of which 2 were waited for; matrix products, arithmetic and copies ran while one was open for 0% of the time, Pallas kernels for 0%

profile of v1, /device:TPU:0, one launch (start us, length us, event | category | flops | bytes accessed | tf_op | source)
XLA Modules:
  0.0 28.2 jit_solution(17178901915995562015)
XLA Ops:
  0.0 0.0 copy-start.1
  0.0 0.9 %copy-done.1 = f32[4,1,64,256]{3,2,1,0:T(8,128)S(1)} copy-done((f32[4,1,64,256]{3,2,1,0:T(8,128)S(1)}, f32[4,1,64,256]{3,2,1,0:T(8,128)}, u32[]{:S(2)}) %copy-start.1) | copy-done | bytes 262168
  1.0 0.0 copy-start.2
  1.0 0.9 %copy-done.2 = f32[256,256]{1,0:T(8,128)S(1)} copy-done((f32[256,256]{1,0:T(8,128)S(1)}, f32[256,256]{1,0:T(8,128)}, u32[]{:S(2)}) %copy-start.2) | copy-done | bytes 262168
  1.9 0.6 %factor.1.refs_0_ = bf16[2,64,256]{2,1,0:T(8,128)(2,1)S(1)} custom-call(f32[4,1,64,256]{3,2,1,0:T(8,128)S(1)} %copy-done.1, f32[256,256]{1,0:T(8,128)S(1)} %copy-done.2), custom_call_target="tpu_custom_call" | custom-call | tf_op jit(solution)/shard_map/factor/pallas_call | solution.py:38
  2.5 0.7 %collective-permute-start.3 = (bf16[2,64,256]{2,1,0:T(8,128)(2,1)S(1)}, bf16[2,64,256]{2,1,0:T(8,128)(2,1)S(1)}, u32[]{:S(2)}, u32[]{:S(2)}) collective-permute-start(bf16[2,64,256]{2,1,0:T(8,128)(2,1)S(1)} %factor.1.refs_0_), channel_id=1, source_target_pairs={{0,0},{2,8},{4,16},{6,24},{8,2},{10,10},{12,18},{14,26},{16,4},{18... | collective-permute-start | bytes 196616 | tf_op jit(solution)/shard_map/ppermute | solution.py:133
  3.2 8.5 %collective-permute-start.2 = (bf16[2,64,256]{2,1,0:T(8,128)(2,1)S(1)}, bf16[2,64,256]{2,1,0:T(8,128)(2,1)S(1)}, u32[]{:S(2)}, u32[]{:S(2)}) collective-permute-start(bf16[2,64,256]{2,1,0:T(8,128)(2,1)S(1)} %factor.1.refs_0_), channel_id=1, source_target_pairs={{6,0},{4,2},{2,4},{0,6},{7,1},{5,3},{3,5},{1,7},{14,8},{12,10},{10... | collective-permute-start | bytes 196616 | tf_op jit(solution)/shard_map/ppermute | solution.py:141
  11.6 0.0 collective-permute-start.1
  11.6 0.0 collective-permute-done.3.refs_4_
  11.6 5.3 %collective-permute-start.6 = (bf16[2,64,256]{2,1,0:T(8,128)(2,1)S(1)}, bf16[2,64,256]{2,1,0:T(8,128)(2,1)S(1)}, u32[]{:S(2)}, u32[]{:S(2)}) collective-permute-start(bf16[2,64,256]{2,1,0:T(8,128)(2,1)S(1)} %collective-permute-done.3.refs_4_), channel_id=1, source_target_pairs={{0,24},{8,16},{16,8},{24,0},{1,25},{9,17},{17,9},{25,1},{2,26},{10... | collective-permute-start | bytes 196616 | tf_op jit(solution)/shard_map/ppermute | solution.py:138
  16.9 1.1 %collective-permute-start.5 = (bf16[2,64,256]{2,1,0:T(8,128)(2,1)S(1)}, bf16[2,64,256]{2,1,0:T(8,128)(2,1)S(1)}, u32[]{:S(2)}, u32[]{:S(2)}) collective-permute-start(bf16[2,64,256]{2,1,0:T(8,128)(2,1)S(1)} %collective-permute-done.3.refs_4_), channel_id=1, source_target_pairs={{0,16},{8,24},{16,0},{24,8},{1,17},{9,25},{17,1},{25,9},{2,18},{10... | collective-permute-start | bytes 196616 | tf_op jit(solution)/shard_map/ppermute | solution.py:138
  18.0 1.5 %collective-permute-start.4 = (bf16[2,64,256]{2,1,0:T(8,128)(2,1)S(1)}, bf16[2,64,256]{2,1,0:T(8,128)(2,1)S(1)}, u32[]{:S(2)}, u32[]{:S(2)}) collective-permute-start(bf16[2,64,256]{2,1,0:T(8,128)(2,1)S(1)} %collective-permute-done.3.refs_4_), channel_id=1, source_target_pairs={{0,8},{8,0},{16,24},{24,16},{1,9},{9,1},{17,25},{25,17},{2,10},{10... | collective-permute-start | bytes 196616 | tf_op jit(solution)/shard_map/ppermute | solution.py:138
  19.5 0.0 collective-permute-done.2.refs_3_
  19.5 1.8 %collective-permute-start = (bf16[2,64,256]{2,1,0:T(8,128)(2,1)S(1)}, bf16[2,64,256]{2,1,0:T(8,128)(2,1)S(1)}, u32[]{:S(2)}, u32[]{:S(2)}) collective-permute-start(bf16[2,64,256]{2,1,0:T(8,128)(2,1)S(1)} %factor.1.refs_0_), channel_id=1, source_target_pairs={{2,0},{0,2},{6,4},{4,6},{3,1},{1,3},{7,5},{5,7},{10,8},{8,10},{14,... | collective-permute-start | bytes 196616 | tf_op jit(solution)/shard_map/ppermute | solution.py:141
  21.3 0.0 collective-permute-done.1.refs_2_
  21.3 0.0 collective-permute-start.7
  21.3 0.0 collective-permute-done.6.refs_7_
  21.3 0.5 %collective-permute-start.10 = (bf16[2,64,256]{2,1,0:T(8,128)(2,1)S(1)}, bf16[2,64,256]{2,1,0:T(8,128)(2,1)S(1)}, u32[]{:S(2)}, u32[]{:S(2)}) collective-permute-start(bf16[2,64,256]{2,1,0:T(8,128)(2,1)S(1)} %collective-permute-done.6.refs_7_), channel_id=1, source_target_pairs={{1,0},{0,1},{3,2},{2,3},{5,4},{4,5},{7,6},{6,7},{9,8},{8,9},{11,10... | collective-permute-start | bytes 196616 | tf_op jit(solution)/shard_map/ppermute | solution.py:145
  21.8 0.0 collective-permute-done.5.refs_6_
  21.8 0.1 collective-permute-start.9
  21.9 0.5 %collective-permute-done.4.refs_5_ = bf16[2,64,256]{2,1,0:T(8,128)(2,1)S(1)} collective-permute-done((bf16[2,64,256]{2,1,0:T(8,128)(2,1)S(1)}, bf16[2,64,256]{2,1,0:T(8,128)(2,1)S(1)}, u32[]{:S(2)}, u32[]{:S(2)}) %collective-permute-start.4) | collective-permute-done | bytes 65568 | tf_op jit(solution)/shard_map/ppermute | solution.py:138
  22.4 0.0 collective-permute-start.8
  22.4 1.3 %collective-permute-done.refs_1_ = bf16[2,64,256]{2,1,0:T(8,128)(2,1)S(1)} collective-permute-done((bf16[2,64,256]{2,1,0:T(8,128)(2,1)S(1)}, bf16[2,64,256]{2,1,0:T(8,128)(2,1)S(1)}, u32[]{:S(2)}, u32[]{:S(2)}) %collective-permute-start) | collective-permute-done | bytes 65568 | tf_op jit(solution)/shard_map/ppermute | solution.py:141
  23.7 0.0 collective-permute-done.7.refs_8_
  23.8 0.0 collective-permute-done.10.refs_11_
  23.8 0.0 collective-permute-done.9.refs_10_
  23.8 0.0 collective-permute-done.8.refs_9_
  23.8 0.0 copy-start
  23.8 2.2 %copy-done = f32[4,1,256,4,1,256]{5,4,3,2,1,0:T(1,128)S(1)} copy-done((f32[4,1,256,4,1,256]{5,4,3,2,1,0:T(1,128)S(1)}, f32[4,1,256,4,1,256]{5,4,3,2,1,0:T(1,128)}, u32[]{:S(2)}) %copy-start) | copy-done | bytes 4194328
  26.0 2.2 %update.1 = f32[4096,128]{1,0:T(8,128)} custom-call(bf16[2,64,256]{2,1,0:T(8,128)(2,1)S(1)} %factor.1.refs_0_, bf16[2,64,256]{2,1,0:T(8,128)(2,1)S(1)} %collective-permute-done.refs_1_, bf16[2,64,256]{2,1,0:T(8,128)(2,1)S(1)} %collective-permute-done.1.refs_2_, bf16[2,64,256]{2,1,0:T(8,128)(2,1)S(1)} %collective-permute-done.2.refs_3_, ...), custom_call_target="tpu_custom_call" | custom-call | tf_op jit(solution)/shard_map/update/pallas_call | solution.py:108
Async XLA Ops:
  0.0 0.9 %copy-start.1 = (f32[4,1,64,256]{3,2,1,0:T(8,128)S(1)}, f32[4,1,64,256]{3,2,1,0:T(8,128)}, u32[]{:S(2)}) copy-start(f32[4,1,64,256]{3,2,1,0:T(8,128)} %panel_ref.1) | copy-start | bytes 786436
  1.0 0.9 %copy-start.2 = (f32[256,256]{1,0:T(8,128)S(1)}, f32[256,256]{1,0:T(8,128)}, u32[]{:S(2)}) copy-start(f32[256,256]{1,0:T(8,128)} %inverse_ref.1) | copy-start | bytes 786436
  2.5 9.1 %collective-permute-start.3 = (bf16[2,64,256]{2,1,0:T(8,128)(2,1)S(1)}, bf16[2,64,256]{2,1,0:T(8,128)(2,1)S(1)}, u32[]{:S(2)}, u32[]{:S(2)}) collective-permute-start(bf16[2,64,256]{2,1,0:T(8,128)(2,1)S(1)} %factor.1.refs_0_), channel_id=1, source_target_pairs={{0,0},{2,8},{4,16},{6,24},{8,2},{10,10},{12,18},{14,26},{16,4},{18... | collective-permute-start | bytes 196616 | tf_op jit(solution)/shard_map/ppermute | solution.py:133
  3.2 16.3 %collective-permute-start.2 = (bf16[2,64,256]{2,1,0:T(8,128)(2,1)S(1)}, bf16[2,64,256]{2,1,0:T(8,128)(2,1)S(1)}, u32[]{:S(2)}, u32[]{:S(2)}) collective-permute-start(bf16[2,64,256]{2,1,0:T(8,128)(2,1)S(1)} %factor.1.refs_0_), channel_id=1, source_target_pairs={{6,0},{4,2},{2,4},{0,6},{7,1},{5,3},{3,5},{1,7},{14,8},{12,10},{10... | collective-permute-start | bytes 196616 | tf_op jit(solution)/shard_map/ppermute | solution.py:141
  11.6 9.7 %collective-permute-start.1 = (bf16[2,64,256]{2,1,0:T(8,128)(2,1)S(1)}, bf16[2,64,256]{2,1,0:T(8,128)(2,1)S(1)}, u32[]{:S(2)}, u32[]{:S(2)}) collective-permute-start(bf16[2,64,256]{2,1,0:T(8,128)(2,1)S(1)} %factor.1.refs_0_), channel_id=1, source_target_pairs={{4,0},{6,2},{0,4},{2,6},{5,1},{7,3},{1,5},{3,7},{12,8},{14,10},{8,... | collective-permute-start | bytes 196616 | tf_op jit(solution)/shard_map/ppermute | solution.py:141
  11.6 9.7 %collective-permute-start.6 = (bf16[2,64,256]{2,1,0:T(8,128)(2,1)S(1)}, bf16[2,64,256]{2,1,0:T(8,128)(2,1)S(1)}, u32[]{:S(2)}, u32[]{:S(2)}) collective-permute-start(bf16[2,64,256]{2,1,0:T(8,128)(2,1)S(1)} %collective-permute-done.3.refs_4_), channel_id=1, source_target_pairs={{0,24},{8,16},{16,8},{24,0},{1,25},{9,17},{17,9},{25,1},{2,26},{10... | collective-permute-start | bytes 196616 | tf_op jit(solution)/shard_map/ppermute | solution.py:138
  16.9 4.9 %collective-permute-start.5 = (bf16[2,64,256]{2,1,0:T(8,128)(2,1)S(1)}, bf16[2,64,256]{2,1,0:T(8,128)(2,1)S(1)}, u32[]{:S(2)}, u32[]{:S(2)}) collective-permute-start(bf16[2,64,256]{2,1,0:T(8,128)(2,1)S(1)} %collective-permute-done.3.refs_4_), channel_id=1, source_target_pairs={{0,16},{8,24},{16,0},{24,8},{1,17},{9,25},{17,1},{25,9},{2,18},{10... | collective-permute-start | bytes 196616 | tf_op jit(solution)/shard_map/ppermute | solution.py:138
  18.0 4.4 %collective-permute-start.4 = (bf16[2,64,256]{2,1,0:T(8,128)(2,1)S(1)}, bf16[2,64,256]{2,1,0:T(8,128)(2,1)S(1)}, u32[]{:S(2)}, u32[]{:S(2)}) collective-permute-start(bf16[2,64,256]{2,1,0:T(8,128)(2,1)S(1)} %collective-permute-done.3.refs_4_), channel_id=1, source_target_pairs={{0,8},{8,0},{16,24},{24,16},{1,9},{9,1},{17,25},{25,17},{2,10},{10... | collective-permute-start | bytes 196616 | tf_op jit(solution)/shard_map/ppermute | solution.py:138
  19.5 4.3 %collective-permute-start = (bf16[2,64,256]{2,1,0:T(8,128)(2,1)S(1)}, bf16[2,64,256]{2,1,0:T(8,128)(2,1)S(1)}, u32[]{:S(2)}, u32[]{:S(2)}) collective-permute-start(bf16[2,64,256]{2,1,0:T(8,128)(2,1)S(1)} %factor.1.refs_0_), channel_id=1, source_target_pairs={{2,0},{0,2},{6,4},{4,6},{3,1},{1,3},{7,5},{5,7},{10,8},{8,10},{14,... | collective-permute-start | bytes 196616 | tf_op jit(solution)/shard_map/ppermute | solution.py:141
  21.3 2.5 %collective-permute-start.7 = (bf16[2,64,256]{2,1,0:T(8,128)(2,1)S(1)}, bf16[2,64,256]{2,1,0:T(8,128)(2,1)S(1)}, u32[]{:S(2)}, u32[]{:S(2)}) collective-permute-start(bf16[2,64,256]{2,1,0:T(8,128)(2,1)S(1)} %collective-permute-done.3.refs_4_), channel_id=1, source_target_pairs={{1,0},{0,1},{3,2},{2,3},{5,4},{4,5},{7,6},{6,7},{9,8},{8,9},{11,10... | collective-permute-start | bytes 196616 | tf_op jit(solution)/shard_map/ppermute | solution.py:145
  21.3 2.5 %collective-permute-start.10 = (bf16[2,64,256]{2,1,0:T(8,128)(2,1)S(1)}, bf16[2,64,256]{2,1,0:T(8,128)(2,1)S(1)}, u32[]{:S(2)}, u32[]{:S(2)}) collective-permute-start(bf16[2,64,256]{2,1,0:T(8,128)(2,1)S(1)} %collective-permute-done.6.refs_7_), channel_id=1, source_target_pairs={{1,0},{0,1},{3,2},{2,3},{5,4},{4,5},{7,6},{6,7},{9,8},{8,9},{11,10... | collective-permute-start | bytes 196616 | tf_op jit(solution)/shard_map/ppermute | solution.py:145
  21.8 2.0 %collective-permute-start.9 = (bf16[2,64,256]{2,1,0:T(8,128)(2,1)S(1)}, bf16[2,64,256]{2,1,0:T(8,128)(2,1)S(1)}, u32[]{:S(2)}, u32[]{:S(2)}) collective-permute-start(bf16[2,64,256]{2,1,0:T(8,128)(2,1)S(1)} %collective-permute-done.5.refs_6_), channel_id=1, source_target_pairs={{1,0},{0,1},{3,2},{2,3},{5,4},{4,5},{7,6},{6,7},{9,8},{8,9},{11,10... | collective-permute-start | bytes 196616 | tf_op jit(solution)/shard_map/ppermute | solution.py:145
  22.4 1.3 %collective-permute-start.8 = (bf16[2,64,256]{2,1,0:T(8,128)(2,1)S(1)}, bf16[2,64,256]{2,1,0:T(8,128)(2,1)S(1)}, u32[]{:S(2)}, u32[]{:S(2)}) collective-permute-start(bf16[2,64,256]{2,1,0:T(8,128)(2,1)S(1)} %collective-permute-done.4.refs_5_), channel_id=1, source_target_pairs={{1,0},{0,1},{3,2},{2,3},{5,4},{4,5},{7,6},{6,7},{9,8},{8,9},{11,10... | collective-permute-start | bytes 196616 | tf_op jit(solution)/shard_map/ppermute | solution.py:145
  23.8 2.2 %copy-start = (f32[4,1,256,4,1,256]{5,4,3,2,1,0:T(1,128)S(1)}, f32[4,1,256,4,1,256]{5,4,3,2,1,0:T(1,128)}, u32[]{:S(2)}) copy-start(f32[4,1,256,4,1,256]{5,4,3,2,1,0:T(1,128)} %param.3) | copy-start | bytes 12582916

commit v2 on v1

v2 whole, which is shorter than its diff:
```python
import jax
import jax.numpy as jnp
from jax import lax
from jax.experimental import pallas as pl
from jax.experimental.pallas import tpu as pltpu
from jax.sharding import PartitionSpec as P

LANES = 128
VMEM_BYTES = 24 * 1024 * 1024
FACTOR_VMEM_BYTES = 56 * 1024 * 1024
AXES = ("row", "col", "layer")


def factor_kernel(panel_ref, inverse_ref, factor_ref, panel_buf, inverse_buf, sems):
    half = factor_ref.shape[0]
    tile_rows = factor_ref.shape[1]
    width = factor_ref.shape[2]
    layer = lax.axis_index("layer")
    copies = [
        pltpu.make_async_copy(panel_ref.at[pl.ds(layer * half, half), 0], panel_buf, sems.at[0]),
        pltpu.make_async_copy(inverse_ref, inverse_buf, sems.at[1]),
    ]
    for copy in copies:
        copy.start()
    for copy in copies:
        copy.wait()
    product = lax.dot_general(
        panel_buf[...].reshape(half * tile_rows, width),
        inverse_buf[...],
        (((1,), (1,)), ((), ())),
        precision=lax.Precision.HIGHEST,
        preferred_element_type=jnp.float32,
    )
    factor_ref[...] = product.astype(jnp.bfloat16).reshape(factor_ref.shape)


def make_factor(panel, inverse_factor, half):
    _, _, tile_rows, width = panel.shape
    return pl.pallas_call(
        factor_kernel,
        out_shape=jax.ShapeDtypeStruct((half, tile_rows, width), jnp.bfloat16),
        in_specs=[pl.BlockSpec(memory_space=pltpu.HBM)] * 2,
        out_specs=pl.BlockSpec(memory_space=pltpu.VMEM),
        scratch_shapes=[
            pltpu.VMEM((half, tile_rows, width), jnp.float32),
            pltpu.VMEM((width, width), jnp.float32),
            pltpu.SemaphoreType.DMA((2,)),
        ],
        compiler_params=pltpu.CompilerParams(vmem_limit_bytes=FACTOR_VMEM_BYTES),
        name="factor",
    )(panel, inverse_factor)


def partner(index, step, count):
    return index ^ step if count & (count - 1) == 0 else (index + step) % count


def plane_slots(count):
    if count == 4:
        return ((1, 3, 2, 0), (0, 2, 1, 3), (2, 0, 3, 1), (3, 1, 0, 2))
    return tuple(tuple(count - 1 - b for b in range(count)) for _ in range(count))


def slab_of(slots, plane, place):
    slab = jnp.int32(0)
    for at, row in enumerate(slots):
        for b, slot in enumerate(row):
            slab = jnp.where((plane == at) & (place == slot), b, slab)
    return slab


def update_kernel(pieces, layers, half, tile, tile_rows, col_tiles, *refs):
    row_refs = refs[:pieces]
    col_refs = refs[pieces : pieces * (1 + layers)]
    share_ref, out_ref, row_buf, col_buf, out_buf, out_sems = refs[pieces * (1 + layers) :]
    r, c, layer = (lax.axis_index(axis) for axis in AXES)
    slots = plane_slots(pieces)
    lines = tile * col_tiles * tile // LANES
    per_row = col_tiles * tile // LANES
    for step in range(pieces):
        row_at = pl.multiple_of(partner(c, step, pieces) * tile_rows, tile_rows)
        slab = slab_of(slots, c, partner(r, step, pieces))
        col_at = pl.multiple_of(slab * tile_rows, tile_rows)
        for k in range(half):
            row_buf[k, pl.ds(row_at, tile_rows), :] = row_refs[step][k]
        for shift in range(layers):
            owner = lax.rem(layer + shift, layers)
            for k in range(half):
                col_buf[owner * half + k, pl.ds(col_at, tile_rows), :] = col_refs[shift * pieces + step][k]
    stores = []
    for k in range(half):
        for j in range(col_tiles):
            update = lax.dot_general(
                row_buf[k], col_buf[j], (((1,), (1,)), ((), ())), preferred_element_type=jnp.float32
            )
            for part in range(tile // LANES):
                first = j * (tile // LANES) + part
                out_buf[pl.ds(k * lines + first, tile, stride=per_row), :] = (
                    share_ref[pl.ds(k * lines + first, tile, stride=per_row), :]
                    - update[:, part * LANES : (part + 1) * LANES]
                )
        share = pl.ds(k * lines, lines)
        store = pltpu.make_async_copy(out_buf.at[share], out_ref.at[share], out_sems.at[k])
        store.start()
        stores.append(store)
    for store in stores:
        store.wait()


def update_trailing(row_pieces, col_pieces, share, half, layers, tile, col_tiles):
    pieces = len(row_pieces)
    tile_rows = row_pieces[0].shape[1]
    width = row_pieces[0].shape[2]

    def body(*refs):
        update_kernel(pieces, layers, half, tile, tile_rows, col_tiles, *refs)

    result = pl.pallas_call(
        body,
        out_shape=jax.ShapeDtypeStruct(share.shape, jnp.float32),
        in_specs=[pl.BlockSpec(memory_space=pltpu.VMEM)] * (pieces * (1 + layers) + 1),
        out_specs=pl.BlockSpec(memory_space=pltpu.HBM),
        scratch_shapes=[
            pltpu.VMEM((half, tile, width), jnp.bfloat16),
            pltpu.VMEM((half * layers, tile, width), jnp.bfloat16),
            pltpu.VMEM(share.shape, jnp.float32),
            pltpu.SemaphoreType.DMA((half,)),
        ],
        compiler_params=pltpu.CompilerParams(vmem_limit_bytes=VMEM_BYTES),
        name="update",
    )(*row_pieces, *col_pieces, share)
    return result.reshape(half, 1, tile, col_tiles, 1, tile)


def per_device(trailing, panel, inverse_factor):
    layers = lax.axis_size("layer")
    count = lax.axis_size("row")
    row_tiles, _, tile, col_tiles, _, _ = trailing.shape
    half = row_tiles // layers
    slots = plane_slots(count)
    factor = make_factor(panel, inverse_factor, half)
    moved = lax.ppermute(
        factor, ("row", "col"), [(a * count + b, slots[a][b] * count + a) for a in range(count) for b in range(count)]
    )
    line = [factor] + [None] * (count - 1)
    for step in reversed(range(1, count)):
        line[step] = lax.ppermute(factor, "col", [(partner(b, step, count), b) for b in range(count)])
    lines = trailing.reshape(-1, LANES)
    share_lines = lines.shape[0] // layers
    share = lax.dynamic_slice_in_dim(lines, lax.axis_index("layer") * share_lines, share_lines, 0)
    moved, share = lax.optimization_barrier((moved, share))
    plane = [moved] + [None] * (count - 1)
    for step in reversed(range(1, count)):
        plane[step] = lax.ppermute(moved, "row", [(partner(a, step, count), a) for a in range(count)])
    others = []
    for shift in range(1, layers):
        pairs = [((l + shift) % layers, l) for l in range(layers)]
        others += [lax.ppermute(piece, "layer", pairs) for piece in plane]
    return update_trailing(line, plane + others, share, half, layers, tile, col_tiles)


def solution(mesh):
    assert mesh.shape["row"] == mesh.shape["col"]
    return jax.shard_map(
        per_device,
        mesh=mesh,
        in_specs=(P(None, "row", None, None, "col", None), P(None, "row", "col", None), P()),
        out_specs=P("layer", "row", None, None, "col", None),
        check_vma=False,
    )
```

time: 28.6 us -> 24.1 us (0.84)
  the two profiles are of different devices: /device:TPU:0 before, /device:TPU:25 now
where the time goes in v2:
time: 24.1 us; the launch traced here: 24 us
  starting transfers between devices  16.2 us (67%)
  Pallas kernels  4 us (17%)
  waiting for transfers between devices  1.94 us (8%)
  local copies, waits for them, and re-layouts  1.76 us (7%)
    ppermute x4, starting transfers between devices, per_device(): others += [lax.ppermute(piece, 'layer', pairs) for piece in plane]  8.98 us
    ppermute x3, starting transfers between devices, per_device(): lax.ppermute(factor, 'col', [(partner(b, step, count), b) for b in range(...  4.55 us
    ppermute x3, starting transfers between devices, per_device(): lax.ppermute(moved, 'row', [(partner(a, step, count), a) for a in range(c...  2.65 us
    pallas_call x1, Pallas kernels, make_factor(): pl.pallas_call(factor_kernel, out_shape=jax.ShapeDtypeStruct((half, tile_...  2.07 us
    pallas_call x1, Pallas kernels, update_trailing(): pl.pallas_call(body, out_shape=jax.ShapeDtypeStruct(share.shape, jnp.floa...  1.93 us
    dynamic_slice x1, local copies, waits for them, and re-layouts, per_device(): lax.dynamic_slice_in_dim(lines, lax.axis_index('layer') * share_lines, sh...  1.76 us
    ppermute x1, waiting for transfers between devices, per_device(): lax.ppermute(factor, ('row', 'col'), [(a * count + b, slots[a][b] * count...  1.04 us
    ppermute x4, waiting for transfers between devices, per_device(): others += [lax.ppermute(piece, 'layer', pairs) for piece in plane]  0.89 us
  transfers between devices with their start and end apart: 11, of which 2 were waited for; matrix products, arithmetic and copies ran while one was open for 7% of the time, Pallas kernels for 0%

profile of v2, /device:TPU:25, one launch (start us, length us, event | category | flops | bytes accessed | tf_op | source)
XLA Modules:
  0.0 24.0 jit_solution(15902427221221723350)
XLA Ops:
  0.0 2.1 %factor.1.refs_0_ = bf16[2,64,256]{2,1,0:T(8,128)(2,1)} custom-call(f32[4,1,64,256]{3,2,1,0:T(8,128)} %panel_ref.1, f32[256,256]{1,0:T(8,128)} %inverse_ref.1), custom_call_target="tpu_custom_call" | custom-call | tf_op jit(solution)/shard_map/factor/pallas_call | solution.py:39
  2.1 0.1 collective-permute-start.3
  2.1 1.1 %collective-permute-start.2 = (bf16[2,64,256]{2,1,0:T(8,128)(2,1)}, bf16[2,64,256]{2,1,0:T(8,128)(2,1)S(1)}, u32[]{:S(2)}, u32[]{:S(2)}) collective-permute-start(bf16[2,64,256]{2,1,0:T(8,128)(2,1)} %factor.1.refs_0_), channel_id=1, source_target_pairs={{6,0},{4,2},{2,4},{0,6},{7,1},{5,3},{3,5},{1,7},{14,8},{12,10},{10... | collective-permute-start | bytes 196616 | tf_op jit(solution)/shard_map/ppermute | solution.py:147
  3.3 1.2 %collective-permute-start.1 = (bf16[2,64,256]{2,1,0:T(8,128)(2,1)}, bf16[2,64,256]{2,1,0:T(8,128)(2,1)S(1)}, u32[]{:S(2)}, u32[]{:S(2)}) collective-permute-start(bf16[2,64,256]{2,1,0:T(8,128)(2,1)} %factor.1.refs_0_), channel_id=1, source_target_pairs={{4,0},{6,2},{0,4},{2,6},{5,1},{7,3},{1,5},{3,7},{12,8},{14,10},{8,... | collective-permute-start | bytes 196616 | tf_op jit(solution)/shard_map/ppermute | solution.py:147
  4.5 0.0 copy-start
  4.5 1.8 %constant_dynamic-slice_fusion.refs_12_ = f32[4096,128]{1,0:T(8,128)S(1)} fusion(f32[8192,128]{1,0:T(8,128)} %bitcast.2, s32[]{:T(128)S(6)} %select_n.3), kind=kLoop, calls=%fused_computation | loop fusion | bytes 4194308 | tf_op jit(solution)/shard_map/dynamic_slice | solution.py:150
  6.3 1.0 %collective-permute-done.3.refs_4_ = bf16[2,64,256]{2,1,0:T(8,128)(2,1)S(1)} collective-permute-done((bf16[2,64,256]{2,1,0:T(8,128)(2,1)}, bf16[2,64,256]{2,1,0:T(8,128)(2,1)S(1)}, u32[]{:S(2)}, u32[]{:S(2)}) %collective-permute-start.3) | collective-permute-done | bytes 65568 | tf_op jit(solution)/shard_map/ppermute | solution.py:142
  7.3 2.2 %collective-permute-start.6 = (bf16[2,64,256]{2,1,0:T(8,128)(2,1)S(1)}, bf16[2,64,256]{2,1,0:T(8,128)(2,1)S(1)}, u32[]{:S(2)}, u32[]{:S(2)}) collective-permute-start(bf16[2,64,256]{2,1,0:T(8,128)(2,1)S(1)} %collective-permute-done.3.refs_4_), channel_id=1, source_target_pairs={{24,0},{16,8},{8,16},{0,24},{25,1},{17,9},{9,17},{1,25},{26,2},{18... | collective-permute-start | bytes 196616 | tf_op jit(solution)/shard_map/ppermute | solution.py:154
  9.5 0.2 collective-permute-start.5
  9.7 0.2 %collective-permute-start.4 = (bf16[2,64,256]{2,1,0:T(8,128)(2,1)S(1)}, bf16[2,64,256]{2,1,0:T(8,128)(2,1)S(1)}, u32[]{:S(2)}, u32[]{:S(2)}) collective-permute-start(bf16[2,64,256]{2,1,0:T(8,128)(2,1)S(1)} %collective-permute-done.3.refs_4_), channel_id=1, source_target_pairs={{8,0},{0,8},{24,16},{16,24},{9,1},{1,9},{25,17},{17,25},{10,2},{2,... | collective-permute-start | bytes 196616 | tf_op jit(solution)/shard_map/ppermute | solution.py:154
  9.9 0.0 collective-permute-done.2.refs_3_
  9.9 0.0 copy-done
  10.0 2.2 %collective-permute-start = (bf16[2,64,256]{2,1,0:T(8,128)(2,1)S(1)}, bf16[2,64,256]{2,1,0:T(8,128)(2,1)S(1)}, u32[]{:S(2)}, u32[]{:S(2)}) collective-permute-start(bf16[2,64,256]{2,1,0:T(8,128)(2,1)S(1)} %copy-done), channel_id=1, source_target_pairs={{2,0},{0,2},{6,4},{4,6},{3,1},{1,3},{7,5},{5,7},{10,8},{8,10},{14,... | collective-permute-start | bytes 196616 | tf_op jit(solution)/shard_map/ppermute | solution.py:147
  12.2 0.0 collective-permute-done.1.refs_2_
  12.2 4.9 %collective-permute-start.7 = (bf16[2,64,256]{2,1,0:T(8,128)(2,1)S(1)}, bf16[2,64,256]{2,1,0:T(8,128)(2,1)S(1)}, u32[]{:S(2)}, u32[]{:S(2)}) collective-permute-start(bf16[2,64,256]{2,1,0:T(8,128)(2,1)S(1)} %collective-permute-done.3.refs_4_), channel_id=1, source_target_pairs={{1,0},{0,1},{3,2},{2,3},{5,4},{4,5},{7,6},{6,7},{9,8},{8,9},{11,10... | collective-permute-start | bytes 196616 | tf_op jit(solution)/shard_map/ppermute | solution.py:158
  17.0 0.0 collective-permute-done.6.refs_7_
  17.1 0.1 collective-permute-start.10
  17.1 0.0 collective-permute-done.5.refs_6_
  17.1 2.0 %collective-permute-start.9 = (bf16[2,64,256]{2,1,0:T(8,128)(2,1)S(1)}, bf16[2,64,256]{2,1,0:T(8,128)(2,1)S(1)}, u32[]{:S(2)}, u32[]{:S(2)}) collective-permute-start(bf16[2,64,256]{2,1,0:T(8,128)(2,1)S(1)} %collective-permute-done.5.refs_6_), channel_id=1, source_target_pairs={{1,0},{0,1},{3,2},{2,3},{5,4},{4,5},{7,6},{6,7},{9,8},{8,9},{11,10... | collective-permute-start | bytes 196616 | tf_op jit(solution)/shard_map/ppermute | solution.py:158
  19.1 0.0 collective-permute-done.4.refs_5_
  19.1 2.0 %collective-permute-start.8 = (bf16[2,64,256]{2,1,0:T(8,128)(2,1)S(1)}, bf16[2,64,256]{2,1,0:T(8,128)(2,1)S(1)}, u32[]{:S(2)}, u32[]{:S(2)}) collective-permute-start(bf16[2,64,256]{2,1,0:T(8,128)(2,1)S(1)} %collective-permute-done.4.refs_5_), channel_id=1, source_target_pairs={{1,0},{0,1},{3,2},{2,3},{5,4},{4,5},{7,6},{6,7},{9,8},{8,9},{11,10... | collective-permute-start | bytes 196616 | tf_op jit(solution)/shard_map/ppermute | solution.py:158
  21.1 0.0 collective-permute-done.refs_1_
  21.2 0.0 collective-permute-done.7.refs_8_
  21.2 0.0 collective-permute-done.10.refs_11_
  21.2 0.0 collective-permute-done.9.refs_10_
  21.2 0.9 %collective-permute-done.8.refs_9_ = bf16[2,64,256]{2,1,0:T(8,128)(2,1)S(1)} collective-permute-done((bf16[2,64,256]{2,1,0:T(8,128)(2,1)S(1)}, bf16[2,64,256]{2,1,0:T(8,128)(2,1)S(1)}, u32[]{:S(2)}, u32[]{:S(2)}) %collective-permute-start.8) | collective-permute-done | bytes 65568 | tf_op jit(solution)/shard_map/ppermute | solution.py:158
  22.1 1.9 %update.1 = f32[4096,128]{1,0:T(8,128)} custom-call(bf16[2,64,256]{2,1,0:T(8,128)(2,1)S(1)} %copy-done, bf16[2,64,256]{2,1,0:T(8,128)(2,1)S(1)} %collective-permute-done.refs_1_, bf16[2,64,256]{2,1,0:T(8,128)(2,1)S(1)} %collective-permute-done.1.refs_2_, bf16[2,64,256]{2,1,0:T(8,128)(2,1)S(1)} %collective-permute-done.2.refs_3_, ...), custom_call_target="tpu_custom_call" | custom-call | tf_op jit(solution)/shard_map/update/pallas_call | solution.py:118
Async XLA Ops:
  2.1 5.2 %collective-permute-start.3 = (bf16[2,64,256]{2,1,0:T(8,128)(2,1)}, bf16[2,64,256]{2,1,0:T(8,128)(2,1)S(1)}, u32[]{:S(2)}, u32[]{:S(2)}) collective-permute-start(bf16[2,64,256]{2,1,0:T(8,128)(2,1)} %factor.1.refs_0_), channel_id=1, source_target_pairs={{0,8},{2,24},{4,16},{6,0},{8,2},{10,18},{12,10},{14,26},{16,20},{1... | collective-permute-start | bytes 196616 | tf_op jit(solution)/shard_map/ppermute | solution.py:142
  2.1 7.8 %collective-permute-start.2 = (bf16[2,64,256]{2,1,0:T(8,128)(2,1)}, bf16[2,64,256]{2,1,0:T(8,128)(2,1)S(1)}, u32[]{:S(2)}, u32[]{:S(2)}) collective-permute-start(bf16[2,64,256]{2,1,0:T(8,128)(2,1)} %factor.1.refs_0_), channel_id=1, source_target_pairs={{6,0},{4,2},{2,4},{0,6},{7,1},{5,3},{3,5},{1,7},{14,8},{12,10},{10... | collective-permute-start | bytes 196616 | tf_op jit(solution)/shard_map/ppermute | solution.py:147
  3.3 8.9 %collective-permute-start.1 = (bf16[2,64,256]{2,1,0:T(8,128)(2,1)}, bf16[2,64,256]{2,1,0:T(8,128)(2,1)S(1)}, u32[]{:S(2)}, u32[]{:S(2)}) collective-permute-start(bf16[2,64,256]{2,1,0:T(8,128)(2,1)} %factor.1.refs_0_), channel_id=1, source_target_pairs={{4,0},{6,2},{0,4},{2,6},{5,1},{7,3},{1,5},{3,7},{12,8},{14,10},{8,... | collective-permute-start | bytes 196616 | tf_op jit(solution)/shard_map/ppermute | solution.py:147
  4.5 5.5 %copy-start = (bf16[2,64,256]{2,1,0:T(8,128)(2,1)S(1)}, bf16[2,64,256]{2,1,0:T(8,128)(2,1)}, u32[]{:S(2)}) copy-start(bf16[2,64,256]{2,1,0:T(8,128)(2,1)} %factor.1.refs_0_) | copy-start | bytes 196612
  7.3 9.8 %collective-permute-start.6 = (bf16[2,64,256]{2,1,0:T(8,128)(2,1)S(1)}, bf16[2,64,256]{2,1,0:T(8,128)(2,1)S(1)}, u32[]{:S(2)}, u32[]{:S(2)}) collective-permute-start(bf16[2,64,256]{2,1,0:T(8,128)(2,1)S(1)} %collective-permute-done.3.refs_4_), channel_id=1, source_target_pairs={{24,0},{16,8},{8,16},{0,24},{25,1},{17,9},{9,17},{1,25},{26,2},{18... | collective-permute-start | bytes 196616 | tf_op jit(solution)/shard_map/ppermute | solution.py:154
  9.5 7.6 %collective-permute-start.5 = (bf16[2,64,256]{2,1,0:T(8,128)(2,1)S(1)}, bf16[2,64,256]{2,1,0:T(8,128)(2,1)S(1)}, u32[]{:S(2)}, u32[]{:S(2)}) collective-permute-start(bf16[2,64,256]{2,1,0:T(8,128)(2,1)S(1)} %collective-permute-done.3.refs_4_), channel_id=1, source_target_pairs={{16,0},{24,8},{0,16},{8,24},{17,1},{25,9},{1,17},{9,25},{18,2},{26... | collective-permute-start | bytes 196616 | tf_op jit(solution)/shard_map/ppermute | solution.py:154
  9.7 9.4 %collective-permute-start.4 = (bf16[2,64,256]{2,1,0:T(8,128)(2,1)S(1)}, bf16[2,64,256]{2,1,0:T(8,128)(2,1)S(1)}, u32[]{:S(2)}, u32[]{:S(2)}) collective-permute-start(bf16[2,64,256]{2,1,0:T(8,128)(2,1)S(1)} %collective-permute-done.3.refs_4_), channel_id=1, source_target_pairs={{8,0},{0,8},{24,16},{16,24},{9,1},{1,9},{25,17},{17,25},{10,2},{2,... | collective-permute-start | bytes 196616 | tf_op jit(solution)/shard_map/ppermute | solution.py:154
  10.0 11.2 %collective-permute-start = (bf16[2,64,256]{2,1,0:T(8,128)(2,1)S(1)}, bf16[2,64,256]{2,1,0:T(8,128)(2,1)S(1)}, u32[]{:S(2)}, u32[]{:S(2)}) collective-permute-start(bf16[2,64,256]{2,1,0:T(8,128)(2,1)S(1)} %copy-done), channel_id=1, source_target_pairs={{2,0},{0,2},{6,4},{4,6},{3,1},{1,3},{7,5},{5,7},{10,8},{8,10},{14,... | collective-permute-start | bytes 196616 | tf_op jit(solution)/shard_map/ppermute | solution.py:147
  12.2 9.0 %collective-permute-start.7 = (bf16[2,64,256]{2,1,0:T(8,128)(2,1)S(1)}, bf16[2,64,256]{2,1,0:T(8,128)(2,1)S(1)}, u32[]{:S(2)}, u32[]{:S(2)}) collective-permute-start(bf16[2,64,256]{2,1,0:T(8,128)(2,1)S(1)} %collective-permute-done.3.refs_4_), channel_id=1, source_target_pairs={{1,0},{0,1},{3,2},{2,3},{5,4},{4,5},{7,6},{6,7},{9,8},{8,9},{11,10... | collective-permute-start | bytes 196616 | tf_op jit(solution)/shard_map/ppermute | solution.py:158
  17.1 4.1 %collective-permute-start.10 = (bf16[2,64,256]{2,1,0:T(8,128)(2,1)S(1)}, bf16[2,64,256]{2,1,0:T(8,128)(2,1)S(1)}, u32[]{:S(2)}, u32[]{:S(2)}) collective-permute-start(bf16[2,64,256]{2,1,0:T(8,128)(2,1)S(1)} %collective-permute-done.6.refs_7_), channel_id=1, source_target_pairs={{1,0},{0,1},{3,2},{2,3},{5,4},{4,5},{7,6},{6,7},{9,8},{8,9},{11,10... | collective-permute-start | bytes 196616 | tf_op jit(solution)/shard_map/ppermute | solution.py:158
  17.1 4.0 %collective-permute-start.9 = (bf16[2,64,256]{2,1,0:T(8,128)(2,1)S(1)}, bf16[2,64,256]{2,1,0:T(8,128)(2,1)S(1)}, u32[]{:S(2)}, u32[]{:S(2)}) collective-permute-start(bf16[2,64,256]{2,1,0:T(8,128)(2,1)S(1)} %collective-permute-done.5.refs_6_), channel_id=1, source_target_pairs={{1,0},{0,1},{3,2},{2,3},{5,4},{4,5},{7,6},{6,7},{9,8},{8,9},{11,10... | collective-permute-start | bytes 196616 | tf_op jit(solution)/shard_map/ppermute | solution.py:158
  19.1 2.9 %collective-permute-start.8 = (bf16[2,64,256]{2,1,0:T(8,128)(2,1)S(1)}, bf16[2,64,256]{2,1,0:T(8,128)(2,1)S(1)}, u32[]{:S(2)}, u32[]{:S(2)}) collective-permute-start(bf16[2,64,256]{2,1,0:T(8,128)(2,1)S(1)} %collective-permute-done.4.refs_5_), channel_id=1, source_target_pairs={{1,0},{0,1},{3,2},{2,3},{5,4},{4,5},{7,6},{6,7},{9,8},{8,9},{11,10... | collective-permute-start | bytes 196616 | tf_op jit(solution)/shard_map/ppermute | solution.py:158

commit v3 on v2

--- a/solution.py
+++ b/solution.py
@@ -69,20 +69,62 @@
     return slab
 
 
-def update_kernel(pieces, layers, half, tile, tile_rows, col_tiles, *refs):
-    row_refs = refs[:pieces]
-    col_refs = refs[pieces : pieces * (1 + layers)]
-    share_ref, out_ref, row_buf, col_buf, out_buf, out_sems = refs[pieces * (1 + layers) :]
+def gather_line(factor, count):
+    everywhere = range(count)
+    if count != 4:
+        pairs = {step: [(partner(b, step, count), b) for b in everywhere] for step in range(1, count)}
+        moves = [(lax.ppermute(factor, "col", pairs[step]), {b: a for a, b in pairs[step]}) for step in pairs]
+        return [(factor, {b: b for b in everywhere})] + moves
+    near = [(0, 1), (1, 0), (2, 3), (3, 2)]
+    far = [(0, 2), (2, 0), (1, 3), (3, 1)]
+    inner = [(1, 2), (2, 1)]
+    outer = [(1, 0), (2, 3)]
+    from_far = lax.ppermute(factor, "col", far)
+    from_near = lax.ppermute(factor, "col", near)
+    from_inner = lax.ppermute(factor, "col", inner)
+    from_outer = lax.ppermute(from_far, "col", outer)
+    return [
+        (factor, {b: b for b in everywhere}),
+        (from_near, {b: a for a, b in near}),
+        (from_far, {b: a for a, b in far}),
+        (from_inner, {b: a for a, b in inner}),
+        (from_outer, {0: 3, 3: 0}),
+    ]
+
+
+def lookup(table, index):
+    value = jnp.int32(0)
+    for key, entry in table.items():
+        value = jnp.where(index == key, entry, value)
+    return value
+
+
+def update_kernel(sources, pieces, layers, half, tile, tile_rows, col_tiles, *refs):
+    rows = len(sources)
+    row_refs = refs[:rows]
+    col_refs = refs[rows : rows + pieces * layers]
+    share_ref, out_ref, row_buf, col_buf, out_buf, out_sems = refs[rows + pieces * layers :]
     r, c, layer = (lax.axis_index(axis) for axis in AXES)
     slots = plane_slots(pieces)
     lines = tile * col_tiles * tile // LANES
     per_row = col_tiles * tile // LANES
+    for source, row_ref in zip(sources, row_refs):
+        row_at = pl.multiple_of(lookup(source, c) * tile_rows, tile_rows)
+
+        def place_rows(row_ref=row_ref, row_at=row_at):
+            for k in range(half):
+                row_buf[k, pl.ds(row_at, tile_rows), :] = row_ref[k]
+
+        if len(source) == pieces:
+            place_rows()
+        else:
+            here = c == next(iter(source))
+            for key in source:
+                here = here | (c == key)
+            pl.when(here)(place_rows)
     for step in range(pieces):
-        row_at = pl.multiple_of(partner(c, step, pieces) * tile_rows, tile_rows)
         slab = slab_of(slots, c, partner(r, step, pieces))
         col_at = pl.multiple_of(slab * tile_rows, tile_rows)
-        for k in range(half):
-            row_buf[k, pl.ds(row_at, tile_rows), :] = row_refs[step][k]
         for shift in range(layers):
             owner = lax.rem(layer + shift, layers)
             for k in range(half):
@@ -107,18 +149,19 @@
         store.wait()
 
 
-def update_trailing(row_pieces, col_pieces, share, half, layers, tile, col_tiles):
-    pieces = len(row_pieces)
+def update_trailing(line, col_pieces, share, half, layers, tile, col_tiles):
+    row_pieces, sources = zip(*line)
+    pieces = len(col_pieces) // layers
     tile_rows = row_pieces[0].shape[1]
     width = row_pieces[0].shape[2]
 
     def body(*refs):
-        update_kernel(pieces, layers, half, tile, tile_rows, col_tiles, *refs)
+        update_kernel(sources, pieces, layers, half, tile, tile_rows, col_tiles, *refs)
 
     result = pl.pallas_call(
         body,
         out_shape=jax.ShapeDtypeStruct(share.shape, jnp.float32),
-        in_specs=[pl.BlockSpec(memory_space=pltpu.VMEM)] * (pieces * (1 + layers) + 1),
+        in_specs=[pl.BlockSpec(memory_space=pltpu.VMEM)] * (len(row_pieces) + len(col_pieces) + 1),
         out_specs=pl.BlockSpec(memory_space=pltpu.HBM),
         scratch_shapes=[
             pltpu.VMEM((half, tile, width), jnp.bfloat16),
@@ -142,9 +185,7 @@
     moved = lax.ppermute(
         factor, ("row", "col"), [(a * count + b, slots[a][b] * count + a) for a in range(count) for b in range(count)]
     )
-    line = [factor] + [None] * (count - 1)
-    for step in reversed(range(1, count)):
-        line[step] = lax.ppermute(factor, "col", [(partner(b, step, count), b) for b in range(count)])
+    line = gather_line(factor, count)
     lines = trailing.reshape(-1, LANES)
     share_lines = lines.shape[0] // layers
     share = lax.dynamic_slice_in_dim(lines, lax.axis_index("layer") * share_lines, share_lines, 0)

time: 24.1 us -> 24.8 us (1.029)
  the two profiles are of different devices: /device:TPU:25 before, /device:TPU:0 now
where the time goes in v3:
time: 24.8 us; the launch traced here: 24.6 us
  starting transfers between devices  14.4 us (58%)
  waiting for transfers between devices  4.41 us (18%)
  Pallas kernels  4.03 us (16%)
  local copies, waits for them, and re-layouts  1.76 us (7%)
    ppermute x1, starting transfers between devices, gather_line(): from_far = lax.ppermute(factor, 'col', far)  5.19 us
    ppermute x3, starting transfers between devices, per_device(): lax.ppermute(moved, 'row', [(partner(a, step, count), a) for a in range(c...  3.55 us
    ppermute x1, starting transfers between devices, per_device(): lax.ppermute(factor, ('row', 'col'), [(a * count + b, slots[a][b] * count...  2.99 us
    ppermute x1, waiting for transfers between devices, gather_line(): from_outer = lax.ppermute(from_far, 'col', outer)  2.46 us
    pallas_call x1, Pallas kernels, make_factor(): pl.pallas_call(factor_kernel, out_shape=jax.ShapeDtypeStruct((half, tile_...  2.07 us
    pallas_call x1, Pallas kernels, update_trailing(): pl.pallas_call(body, out_shape=jax.ShapeDtypeStruct(share.shape, jnp.floa...  1.96 us
    ppermute x3, waiting for transfers between devices, per_device(): lax.ppermute(moved, 'row', [(partner(a, step, count), a) for a in range(c...  1.93 us
    dynamic_slice x1, local copies, waits for them, and re-layouts, per_device(): lax.dynamic_slice_in_dim(lines, lax.axis_index('layer') * share_lines, sh...  1.76 us
  transfers between devices with their start and end apart: 12, of which 3 were waited for; matrix products, arithmetic and copies ran while one was open for 7% of the time, Pallas kernels for 0%

profile of v3, /device:TPU:0, one launch (start us, length us, event | category | flops | bytes accessed | tf_op | source)
XLA Modules:
  0.0 24.6 jit_solution(4684974257022368184)
XLA Ops:
  0.0 2.1 %factor.1.refs_0_ = bf16[2,64,256]{2,1,0:T(8,128)(2,1)} custom-call(f32[4,1,64,256]{3,2,1,0:T(8,128)} %panel_ref.1, f32[256,256]{1,0:T(8,128)} %inverse_ref.1), custom_call_target="tpu_custom_call" | custom-call | tf_op jit(solution)/shard_map/factor/pallas_call | solution.py:39
  2.1 3.0 %collective-permute-start.4 = (bf16[2,64,256]{2,1,0:T(8,128)(2,1)}, bf16[2,64,256]{2,1,0:T(8,128)(2,1)S(1)}, u32[]{:S(2)}, u32[]{:S(2)}) collective-permute-start(bf16[2,64,256]{2,1,0:T(8,128)(2,1)} %factor.1.refs_0_), channel_id=1, source_target_pairs={{0,8},{2,24},{4,16},{6,0},{8,2},{10,18},{12,10},{14,26},{16,20},{1... | collective-permute-start | bytes 196616 | tf_op jit(solution)/shard_map/ppermute | solution.py:185
  5.1 0.7 %collective-permute-start.2 = (bf16[2,64,256]{2,1,0:T(8,128)(2,1)}, bf16[2,64,256]{2,1,0:T(8,128)(2,1)S(1)}, u32[]{:S(2)}, u32[]{:S(2)}) collective-permute-start(bf16[2,64,256]{2,1,0:T(8,128)(2,1)} %factor.1.refs_0_), channel_id=1, source_target_pairs={{2,4},{4,2},{3,5},{5,3},{10,12},{12,10},{11,13},{13,11},{18,20},{2... | collective-permute-start | bytes 196616 | tf_op jit(solution)/shard_map/ppermute | solution.py:84
  5.7 5.2 %collective-permute-start.1 = (bf16[2,64,256]{2,1,0:T(8,128)(2,1)}, bf16[2,64,256]{2,1,0:T(8,128)(2,1)S(1)}, u32[]{:S(2)}, u32[]{:S(2)}) collective-permute-start(bf16[2,64,256]{2,1,0:T(8,128)(2,1)} %factor.1.refs_0_), channel_id=1, source_target_pairs={{0,4},{4,0},{2,6},{6,2},{1,5},{5,1},{3,7},{7,3},{8,12},{12,8},{10,... | collective-permute-start | bytes 196616 | tf_op jit(solution)/shard_map/ppermute | solution.py:82
  10.9 0.0 collective-permute-start
  10.9 0.0 copy-start
  10.9 1.8 %constant_dynamic-slice_fusion.refs_13_ = f32[4096,128]{1,0:T(8,128)S(1)} fusion(f32[8192,128]{1,0:T(8,128)} %bitcast.2, s32[]{:T(128)S(6)} %select_n.3), kind=kLoop, calls=%fused_computation | loop fusion | bytes 4194308 | tf_op jit(solution)/shard_map/dynamic_slice | solution.py:191
  12.7 0.0 collective-permute-done.4.refs_5_
  12.7 2.7 %collective-permute-start.7 = (bf16[2,64,256]{2,1,0:T(8,128)(2,1)S(1)}, bf16[2,64,256]{2,1,0:T(8,128)(2,1)S(1)}, u32[]{:S(2)}, u32[]{:S(2)}) collective-permute-start(bf16[2,64,256]{2,1,0:T(8,128)(2,1)S(1)} %collective-permute-done.4.refs_5_), channel_id=1, source_target_pairs={{24,0},{16,8},{8,16},{0,24},{25,1},{17,9},{9,17},{1,25},{26,2},{18... | collective-permute-start | bytes 196616 | tf_op jit(solution)/shard_map/ppermute | solution.py:195
  15.4 0.0 collective-permute-start.6
  15.4 0.0 collective-permute-done.2.refs_3_
  15.4 0.8 %collective-permute-start.5 = (bf16[2,64,256]{2,1,0:T(8,128)(2,1)S(1)}, bf16[2,64,256]{2,1,0:T(8,128)(2,1)S(1)}, u32[]{:S(2)}, u32[]{:S(2)}) collective-permute-start(bf16[2,64,256]{2,1,0:T(8,128)(2,1)S(1)} %collective-permute-done.4.refs_5_), channel_id=1, source_target_pairs={{8,0},{0,8},{24,16},{16,24},{9,1},{1,9},{25,17},{17,25},{10,2},{2,... | collective-permute-start | bytes 196616 | tf_op jit(solution)/shard_map/ppermute | solution.py:195
  16.3 0.0 collective-permute-done.1.refs_2_
  16.3 0.0 collective-permute-start.8
  16.3 0.0 collective-permute-done.refs_1_
  16.3 1.3 %collective-permute-start.3 = (bf16[2,64,256]{2,1,0:T(8,128)(2,1)S(1)}, bf16[2,64,256]{2,1,0:T(8,128)(2,1)S(1)}, u32[]{:S(2)}, u32[]{:S(2)}) collective-permute-start(bf16[2,64,256]{2,1,0:T(8,128)(2,1)S(1)} %collective-permute-done.1.refs_2_), channel_id=1, source_target_pairs={{2,0},{4,6},{3,1},{5,7},{10,8},{12,14},{11,9},{13,15},{18,16},{20,... | collective-permute-start | bytes 196616 | tf_op jit(solution)/shard_map/ppermute | solution.py:85
  17.6 0.4 %collective-permute-done.7.refs_8_ = bf16[2,64,256]{2,1,0:T(8,128)(2,1)S(1)} collective-permute-done((bf16[2,64,256]{2,1,0:T(8,128)(2,1)S(1)}, bf16[2,64,256]{2,1,0:T(8,128)(2,1)S(1)}, u32[]{:S(2)}, u32[]{:S(2)}) %collective-permute-start.7) | collective-permute-done | bytes 65568 | tf_op jit(solution)/shard_map/ppermute | solution.py:195
  18.0 0.2 collective-permute-start.11
  18.1 1.5 %collective-permute-done.6.refs_7_ = bf16[2,64,256]{2,1,0:T(8,128)(2,1)S(1)} collective-permute-done((bf16[2,64,256]{2,1,0:T(8,128)(2,1)S(1)}, bf16[2,64,256]{2,1,0:T(8,128)(2,1)S(1)}, u32[]{:S(2)}, u32[]{:S(2)}) %collective-permute-start.6) | collective-permute-done | bytes 65568 | tf_op jit(solution)/shard_map/ppermute | solution.py:195
  19.7 0.0 collective-permute-start.10
  19.7 0.0 collective-permute-done.5.refs_6_
  19.7 0.5 %collective-permute-start.9 = (bf16[2,64,256]{2,1,0:T(8,128)(2,1)S(1)}, bf16[2,64,256]{2,1,0:T(8,128)(2,1)S(1)}, u32[]{:S(2)}, u32[]{:S(2)}) collective-permute-start(bf16[2,64,256]{2,1,0:T(8,128)(2,1)S(1)} %collective-permute-done.5.refs_6_), channel_id=1, source_target_pairs={{1,0},{0,1},{3,2},{2,3},{5,4},{4,5},{7,6},{6,7},{9,8},{8,9},{11,10... | collective-permute-start | bytes 196616 | tf_op jit(solution)/shard_map/ppermute | solution.py:199
  20.2 2.5 %collective-permute-done.3.refs_4_ = bf16[2,64,256]{2,1,0:T(8,128)(2,1)S(1)} collective-permute-done((bf16[2,64,256]{2,1,0:T(8,128)(2,1)S(1)}, bf16[2,64,256]{2,1,0:T(8,128)(2,1)S(1)}, u32[]{:S(2)}, u32[]{:S(2)}) %collective-permute-start.3) | collective-permute-done | bytes 65568 | tf_op jit(solution)/shard_map/ppermute | solution.py:85
  22.6 0.0 collective-permute-done.8.refs_9_
  22.7 0.0 collective-permute-done.11.refs_12_
  22.7 0.0 collective-permute-done.10.refs_11_
  22.7 0.0 collective-permute-done.9.refs_10_
  22.7 0.0 copy-done
  22.7 2.0 %update.1 = f32[4096,128]{1,0:T(8,128)} custom-call(bf16[2,64,256]{2,1,0:T(8,128)(2,1)S(1)} %copy-done, bf16[2,64,256]{2,1,0:T(8,128)(2,1)S(1)} %collective-permute-done.refs_1_, bf16[2,64,256]{2,1,0:T(8,128)(2,1)S(1)} %collective-permute-done.1.refs_2_, bf16[2,64,256]{2,1,0:T(8,128)(2,1)S(1)} %collective-permute-done.2.refs_3_, ...), custom_call_target="tpu_custom_call" | custom-call | tf_op jit(solution)/shard_map/update/pallas_call | solution.py:161
Async XLA Ops:
  2.1 10.6 %collective-permute-start.4 = (bf16[2,64,256]{2,1,0:T(8,128)(2,1)}, bf16[2,64,256]{2,1,0:T(8,128)(2,1)S(1)}, u32[]{:S(2)}, u32[]{:S(2)}) collective-permute-start(bf16[2,64,256]{2,1,0:T(8,128)(2,1)} %factor.1.refs_0_), channel_id=1, source_target_pairs={{0,8},{2,24},{4,16},{6,0},{8,2},{10,18},{12,10},{14,26},{16,20},{1... | collective-permute-start | bytes 196616 | tf_op jit(solution)/shard_map/ppermute | solution.py:185
  5.1 10.3 %collective-permute-start.2 = (bf16[2,64,256]{2,1,0:T(8,128)(2,1)}, bf16[2,64,256]{2,1,0:T(8,128)(2,1)S(1)}, u32[]{:S(2)}, u32[]{:S(2)}) collective-permute-start(bf16[2,64,256]{2,1,0:T(8,128)(2,1)} %factor.1.refs_0_), channel_id=1, source_target_pairs={{2,4},{4,2},{3,5},{5,3},{10,12},{12,10},{11,13},{13,11},{18,20},{2... | collective-permute-start | bytes 196616 | tf_op jit(solution)/shard_map/ppermute | solution.py:84
  5.7 10.5 %collective-permute-start.1 = (bf16[2,64,256]{2,1,0:T(8,128)(2,1)}, bf16[2,64,256]{2,1,0:T(8,128)(2,1)S(1)}, u32[]{:S(2)}, u32[]{:S(2)}) collective-permute-start(bf16[2,64,256]{2,1,0:T(8,128)(2,1)} %factor.1.refs_0_), channel_id=1, source_target_pairs={{0,4},{4,0},{2,6},{6,2},{1,5},{5,1},{3,7},{7,3},{8,12},{12,8},{10,... | collective-permute-start | bytes 196616 | tf_op jit(solution)/shard_map/ppermute | solution.py:82
  10.9 5.3 %collective-permute-start = (bf16[2,64,256]{2,1,0:T(8,128)(2,1)}, bf16[2,64,256]{2,1,0:T(8,128)(2,1)S(1)}, u32[]{:S(2)}, u32[]{:S(2)}) collective-permute-start(bf16[2,64,256]{2,1,0:T(8,128)(2,1)} %factor.1.refs_0_), channel_id=1, source_target_pairs={{0,2},{2,0},{4,6},{6,4},{1,3},{3,1},{5,7},{7,5},{8,10},{10,8},{12,... | collective-permute-start | bytes 196616 | tf_op jit(solution)/shard_map/ppermute | solution.py:83
  10.9 11.8 %copy-start = (bf16[2,64,256]{2,1,0:T(8,128)(2,1)S(1)}, bf16[2,64,256]{2,1,0:T(8,128)(2,1)}, u32[]{:S(2)}) copy-start(bf16[2,64,256]{2,1,0:T(8,128)(2,1)} %factor.1.refs_0_) | copy-start | bytes 196612
  12.7 5.3 %collective-permute-start.7 = (bf16[2,64,256]{2,1,0:T(8,128)(2,1)S(1)}, bf16[2,64,256]{2,1,0:T(8,128)(2,1)S(1)}, u32[]{:S(2)}, u32[]{:S(2)}) collective-permute-start(bf16[2,64,256]{2,1,0:T(8,128)(2,1)S(1)} %collective-permute-done.4.refs_5_), channel_id=1, source_target_pairs={{24,0},{16,8},{8,16},{0,24},{25,1},{17,9},{9,17},{1,25},{26,2},{18... | collective-permute-start | bytes 196616 | tf_op jit(solution)/shard_map/ppermute | solution.py:195
  15.4 4.3 %collective-permute-start.6 = (bf16[2,64,256]{2,1,0:T(8,128)(2,1)S(1)}, bf16[2,64,256]{2,1,0:T(8,128)(2,1)S(1)}, u32[]{:S(2)}, u32[]{:S(2)}) collective-permute-start(bf16[2,64,256]{2,1,0:T(8,128)(2,1)S(1)} %collective-permute-done.4.refs_5_), channel_id=1, source_target_pairs={{16,0},{24,8},{0,16},{8,24},{17,1},{25,9},{1,17},{9,25},{18,2},{26... | collective-permute-start | bytes 196616 | tf_op jit(solution)/shard_map/ppermute | solution.py:195
  15.4 4.3 %collective-permute-start.5 = (bf16[2,64,256]{2,1,0:T(8,128)(2,1)S(1)}, bf16[2,64,256]{2,1,0:T(8,128)(2,1)S(1)}, u32[]{:S(2)}, u32[]{:S(2)}) collective-permute-start(bf16[2,64,256]{2,1,0:T(8,128)(2,1)S(1)} %collective-permute-done.4.refs_5_), channel_id=1, source_target_pairs={{8,0},{0,8},{24,16},{16,24},{9,1},{1,9},{25,17},{17,25},{10,2},{2,... | collective-permute-start | bytes 196616 | tf_op jit(solution)/shard_map/ppermute | solution.py:195
  16.3 6.4 %collective-permute-start.8 = (bf16[2,64,256]{2,1,0:T(8,128)(2,1)S(1)}, bf16[2,64,256]{2,1,0:T(8,128)(2,1)S(1)}, u32[]{:S(2)}, u32[]{:S(2)}) collective-permute-start(bf16[2,64,256]{2,1,0:T(8,128)(2,1)S(1)} %collective-permute-done.4.refs_5_), channel_id=1, source_target_pairs={{1,0},{0,1},{3,2},{2,3},{5,4},{4,5},{7,6},{6,7},{9,8},{8,9},{11,10... | collective-permute-start | bytes 196616 | tf_op jit(solution)/shard_map/ppermute | solution.py:199
  16.3 6.4 %collective-permute-start.3 = (bf16[2,64,256]{2,1,0:T(8,128)(2,1)S(1)}, bf16[2,64,256]{2,1,0:T(8,128)(2,1)S(1)}, u32[]{:S(2)}, u32[]{:S(2)}) collective-permute-start(bf16[2,64,256]{2,1,0:T(8,128)(2,1)S(1)} %collective-permute-done.1.refs_2_), channel_id=1, source_target_pairs={{2,0},{4,6},{3,1},{5,7},{10,8},{12,14},{11,9},{13,15},{18,16},{20,... | collective-permute-start | bytes 196616 | tf_op jit(solution)/shard_map/ppermute | solution.py:85
  18.0 4.7 %collective-permute-start.11 = (bf16[2,64,256]{2,1,0:T(8,128)(2,1)S(1)}, bf16[2,64,256]{2,1,0:T(8,128)(2,1)S(1)}, u32[]{:S(2)}, u32[]{:S(2)}) collective-permute-start(bf16[2,64,256]{2,1,0:T(8,128)(2,1)S(1)} %collective-permute-done.7.refs_8_), channel_id=1, source_target_pairs={{1,0},{0,1},{3,2},{2,3},{5,4},{4,5},{7,6},{6,7},{9,8},{8,9},{11,10... | collective-permute-start | bytes 196616 | tf_op jit(solution)/shard_map/ppermute | solution.py:199
  19.7 3.0 %collective-permute-start.10 = (bf16[2,64,256]{2,1,0:T(8,128)(2,1)S(1)}, bf16[2,64,256]{2,1,0:T(8,128)(2,1)S(1)}, u32[]{:S(2)}, u32[]{:S(2)}) collective-permute-start(bf16[2,64,256]{2,1,0:T(8,128)(2,1)S(1)} %collective-permute-done.6.refs_7_), channel_id=1, source_target_pairs={{1,0},{0,1},{3,2},{2,3},{5,4},{4,5},{7,6},{6,7},{9,8},{8,9},{11,10... | collective-permute-start | bytes 196616 | tf_op jit(solution)/shard_map/ppermute | solution.py:199
  19.7 3.0 %collective-permute-start.9 = (bf16[2,64,256]{2,1,0:T(8,128)(2,1)S(1)}, bf16[2,64,256]{2,1,0:T(8,128)(2,1)S(1)}, u32[]{:S(2)}, u32[]{:S(2)}) collective-permute-start(bf16[2,64,256]{2,1,0:T(8,128)(2,1)S(1)} %collective-permute-done.5.refs_6_), channel_id=1, source_target_pairs={{1,0},{0,1},{3,2},{2,3},{5,4},{4,5},{7,6},{6,7},{9,8},{8,9},{11,10... | collective-permute-start | bytes 196616 | tf_op jit(solution)/shard_map/ppermute | solution.py:199

commit v4 on v2

--- a/solution.py
+++ b/solution.py
@@ -7,7 +7,8 @@
 
 LANES = 128
 VMEM_BYTES = 24 * 1024 * 1024
-FACTOR_VMEM_BYTES = 56 * 1024 * 1024
+LOAD_VMEM_BYTES = 52000 * 1024
+FACTOR_VMEM_BYTES = 55040 * 1024
 AXES = ("row", "col", "layer")
 
 
@@ -67,6 +68,40 @@
         for b, slot in enumerate(row):
             slab = jnp.where((plane == at) & (place == slot), b, slab)
     return slab
+
+
+def gather_line(factor, count):
+    if count != 4:
+        line = [factor]
+        for step in range(1, count):
+            line.append(lax.ppermute(factor, "col", [(partner(b, step, count), b) for b in range(count)]))
+        return line
+    far = lax.ppermute(factor, "col", [(b ^ 2, b) for b in range(count)])
+    near = lax.ppermute(factor, "col", [(b ^ 1, b) for b in range(count)])
+    both = lax.ppermute(far, "col", [(b ^ 1, b) for b in range(count)])
+    return [factor, near, far, both]
+
+
+def load_kernel(after_ref, lines_ref, share_ref, sem):
+    rows = share_ref.shape[0]
+    layer = lax.axis_index("layer")
+    load = pltpu.make_async_copy(lines_ref.at[pl.ds(layer * rows, rows)], share_ref, sem)
+    load.start()
+    load.wait()
+
+
+def load_share(after, lines, layers):
+    rows = lines.shape[0] // layers
+    return pl.pallas_call(
+        load_kernel,
+        out_shape=jax.ShapeDtypeStruct((rows, LANES), jnp.float32),
+        in_specs=[pl.BlockSpec(memory_space=pl.ANY), pl.BlockSpec(memory_space=pltpu.HBM)],
+        out_specs=pl.BlockSpec(memory_space=pltpu.VMEM),
+        scratch_shapes=[pltpu.SemaphoreType.DMA],
+        compiler_params=pltpu.CompilerParams(vmem_limit_bytes=LOAD_VMEM_BYTES),
+        cost_estimate=pl.CostEstimate(flops=0, bytes_accessed=rows * LANES * 8, transcendentals=0),
+        name="load_share",
+    )(after, lines)
 
 
 def update_kernel(pieces, layers, half, tile, tile_rows, col_tiles, *refs):
@@ -142,12 +177,8 @@
     moved = lax.ppermute(
         factor, ("row", "col"), [(a * count + b, slots[a][b] * count + a) for a in range(count) for b in range(count)]
     )
-    line = [factor] + [None] * (count - 1)
-    for step in reversed(range(1, count)):
-        line[step] = lax.ppermute(factor, "col", [(partner(b, step, count), b) for b in range(count)])
-    lines = trailing.reshape(-1, LANES)
-    share_lines = lines.shape[0] // layers
-    share = lax.dynamic_slice_in_dim(lines, lax.axis_index("layer") * share_lines, share_lines, 0)
+    line = gather_line(factor, count)
+    share = load_share(factor, trailing.reshape(-1, LANES), layers)
     moved, share = lax.optimization_barrier((moved, share))
     plane = [moved] + [None] * (count - 1)
     for step in reversed(range(1, count)):

time: 24.1 us -> 21.9 us (0.909)
  the two profiles are of different devices: /device:TPU:25 before, /device:TPU:0 now
where the time goes in v4:
time: 21.9 us; the launch traced here: 21.6 us
  starting transfers between devices  12.3 us (56%)
  Pallas kernels  4.97 us (23%)
  waiting for transfers between devices  4.26 us (19%)
    ppermute x3, starting transfers between devices, per_device(): lax.ppermute(moved, 'row', [(partner(a, step, count), a) for a in range(c...  5.78 us
    ppermute x3, waiting for transfers between devices, per_device(): lax.ppermute(moved, 'row', [(partner(a, step, count), a) for a in range(c...  3.26 us
    ppermute x1, starting transfers between devices, per_device(): lax.ppermute(factor, ('row', 'col'), [(a * count + b, slots[a][b] * count...  2.99 us
    ppermute x1, starting transfers between devices, gather_line(): far = lax.ppermute(factor, 'col', [(b ^ 2, b) for b in range(count)])  2.39 us
    pallas_call x1, Pallas kernels, update_trailing(): pl.pallas_call(body, out_shape=jax.ShapeDtypeStruct(share.shape, jnp.floa...  1.93 us
    pallas_call x1, Pallas kernels, load_share(): pl.pallas_call(load_kernel, out_shape=jax.ShapeDtypeStruct((rows, LANES),...  1.6 us
    pallas_call x1, Pallas kernels, make_factor(): pl.pallas_call(factor_kernel, out_shape=jax.ShapeDtypeStruct((half, tile_...  1.44 us
    ppermute x4, waiting for transfers between devices, per_device(): others += [lax.ppermute(piece, 'layer', pairs) for piece in plane]  0.48 us
  transfers between devices with their start and end apart: 11, of which 7 were waited for; matrix products, arithmetic and copies ran while one was open for 0% of the time, Pallas kernels for 7%

profile of v4, /device:TPU:0, one launch (start us, length us, event | category | flops | bytes accessed | tf_op | source)
XLA Modules:
  0.0 21.6 jit_solution(10581541299972087956)
XLA Ops:
  0.0 1.4 %factor.1.after_ref.refs_0_ = bf16[2,64,256]{2,1,0:T(8,128)(2,1)S(1)} custom-call(f32[4,1,64,256]{3,2,1,0:T(8,128)} %panel_ref.1, f32[256,256]{1,0:T(8,128)} %inverse_ref.1), custom_call_target="tpu_custom_call" | custom-call | tf_op jit(solution)/shard_map/factor/pallas_call | solution.py:40
  1.4 3.0 %collective-permute-start.3 = (bf16[2,64,256]{2,1,0:T(8,128)(2,1)S(1)}, bf16[2,64,256]{2,1,0:T(8,128)(2,1)S(1)}, u32[]{:S(2)}, u32[]{:S(2)}) collective-permute-start(bf16[2,64,256]{2,1,0:T(8,128)(2,1)S(1)} %factor.1.after_ref.refs_0_), channel_id=1, source_target_pairs={{0,8},{2,24},{4,16},{6,0},{8,2},{10,18},{12,10},{14,26},{16,20},{1... | collective-permute-start | bytes 196616 | tf_op jit(solution)/shard_map/ppermute | solution.py:177
  4.4 2.4 %collective-permute-start.1 = (bf16[2,64,256]{2,1,0:T(8,128)(2,1)S(1)}, bf16[2,64,256]{2,1,0:T(8,128)(2,1)S(1)}, u32[]{:S(2)}, u32[]{:S(2)}) collective-permute-start(bf16[2,64,256]{2,1,0:T(8,128)(2,1)S(1)} %factor.1.after_ref.refs_0_), channel_id=1, source_target_pairs={{4,0},{6,2},{0,4},{2,6},{5,1},{7,3},{1,5},{3,7},{12,8},{14,10},{8,... | collective-permute-start | bytes 196616 | tf_op jit(solution)/shard_map/ppermute | solution.py:79
  6.8 0.4 %collective-permute-start = (bf16[2,64,256]{2,1,0:T(8,128)(2,1)S(1)}, bf16[2,64,256]{2,1,0:T(8,128)(2,1)S(1)}, u32[]{:S(2)}, u32[]{:S(2)}) collective-permute-start(bf16[2,64,256]{2,1,0:T(8,128)(2,1)S(1)} %factor.1.after_ref.refs_0_), channel_id=1, source_target_pairs={{2,0},{0,2},{6,4},{4,6},{3,1},{1,3},{7,5},{5,7},{10,8},{8,10},{14,... | collective-permute-start | bytes 196616 | tf_op jit(solution)/shard_map/ppermute | solution.py:80
  7.2 1.6 %load_share.1.refs_12_ = f32[4096,128]{1,0:T(8,128)S(1)} custom-call(bf16[2,64,256]{2,1,0:T(8,128)(2,1)S(1)} %factor.1.after_ref.refs_0_, f32[8192,128]{1,0:T(8,128)} %bitcast.2), custom_call_target="tpu_custom_call" | custom-call | bytes 4194304 | tf_op jit(solution)/shard_map/load_share/pallas_call | solution.py:95
  8.8 0.1 collective-permute-done.3.refs_4_
  8.9 5.1 %collective-permute-start.6 = (bf16[2,64,256]{2,1,0:T(8,128)(2,1)S(1)}, bf16[2,64,256]{2,1,0:T(8,128)(2,1)S(1)}, u32[]{:S(2)}, u32[]{:S(2)}) collective-permute-start(bf16[2,64,256]{2,1,0:T(8,128)(2,1)S(1)} %collective-permute-done.3.refs_4_), channel_id=1, source_target_pairs={{24,0},{16,8},{8,16},{0,24},{25,1},{17,9},{9,17},{1,25},{26,2},{18... | collective-permute-start | bytes 196616 | tf_op jit(solution)/shard_map/ppermute | solution.py:185
  14.0 0.0 collective-permute-start.5
  14.0 0.7 %collective-permute-start.4 = (bf16[2,64,256]{2,1,0:T(8,128)(2,1)S(1)}, bf16[2,64,256]{2,1,0:T(8,128)(2,1)S(1)}, u32[]{:S(2)}, u32[]{:S(2)}) collective-permute-start(bf16[2,64,256]{2,1,0:T(8,128)(2,1)S(1)} %collective-permute-done.3.refs_4_), channel_id=1, source_target_pairs={{8,0},{0,8},{24,16},{16,24},{9,1},{1,9},{25,17},{17,25},{10,2},{2,... | collective-permute-start | bytes 196616 | tf_op jit(solution)/shard_map/ppermute | solution.py:185
  14.7 0.0 collective-permute-done.1.refs_2_
  14.7 0.0 collective-permute-start.7
  14.7 0.0 collective-permute-done.refs_1_
  14.7 0.4 %collective-permute-start.2 = (bf16[2,64,256]{2,1,0:T(8,128)(2,1)S(1)}, bf16[2,64,256]{2,1,0:T(8,128)(2,1)S(1)}, u32[]{:S(2)}, u32[]{:S(2)}) collective-permute-start(bf16[2,64,256]{2,1,0:T(8,128)(2,1)S(1)} %collective-permute-done.1.refs_2_), channel_id=1, source_target_pairs={{2,0},{0,2},{6,4},{4,6},{3,1},{1,3},{7,5},{5,7},{10,8},{8,10},{14,... | collective-permute-start | bytes 196616 | tf_op jit(solution)/shard_map/ppermute | solution.py:81
  15.0 1.2 %collective-permute-done.6.refs_7_ = bf16[2,64,256]{2,1,0:T(8,128)(2,1)S(1)} collective-permute-done((bf16[2,64,256]{2,1,0:T(8,128)(2,1)S(1)}, bf16[2,64,256]{2,1,0:T(8,128)(2,1)S(1)}, u32[]{:S(2)}, u32[]{:S(2)}) %collective-permute-start.6) | collective-permute-done | bytes 65568 | tf_op jit(solution)/shard_map/ppermute | solution.py:185
  16.2 0.0 collective-permute-start.10
  16.2 2.0 %collective-permute-done.5.refs_6_ = bf16[2,64,256]{2,1,0:T(8,128)(2,1)S(1)} collective-permute-done((bf16[2,64,256]{2,1,0:T(8,128)(2,1)S(1)}, bf16[2,64,256]{2,1,0:T(8,128)(2,1)S(1)}, u32[]{:S(2)}, u32[]{:S(2)}) %collective-permute-start.5) | collective-permute-done | bytes 65568 | tf_op jit(solution)/shard_map/ppermute | solution.py:185
  18.2 0.0 collective-permute-start.9
  18.3 0.1 collective-permute-done.4.refs_5_
  18.3 0.5 %collective-permute-start.8 = (bf16[2,64,256]{2,1,0:T(8,128)(2,1)S(1)}, bf16[2,64,256]{2,1,0:T(8,128)(2,1)S(1)}, u32[]{:S(2)}, u32[]{:S(2)}) collective-permute-start(bf16[2,64,256]{2,1,0:T(8,128)(2,1)S(1)} %collective-permute-done.4.refs_5_), channel_id=1, source_target_pairs={{1,0},{0,1},{3,2},{2,3},{5,4},{4,5},{7,6},{6,7},{9,8},{8,9},{11,10... | collective-permute-start | bytes 196616 | tf_op jit(solution)/shard_map/ppermute | solution.py:189
  18.8 0.4 %collective-permute-done.2.refs_3_ = bf16[2,64,256]{2,1,0:T(8,128)(2,1)S(1)} collective-permute-done((bf16[2,64,256]{2,1,0:T(8,128)(2,1)S(1)}, bf16[2,64,256]{2,1,0:T(8,128)(2,1)S(1)}, u32[]{:S(2)}, u32[]{:S(2)}) %collective-permute-start.2) | collective-permute-done | bytes 65568 | tf_op jit(solution)/shard_map/ppermute | solution.py:81
  19.2 0.0 collective-permute-done.7.refs_8_
  19.2 0.0 collective-permute-done.10.refs_11_
  19.2 0.3 %collective-permute-done.9.refs_10_ = bf16[2,64,256]{2,1,0:T(8,128)(2,1)S(1)} collective-permute-done((bf16[2,64,256]{2,1,0:T(8,128)(2,1)S(1)}, bf16[2,64,256]{2,1,0:T(8,128)(2,1)S(1)}, u32[]{:S(2)}, u32[]{:S(2)}) %collective-permute-start.9) | collective-permute-done | bytes 65568 | tf_op jit(solution)/shard_map/ppermute | solution.py:189
  19.5 0.2 collective-permute-done.8.refs_9_
  19.7 1.9 %update.1 = f32[4096,128]{1,0:T(8,128)} custom-call(bf16[2,64,256]{2,1,0:T(8,128)(2,1)S(1)} %factor.1.after_ref.refs_0_, bf16[2,64,256]{2,1,0:T(8,128)(2,1)S(1)} %collective-permute-done.refs_1_, bf16[2,64,256]{2,1,0:T(8,128)(2,1)S(1)} %collective-permute-done.1.refs_2_, bf16[2,64,256]{2,1,0:T(8,128)(2,1)S(1)} %collective-permute-done.2.refs_3_, ...), custom_call_target="tpu_custom_call" | custom-call | tf_op jit(solution)/shard_map/update/pallas_call | solution.py:153
Async XLA Ops:
  1.4 7.4 %collective-permute-start.3 = (bf16[2,64,256]{2,1,0:T(8,128)(2,1)S(1)}, bf16[2,64,256]{2,1,0:T(8,128)(2,1)S(1)}, u32[]{:S(2)}, u32[]{:S(2)}) collective-permute-start(bf16[2,64,256]{2,1,0:T(8,128)(2,1)S(1)} %factor.1.after_ref.refs_0_), channel_id=1, source_target_pairs={{0,8},{2,24},{4,16},{6,0},{8,2},{10,18},{12,10},{14,26},{16,20},{1... | collective-permute-start | bytes 196616 | tf_op jit(solution)/shard_map/ppermute | solution.py:177
  4.4 10.2 %collective-permute-start.1 = (bf16[2,64,256]{2,1,0:T(8,128)(2,1)S(1)}, bf16[2,64,256]{2,1,0:T(8,128)(2,1)S(1)}, u32[]{:S(2)}, u32[]{:S(2)}) collective-permute-start(bf16[2,64,256]{2,1,0:T(8,128)(2,1)S(1)} %factor.1.after_ref.refs_0_), channel_id=1, source_target_pairs={{4,0},{6,2},{0,4},{2,6},{5,1},{7,3},{1,5},{3,7},{12,8},{14,10},{8,... | collective-permute-start | bytes 196616 | tf_op jit(solution)/shard_map/ppermute | solution.py:79
  6.8 7.9 %collective-permute-start = (bf16[2,64,256]{2,1,0:T(8,128)(2,1)S(1)}, bf16[2,64,256]{2,1,0:T(8,128)(2,1)S(1)}, u32[]{:S(2)}, u32[]{:S(2)}) collective-permute-start(bf16[2,64,256]{2,1,0:T(8,128)(2,1)S(1)} %factor.1.after_ref.refs_0_), channel_id=1, source_target_pairs={{2,0},{0,2},{6,4},{4,6},{3,1},{1,3},{7,5},{5,7},{10,8},{8,10},{14,... | collective-permute-start | bytes 196616 | tf_op jit(solution)/shard_map/ppermute | solution.py:80
  8.9 7.3 %collective-permute-start.6 = (bf16[2,64,256]{2,1,0:T(8,128)(2,1)S(1)}, bf16[2,64,256]{2,1,0:T(8,128)(2,1)S(1)}, u32[]{:S(2)}, u32[]{:S(2)}) collective-permute-start(bf16[2,64,256]{2,1,0:T(8,128)(2,1)S(1)} %collective-permute-done.3.refs_4_), channel_id=1, source_target_pairs={{24,0},{16,8},{8,16},{0,24},{25,1},{17,9},{9,17},{1,25},{26,2},{18... | collective-permute-start | bytes 196616 | tf_op jit(solution)/shard_map/ppermute | solution.py:185
  14.0 4.3 %collective-permute-start.5 = (bf16[2,64,256]{2,1,0:T(8,128)(2,1)S(1)}, bf16[2,64,256]{2,1,0:T(8,128)(2,1)S(1)}, u32[]{:S(2)}, u32[]{:S(2)}) collective-permute-start(bf16[2,64,256]{2,1,0:T(8,128)(2,1)S(1)} %collective-permute-done.3.refs_4_), channel_id=1, source_target_pairs={{16,0},{24,8},{0,16},{8,24},{17,1},{25,9},{1,17},{9,25},{18,2},{26... | collective-permute-start | bytes 196616 | tf_op jit(solution)/shard_map/ppermute | solution.py:185
  14.0 4.3 %collective-permute-start.4 = (bf16[2,64,256]{2,1,0:T(8,128)(2,1)S(1)}, bf16[2,64,256]{2,1,0:T(8,128)(2,1)S(1)}, u32[]{:S(2)}, u32[]{:S(2)}) collective-permute-start(bf16[2,64,256]{2,1,0:T(8,128)(2,1)S(1)} %collective-permute-done.3.refs_4_), channel_id=1, source_target_pairs={{8,0},{0,8},{24,16},{16,24},{9,1},{1,9},{25,17},{17,25},{10,2},{2,... | collective-permute-start | bytes 196616 | tf_op jit(solution)/shard_map/ppermute | solution.py:185
  14.7 4.5 %collective-permute-start.7 = (bf16[2,64,256]{2,1,0:T(8,128)(2,1)S(1)}, bf16[2,64,256]{2,1,0:T(8,128)(2,1)S(1)}, u32[]{:S(2)}, u32[]{:S(2)}) collective-permute-start(bf16[2,64,256]{2,1,0:T(8,128)(2,1)S(1)} %collective-permute-done.3.refs_4_), channel_id=1, source_target_pairs={{1,0},{0,1},{3,2},{2,3},{5,4},{4,5},{7,6},{6,7},{9,8},{8,9},{11,10... | collective-permute-start | bytes 196616 | tf_op jit(solution)/shard_map/ppermute | solution.py:189
  14.7 4.5 %collective-permute-start.2 = (bf16[2,64,256]{2,1,0:T(8,128)(2,1)S(1)}, bf16[2,64,256]{2,1,0:T(8,128)(2,1)S(1)}, u32[]{:S(2)}, u32[]{:S(2)}) collective-permute-start(bf16[2,64,256]{2,1,0:T(8,128)(2,1)S(1)} %collective-permute-done.1.refs_2_), channel_id=1, source_target_pairs={{2,0},{0,2},{6,4},{4,6},{3,1},{1,3},{7,5},{5,7},{10,8},{8,10},{14,... | collective-permute-start | bytes 196616 | tf_op jit(solution)/shard_map/ppermute | solution.py:81
  16.2 3.0 %collective-permute-start.10 = (bf16[2,64,256]{2,1,0:T(8,128)(2,1)S(1)}, bf16[2,64,256]{2,1,0:T(8,128)(2,1)S(1)}, u32[]{:S(2)}, u32[]{:S(2)}) collective-permute-start(bf16[2,64,256]{2,1,0:T(8,128)(2,1)S(1)} %collective-permute-done.6.refs_7_), channel_id=1, source_target_pairs={{1,0},{0,1},{3,2},{2,3},{5,4},{4,5},{7,6},{6,7},{9,8},{8,9},{11,10... | collective-permute-start | bytes 196616 | tf_op jit(solution)/shard_map/ppermute | solution.py:189
  18.2 1.3 %collective-permute-start.9 = (bf16[2,64,256]{2,1,0:T(8,128)(2,1)S(1)}, bf16[2,64,256]{2,1,0:T(8,128)(2,1)S(1)}, u32[]{:S(2)}, u32[]{:S(2)}) collective-permute-start(bf16[2,64,256]{2,1,0:T(8,128)(2,1)S(1)} %collective-permute-done.5.refs_6_), channel_id=1, source_target_pairs={{1,0},{0,1},{3,2},{2,3},{5,4},{4,5},{7,6},{6,7},{9,8},{8,9},{11,10... | collective-permute-start | bytes 196616 | tf_op jit(solution)/shard_map/ppermute | solution.py:189
  18.3 1.4 %collective-permute-start.8 = (bf16[2,64,256]{2,1,0:T(8,128)(2,1)S(1)}, bf16[2,64,256]{2,1,0:T(8,128)(2,1)S(1)}, u32[]{:S(2)}, u32[]{:S(2)}) collective-permute-start(bf16[2,64,256]{2,1,0:T(8,128)(2,1)S(1)} %collective-permute-done.4.refs_5_), channel_id=1, source_target_pairs={{1,0},{0,1},{3,2},{2,3},{5,4},{4,5},{7,6},{6,7},{9,8},{8,9},{11,10... | collective-permute-start | bytes 196616 | tf_op jit(solution)/shard_map/ppermute | solution.py:189

commit v5 on v4

--- a/solution.py
+++ b/solution.py
@@ -6,6 +6,7 @@
 from jax.sharding import PartitionSpec as P
 
 LANES = 128
+CHUNK_ROWS = 128
 VMEM_BYTES = 24 * 1024 * 1024
 LOAD_VMEM_BYTES = 52000 * 1024
 FACTOR_VMEM_BYTES = 55040 * 1024
@@ -110,7 +111,6 @@
     share_ref, out_ref, row_buf, col_buf, out_buf, out_sems = refs[pieces * (1 + layers) :]
     r, c, layer = (lax.axis_index(axis) for axis in AXES)
     slots = plane_slots(pieces)
-    lines = tile * col_tiles * tile // LANES
     per_row = col_tiles * tile // LANES
     for step in range(pieces):
         row_at = pl.multiple_of(partner(c, step, pieces) * tile_rows, tile_rows)
@@ -122,20 +122,24 @@
             owner = lax.rem(layer + shift, layers)
             for k in range(half):
                 col_buf[owner * half + k, pl.ds(col_at, tile_rows), :] = col_refs[shift * pieces + step][k]
+    chunks = half * (tile // CHUNK_ROWS)
+    chunk_lines = CHUNK_ROWS * per_row
     stores = []
-    for k in range(half):
+    for chunk in range(chunks):
+        k, first_row = divmod(chunk * CHUNK_ROWS, tile)
         for j in range(col_tiles):
             update = lax.dot_general(
-                row_buf[k], col_buf[j], (((1,), (1,)), ((), ())), preferred_element_type=jnp.float32
+                row_buf[k, first_row : first_row + CHUNK_ROWS, :],
+                col_buf[j],
+                (((1,), (1,)), ((), ())),
+                preferred_element_type=jnp.float32,
             )
             for part in range(tile // LANES):
-                first = j * (tile // LANES) + part
-                out_buf[pl.ds(k * lines + first, tile, stride=per_row), :] = (
-                    share_ref[pl.ds(k * lines + first, tile, stride=per_row), :]
-                    - update[:, part * LANES : (part + 1) * LANES]
-                )
-        share = pl.ds(k * lines, lines)
-        store = pltpu.make_async_copy(out_buf.at[share], out_ref.at[share], out_sems.at[k])
+                first = chunk * chunk_lines + j * (tile // LANES) + part
+                at = pl.ds(first, CHUNK_ROWS, stride=per_row)
+                out_buf[at, :] = share_ref[at, :] - update[:, part * LANES : (part + 1) * LANES]
+        written = pl.ds(chunk * chunk_lines, chunk_lines)
+        store = pltpu.make_async_copy(out_buf.at[written], out_ref.at[written], out_sems.at[chunk])
         store.start()
         stores.append(store)
     for store in stores:
@@ -159,7 +163,7 @@
             pltpu.VMEM((half, tile, width), jnp.bfloat16),
             pltpu.VMEM((half * layers, tile, width), jnp.bfloat16),
             pltpu.VMEM(share.shape, jnp.float32),
-            pltpu.SemaphoreType.DMA((half,)),
+            pltpu.SemaphoreType.DMA((half * (tile // CHUNK_ROWS),)),
         ],
         compiler_params=pltpu.CompilerParams(vmem_limit_bytes=VMEM_BYTES),
         name="update",
@@ -177,9 +181,9 @@
     moved = lax.ppermute(
         factor, ("row", "col"), [(a * count + b, slots[a][b] * count + a) for a in range(count) for b in range(count)]
     )
-    line = gather_line(factor, count)
     share = load_share(factor, trailing.reshape(-1, LANES), layers)
-    moved, share = lax.optimization_barrier((moved, share))
+    loaded_factor, share = lax.optimization_barrier((factor, share))
+    line = gather_line(loaded_factor, count)
     plane = [moved] + [None] * (count - 1)
     for step in reversed(range(1, count)):
         plane[step] = lax.ppermute(moved, "row", [(partner(a, step, count), a) for a in range(count)])

time: 21.9 us -> 23 us (1.050)
  starting transfers between devices: 12.3 us -> 13.4 us
  waiting for transfers between devices: 4.26 us -> 4.57 us
    ppermute x3, starting transfers between devices: 5.78 us -> 6.98 us  [per_device(): lax.ppermute(moved, 'row', [(partner(a, step, count), a) for a in range(c...]
    ppermute x3, waiting for transfers between devices: 3.26 us -> 3.57 us  [per_device(): lax.ppermute(moved, 'row', [(partner(a, step, count), a) for a in range(c...]
    ppermute x1, starting transfers between devices: 0.36 us -> 0.11 us  [gather_line(): both = lax.ppermute(far, 'col', [(b ^ 1, b) for b in range(count)])]
  transfers between devices with their start and end apart: 11 -> 11, of which waited for: 7 -> 6; matrix products, arithmetic and copies ran while one was open for 0% -> 0% of each run, Pallas kernels for 7% -> 7%
where the time goes in v5:
time: 23 us; the launch traced here: 22.8 us
  starting transfers between devices  13.4 us (58%)
  Pallas kernels  4.88 us (21%)
  waiting for transfers between devices  4.57 us (20%)
    ppermute x3, starting transfers between devices, per_device(): lax.ppermute(moved, 'row', [(partner(a, step, count), a) for a in range(c...  6.98 us
    ppermute x3, waiting for transfers between devices, per_device(): lax.ppermute(moved, 'row', [(partner(a, step, count), a) for a in range(c...  3.57 us
    ppermute x1, starting transfers between devices, per_device(): lax.ppermute(factor, ('row', 'col'), [(a * count + b, slots[a][b] * count...  2.99 us
    ppermute x1, starting transfers between devices, gather_line(): far = lax.ppermute(factor, 'col', [(b ^ 2, b) for b in range(count)])  2.46 us
    pallas_call x1, Pallas kernels, update_trailing(): pl.pallas_call(body, out_shape=jax.ShapeDtypeStruct(share.shape, jnp.floa...  1.84 us
    pallas_call x1, Pallas kernels, load_share(): pl.pallas_call(load_kernel, out_shape=jax.ShapeDtypeStruct((rows, LANES),...  1.6 us
    pallas_call x1, Pallas kernels, make_factor(): pl.pallas_call(factor_kernel, out_shape=jax.ShapeDtypeStruct((half, tile_...  1.44 us
    ppermute x4, waiting for transfers between devices, per_device(): others += [lax.ppermute(piece, 'layer', pairs) for piece in plane]  0.6 us
  transfers between devices with their start and end apart: 11, of which 6 were waited for; matrix products, arithmetic and copies ran while one was open for 0% of the time, Pallas kernels for 7%

profile of v5, /device:TPU:0, one launch (start us, length us, event | category | flops | bytes accessed | tf_op | source)
XLA Modules:
  0.0 22.8 jit_solution(3530420746744674098)
XLA Ops:
  0.0 1.4 %factor.1.after_ref.refs_0_ = bf16[2,64,256]{2,1,0:T(8,128)(2,1)S(1)} custom-call(f32[4,1,64,256]{3,2,1,0:T(8,128)} %panel_ref.1, f32[256,256]{1,0:T(8,128)} %inverse_ref.1), custom_call_target="tpu_custom_call" | custom-call | tf_op jit(solution)/shard_map/factor/pallas_call | solution.py:41
  1.4 3.0 %collective-permute-start.3 = (bf16[2,64,256]{2,1,0:T(8,128)(2,1)S(1)}, bf16[2,64,256]{2,1,0:T(8,128)(2,1)S(1)}, u32[]{:S(2)}, u32[]{:S(2)}) collective-permute-start(bf16[2,64,256]{2,1,0:T(8,128)(2,1)S(1)} %factor.1.after_ref.refs_0_), channel_id=1, source_target_pairs={{0,8},{2,24},{4,16},{6,0},{8,2},{10,18},{12,10},{14,26},{16,20},{1... | collective-permute-start | bytes 196616 | tf_op jit(solution)/shard_map/ppermute | solution.py:181
  4.4 1.6 %load_share.1.refs_12_ = f32[4096,128]{1,0:T(8,128)S(1)} custom-call(bf16[2,64,256]{2,1,0:T(8,128)(2,1)S(1)} %factor.1.after_ref.refs_0_, f32[8192,128]{1,0:T(8,128)} %bitcast.2), custom_call_target="tpu_custom_call" | custom-call | bytes 4194304 | tf_op jit(solution)/shard_map/load_share/pallas_call | solution.py:96
  6.0 2.5 %collective-permute-start.1 = (bf16[2,64,256]{2,1,0:T(8,128)(2,1)S(1)}, bf16[2,64,256]{2,1,0:T(8,128)(2,1)S(1)}, u32[]{:S(2)}, u32[]{:S(2)}) collective-permute-start(bf16[2,64,256]{2,1,0:T(8,128)(2,1)S(1)} %factor.1.after_ref.refs_0_), channel_id=1, source_target_pairs={{4,0},{6,2},{0,4},{2,6},{5,1},{7,3},{1,5},{3,7},{12,8},{14,10},{8,... | collective-permute-start | bytes 196616 | tf_op jit(solution)/shard_map/ppermute | solution.py:80
  8.5 0.3 %collective-permute-start = (bf16[2,64,256]{2,1,0:T(8,128)(2,1)S(1)}, bf16[2,64,256]{2,1,0:T(8,128)(2,1)S(1)}, u32[]{:S(2)}, u32[]{:S(2)}) collective-permute-start(bf16[2,64,256]{2,1,0:T(8,128)(2,1)S(1)} %factor.1.after_ref.refs_0_), channel_id=1, source_target_pairs={{2,0},{0,2},{6,4},{4,6},{3,1},{1,3},{7,5},{5,7},{10,8},{8,10},{14,... | collective-permute-start | bytes 196616 | tf_op jit(solution)/shard_map/ppermute | solution.py:81
  8.8 0.1 collective-permute-done.3.refs_4_
  8.9 6.4 %collective-permute-start.6 = (bf16[2,64,256]{2,1,0:T(8,128)(2,1)S(1)}, bf16[2,64,256]{2,1,0:T(8,128)(2,1)S(1)}, u32[]{:S(2)}, u32[]{:S(2)}) collective-permute-start(bf16[2,64,256]{2,1,0:T(8,128)(2,1)S(1)} %collective-permute-done.3.refs_4_), channel_id=1, source_target_pairs={{24,0},{16,8},{8,16},{0,24},{25,1},{17,9},{9,17},{1,25},{26,2},{18... | collective-permute-start | bytes 196616 | tf_op jit(solution)/shard_map/ppermute | solution.py:189
  15.3 0.0 collective-permute-start.5
  15.3 0.6 %collective-permute-start.4 = (bf16[2,64,256]{2,1,0:T(8,128)(2,1)S(1)}, bf16[2,64,256]{2,1,0:T(8,128)(2,1)S(1)}, u32[]{:S(2)}, u32[]{:S(2)}) collective-permute-start(bf16[2,64,256]{2,1,0:T(8,128)(2,1)S(1)} %collective-permute-done.3.refs_4_), channel_id=1, source_target_pairs={{8,0},{0,8},{24,16},{16,24},{9,1},{1,9},{25,17},{17,25},{10,2},{2,... | collective-permute-start | bytes 196616 | tf_op jit(solution)/shard_map/ppermute | solution.py:189
  15.9 0.0 collective-permute-done.1.refs_2_
  15.9 0.0 collective-permute-start.7
  15.9 0.0 collective-permute-done.refs_1_
  15.9 0.1 collective-permute-start.2
  16.0 1.6 %collective-permute-done.6.refs_7_ = bf16[2,64,256]{2,1,0:T(8,128)(2,1)S(1)} collective-permute-done((bf16[2,64,256]{2,1,0:T(8,128)(2,1)S(1)}, bf16[2,64,256]{2,1,0:T(8,128)(2,1)S(1)}, u32[]{:S(2)}, u32[]{:S(2)}) %collective-permute-start.6) | collective-permute-done | bytes 65568 | tf_op jit(solution)/shard_map/ppermute | solution.py:189
  17.5 0.0 collective-permute-start.10
  17.6 2.0 %collective-permute-done.5.refs_6_ = bf16[2,64,256]{2,1,0:T(8,128)(2,1)S(1)} collective-permute-done((bf16[2,64,256]{2,1,0:T(8,128)(2,1)S(1)}, bf16[2,64,256]{2,1,0:T(8,128)(2,1)S(1)}, u32[]{:S(2)}, u32[]{:S(2)}) %collective-permute-start.5) | collective-permute-done | bytes 65568 | tf_op jit(solution)/shard_map/ppermute | solution.py:189
  19.6 0.0 collective-permute-start.9
  19.6 0.0 collective-permute-done.4.refs_5_
  19.6 0.5 %collective-permute-start.8 = (bf16[2,64,256]{2,1,0:T(8,128)(2,1)S(1)}, bf16[2,64,256]{2,1,0:T(8,128)(2,1)S(1)}, u32[]{:S(2)}, u32[]{:S(2)}) collective-permute-start(bf16[2,64,256]{2,1,0:T(8,128)(2,1)S(1)} %collective-permute-done.4.refs_5_), channel_id=1, source_target_pairs={{1,0},{0,1},{3,2},{2,3},{5,4},{4,5},{7,6},{6,7},{9,8},{8,9},{11,10... | collective-permute-start | bytes 196616 | tf_op jit(solution)/shard_map/ppermute | solution.py:193
  20.1 0.0 collective-permute-done.7.refs_8_
  20.1 0.3 %collective-permute-done.2.refs_3_ = bf16[2,64,256]{2,1,0:T(8,128)(2,1)S(1)} collective-permute-done((bf16[2,64,256]{2,1,0:T(8,128)(2,1)S(1)}, bf16[2,64,256]{2,1,0:T(8,128)(2,1)S(1)}, u32[]{:S(2)}, u32[]{:S(2)}) %collective-permute-start.2) | collective-permute-done | bytes 65568 | tf_op jit(solution)/shard_map/ppermute | solution.py:82
  20.4 0.0 collective-permute-done.10.refs_11_
  20.4 0.4 %collective-permute-done.9.refs_10_ = bf16[2,64,256]{2,1,0:T(8,128)(2,1)S(1)} collective-permute-done((bf16[2,64,256]{2,1,0:T(8,128)(2,1)S(1)}, bf16[2,64,256]{2,1,0:T(8,128)(2,1)S(1)}, u32[]{:S(2)}, u32[]{:S(2)}) %collective-permute-start.9) | collective-permute-done | bytes 65568 | tf_op jit(solution)/shard_map/ppermute | solution.py:193
  20.8 0.2 collective-permute-done.8.refs_9_
  21.0 1.8 %update.1 = f32[4096,128]{1,0:T(8,128)} custom-call(bf16[2,64,256]{2,1,0:T(8,128)(2,1)S(1)} %factor.1.after_ref.refs_0_, bf16[2,64,256]{2,1,0:T(8,128)(2,1)S(1)} %collective-permute-done.refs_1_, bf16[2,64,256]{2,1,0:T(8,128)(2,1)S(1)} %collective-permute-done.1.refs_2_, bf16[2,64,256]{2,1,0:T(8,128)(2,1)S(1)} %collective-permute-done.2.refs_3_, ...), custom_call_target="tpu_custom_call" | custom-call | tf_op jit(solution)/shard_map/update/pallas_call | solution.py:157
Async XLA Ops:
  1.4 7.4 %collective-permute-start.3 = (bf16[2,64,256]{2,1,0:T(8,128)(2,1)S(1)}, bf16[2,64,256]{2,1,0:T(8,128)(2,1)S(1)}, u32[]{:S(2)}, u32[]{:S(2)}) collective-permute-start(bf16[2,64,256]{2,1,0:T(8,128)(2,1)S(1)} %factor.1.after_ref.refs_0_), channel_id=1, source_target_pairs={{0,8},{2,24},{4,16},{6,0},{8,2},{10,18},{12,10},{14,26},{16,20},{1... | collective-permute-start | bytes 196616 | tf_op jit(solution)/shard_map/ppermute | solution.py:181
  6.0 9.8 %collective-permute-start.1 = (bf16[2,64,256]{2,1,0:T(8,128)(2,1)S(1)}, bf16[2,64,256]{2,1,0:T(8,128)(2,1)S(1)}, u32[]{:S(2)}, u32[]{:S(2)}) collective-permute-start(bf16[2,64,256]{2,1,0:T(8,128)(2,1)S(1)} %factor.1.after_ref.refs_0_), channel_id=1, source_target_pairs={{4,0},{6,2},{0,4},{2,6},{5,1},{7,3},{1,5},{3,7},{12,8},{14,10},{8,... | collective-permute-start | bytes 196616 | tf_op jit(solution)/shard_map/ppermute | solution.py:80
  8.5 7.4 %collective-permute-start = (bf16[2,64,256]{2,1,0:T(8,128)(2,1)S(1)}, bf16[2,64,256]{2,1,0:T(8,128)(2,1)S(1)}, u32[]{:S(2)}, u32[]{:S(2)}) collective-permute-start(bf16[2,64,256]{2,1,0:T(8,128)(2,1)S(1)} %factor.1.after_ref.refs_0_), channel_id=1, source_target_pairs={{2,0},{0,2},{6,4},{4,6},{3,1},{1,3},{7,5},{5,7},{10,8},{8,10},{14,... | collective-permute-start | bytes 196616 | tf_op jit(solution)/shard_map/ppermute | solution.py:81
  8.9 8.7 %collective-permute-start.6 = (bf16[2,64,256]{2,1,0:T(8,128)(2,1)S(1)}, bf16[2,64,256]{2,1,0:T(8,128)(2,1)S(1)}, u32[]{:S(2)}, u32[]{:S(2)}) collective-permute-start(bf16[2,64,256]{2,1,0:T(8,128)(2,1)S(1)} %collective-permute-done.3.refs_4_), channel_id=1, source_target_pairs={{24,0},{16,8},{8,16},{0,24},{25,1},{17,9},{9,17},{1,25},{26,2},{18... | collective-permute-start | bytes 196616 | tf_op jit(solution)/shard_map/ppermute | solution.py:189
  15.3 4.3 %collective-permute-start.5 = (bf16[2,64,256]{2,1,0:T(8,128)(2,1)S(1)}, bf16[2,64,256]{2,1,0:T(8,128)(2,1)S(1)}, u32[]{:S(2)}, u32[]{:S(2)}) collective-permute-start(bf16[2,64,256]{2,1,0:T(8,128)(2,1)S(1)} %collective-permute-done.3.refs_4_), channel_id=1, source_target_pairs={{16,0},{24,8},{0,16},{8,24},{17,1},{25,9},{1,17},{9,25},{18,2},{26... | collective-permute-start | bytes 196616 | tf_op jit(solution)/shard_map/ppermute | solution.py:189
  15.3 4.3 %collective-permute-start.4 = (bf16[2,64,256]{2,1,0:T(8,128)(2,1)S(1)}, bf16[2,64,256]{2,1,0:T(8,128)(2,1)S(1)}, u32[]{:S(2)}, u32[]{:S(2)}) collective-permute-start(bf16[2,64,256]{2,1,0:T(8,128)(2,1)S(1)} %collective-permute-done.3.refs_4_), channel_id=1, source_target_pairs={{8,0},{0,8},{24,16},{16,24},{9,1},{1,9},{25,17},{17,25},{10,2},{2,... | collective-permute-start | bytes 196616 | tf_op jit(solution)/shard_map/ppermute | solution.py:189
  15.9 4.2 %collective-permute-start.7 = (bf16[2,64,256]{2,1,0:T(8,128)(2,1)S(1)}, bf16[2,64,256]{2,1,0:T(8,128)(2,1)S(1)}, u32[]{:S(2)}, u32[]{:S(2)}) collective-permute-start(bf16[2,64,256]{2,1,0:T(8,128)(2,1)S(1)} %collective-permute-done.3.refs_4_), channel_id=1, source_target_pairs={{1,0},{0,1},{3,2},{2,3},{5,4},{4,5},{7,6},{6,7},{9,8},{8,9},{11,10... | collective-permute-start | bytes 196616 | tf_op jit(solution)/shard_map/ppermute | solution.py:193
  15.9 4.5 %collective-permute-start.2 = (bf16[2,64,256]{2,1,0:T(8,128)(2,1)S(1)}, bf16[2,64,256]{2,1,0:T(8,128)(2,1)S(1)}, u32[]{:S(2)}, u32[]{:S(2)}) collective-permute-start(bf16[2,64,256]{2,1,0:T(8,128)(2,1)S(1)} %collective-permute-done.1.refs_2_), channel_id=1, source_target_pairs={{2,0},{0,2},{6,4},{4,6},{3,1},{1,3},{7,5},{5,7},{10,8},{8,10},{14,... | collective-permute-start | bytes 196616 | tf_op jit(solution)/shard_map/ppermute | solution.py:82
  17.5 2.8 %collective-permute-start.10 = (bf16[2,64,256]{2,1,0:T(8,128)(2,1)S(1)}, bf16[2,64,256]{2,1,0:T(8,128)(2,1)S(1)}, u32[]{:S(2)}, u32[]{:S(2)}) collective-permute-start(bf16[2,64,256]{2,1,0:T(8,128)(2,1)S(1)} %collective-permute-done.6.refs_7_), channel_id=1, source_target_pairs={{1,0},{0,1},{3,2},{2,3},{5,4},{4,5},{7,6},{6,7},{9,8},{8,9},{11,10... | collective-permute-start | bytes 196616 | tf_op jit(solution)/shard_map/ppermute | solution.py:193
  19.6 1.3 %collective-permute-start.9 = (bf16[2,64,256]{2,1,0:T(8,128)(2,1)S(1)}, bf16[2,64,256]{2,1,0:T(8,128)(2,1)S(1)}, u32[]{:S(2)}, u32[]{:S(2)}) collective-permute-start(bf16[2,64,256]{2,1,0:T(8,128)(2,1)S(1)} %collective-permute-done.5.refs_6_), channel_id=1, source_target_pairs={{1,0},{0,1},{3,2},{2,3},{5,4},{4,5},{7,6},{6,7},{9,8},{8,9},{11,10... | collective-permute-start | bytes 196616 | tf_op jit(solution)/shard_map/ppermute | solution.py:193
  19.6 1.4 %collective-permute-start.8 = (bf16[2,64,256]{2,1,0:T(8,128)(2,1)S(1)}, bf16[2,64,256]{2,1,0:T(8,128)(2,1)S(1)}, u32[]{:S(2)}, u32[]{:S(2)}) collective-permute-start(bf16[2,64,256]{2,1,0:T(8,128)(2,1)S(1)} %collective-permute-done.4.refs_5_), channel_id=1, source_target_pairs={{1,0},{0,1},{3,2},{2,3},{5,4},{4,5},{7,6},{6,7},{9,8},{8,9},{11,10... | collective-permute-start | bytes 196616 | tf_op jit(solution)/shard_map/ppermute | solution.py:193

commit v6 on v5

--- a/solution.py
+++ b/solution.py
@@ -79,8 +79,7 @@
         return line
     far = lax.ppermute(factor, "col", [(b ^ 2, b) for b in range(count)])
     near = lax.ppermute(factor, "col", [(b ^ 1, b) for b in range(count)])
-    both = lax.ppermute(far, "col", [(b ^ 1, b) for b in range(count)])
-    return [factor, near, far, both]
+    return [factor, near, far]
 
 
 def load_kernel(after_ref, lines_ref, share_ref, sem):
@@ -107,21 +106,21 @@
 
 def update_kernel(pieces, layers, half, tile, tile_rows, col_tiles, *refs):
     row_refs = refs[:pieces]
-    col_refs = refs[pieces : pieces * (1 + layers)]
-    share_ref, out_ref, row_buf, col_buf, out_buf, out_sems = refs[pieces * (1 + layers) :]
+    plane_refs = refs[pieces : pieces + layers]
+    share_ref, out_ref, row_buf, col_buf, out_buf, out_sems = refs[pieces + layers :]
     r, c, layer = (lax.axis_index(axis) for axis in AXES)
     slots = plane_slots(pieces)
     per_row = col_tiles * tile // LANES
     for step in range(pieces):
         row_at = pl.multiple_of(partner(c, step, pieces) * tile_rows, tile_rows)
-        slab = slab_of(slots, c, partner(r, step, pieces))
+        slab = slab_of(slots, c, step)
         col_at = pl.multiple_of(slab * tile_rows, tile_rows)
         for k in range(half):
             row_buf[k, pl.ds(row_at, tile_rows), :] = row_refs[step][k]
         for shift in range(layers):
             owner = lax.rem(layer + shift, layers)
             for k in range(half):
-                col_buf[owner * half + k, pl.ds(col_at, tile_rows), :] = col_refs[shift * pieces + step][k]
+                col_buf[owner * half + k, pl.ds(col_at, tile_rows), :] = plane_refs[shift][step, k]
     chunks = half * (tile // CHUNK_ROWS)
     chunk_lines = CHUNK_ROWS * per_row
     stores = []
@@ -146,7 +145,7 @@
         store.wait()
 
 
-def update_trailing(row_pieces, col_pieces, share, half, layers, tile, col_tiles):
+def update_trailing(row_pieces, planes, share, half, layers, tile, col_tiles):
     pieces = len(row_pieces)
     tile_rows = row_pieces[0].shape[1]
     width = row_pieces[0].shape[2]
@@ -157,7 +156,7 @@
     result = pl.pallas_call(
         body,
         out_shape=jax.ShapeDtypeStruct(share.shape, jnp.float32),
-        in_specs=[pl.BlockSpec(memory_space=pltpu.VMEM)] * (pieces * (1 + layers) + 1),
+        in_specs=[pl.BlockSpec(memory_space=pltpu.VMEM)] * (pieces + layers + 1),
         out_specs=pl.BlockSpec(memory_space=pltpu.HBM),
         scratch_shapes=[
             pltpu.VMEM((half, tile, width), jnp.bfloat16),
@@ -167,7 +166,7 @@
         ],
         compiler_params=pltpu.CompilerParams(vmem_limit_bytes=VMEM_BYTES),
         name="update",
-    )(*row_pieces, *col_pieces, share)
+    )(*row_pieces, *planes, share)
     return result.reshape(half, 1, tile, col_tiles, 1, tile)
 
 
@@ -184,14 +183,15 @@
     share = load_share(factor, trailing.reshape(-1, LANES), layers)
     loaded_factor, share = lax.optimization_barrier((factor, share))
     line = gather_line(loaded_factor, count)
-    plane = [moved] + [None] * (count - 1)
-    for step in reversed(range(1, count)):
-        plane[step] = lax.ppermute(moved, "row", [(partner(a, step, count), a) for a in range(count)])
-    others = []
+    copies = jnp.broadcast_to(moved[None], (count,) + moved.shape)
+    copies, share, line[1:3] = lax.optimization_barrier((copies, share, line[1:3]))
+    if count == 4:
+        line.append(lax.ppermute(line[2], "col", [(b ^ 1, b) for b in range(count)]))
+    plane = lax.all_to_all(copies, "row", 0, 0)
+    planes = [plane]
     for shift in range(1, layers):
-        pairs = [((l + shift) % layers, l) for l in range(layers)]
-        others += [lax.ppermute(piece, "layer", pairs) for piece in plane]
-    return update_trailing(line, plane + others, share, half, layers, tile, col_tiles)
+        planes.append(lax.ppermute(plane, "layer", [((l + shift) % layers, l) for l in range(layers)]))
+    return update_trailing(line, planes, share, half, layers, tile, col_tiles)
 
 
 def solution(mesh):

time: 23 us -> 29.8 us (1.30)
  blocking collectives: 0 us -> 9.05 us
  starting transfers between devices: 13.4 us -> 6.21 us
  waiting for transfers between devices: 4.57 us -> 9.49 us
    all_to_all x0 -> x1, blocking collectives: none -> 9.05 us  [per_device(): plane = lax.all_to_all(copies, 'row', 0, 0)]
    ppermute x8 -> x2, starting transfers between devices: 7.6 us -> 0.46 us  [the longest x1 0.46 us: per_device(): lax.ppermute(line[2], 'col', [(b ^ 1, b) for b in range(count)])]
    ppermute x1, waiting for transfers between devices: 0.01 us -> 3.4 us  [gather_line(): far = lax.ppermute(factor, 'col', [(b ^ 2, b) for b in range(count)])]
    ppermute x1, waiting for transfers between devices: 0.01 us -> 1.96 us  [gather_line(): near = lax.ppermute(factor, 'col', [(b ^ 1, b) for b in range(count)])]
    ppermute x8 -> x2, waiting for transfers between devices: 4.47 us -> 4.05 us  [the longest x1 4.04 us: per_device(): lax.ppermute(line[2], 'col', [(b ^ 1, b) for b in range(count)])]
  transfers between devices with their start and end apart: 11 -> 5, of which waited for: 6 -> 4; matrix products, arithmetic and copies ran while one was open for 0% -> 0% of each run, Pallas kernels for 7% -> 5%
where the time goes in v6:
time: 29.8 us; the launch traced here: 29.6 us
  waiting for transfers between devices  9.49 us (32%)
  blocking collectives  9.05 us (30%)
  starting transfers between devices  6.21 us (21%)
  Pallas kernels  4.84 us (16%)
    all_to_all x1, blocking collectives, per_device(): plane = lax.all_to_all(copies, 'row', 0, 0)  9.05 us
    ppermute x1, waiting for transfers between devices, per_device(): lax.ppermute(line[2], 'col', [(b ^ 1, b) for b in range(count)])  4.04 us
    ppermute x1, waiting for transfers between devices, gather_line(): far = lax.ppermute(factor, 'col', [(b ^ 2, b) for b in range(count)])  3.4 us
    ppermute x1, starting transfers between devices, per_device(): lax.ppermute(factor, ('row', 'col'), [(a * count + b, slots[a][b] * count...  2.99 us
    ppermute x1, starting transfers between devices, gather_line(): far = lax.ppermute(factor, 'col', [(b ^ 2, b) for b in range(count)])  2.46 us
    ppermute x1, waiting for transfers between devices, gather_line(): near = lax.ppermute(factor, 'col', [(b ^ 1, b) for b in range(count)])  1.96 us
    pallas_call x1, Pallas kernels, update_trailing(): pl.pallas_call(body, out_shape=jax.ShapeDtypeStruct(share.shape, jnp.floa...  1.81 us
    pallas_call x1, Pallas kernels, load_share(): pl.pallas_call(load_kernel, out_shape=jax.ShapeDtypeStruct((rows, LANES),...  1.6 us
  transfers between devices with their start and end apart: 5, of which 4 were waited for; matrix products, arithmetic and copies ran while one was open for 0% of the time, Pallas kernels for 5%

profile of v6, /device:TPU:0, one launch (start us, length us, event | category | flops | bytes accessed | tf_op | source)
XLA Modules:
  0.0 29.6 jit_solution(14920911796439349780)
XLA Ops:
  0.0 1.4 %factor.1.after_ref.refs_0_ = bf16[2,64,256]{2,1,0:T(8,128)(2,1)S(1)} custom-call(f32[4,1,64,256]{3,2,1,0:T(8,128)} %panel_ref.1, f32[256,256]{1,0:T(8,128)} %inverse_ref.1), custom_call_target="tpu_custom_call" | custom-call | tf_op jit(solution)/shard_map/factor/pallas_call | solution.py:41
  1.4 3.0 %collective-permute-start = (bf16[2,64,256]{2,1,0:T(8,128)(2,1)S(1)}, bf16[2,64,256]{2,1,0:T(8,128)(2,1)S(1)}, u32[]{:S(2)}, u32[]{:S(2)}) collective-permute-start(bf16[2,64,256]{2,1,0:T(8,128)(2,1)S(1)} %factor.1.after_ref.refs_0_), channel_id=1, source_target_pairs={{0,8},{2,24},{4,16},{6,0},{8,2},{10,18},{12,10},{14,26},{16,20},{1... | collective-permute-start | bytes 196616 | tf_op jit(solution)/shard_map/ppermute | solution.py:180
  4.4 1.6 %load_share.1.refs_6_ = f32[4096,128]{1,0:T(8,128)S(1)} custom-call(bf16[2,64,256]{2,1,0:T(8,128)(2,1)S(1)} %factor.1.after_ref.refs_0_, f32[8192,128]{1,0:T(8,128)} %bitcast.2), custom_call_target="tpu_custom_call" | custom-call | bytes 4194304 | tf_op jit(solution)/shard_map/load_share/pallas_call | solution.py:95
  6.0 2.5 %collective-permute-start.2 = (bf16[2,64,256]{2,1,0:T(8,128)(2,1)S(1)}, bf16[2,64,256]{2,1,0:T(8,128)(2,1)S(1)}, u32[]{:S(2)}, u32[]{:S(2)}) collective-permute-start(bf16[2,64,256]{2,1,0:T(8,128)(2,1)S(1)} %factor.1.after_ref.refs_0_), channel_id=1, source_target_pairs={{4,0},{6,2},{0,4},{2,6},{5,1},{7,3},{1,5},{3,7},{12,8},{14,10},{8,... | collective-permute-start | bytes 196616 | tf_op jit(solution)/shard_map/ppermute | solution.py:80
  8.5 0.3 %collective-permute-start.1 = (bf16[2,64,256]{2,1,0:T(8,128)(2,1)S(1)}, bf16[2,64,256]{2,1,0:T(8,128)(2,1)S(1)}, u32[]{:S(2)}, u32[]{:S(2)}) collective-permute-start(bf16[2,64,256]{2,1,0:T(8,128)(2,1)S(1)} %factor.1.after_ref.refs_0_), channel_id=1, source_target_pairs={{2,0},{0,2},{6,4},{4,6},{3,1},{1,3},{7,5},{5,7},{10,8},{8,10},{14,... | collective-permute-start | bytes 196616 | tf_op jit(solution)/shard_map/ppermute | solution.py:81
  8.8 0.1 collective-permute-done
  8.9 3.4 %collective-permute-done.2.refs_2_ = bf16[2,64,256]{2,1,0:T(8,128)(2,1)S(1)} collective-permute-done((bf16[2,64,256]{2,1,0:T(8,128)(2,1)S(1)}, bf16[2,64,256]{2,1,0:T(8,128)(2,1)S(1)}, u32[]{:S(2)}, u32[]{:S(2)}) %collective-permute-start.2) | collective-permute-done | bytes 65568 | tf_op jit(solution)/shard_map/ppermute | solution.py:80
  12.3 2.0 %collective-permute-done.1.refs_1_ = bf16[2,64,256]{2,1,0:T(8,128)(2,1)S(1)} collective-permute-done((bf16[2,64,256]{2,1,0:T(8,128)(2,1)S(1)}, bf16[2,64,256]{2,1,0:T(8,128)(2,1)S(1)}, u32[]{:S(2)}, u32[]{:S(2)}) %collective-permute-start.1) | collective-permute-done | bytes 65568 | tf_op jit(solution)/shard_map/ppermute | solution.py:81
  14.3 9.1 %all_to_all.5.refs_4_ = bf16[4,2,64,256]{3,2,1,0:T(8,128)(2,1)S(1)} all-to-all(bf16[4,2,64,256]{3,2,1,0:T(8,128)(2,1)S(1)} %broadcast_in_dim.2), channel_id=1, replica_groups=mesh['row'=4,'col'=4,'layer'=2] {'row'}, dimensions={0} | all-to-all | bytes 524288 | tf_op jit(solution)/shard_map/all_to_all | solution.py:190
  23.3 0.0 collective-permute-start.4
  23.3 0.5 %collective-permute-start.3 = (bf16[2,64,256]{2,1,0:T(8,128)(2,1)S(1)}, bf16[2,64,256]{2,1,0:T(8,128)(2,1)S(1)}, u32[]{:S(2)}, u32[]{:S(2)}) collective-permute-start(bf16[2,64,256]{2,1,0:T(8,128)(2,1)S(1)} %collective-permute-done.2.refs_2_), channel_id=1, source_target_pairs={{2,0},{0,2},{6,4},{4,6},{3,1},{1,3},{7,5},{5,7},{10,8},{8,10},{14,... | collective-permute-start | bytes 196616 | tf_op jit(solution)/shard_map/ppermute | solution.py:189
  23.8 4.0 %collective-permute-done.3.refs_3_ = bf16[2,64,256]{2,1,0:T(8,128)(2,1)S(1)} collective-permute-done((bf16[2,64,256]{2,1,0:T(8,128)(2,1)S(1)}, bf16[2,64,256]{2,1,0:T(8,128)(2,1)S(1)}, u32[]{:S(2)}, u32[]{:S(2)}) %collective-permute-start.3) | collective-permute-done | bytes 65568 | tf_op jit(solution)/shard_map/ppermute | solution.py:189
  27.8 0.0 collective-permute-done.4.refs_5_
  27.8 1.8 %update.1 = f32[4096,128]{1,0:T(8,128)} custom-call(bf16[2,64,256]{2,1,0:T(8,128)(2,1)S(1)} %factor.1.after_ref.refs_0_, bf16[2,64,256]{2,1,0:T(8,128)(2,1)S(1)} %collective-permute-done.1.refs_1_, bf16[2,64,256]{2,1,0:T(8,128)(2,1)S(1)} %collective-permute-done.2.refs_2_, bf16[2,64,256]{2,1,0:T(8,128)(2,1)S(1)} %collective-permute-done.3.refs_3_, ...), custom_call_target="tpu_custom_call" | custom-call | tf_op jit(solution)/shard_map/update/pallas_call | solution.py:156
  (1 shorter events, 0.0 us)
Async XLA Ops:
  1.4 7.4 %collective-permute-start = (bf16[2,64,256]{2,1,0:T(8,128)(2,1)S(1)}, bf16[2,64,256]{2,1,0:T(8,128)(2,1)S(1)}, u32[]{:S(2)}, u32[]{:S(2)}) collective-permute-start(bf16[2,64,256]{2,1,0:T(8,128)(2,1)S(1)} %factor.1.after_ref.refs_0_), channel_id=1, source_target_pairs={{0,8},{2,24},{4,16},{6,0},{8,2},{10,18},{12,10},{14,26},{16,20},{1... | collective-permute-start | bytes 196616 | tf_op jit(solution)/shard_map/ppermute | solution.py:180
  6.0 6.2 %collective-permute-start.2 = (bf16[2,64,256]{2,1,0:T(8,128)(2,1)S(1)}, bf16[2,64,256]{2,1,0:T(8,128)(2,1)S(1)}, u32[]{:S(2)}, u32[]{:S(2)}) collective-permute-start(bf16[2,64,256]{2,1,0:T(8,128)(2,1)S(1)} %factor.1.after_ref.refs_0_), channel_id=1, source_target_pairs={{4,0},{6,2},{0,4},{2,6},{5,1},{7,3},{1,5},{3,7},{12,8},{14,10},{8,... | collective-permute-start | bytes 196616 | tf_op jit(solution)/shard_map/ppermute | solution.py:80
  8.5 5.8 %collective-permute-start.1 = (bf16[2,64,256]{2,1,0:T(8,128)(2,1)S(1)}, bf16[2,64,256]{2,1,0:T(8,128)(2,1)S(1)}, u32[]{:S(2)}, u32[]{:S(2)}) collective-permute-start(bf16[2,64,256]{2,1,0:T(8,128)(2,1)S(1)} %factor.1.after_ref.refs_0_), channel_id=1, source_target_pairs={{2,0},{0,2},{6,4},{4,6},{3,1},{1,3},{7,5},{5,7},{10,8},{8,10},{14,... | collective-permute-start | bytes 196616 | tf_op jit(solution)/shard_map/ppermute | solution.py:81
  23.3 4.5 %collective-permute-start.4 = (bf16[4,2,64,256]{3,2,1,0:T(8,128)(2,1)S(1)}, bf16[4,2,64,256]{3,2,1,0:T(8,128)(2,1)S(1)}, u32[]{:S(2)}, u32[]{:S(2)}) collective-permute-start(bf16[4,2,64,256]{3,2,1,0:T(8,128)(2,1)S(1)} %all_to_all.5.refs_4_), channel_id=1, source_target_pairs={{1,0},{0,1},{3,2},{2,3},{5,4},{4,5},{7,6},{6,7},{9,8},{8,9},{11,10... | collective-permute-start | bytes 786440 | tf_op jit(solution)/shard_map/ppermute | solution.py:193
  23.3 4.5 %collective-permute-start.3 = (bf16[2,64,256]{2,1,0:T(8,128)(2,1)S(1)}, bf16[2,64,256]{2,1,0:T(8,128)(2,1)S(1)}, u32[]{:S(2)}, u32[]{:S(2)}) collective-permute-start(bf16[2,64,256]{2,1,0:T(8,128)(2,1)S(1)} %collective-permute-done.2.refs_2_), channel_id=1, source_target_pairs={{2,0},{0,2},{6,4},{4,6},{3,1},{1,3},{7,5},{5,7},{10,8},{8,10},{14,... | collective-permute-start | bytes 196616 | tf_op jit(solution)/shard_map/ppermute | solution.py:189

commit v7 on v5

--- a/solution.py
+++ b/solution.py
@@ -59,7 +59,7 @@
 
 def plane_slots(count):
     if count == 4:
-        return ((1, 3, 2, 0), (0, 2, 1, 3), (2, 0, 3, 1), (3, 1, 0, 2))
+        return ((3, 1, 2, 0), (3, 2, 0, 1), (2, 3, 1, 0), (3, 1, 2, 0))
     return tuple(tuple(count - 1 - b for b in range(count)) for _ in range(count))
 
 
@@ -127,18 +127,14 @@
     stores = []
     for chunk in range(chunks):
         k, first_row = divmod(chunk * CHUNK_ROWS, tile)
-        for j in range(col_tiles):
-            update = lax.dot_general(
-                row_buf[k, first_row : first_row + CHUNK_ROWS, :],
-                col_buf[j],
-                (((1,), (1,)), ((), ())),
-                preferred_element_type=jnp.float32,
-            )
-            for part in range(tile // LANES):
-                first = chunk * chunk_lines + j * (tile // LANES) + part
-                at = pl.ds(first, CHUNK_ROWS, stride=per_row)
-                out_buf[at, :] = share_ref[at, :] - update[:, part * LANES : (part + 1) * LANES]
+        update = lax.dot_general(
+            row_buf[k, first_row : first_row + CHUNK_ROWS, :],
+            col_buf[...].reshape(col_tiles * tile, -1),
+            (((1,), (1,)), ((), ())),
+            preferred_element_type=jnp.float32,
+        )
         written = pl.ds(chunk * chunk_lines, chunk_lines)
+        out_buf[written, :] = share_ref[written, :] - update.reshape(chunk_lines, LANES)
         store = pltpu.make_async_copy(out_buf.at[written], out_ref.at[written], out_sems.at[chunk])
         store.start()
         stores.append(store)

time: 23 us -> 22.6 us (0.983)
  starting transfers between devices: 13.4 us -> 12.5 us
  waiting for transfers between devices: 4.57 us -> 5.01 us
    ppermute x1, starting transfers between devices: 2.46 us -> 1.5 us  [gather_line(): far = lax.ppermute(factor, 'col', [(b ^ 2, b) for b in range(count)])]
    ppermute x1, starting transfers between devices: 2.99 us -> 3.95 us  [per_device(): lax.ppermute(factor, ('row', 'col'), [(a * count + b, slots[a][b] * count...]
    ppermute x3, starting transfers between devices: 6.98 us -> 6.17 us  [per_device(): lax.ppermute(moved, 'row', [(partner(a, step, count), a) for a in range(c...]
    ppermute x4, waiting for transfers between devices: 0.6 us -> 0.99 us  [per_device(): others += [lax.ppermute(piece, 'layer', pairs) for piece in plane]]
  transfers between devices with their start and end apart: 11 -> 11, of which waited for: 6 -> 5; matrix products, arithmetic and copies ran while one was open for 0% -> 0% of each run, Pallas kernels for 7% -> 7%
where the time goes in v7:
time: 22.6 us; the launch traced here: 22.4 us
  starting transfers between devices  12.5 us (55%)
  waiting for transfers between devices  5.01 us (22%)
  Pallas kernels  4.9 us (22%)
    ppermute x3, starting transfers between devices, per_device(): lax.ppermute(moved, 'row', [(partner(a, step, count), a) for a in range(c...  6.17 us
    ppermute x1, starting transfers between devices, per_device(): lax.ppermute(factor, ('row', 'col'), [(a * count + b, slots[a][b] * count...  3.95 us
    ppermute x3, waiting for transfers between devices, per_device(): lax.ppermute(moved, 'row', [(partner(a, step, count), a) for a in range(c...  3.67 us
    pallas_call x1, Pallas kernels, update_trailing(): pl.pallas_call(body, out_shape=jax.ShapeDtypeStruct(share.shape, jnp.floa...  1.86 us
    pallas_call x1, Pallas kernels, load_share(): pl.pallas_call(load_kernel, out_shape=jax.ShapeDtypeStruct((rows, LANES),...  1.6 us
    ppermute x1, starting transfers between devices, gather_line(): far = lax.ppermute(factor, 'col', [(b ^ 2, b) for b in range(count)])  1.5 us
    pallas_call x1, Pallas kernels, make_factor(): pl.pallas_call(factor_kernel, out_shape=jax.ShapeDtypeStruct((half, tile_...  1.44 us
    ppermute x4, waiting for transfers between devices, per_device(): others += [lax.ppermute(piece, 'layer', pairs) for piece in plane]  0.99 us
  transfers between devices with their start and end apart: 11, of which 5 were waited for; matrix products, arithmetic and copies ran while one was open for 0% of the time, Pallas kernels for 7%

profile of v7, /device:TPU:0, one launch (start us, length us, event | category | flops | bytes accessed | tf_op | source)
XLA Modules:
  0.0 22.4 jit_solution(6398893203702980601)
XLA Ops:
  0.0 1.4 %factor.1.after_ref.refs_0_ = bf16[2,64,256]{2,1,0:T(8,128)(2,1)S(1)} custom-call(f32[4,1,64,256]{3,2,1,0:T(8,128)} %panel_ref.1, f32[256,256]{1,0:T(8,128)} %inverse_ref.1), custom_call_target="tpu_custom_call" | custom-call | tf_op jit(solution)/shard_map/factor/pallas_call | solution.py:41
  1.4 3.9 %collective-permute-start.3 = (bf16[2,64,256]{2,1,0:T(8,128)(2,1)S(1)}, bf16[2,64,256]{2,1,0:T(8,128)(2,1)S(1)}, u32[]{:S(2)}, u32[]{:S(2)}) collective-permute-start(bf16[2,64,256]{2,1,0:T(8,128)(2,1)S(1)} %factor.1.after_ref.refs_0_), channel_id=1, source_target_pairs={{0,24},{2,8},{4,16},{6,0},{8,26},{10,18},{12,2},{14,10},{16,20},{1... | collective-permute-start | bytes 196616 | tf_op jit(solution)/shard_map/ppermute | solution.py:177
  5.4 1.6 %load_share.1.refs_12_ = f32[4096,128]{1,0:T(8,128)S(1)} custom-call(bf16[2,64,256]{2,1,0:T(8,128)(2,1)S(1)} %factor.1.after_ref.refs_0_, f32[8192,128]{1,0:T(8,128)} %bitcast.2), custom_call_target="tpu_custom_call" | custom-call | bytes 4194304 | tf_op jit(solution)/shard_map/load_share/pallas_call | solution.py:96
  7.0 1.5 %collective-permute-start.1 = (bf16[2,64,256]{2,1,0:T(8,128)(2,1)S(1)}, bf16[2,64,256]{2,1,0:T(8,128)(2,1)S(1)}, u32[]{:S(2)}, u32[]{:S(2)}) collective-permute-start(bf16[2,64,256]{2,1,0:T(8,128)(2,1)S(1)} %factor.1.after_ref.refs_0_), channel_id=1, source_target_pairs={{4,0},{6,2},{0,4},{2,6},{5,1},{7,3},{1,5},{3,7},{12,8},{14,10},{8,... | collective-permute-start | bytes 196616 | tf_op jit(solution)/shard_map/ppermute | solution.py:80
  8.5 0.3 %collective-permute-start = (bf16[2,64,256]{2,1,0:T(8,128)(2,1)S(1)}, bf16[2,64,256]{2,1,0:T(8,128)(2,1)S(1)}, u32[]{:S(2)}, u32[]{:S(2)}) collective-permute-start(bf16[2,64,256]{2,1,0:T(8,128)(2,1)S(1)} %factor.1.after_ref.refs_0_), channel_id=1, source_target_pairs={{2,0},{0,2},{6,4},{4,6},{3,1},{1,3},{7,5},{5,7},{10,8},{8,10},{14,... | collective-permute-start | bytes 196616 | tf_op jit(solution)/shard_map/ppermute | solution.py:81
  8.8 0.1 collective-permute-done.3.refs_4_
  8.9 2.8 %collective-permute-start.6 = (bf16[2,64,256]{2,1,0:T(8,128)(2,1)S(1)}, bf16[2,64,256]{2,1,0:T(8,128)(2,1)S(1)}, u32[]{:S(2)}, u32[]{:S(2)}) collective-permute-start(bf16[2,64,256]{2,1,0:T(8,128)(2,1)S(1)} %collective-permute-done.3.refs_4_), channel_id=1, source_target_pairs={{24,0},{16,8},{8,16},{0,24},{25,1},{17,9},{9,17},{1,25},{26,2},{18... | collective-permute-start | bytes 196616 | tf_op jit(solution)/shard_map/ppermute | solution.py:185
  11.7 3.4 %collective-permute-start.5 = (bf16[2,64,256]{2,1,0:T(8,128)(2,1)S(1)}, bf16[2,64,256]{2,1,0:T(8,128)(2,1)S(1)}, u32[]{:S(2)}, u32[]{:S(2)}) collective-permute-start(bf16[2,64,256]{2,1,0:T(8,128)(2,1)S(1)} %collective-permute-done.3.refs_4_), channel_id=1, source_target_pairs={{16,0},{24,8},{0,16},{8,24},{17,1},{25,9},{1,17},{9,25},{18,2},{26... | collective-permute-start | bytes 196616 | tf_op jit(solution)/shard_map/ppermute | solution.py:185
  15.1 0.0 collective-permute-start.4
  15.1 0.0 collective-permute-done.1.refs_2_
  15.1 0.0 collective-permute-start.7
  15.1 0.0 collective-permute-done.refs_1_
  15.1 0.1 collective-permute-start.2
  15.2 0.0 collective-permute-done.6.refs_7_
  15.2 0.5 %collective-permute-start.10 = (bf16[2,64,256]{2,1,0:T(8,128)(2,1)S(1)}, bf16[2,64,256]{2,1,0:T(8,128)(2,1)S(1)}, u32[]{:S(2)}, u32[]{:S(2)}) collective-permute-start(bf16[2,64,256]{2,1,0:T(8,128)(2,1)S(1)} %collective-permute-done.6.refs_7_), channel_id=1, source_target_pairs={{1,0},{0,1},{3,2},{2,3},{5,4},{4,5},{7,6},{6,7},{9,8},{8,9},{11,10... | collective-permute-start | bytes 196616 | tf_op jit(solution)/shard_map/ppermute | solution.py:189
  15.7 1.6 %collective-permute-done.5.refs_6_ = bf16[2,64,256]{2,1,0:T(8,128)(2,1)S(1)} collective-permute-done((bf16[2,64,256]{2,1,0:T(8,128)(2,1)S(1)}, bf16[2,64,256]{2,1,0:T(8,128)(2,1)S(1)}, u32[]{:S(2)}, u32[]{:S(2)}) %collective-permute-start.5) | collective-permute-done | bytes 65568 | tf_op jit(solution)/shard_map/ppermute | solution.py:185
  17.3 0.0 collective-permute-start.9
  17.3 2.0 %collective-permute-done.4.refs_5_ = bf16[2,64,256]{2,1,0:T(8,128)(2,1)S(1)} collective-permute-done((bf16[2,64,256]{2,1,0:T(8,128)(2,1)S(1)}, bf16[2,64,256]{2,1,0:T(8,128)(2,1)S(1)}, u32[]{:S(2)}, u32[]{:S(2)}) %collective-permute-start.4) | collective-permute-done | bytes 65568 | tf_op jit(solution)/shard_map/ppermute | solution.py:185
  19.3 0.0 collective-permute-start.8
  19.3 0.0 collective-permute-done.7.refs_8_
  19.3 0.3 %collective-permute-done.2.refs_3_ = bf16[2,64,256]{2,1,0:T(8,128)(2,1)S(1)} collective-permute-done((bf16[2,64,256]{2,1,0:T(8,128)(2,1)S(1)}, bf16[2,64,256]{2,1,0:T(8,128)(2,1)S(1)}, u32[]{:S(2)}, u32[]{:S(2)}) %collective-permute-start.2) | collective-permute-done | bytes 65568 | tf_op jit(solution)/shard_map/ppermute | solution.py:82
  19.6 0.0 collective-permute-done.10.refs_11_
  19.6 0.0 collective-permute-done.9.refs_10_
  19.6 1.0 %collective-permute-done.8.refs_9_ = bf16[2,64,256]{2,1,0:T(8,128)(2,1)S(1)} collective-permute-done((bf16[2,64,256]{2,1,0:T(8,128)(2,1)S(1)}, bf16[2,64,256]{2,1,0:T(8,128)(2,1)S(1)}, u32[]{:S(2)}, u32[]{:S(2)}) %collective-permute-start.8) | collective-permute-done | bytes 65568 | tf_op jit(solution)/shard_map/ppermute | solution.py:189
  20.6 1.9 %update.1 = f32[4096,128]{1,0:T(8,128)} custom-call(bf16[2,64,256]{2,1,0:T(8,128)(2,1)S(1)} %factor.1.after_ref.refs_0_, bf16[2,64,256]{2,1,0:T(8,128)(2,1)S(1)} %collective-permute-done.refs_1_, bf16[2,64,256]{2,1,0:T(8,128)(2,1)S(1)} %collective-permute-done.1.refs_2_, bf16[2,64,256]{2,1,0:T(8,128)(2,1)S(1)} %collective-permute-done.2.refs_3_, ...), custom_call_target="tpu_custom_call" | custom-call | tf_op jit(solution)/shard_map/update/pallas_call | solution.py:153
Async XLA Ops:
  1.4 7.4 %collective-permute-start.3 = (bf16[2,64,256]{2,1,0:T(8,128)(2,1)S(1)}, bf16[2,64,256]{2,1,0:T(8,128)(2,1)S(1)}, u32[]{:S(2)}, u32[]{:S(2)}) collective-permute-start(bf16[2,64,256]{2,1,0:T(8,128)(2,1)S(1)} %factor.1.after_ref.refs_0_), channel_id=1, source_target_pairs={{0,24},{2,8},{4,16},{6,0},{8,26},{10,18},{12,2},{14,10},{16,20},{1... | collective-permute-start | bytes 196616 | tf_op jit(solution)/shard_map/ppermute | solution.py:177
  7.0 8.1 %collective-permute-start.1 = (bf16[2,64,256]{2,1,0:T(8,128)(2,1)S(1)}, bf16[2,64,256]{2,1,0:T(8,128)(2,1)S(1)}, u32[]{:S(2)}, u32[]{:S(2)}) collective-permute-start(bf16[2,64,256]{2,1,0:T(8,128)(2,1)S(1)} %factor.1.after_ref.refs_0_), channel_id=1, source_target_pairs={{4,0},{6,2},{0,4},{2,6},{5,1},{7,3},{1,5},{3,7},{12,8},{14,10},{8,... | collective-permute-start | bytes 196616 | tf_op jit(solution)/shard_map/ppermute | solution.py:80
  8.5 6.6 %collective-permute-start = (bf16[2,64,256]{2,1,0:T(8,128)(2,1)S(1)}, bf16[2,64,256]{2,1,0:T(8,128)(2,1)S(1)}, u32[]{:S(2)}, u32[]{:S(2)}) collective-permute-start(bf16[2,64,256]{2,1,0:T(8,128)(2,1)S(1)} %factor.1.after_ref.refs_0_), channel_id=1, source_target_pairs={{2,0},{0,2},{6,4},{4,6},{3,1},{1,3},{7,5},{5,7},{10,8},{8,10},{14,... | collective-permute-start | bytes 196616 | tf_op jit(solution)/shard_map/ppermute | solution.py:81
  8.9 6.3 %collective-permute-start.6 = (bf16[2,64,256]{2,1,0:T(8,128)(2,1)S(1)}, bf16[2,64,256]{2,1,0:T(8,128)(2,1)S(1)}, u32[]{:S(2)}, u32[]{:S(2)}) collective-permute-start(bf16[2,64,256]{2,1,0:T(8,128)(2,1)S(1)} %collective-permute-done.3.refs_4_), channel_id=1, source_target_pairs={{24,0},{16,8},{8,16},{0,24},{25,1},{17,9},{9,17},{1,25},{26,2},{18... | collective-permute-start | bytes 196616 | tf_op jit(solution)/shard_map/ppermute | solution.py:185
  11.7 5.6 %collective-permute-start.5 = (bf16[2,64,256]{2,1,0:T(8,128)(2,1)S(1)}, bf16[2,64,256]{2,1,0:T(8,128)(2,1)S(1)}, u32[]{:S(2)}, u32[]{:S(2)}) collective-permute-start(bf16[2,64,256]{2,1,0:T(8,128)(2,1)S(1)} %collective-permute-done.3.refs_4_), channel_id=1, source_target_pairs={{16,0},{24,8},{0,16},{8,24},{17,1},{25,9},{1,17},{9,25},{18,2},{26... | collective-permute-start | bytes 196616 | tf_op jit(solution)/shard_map/ppermute | solution.py:185
  15.1 4.3 %collective-permute-start.4 = (bf16[2,64,256]{2,1,0:T(8,128)(2,1)S(1)}, bf16[2,64,256]{2,1,0:T(8,128)(2,1)S(1)}, u32[]{:S(2)}, u32[]{:S(2)}) collective-permute-start(bf16[2,64,256]{2,1,0:T(8,128)(2,1)S(1)} %collective-permute-done.3.refs_4_), channel_id=1, source_target_pairs={{8,0},{0,8},{24,16},{16,24},{9,1},{1,9},{25,17},{17,25},{10,2},{2,... | collective-permute-start | bytes 196616 | tf_op jit(solution)/shard_map/ppermute | solution.py:185
  15.1 4.3 %collective-permute-start.7 = (bf16[2,64,256]{2,1,0:T(8,128)(2,1)S(1)}, bf16[2,64,256]{2,1,0:T(8,128)(2,1)S(1)}, u32[]{:S(2)}, u32[]{:S(2)}) collective-permute-start(bf16[2,64,256]{2,1,0:T(8,128)(2,1)S(1)} %collective-permute-done.3.refs_4_), channel_id=1, source_target_pairs={{1,0},{0,1},{3,2},{2,3},{5,4},{4,5},{7,6},{6,7},{9,8},{8,9},{11,10... | collective-permute-start | bytes 196616 | tf_op jit(solution)/shard_map/ppermute | solution.py:189
  15.1 4.5 %collective-permute-start.2 = (bf16[2,64,256]{2,1,0:T(8,128)(2,1)S(1)}, bf16[2,64,256]{2,1,0:T(8,128)(2,1)S(1)}, u32[]{:S(2)}, u32[]{:S(2)}) collective-permute-start(bf16[2,64,256]{2,1,0:T(8,128)(2,1)S(1)} %collective-permute-done.1.refs_2_), channel_id=1, source_target_pairs={{2,0},{0,2},{6,4},{4,6},{3,1},{1,3},{7,5},{5,7},{10,8},{8,10},{14,... | collective-permute-start | bytes 196616 | tf_op jit(solution)/shard_map/ppermute | solution.py:82
  15.2 4.4 %collective-permute-start.10 = (bf16[2,64,256]{2,1,0:T(8,128)(2,1)S(1)}, bf16[2,64,256]{2,1,0:T(8,128)(2,1)S(1)}, u32[]{:S(2)}, u32[]{:S(2)}) collective-permute-start(bf16[2,64,256]{2,1,0:T(8,128)(2,1)S(1)} %collective-permute-done.6.refs_7_), channel_id=1, source_target_pairs={{1,0},{0,1},{3,2},{2,3},{5,4},{4,5},{7,6},{6,7},{9,8},{8,9},{11,10... | collective-permute-start | bytes 196616 | tf_op jit(solution)/shard_map/ppermute | solution.py:189
  17.3 2.3 %collective-permute-start.9 = (bf16[2,64,256]{2,1,0:T(8,128)(2,1)S(1)}, bf16[2,64,256]{2,1,0:T(8,128)(2,1)S(1)}, u32[]{:S(2)}, u32[]{:S(2)}) collective-permute-start(bf16[2,64,256]{2,1,0:T(8,128)(2,1)S(1)} %collective-permute-done.5.refs_6_), channel_id=1, source_target_pairs={{1,0},{0,1},{3,2},{2,3},{5,4},{4,5},{7,6},{6,7},{9,8},{8,9},{11,10... | collective-permute-start | bytes 196616 | tf_op jit(solution)/shard_map/ppermute | solution.py:189
  19.3 1.3 %collective-permute-start.8 = (bf16[2,64,256]{2,1,0:T(8,128)(2,1)S(1)}, bf16[2,64,256]{2,1,0:T(8,128)(2,1)S(1)}, u32[]{:S(2)}, u32[]{:S(2)}) collective-permute-start(bf16[2,64,256]{2,1,0:T(8,128)(2,1)S(1)} %collective-permute-done.4.refs_5_), channel_id=1, source_target_pairs={{1,0},{0,1},{3,2},{2,3},{5,4},{4,5},{7,6},{6,7},{9,8},{8,9},{11,10... | collective-permute-start | bytes 196616 | tf_op jit(solution)/shard_map/ppermute | solution.py:189

commit v8 on v7

--- a/solution.py
+++ b/solution.py
@@ -7,6 +7,7 @@
 
 LANES = 128
 CHUNK_ROWS = 128
+LOADS = 8
 VMEM_BYTES = 24 * 1024 * 1024
 LOAD_VMEM_BYTES = 52000 * 1024
 FACTOR_VMEM_BYTES = 55040 * 1024
@@ -83,12 +84,20 @@
     return [factor, near, far, both]
 
 
-def load_kernel(after_ref, lines_ref, share_ref, sem):
+def load_kernel(after_ref, lines_ref, share_ref, sems):
     rows = share_ref.shape[0]
+    part = rows // LOADS
     layer = lax.axis_index("layer")
-    load = pltpu.make_async_copy(lines_ref.at[pl.ds(layer * rows, rows)], share_ref, sem)
-    load.start()
-    load.wait()
+    loads = [
+        pltpu.make_async_copy(
+            lines_ref.at[pl.ds(layer * rows + i * part, part)], share_ref.at[pl.ds(i * part, part)], sems.at[i]
+        )
+        for i in range(LOADS)
+    ]
+    for load in loads:
+        load.start()
+    for load in loads:
+        load.wait()
 
 
 def load_share(after, lines, layers):
@@ -98,7 +107,7 @@
         out_shape=jax.ShapeDtypeStruct((rows, LANES), jnp.float32),
         in_specs=[pl.BlockSpec(memory_space=pl.ANY), pl.BlockSpec(memory_space=pltpu.HBM)],
         out_specs=pl.BlockSpec(memory_space=pltpu.VMEM),
-        scratch_shapes=[pltpu.SemaphoreType.DMA],
+        scratch_shapes=[pltpu.SemaphoreType.DMA((LOADS,))],
         compiler_params=pltpu.CompilerParams(vmem_limit_bytes=LOAD_VMEM_BYTES),
         cost_estimate=pl.CostEstimate(flops=0, bytes_accessed=rows * LANES * 8, transcendentals=0),
         name="load_share",
@@ -181,7 +190,7 @@
     loaded_factor, share = lax.optimization_barrier((factor, share))
     line = gather_line(loaded_factor, count)
     plane = [moved] + [None] * (count - 1)
-    for step in reversed(range(1, count)):
+    for step in (count - 1, *range(1, count - 1)):
         plane[step] = lax.ppermute(moved, "row", [(partner(a, step, count), a) for a in range(count)])
     others = []
     for shift in range(1, layers):

time: 22.6 us -> 22.7 us (level)
  no operation moved by 1% of the time
where the time goes in v8:
time: 22.7 us; the launch traced here: 22.5 us
  starting transfers between devices  12.5 us (55%)
  waiting for transfers between devices  5.04 us (22%)
  Pallas kernels  4.87 us (21%)
    ppermute x3, starting transfers between devices, per_device(): lax.ppermute(moved, 'row', [(partner(a, step, count), a) for a in range(c...  6.23 us
    ppermute x1, starting transfers between devices, per_device(): lax.ppermute(factor, ('row', 'col'), [(a * count + b, slots[a][b] * count...  3.95 us
    ppermute x3, waiting for transfers between devices, per_device(): lax.ppermute(moved, 'row', [(partner(a, step, count), a) for a in range(c...  3.67 us
    pallas_call x1, Pallas kernels, update_trailing(): pl.pallas_call(body, out_shape=jax.ShapeDtypeStruct(share.shape, jnp.floa...  1.86 us
    pallas_call x1, Pallas kernels, load_share(): pl.pallas_call(load_kernel, out_shape=jax.ShapeDtypeStruct((rows, LANES),...  1.57 us
    ppermute x1, starting transfers between devices, gather_line(): far = lax.ppermute(factor, 'col', [(b ^ 2, b) for b in range(count)])  1.5 us
    pallas_call x1, Pallas kernels, make_factor(): pl.pallas_call(factor_kernel, out_shape=jax.ShapeDtypeStruct((half, tile_...  1.44 us
    ppermute x4, waiting for transfers between devices, per_device(): others += [lax.ppermute(piece, 'layer', pairs) for piece in plane]  0.99 us
  transfers between devices with their start and end apart: 11, of which 5 were waited for; matrix products, arithmetic and copies ran while one was open for 0% of the time, Pallas kernels for 7%

profile of v8, /device:TPU:0, one launch (start us, length us, event | category | flops | bytes accessed | tf_op | source)
XLA Modules:
  0.0 22.5 jit_solution(16633248690561698172)
XLA Ops:
  0.0 1.4 %factor.1.after_ref.refs_0_ = bf16[2,64,256]{2,1,0:T(8,128)(2,1)S(1)} custom-call(f32[4,1,64,256]{3,2,1,0:T(8,128)} %panel_ref.1, f32[256,256]{1,0:T(8,128)} %inverse_ref.1), custom_call_target="tpu_custom_call" | custom-call | tf_op jit(solution)/shard_map/factor/pallas_call | solution.py:42
  1.4 3.9 %collective-permute-start.3 = (bf16[2,64,256]{2,1,0:T(8,128)(2,1)S(1)}, bf16[2,64,256]{2,1,0:T(8,128)(2,1)S(1)}, u32[]{:S(2)}, u32[]{:S(2)}) collective-permute-start(bf16[2,64,256]{2,1,0:T(8,128)(2,1)S(1)} %factor.1.after_ref.refs_0_), channel_id=1, source_target_pairs={{0,24},{2,8},{4,16},{6,0},{8,26},{10,18},{12,2},{14,10},{16,20},{1... | collective-permute-start | bytes 196616 | tf_op jit(solution)/shard_map/ppermute | solution.py:186
  5.4 1.6 %load_share.1.refs_12_ = f32[4096,128]{1,0:T(8,128)S(1)} custom-call(bf16[2,64,256]{2,1,0:T(8,128)(2,1)S(1)} %factor.1.after_ref.refs_0_, f32[8192,128]{1,0:T(8,128)} %bitcast.2), custom_call_target="tpu_custom_call" | custom-call | bytes 4194304 | tf_op jit(solution)/shard_map/load_share/pallas_call | solution.py:105
  7.0 1.5 %collective-permute-start.1 = (bf16[2,64,256]{2,1,0:T(8,128)(2,1)S(1)}, bf16[2,64,256]{2,1,0:T(8,128)(2,1)S(1)}, u32[]{:S(2)}, u32[]{:S(2)}) collective-permute-start(bf16[2,64,256]{2,1,0:T(8,128)(2,1)S(1)} %factor.1.after_ref.refs_0_), channel_id=1, source_target_pairs={{4,0},{6,2},{0,4},{2,6},{5,1},{7,3},{1,5},{3,7},{12,8},{14,10},{8,... | collective-permute-start | bytes 196616 | tf_op jit(solution)/shard_map/ppermute | solution.py:81
  8.5 0.3 %collective-permute-start = (bf16[2,64,256]{2,1,0:T(8,128)(2,1)S(1)}, bf16[2,64,256]{2,1,0:T(8,128)(2,1)S(1)}, u32[]{:S(2)}, u32[]{:S(2)}) collective-permute-start(bf16[2,64,256]{2,1,0:T(8,128)(2,1)S(1)} %factor.1.after_ref.refs_0_), channel_id=1, source_target_pairs={{2,0},{0,2},{6,4},{4,6},{3,1},{1,3},{7,5},{5,7},{10,8},{8,10},{14,... | collective-permute-start | bytes 196616 | tf_op jit(solution)/shard_map/ppermute | solution.py:82
  8.8 0.1 collective-permute-done.3.refs_4_
  8.9 2.8 %collective-permute-start.6 = (bf16[2,64,256]{2,1,0:T(8,128)(2,1)S(1)}, bf16[2,64,256]{2,1,0:T(8,128)(2,1)S(1)}, u32[]{:S(2)}, u32[]{:S(2)}) collective-permute-start(bf16[2,64,256]{2,1,0:T(8,128)(2,1)S(1)} %collective-permute-done.3.refs_4_), channel_id=1, source_target_pairs={{24,0},{16,8},{8,16},{0,24},{25,1},{17,9},{9,17},{1,25},{26,2},{18... | collective-permute-start | bytes 196616 | tf_op jit(solution)/shard_map/ppermute | solution.py:194
  11.7 3.4 %collective-permute-start.5 = (bf16[2,64,256]{2,1,0:T(8,128)(2,1)S(1)}, bf16[2,64,256]{2,1,0:T(8,128)(2,1)S(1)}, u32[]{:S(2)}, u32[]{:S(2)}) collective-permute-start(bf16[2,64,256]{2,1,0:T(8,128)(2,1)S(1)} %collective-permute-done.3.refs_4_), channel_id=1, source_target_pairs={{16,0},{24,8},{0,16},{8,24},{17,1},{25,9},{1,17},{9,25},{18,2},{26... | collective-permute-start | bytes 196616 | tf_op jit(solution)/shard_map/ppermute | solution.py:194
  15.1 0.0 collective-permute-start.4
  15.1 0.0 collective-permute-done.1.refs_2_
  15.1 0.0 collective-permute-start.7
  15.1 0.0 collective-permute-done.refs_1_
  15.2 0.1 collective-permute-start.2
  15.2 0.0 collective-permute-done.6.refs_7_
  15.2 0.5 %collective-permute-start.10 = (bf16[2,64,256]{2,1,0:T(8,128)(2,1)S(1)}, bf16[2,64,256]{2,1,0:T(8,128)(2,1)S(1)}, u32[]{:S(2)}, u32[]{:S(2)}) collective-permute-start(bf16[2,64,256]{2,1,0:T(8,128)(2,1)S(1)} %collective-permute-done.6.refs_7_), channel_id=1, source_target_pairs={{1,0},{0,1},{3,2},{2,3},{5,4},{4,5},{7,6},{6,7},{9,8},{8,9},{11,10... | collective-permute-start | bytes 196616 | tf_op jit(solution)/shard_map/ppermute | solution.py:198
  15.7 1.6 %collective-permute-done.5.refs_6_ = bf16[2,64,256]{2,1,0:T(8,128)(2,1)S(1)} collective-permute-done((bf16[2,64,256]{2,1,0:T(8,128)(2,1)S(1)}, bf16[2,64,256]{2,1,0:T(8,128)(2,1)S(1)}, u32[]{:S(2)}, u32[]{:S(2)}) %collective-permute-start.5) | collective-permute-done | bytes 65568 | tf_op jit(solution)/shard_map/ppermute | solution.py:194
  17.4 0.0 collective-permute-start.9
  17.4 2.0 %collective-permute-done.4.refs_5_ = bf16[2,64,256]{2,1,0:T(8,128)(2,1)S(1)} collective-permute-done((bf16[2,64,256]{2,1,0:T(8,128)(2,1)S(1)}, bf16[2,64,256]{2,1,0:T(8,128)(2,1)S(1)}, u32[]{:S(2)}, u32[]{:S(2)}) %collective-permute-start.4) | collective-permute-done | bytes 65568 | tf_op jit(solution)/shard_map/ppermute | solution.py:194
  19.4 0.0 collective-permute-start.8
  19.4 0.0 collective-permute-done.7.refs_8_
  19.4 0.3 %collective-permute-done.2.refs_3_ = bf16[2,64,256]{2,1,0:T(8,128)(2,1)S(1)} collective-permute-done((bf16[2,64,256]{2,1,0:T(8,128)(2,1)S(1)}, bf16[2,64,256]{2,1,0:T(8,128)(2,1)S(1)}, u32[]{:S(2)}, u32[]{:S(2)}) %collective-permute-start.2) | collective-permute-done | bytes 65568 | tf_op jit(solution)/shard_map/ppermute | solution.py:83
  19.7 0.0 collective-permute-done.10.refs_11_
  19.7 0.0 collective-permute-done.9.refs_10_
  19.7 1.0 %collective-permute-done.8.refs_9_ = bf16[2,64,256]{2,1,0:T(8,128)(2,1)S(1)} collective-permute-done((bf16[2,64,256]{2,1,0:T(8,128)(2,1)S(1)}, bf16[2,64,256]{2,1,0:T(8,128)(2,1)S(1)}, u32[]{:S(2)}, u32[]{:S(2)}) %collective-permute-start.8) | collective-permute-done | bytes 65568 | tf_op jit(solution)/shard_map/ppermute | solution.py:198
  20.6 1.9 %update.1 = f32[4096,128]{1,0:T(8,128)} custom-call(bf16[2,64,256]{2,1,0:T(8,128)(2,1)S(1)} %factor.1.after_ref.refs_0_, bf16[2,64,256]{2,1,0:T(8,128)(2,1)S(1)} %collective-permute-done.refs_1_, bf16[2,64,256]{2,1,0:T(8,128)(2,1)S(1)} %collective-permute-done.1.refs_2_, bf16[2,64,256]{2,1,0:T(8,128)(2,1)S(1)} %collective-permute-done.2.refs_3_, ...), custom_call_target="tpu_custom_call" | custom-call | tf_op jit(solution)/shard_map/update/pallas_call | solution.py:162
Async XLA Ops:
  1.4 7.4 %collective-permute-start.3 = (bf16[2,64,256]{2,1,0:T(8,128)(2,1)S(1)}, bf16[2,64,256]{2,1,0:T(8,128)(2,1)S(1)}, u32[]{:S(2)}, u32[]{:S(2)}) collective-permute-start(bf16[2,64,256]{2,1,0:T(8,128)(2,1)S(1)} %factor.1.after_ref.refs_0_), channel_id=1, source_target_pairs={{0,24},{2,8},{4,16},{6,0},{8,26},{10,18},{12,2},{14,10},{16,20},{1... | collective-permute-start | bytes 196616 | tf_op jit(solution)/shard_map/ppermute | solution.py:186
  7.0 8.2 %collective-permute-start.1 = (bf16[2,64,256]{2,1,0:T(8,128)(2,1)S(1)}, bf16[2,64,256]{2,1,0:T(8,128)(2,1)S(1)}, u32[]{:S(2)}, u32[]{:S(2)}) collective-permute-start(bf16[2,64,256]{2,1,0:T(8,128)(2,1)S(1)} %factor.1.after_ref.refs_0_), channel_id=1, source_target_pairs={{4,0},{6,2},{0,4},{2,6},{5,1},{7,3},{1,5},{3,7},{12,8},{14,10},{8,... | collective-permute-start | bytes 196616 | tf_op jit(solution)/shard_map/ppermute | solution.py:81
  8.5 6.7 %collective-permute-start = (bf16[2,64,256]{2,1,0:T(8,128)(2,1)S(1)}, bf16[2,64,256]{2,1,0:T(8,128)(2,1)S(1)}, u32[]{:S(2)}, u32[]{:S(2)}) collective-permute-start(bf16[2,64,256]{2,1,0:T(8,128)(2,1)S(1)} %factor.1.after_ref.refs_0_), channel_id=1, source_target_pairs={{2,0},{0,2},{6,4},{4,6},{3,1},{1,3},{7,5},{5,7},{10,8},{8,10},{14,... | collective-permute-start | bytes 196616 | tf_op jit(solution)/shard_map/ppermute | solution.py:82
  8.9 6.3 %collective-permute-start.6 = (bf16[2,64,256]{2,1,0:T(8,128)(2,1)S(1)}, bf16[2,64,256]{2,1,0:T(8,128)(2,1)S(1)}, u32[]{:S(2)}, u32[]{:S(2)}) collective-permute-start(bf16[2,64,256]{2,1,0:T(8,128)(2,1)S(1)} %collective-permute-done.3.refs_4_), channel_id=1, source_target_pairs={{24,0},{16,8},{8,16},{0,24},{25,1},{17,9},{9,17},{1,25},{26,2},{18... | collective-permute-start | bytes 196616 | tf_op jit(solution)/shard_map/ppermute | solution.py:194
  11.7 5.7 %collective-permute-start.5 = (bf16[2,64,256]{2,1,0:T(8,128)(2,1)S(1)}, bf16[2,64,256]{2,1,0:T(8,128)(2,1)S(1)}, u32[]{:S(2)}, u32[]{:S(2)}) collective-permute-start(bf16[2,64,256]{2,1,0:T(8,128)(2,1)S(1)} %collective-permute-done.3.refs_4_), channel_id=1, source_target_pairs={{16,0},{24,8},{0,16},{8,24},{17,1},{25,9},{1,17},{9,25},{18,2},{26... | collective-permute-start | bytes 196616 | tf_op jit(solution)/shard_map/ppermute | solution.py:194
  15.1 4.3 %collective-permute-start.4 = (bf16[2,64,256]{2,1,0:T(8,128)(2,1)S(1)}, bf16[2,64,256]{2,1,0:T(8,128)(2,1)S(1)}, u32[]{:S(2)}, u32[]{:S(2)}) collective-permute-start(bf16[2,64,256]{2,1,0:T(8,128)(2,1)S(1)} %collective-permute-done.3.refs_4_), channel_id=1, source_target_pairs={{8,0},{0,8},{24,16},{16,24},{9,1},{1,9},{25,17},{17,25},{10,2},{2,... | collective-permute-start | bytes 196616 | tf_op jit(solution)/shard_map/ppermute | solution.py:194
  15.1 4.3 %collective-permute-start.7 = (bf16[2,64,256]{2,1,0:T(8,128)(2,1)S(1)}, bf16[2,64,256]{2,1,0:T(8,128)(2,1)S(1)}, u32[]{:S(2)}, u32[]{:S(2)}) collective-permute-start(bf16[2,64,256]{2,1,0:T(8,128)(2,1)S(1)} %collective-permute-done.3.refs_4_), channel_id=1, source_target_pairs={{1,0},{0,1},{3,2},{2,3},{5,4},{4,5},{7,6},{6,7},{9,8},{8,9},{11,10... | collective-permute-start | bytes 196616 | tf_op jit(solution)/shard_map/ppermute | solution.py:198
  15.2 4.5 %collective-permute-start.2 = (bf16[2,64,256]{2,1,0:T(8,128)(2,1)S(1)}, bf16[2,64,256]{2,1,0:T(8,128)(2,1)S(1)}, u32[]{:S(2)}, u32[]{:S(2)}) collective-permute-start(bf16[2,64,256]{2,1,0:T(8,128)(2,1)S(1)} %collective-permute-done.1.refs_2_), channel_id=1, source_target_pairs={{2,0},{0,2},{6,4},{4,6},{3,1},{1,3},{7,5},{5,7},{10,8},{8,10},{14,... | collective-permute-start | bytes 196616 | tf_op jit(solution)/shard_map/ppermute | solution.py:83
  15.2 4.4 %collective-permute-start.10 = (bf16[2,64,256]{2,1,0:T(8,128)(2,1)S(1)}, bf16[2,64,256]{2,1,0:T(8,128)(2,1)S(1)}, u32[]{:S(2)}, u32[]{:S(2)}) collective-permute-start(bf16[2,64,256]{2,1,0:T(8,128)(2,1)S(1)} %collective-permute-done.6.refs_7_), channel_id=1, source_target_pairs={{1,0},{0,1},{3,2},{2,3},{5,4},{4,5},{7,6},{6,7},{9,8},{8,9},{11,10... | collective-permute-start | bytes 196616 | tf_op jit(solution)/shard_map/ppermute | solution.py:198
  17.4 2.3 %collective-permute-start.9 = (bf16[2,64,256]{2,1,0:T(8,128)(2,1)S(1)}, bf16[2,64,256]{2,1,0:T(8,128)(2,1)S(1)}, u32[]{:S(2)}, u32[]{:S(2)}) collective-permute-start(bf16[2,64,256]{2,1,0:T(8,128)(2,1)S(1)} %collective-permute-done.5.refs_6_), channel_id=1, source_target_pairs={{1,0},{0,1},{3,2},{2,3},{5,4},{4,5},{7,6},{6,7},{9,8},{8,9},{11,10... | collective-permute-start | bytes 196616 | tf_op jit(solution)/shard_map/ppermute | solution.py:198
  19.4 1.3 %collective-permute-start.8 = (bf16[2,64,256]{2,1,0:T(8,128)(2,1)S(1)}, bf16[2,64,256]{2,1,0:T(8,128)(2,1)S(1)}, u32[]{:S(2)}, u32[]{:S(2)}) collective-permute-start(bf16[2,64,256]{2,1,0:T(8,128)(2,1)S(1)} %collective-permute-done.4.refs_5_), channel_id=1, source_target_pairs={{1,0},{0,1},{3,2},{2,3},{5,4},{4,5},{7,6},{6,7},{9,8},{8,9},{11,10... | collective-permute-start | bytes 196616 | tf_op jit(solution)/shard_map/ppermute | solution.py:198

commit v9 on v7

--- a/solution.py
+++ b/solution.py
@@ -63,6 +63,10 @@
     return tuple(tuple(count - 1 - b for b in range(count)) for _ in range(count))
 
 
+def plane_steps(count):
+    return (0, 2, 1, 3) if count == 4 else tuple(range(count))
+
+
 def slab_of(slots, plane, place):
     slab = jnp.int32(0)
     for at, row in enumerate(slots):
@@ -112,9 +116,9 @@
     r, c, layer = (lax.axis_index(axis) for axis in AXES)
     slots = plane_slots(pieces)
     per_row = col_tiles * tile // LANES
-    for step in range(pieces):
+    for step, plane_step in enumerate(plane_steps(pieces)):
         row_at = pl.multiple_of(partner(c, step, pieces) * tile_rows, tile_rows)
-        slab = slab_of(slots, c, partner(r, step, pieces))
+        slab = slab_of(slots, c, partner(r, plane_step, pieces))
         col_at = pl.multiple_of(slab * tile_rows, tile_rows)
         for k in range(half):
             row_buf[k, pl.ds(row_at, tile_rows), :] = row_refs[step][k]
@@ -180,9 +184,9 @@
     share = load_share(factor, trailing.reshape(-1, LANES), layers)
     loaded_factor, share = lax.optimization_barrier((factor, share))
     line = gather_line(loaded_factor, count)
-    plane = [moved] + [None] * (count - 1)
-    for step in reversed(range(1, count)):
-        plane[step] = lax.ppermute(moved, "row", [(partner(a, step, count), a) for a in range(count)])
+    plane = [moved]
+    for step in plane_steps(count)[1:]:
+        plane.append(lax.ppermute(moved, "row", [(partner(a, step, count), a) for a in range(count)]))
     others = []
     for shift in range(1, layers):
         pairs = [((l + shift) % layers, l) for l in range(layers)]

time: 22.6 us -> 21.6 us (0.956)
  waiting for transfers between devices: 5.01 us -> 4.02 us
    ppermute x3, waiting for transfers between devices: 3.67 us -> 2.21 us  [per_device(): lax.ppermute(moved, 'row', [(partner(a, step, count), a) for a in range(c...]
    ppermute x1, waiting for transfers between devices: 0.26 us -> 1.71 us  [gather_line(): both = lax.ppermute(far, 'col', [(b ^ 1, b) for b in range(count)])]
    ppermute x4, waiting for transfers between devices: 0.99 us -> 0.01 us  [per_device(): others += [lax.ppermute(piece, 'layer', pairs) for piece in plane]]
  transfers between devices with their start and end apart: 11 -> 11, of which waited for: 5 -> 4; matrix products, arithmetic and copies ran while one was open for 0% -> 0% of each run, Pallas kernels for 7% -> 7%
where the time goes in v9:
time: 21.6 us; the launch traced here: 21.5 us
  starting transfers between devices  12.5 us (58%)
  Pallas kernels  4.91 us (23%)
  waiting for transfers between devices  4.02 us (19%)
    ppermute x3, starting transfers between devices, per_device(): lax.ppermute(moved, 'row', [(partner(a, step, count), a) for a in range(c...  6.17 us
    ppermute x1, starting transfers between devices, per_device(): lax.ppermute(factor, ('row', 'col'), [(a * count + b, slots[a][b] * count...  3.95 us
    ppermute x3, waiting for transfers between devices, per_device(): lax.ppermute(moved, 'row', [(partner(a, step, count), a) for a in range(c...  2.21 us
    pallas_call x1, Pallas kernels, update_trailing(): pl.pallas_call(body, out_shape=jax.ShapeDtypeStruct(share.shape, jnp.floa...  1.87 us
    ppermute x1, waiting for transfers between devices, gather_line(): both = lax.ppermute(far, 'col', [(b ^ 1, b) for b in range(count)])  1.71 us
    pallas_call x1, Pallas kernels, load_share(): pl.pallas_call(load_kernel, out_shape=jax.ShapeDtypeStruct((rows, LANES),...  1.6 us
    ppermute x1, starting transfers between devices, gather_line(): far = lax.ppermute(factor, 'col', [(b ^ 2, b) for b in range(count)])  1.5 us
    pallas_call x1, Pallas kernels, make_factor(): pl.pallas_call(factor_kernel, out_shape=jax.ShapeDtypeStruct((half, tile_...  1.44 us
  transfers between devices with their start and end apart: 11, of which 4 were waited for; matrix products, arithmetic and copies ran while one was open for 0% of the time, Pallas kernels for 7%

profile of v9, /device:TPU:0, one launch (start us, length us, event | category | flops | bytes accessed | tf_op | source)
XLA Modules:
  0.0 21.5 jit_solution(6915992691290182557)
XLA Ops:
  0.0 1.4 %factor.1.after_ref.refs_0_ = bf16[2,64,256]{2,1,0:T(8,128)(2,1)S(1)} custom-call(f32[4,1,64,256]{3,2,1,0:T(8,128)} %panel_ref.1, f32[256,256]{1,0:T(8,128)} %inverse_ref.1), custom_call_target="tpu_custom_call" | custom-call | tf_op jit(solution)/shard_map/factor/pallas_call | solution.py:41
  1.4 3.9 %collective-permute-start.3 = (bf16[2,64,256]{2,1,0:T(8,128)(2,1)S(1)}, bf16[2,64,256]{2,1,0:T(8,128)(2,1)S(1)}, u32[]{:S(2)}, u32[]{:S(2)}) collective-permute-start(bf16[2,64,256]{2,1,0:T(8,128)(2,1)S(1)} %factor.1.after_ref.refs_0_), channel_id=1, source_target_pairs={{0,24},{2,8},{4,16},{6,0},{8,26},{10,18},{12,2},{14,10},{16,20},{1... | collective-permute-start | bytes 196616 | tf_op jit(solution)/shard_map/ppermute | solution.py:181
  5.4 1.6 %load_share.1.refs_12_ = f32[4096,128]{1,0:T(8,128)S(1)} custom-call(bf16[2,64,256]{2,1,0:T(8,128)(2,1)S(1)} %factor.1.after_ref.refs_0_, f32[8192,128]{1,0:T(8,128)} %bitcast.2), custom_call_target="tpu_custom_call" | custom-call | bytes 4194304 | tf_op jit(solution)/shard_map/load_share/pallas_call | solution.py:100
  7.0 1.5 %collective-permute-start.1 = (bf16[2,64,256]{2,1,0:T(8,128)(2,1)S(1)}, bf16[2,64,256]{2,1,0:T(8,128)(2,1)S(1)}, u32[]{:S(2)}, u32[]{:S(2)}) collective-permute-start(bf16[2,64,256]{2,1,0:T(8,128)(2,1)S(1)} %factor.1.after_ref.refs_0_), channel_id=1, source_target_pairs={{4,0},{6,2},{0,4},{2,6},{5,1},{7,3},{1,5},{3,7},{12,8},{14,10},{8,... | collective-permute-start | bytes 196616 | tf_op jit(solution)/shard_map/ppermute | solution.py:84
  8.5 0.3 %collective-permute-start = (bf16[2,64,256]{2,1,0:T(8,128)(2,1)S(1)}, bf16[2,64,256]{2,1,0:T(8,128)(2,1)S(1)}, u32[]{:S(2)}, u32[]{:S(2)}) collective-permute-start(bf16[2,64,256]{2,1,0:T(8,128)(2,1)S(1)} %factor.1.after_ref.refs_0_), channel_id=1, source_target_pairs={{2,0},{0,2},{6,4},{4,6},{3,1},{1,3},{7,5},{5,7},{10,8},{8,10},{14,... | collective-permute-start | bytes 196616 | tf_op jit(solution)/shard_map/ppermute | solution.py:85
  8.8 0.1 collective-permute-done.3.refs_4_
  8.9 2.8 %collective-permute-start.6 = (bf16[2,64,256]{2,1,0:T(8,128)(2,1)S(1)}, bf16[2,64,256]{2,1,0:T(8,128)(2,1)S(1)}, u32[]{:S(2)}, u32[]{:S(2)}) collective-permute-start(bf16[2,64,256]{2,1,0:T(8,128)(2,1)S(1)} %collective-permute-done.3.refs_4_), channel_id=1, source_target_pairs={{24,0},{16,8},{8,16},{0,24},{25,1},{17,9},{9,17},{1,25},{26,2},{18... | collective-permute-start | bytes 196616 | tf_op jit(solution)/shard_map/ppermute | solution.py:189
  11.7 1.9 %collective-permute-start.5 = (bf16[2,64,256]{2,1,0:T(8,128)(2,1)S(1)}, bf16[2,64,256]{2,1,0:T(8,128)(2,1)S(1)}, u32[]{:S(2)}, u32[]{:S(2)}) collective-permute-start(bf16[2,64,256]{2,1,0:T(8,128)(2,1)S(1)} %collective-permute-done.3.refs_4_), channel_id=1, source_target_pairs={{8,0},{0,8},{24,16},{16,24},{9,1},{1,9},{25,17},{17,25},{10,2},{2,... | collective-permute-start | bytes 196616 | tf_op jit(solution)/shard_map/ppermute | solution.py:189
  13.6 1.5 %collective-permute-start.4 = (bf16[2,64,256]{2,1,0:T(8,128)(2,1)S(1)}, bf16[2,64,256]{2,1,0:T(8,128)(2,1)S(1)}, u32[]{:S(2)}, u32[]{:S(2)}) collective-permute-start(bf16[2,64,256]{2,1,0:T(8,128)(2,1)S(1)} %collective-permute-done.3.refs_4_), channel_id=1, source_target_pairs={{16,0},{24,8},{0,16},{8,24},{17,1},{25,9},{1,17},{9,25},{18,2},{26... | collective-permute-start | bytes 196616 | tf_op jit(solution)/shard_map/ppermute | solution.py:189
  15.1 0.0 collective-permute-done.1.refs_2_
  15.1 0.0 collective-permute-start.7
  15.1 0.0 collective-permute-done.refs_1_
  15.1 0.1 collective-permute-start.2
  15.2 0.0 collective-permute-done.6.refs_7_
  15.2 0.5 %collective-permute-start.10 = (bf16[2,64,256]{2,1,0:T(8,128)(2,1)S(1)}, bf16[2,64,256]{2,1,0:T(8,128)(2,1)S(1)}, u32[]{:S(2)}, u32[]{:S(2)}) collective-permute-start(bf16[2,64,256]{2,1,0:T(8,128)(2,1)S(1)} %collective-permute-done.6.refs_7_), channel_id=1, source_target_pairs={{1,0},{0,1},{3,2},{2,3},{5,4},{4,5},{7,6},{6,7},{9,8},{8,9},{11,10... | collective-permute-start | bytes 196616 | tf_op jit(solution)/shard_map/ppermute | solution.py:193
  15.7 0.9 %collective-permute-done.5.refs_6_ = bf16[2,64,256]{2,1,0:T(8,128)(2,1)S(1)} collective-permute-done((bf16[2,64,256]{2,1,0:T(8,128)(2,1)S(1)}, bf16[2,64,256]{2,1,0:T(8,128)(2,1)S(1)}, u32[]{:S(2)}, u32[]{:S(2)}) %collective-permute-start.5) | collective-permute-done | bytes 65568 | tf_op jit(solution)/shard_map/ppermute | solution.py:189
  16.5 0.0 collective-permute-start.9
  16.6 1.3 %collective-permute-done.4.refs_5_ = bf16[2,64,256]{2,1,0:T(8,128)(2,1)S(1)} collective-permute-done((bf16[2,64,256]{2,1,0:T(8,128)(2,1)S(1)}, bf16[2,64,256]{2,1,0:T(8,128)(2,1)S(1)}, u32[]{:S(2)}, u32[]{:S(2)}) %collective-permute-start.4) | collective-permute-done | bytes 65568 | tf_op jit(solution)/shard_map/ppermute | solution.py:189
  17.9 0.0 collective-permute-start.8
  17.9 0.0 collective-permute-done.7.refs_8_
  17.9 1.7 %collective-permute-done.2.refs_3_ = bf16[2,64,256]{2,1,0:T(8,128)(2,1)S(1)} collective-permute-done((bf16[2,64,256]{2,1,0:T(8,128)(2,1)S(1)}, bf16[2,64,256]{2,1,0:T(8,128)(2,1)S(1)}, u32[]{:S(2)}, u32[]{:S(2)}) %collective-permute-start.2) | collective-permute-done | bytes 65568 | tf_op jit(solution)/shard_map/ppermute | solution.py:86
  19.6 0.0 collective-permute-done.10.refs_11_
  19.6 0.0 collective-permute-done.9.refs_10_
  19.6 0.0 collective-permute-done.8.refs_9_
  19.6 1.9 %update.1 = f32[4096,128]{1,0:T(8,128)} custom-call(bf16[2,64,256]{2,1,0:T(8,128)(2,1)S(1)} %factor.1.after_ref.refs_0_, bf16[2,64,256]{2,1,0:T(8,128)(2,1)S(1)} %collective-permute-done.refs_1_, bf16[2,64,256]{2,1,0:T(8,128)(2,1)S(1)} %collective-permute-done.1.refs_2_, bf16[2,64,256]{2,1,0:T(8,128)(2,1)S(1)} %collective-permute-done.2.refs_3_, ...), custom_call_target="tpu_custom_call" | custom-call | tf_op jit(solution)/shard_map/update/pallas_call | solution.py:157
Async XLA Ops:
  1.4 7.4 %collective-permute-start.3 = (bf16[2,64,256]{2,1,0:T(8,128)(2,1)S(1)}, bf16[2,64,256]{2,1,0:T(8,128)(2,1)S(1)}, u32[]{:S(2)}, u32[]{:S(2)}) collective-permute-start(bf16[2,64,256]{2,1,0:T(8,128)(2,1)S(1)} %factor.1.after_ref.refs_0_), channel_id=1, source_target_pairs={{0,24},{2,8},{4,16},{6,0},{8,26},{10,18},{12,2},{14,10},{16,20},{1... | collective-permute-start | bytes 196616 | tf_op jit(solution)/shard_map/ppermute | solution.py:181
  7.0 8.1 %collective-permute-start.1 = (bf16[2,64,256]{2,1,0:T(8,128)(2,1)S(1)}, bf16[2,64,256]{2,1,0:T(8,128)(2,1)S(1)}, u32[]{:S(2)}, u32[]{:S(2)}) collective-permute-start(bf16[2,64,256]{2,1,0:T(8,128)(2,1)S(1)} %factor.1.after_ref.refs_0_), channel_id=1, source_target_pairs={{4,0},{6,2},{0,4},{2,6},{5,1},{7,3},{1,5},{3,7},{12,8},{14,10},{8,... | collective-permute-start | bytes 196616 | tf_op jit(solution)/shard_map/ppermute | solution.py:84
  8.5 6.6 %collective-permute-start = (bf16[2,64,256]{2,1,0:T(8,128)(2,1)S(1)}, bf16[2,64,256]{2,1,0:T(8,128)(2,1)S(1)}, u32[]{:S(2)}, u32[]{:S(2)}) collective-permute-start(bf16[2,64,256]{2,1,0:T(8,128)(2,1)S(1)} %factor.1.after_ref.refs_0_), channel_id=1, source_target_pairs={{2,0},{0,2},{6,4},{4,6},{3,1},{1,3},{7,5},{5,7},{10,8},{8,10},{14,... | collective-permute-start | bytes 196616 | tf_op jit(solution)/shard_map/ppermute | solution.py:85
  8.9 6.3 %collective-permute-start.6 = (bf16[2,64,256]{2,1,0:T(8,128)(2,1)S(1)}, bf16[2,64,256]{2,1,0:T(8,128)(2,1)S(1)}, u32[]{:S(2)}, u32[]{:S(2)}) collective-permute-start(bf16[2,64,256]{2,1,0:T(8,128)(2,1)S(1)} %collective-permute-done.3.refs_4_), channel_id=1, source_target_pairs={{24,0},{16,8},{8,16},{0,24},{25,1},{17,9},{9,17},{1,25},{26,2},{18... | collective-permute-start | bytes 196616 | tf_op jit(solution)/shard_map/ppermute | solution.py:189
  11.7 4.8 %collective-permute-start.5 = (bf16[2,64,256]{2,1,0:T(8,128)(2,1)S(1)}, bf16[2,64,256]{2,1,0:T(8,128)(2,1)S(1)}, u32[]{:S(2)}, u32[]{:S(2)}) collective-permute-start(bf16[2,64,256]{2,1,0:T(8,128)(2,1)S(1)} %collective-permute-done.3.refs_4_), channel_id=1, source_target_pairs={{8,0},{0,8},{24,16},{16,24},{9,1},{1,9},{25,17},{17,25},{10,2},{2,... | collective-permute-start | bytes 196616 | tf_op jit(solution)/shard_map/ppermute | solution.py:189
  13.6 4.3 %collective-permute-start.4 = (bf16[2,64,256]{2,1,0:T(8,128)(2,1)S(1)}, bf16[2,64,256]{2,1,0:T(8,128)(2,1)S(1)}, u32[]{:S(2)}, u32[]{:S(2)}) collective-permute-start(bf16[2,64,256]{2,1,0:T(8,128)(2,1)S(1)} %collective-permute-done.3.refs_4_), channel_id=1, source_target_pairs={{16,0},{24,8},{0,16},{8,24},{17,1},{25,9},{1,17},{9,25},{18,2},{26... | collective-permute-start | bytes 196616 | tf_op jit(solution)/shard_map/ppermute | solution.py:189
  15.1 2.8 %collective-permute-start.7 = (bf16[2,64,256]{2,1,0:T(8,128)(2,1)S(1)}, bf16[2,64,256]{2,1,0:T(8,128)(2,1)S(1)}, u32[]{:S(2)}, u32[]{:S(2)}) collective-permute-start(bf16[2,64,256]{2,1,0:T(8,128)(2,1)S(1)} %collective-permute-done.3.refs_4_), channel_id=1, source_target_pairs={{1,0},{0,1},{3,2},{2,3},{5,4},{4,5},{7,6},{6,7},{9,8},{8,9},{11,10... | collective-permute-start | bytes 196616 | tf_op jit(solution)/shard_map/ppermute | solution.py:193
  15.1 4.5 %collective-permute-start.2 = (bf16[2,64,256]{2,1,0:T(8,128)(2,1)S(1)}, bf16[2,64,256]{2,1,0:T(8,128)(2,1)S(1)}, u32[]{:S(2)}, u32[]{:S(2)}) collective-permute-start(bf16[2,64,256]{2,1,0:T(8,128)(2,1)S(1)} %collective-permute-done.1.refs_2_), channel_id=1, source_target_pairs={{2,0},{0,2},{6,4},{4,6},{3,1},{1,3},{7,5},{5,7},{10,8},{8,10},{14,... | collective-permute-start | bytes 196616 | tf_op jit(solution)/shard_map/ppermute | solution.py:86
  15.2 4.4 %collective-permute-start.10 = (bf16[2,64,256]{2,1,0:T(8,128)(2,1)S(1)}, bf16[2,64,256]{2,1,0:T(8,128)(2,1)S(1)}, u32[]{:S(2)}, u32[]{:S(2)}) collective-permute-start(bf16[2,64,256]{2,1,0:T(8,128)(2,1)S(1)} %collective-permute-done.6.refs_7_), channel_id=1, source_target_pairs={{1,0},{0,1},{3,2},{2,3},{5,4},{4,5},{7,6},{6,7},{9,8},{8,9},{11,10... | collective-permute-start | bytes 196616 | tf_op jit(solution)/shard_map/ppermute | solution.py:193
  16.5 3.0 %collective-permute-start.9 = (bf16[2,64,256]{2,1,0:T(8,128)(2,1)S(1)}, bf16[2,64,256]{2,1,0:T(8,128)(2,1)S(1)}, u32[]{:S(2)}, u32[]{:S(2)}) collective-permute-start(bf16[2,64,256]{2,1,0:T(8,128)(2,1)S(1)} %collective-permute-done.5.refs_6_), channel_id=1, source_target_pairs={{1,0},{0,1},{3,2},{2,3},{5,4},{4,5},{7,6},{6,7},{9,8},{8,9},{11,10... | collective-permute-start | bytes 196616 | tf_op jit(solution)/shard_map/ppermute | solution.py:193
  17.9 1.7 %collective-permute-start.8 = (bf16[2,64,256]{2,1,0:T(8,128)(2,1)S(1)}, bf16[2,64,256]{2,1,0:T(8,128)(2,1)S(1)}, u32[]{:S(2)}, u32[]{:S(2)}) collective-permute-start(bf16[2,64,256]{2,1,0:T(8,128)(2,1)S(1)} %collective-permute-done.4.refs_5_), channel_id=1, source_target_pairs={{1,0},{0,1},{3,2},{2,3},{5,4},{4,5},{7,6},{6,7},{9,8},{8,9},{11,10... | collective-permute-start | bytes 196616 | tf_op jit(solution)/shard_map/ppermute | solution.py:193

commit v10 on v7

--- a/solution.py
+++ b/solution.py
@@ -63,6 +63,12 @@
     return tuple(tuple(count - 1 - b for b in range(count)) for _ in range(count))
 
 
+def plane_mates(count, layer):
+    if count == 4:
+        return (0, 2, 1, 3) if layer % 2 == 0 else (0, 1, 2, 3)
+    return tuple(range(count))
+
+
 def slab_of(slots, plane, place):
     slab = jnp.int32(0)
     for at, row in enumerate(slots):
@@ -112,14 +118,18 @@
     r, c, layer = (lax.axis_index(axis) for axis in AXES)
     slots = plane_slots(pieces)
     per_row = col_tiles * tile // LANES
+    mates = [plane_mates(pieces, l) for l in range(layers)]
     for step in range(pieces):
         row_at = pl.multiple_of(partner(c, step, pieces) * tile_rows, tile_rows)
-        slab = slab_of(slots, c, partner(r, step, pieces))
-        col_at = pl.multiple_of(slab * tile_rows, tile_rows)
         for k in range(half):
             row_buf[k, pl.ds(row_at, tile_rows), :] = row_refs[step][k]
         for shift in range(layers):
             owner = lax.rem(layer + shift, layers)
+            mate = jnp.int32(mates[0][step])
+            for l in range(1, layers):
+                mate = jnp.where(owner == l, mates[l][step], mate)
+            slab = slab_of(slots, c, partner(r, mate, pieces))
+            col_at = pl.multiple_of(slab * tile_rows, tile_rows)
             for k in range(half):
                 col_buf[owner * half + k, pl.ds(col_at, tile_rows), :] = col_refs[shift * pieces + step][k]
     chunks = half * (tile // CHUNK_ROWS)
@@ -180,9 +190,14 @@
     share = load_share(factor, trailing.reshape(-1, LANES), layers)
     loaded_factor, share = lax.optimization_barrier((factor, share))
     line = gather_line(loaded_factor, count)
-    plane = [moved] + [None] * (count - 1)
-    for step in reversed(range(1, count)):
-        plane[step] = lax.ppermute(moved, "row", [(partner(a, step, count), a) for a in range(count)])
+    plane = [moved]
+    for step in range(1, count):
+        pairs = [
+            (partner(a, plane_mates(count, l)[step], count) * layers + l, a * layers + l)
+            for a in range(count)
+            for l in range(layers)
+        ]
+        plane.append(lax.ppermute(moved, ("row", "layer"), pairs))
     others = []
     for shift in range(1, layers):
         pairs = [((l + shift) % layers, l) for l in range(layers)]

time: 22.6 us -> 21.7 us (0.960)
  waiting for transfers between devices: 5.01 us -> 4.02 us
    ppermute x3, waiting for transfers between devices: 3.67 us -> 2.21 us  [per_device(): plane.append(lax.ppermute(moved, ('row', 'layer'), pairs))]
    ppermute x1, waiting for transfers between devices: 0.26 us -> 1.71 us  [gather_line(): both = lax.ppermute(far, 'col', [(b ^ 1, b) for b in range(count)])]
    ppermute x4, waiting for transfers between devices: 0.99 us -> 0.01 us  [per_device(): others += [lax.ppermute(piece, 'layer', pairs) for piece in plane]]
  transfers between devices with their start and end apart: 11 -> 11, of which waited for: 5 -> 4; matrix products, arithmetic and copies ran while one was open for 0% -> 0% of each run, Pallas kernels for 7% -> 7%
where the time goes in v10:
time: 21.7 us; the launch traced here: 21.5 us
  starting transfers between devices  12.5 us (58%)
  Pallas kernels  4.95 us (23%)
  waiting for transfers between devices  4.02 us (19%)
    ppermute x3, starting transfers between devices, per_device(): plane.append(lax.ppermute(moved, ('row', 'layer'), pairs))  6.17 us
    ppermute x1, starting transfers between devices, per_device(): lax.ppermute(factor, ('row', 'col'), [(a * count + b, slots[a][b] * count...  3.95 us
    ppermute x3, waiting for transfers between devices, per_device(): plane.append(lax.ppermute(moved, ('row', 'layer'), pairs))  2.21 us
    pallas_call x1, Pallas kernels, update_trailing(): pl.pallas_call(body, out_shape=jax.ShapeDtypeStruct(share.shape, jnp.floa...  1.91 us
    ppermute x1, waiting for transfers between devices, gather_line(): both = lax.ppermute(far, 'col', [(b ^ 1, b) for b in range(count)])  1.71 us
    pallas_call x1, Pallas kernels, load_share(): pl.pallas_call(load_kernel, out_shape=jax.ShapeDtypeStruct((rows, LANES),...  1.6 us
    ppermute x1, starting transfers between devices, gather_line(): far = lax.ppermute(factor, 'col', [(b ^ 2, b) for b in range(count)])  1.5 us
    pallas_call x1, Pallas kernels, make_factor(): pl.pallas_call(factor_kernel, out_shape=jax.ShapeDtypeStruct((half, tile_...  1.44 us
  transfers between devices with their start and end apart: 11, of which 4 were waited for; matrix products, arithmetic and copies ran while one was open for 0% of the time, Pallas kernels for 7%

profile of v10, /device:TPU:0, one launch (start us, length us, event | category | flops | bytes accessed | tf_op | source)
XLA Modules:
  0.0 21.5 jit_solution(4535681442232880906)
XLA Ops:
  0.0 1.4 %factor.1.after_ref.refs_0_ = bf16[2,64,256]{2,1,0:T(8,128)(2,1)S(1)} custom-call(f32[4,1,64,256]{3,2,1,0:T(8,128)} %panel_ref.1, f32[256,256]{1,0:T(8,128)} %inverse_ref.1), custom_call_target="tpu_custom_call" | custom-call | tf_op jit(solution)/shard_map/factor/pallas_call | solution.py:41
  1.4 3.9 %collective-permute-start.3 = (bf16[2,64,256]{2,1,0:T(8,128)(2,1)S(1)}, bf16[2,64,256]{2,1,0:T(8,128)(2,1)S(1)}, u32[]{:S(2)}, u32[]{:S(2)}) collective-permute-start(bf16[2,64,256]{2,1,0:T(8,128)(2,1)S(1)} %factor.1.after_ref.refs_0_), channel_id=1, source_target_pairs={{0,24},{2,8},{4,16},{6,0},{8,26},{10,18},{12,2},{14,10},{16,20},{1... | collective-permute-start | bytes 196616 | tf_op jit(solution)/shard_map/ppermute | solution.py:187
  5.4 1.6 %load_share.1.refs_12_ = f32[4096,128]{1,0:T(8,128)S(1)} custom-call(bf16[2,64,256]{2,1,0:T(8,128)(2,1)S(1)} %factor.1.after_ref.refs_0_, f32[8192,128]{1,0:T(8,128)} %bitcast.2), custom_call_target="tpu_custom_call" | custom-call | bytes 4194304 | tf_op jit(solution)/shard_map/load_share/pallas_call | solution.py:102
  7.0 1.5 %collective-permute-start.1 = (bf16[2,64,256]{2,1,0:T(8,128)(2,1)S(1)}, bf16[2,64,256]{2,1,0:T(8,128)(2,1)S(1)}, u32[]{:S(2)}, u32[]{:S(2)}) collective-permute-start(bf16[2,64,256]{2,1,0:T(8,128)(2,1)S(1)} %factor.1.after_ref.refs_0_), channel_id=1, source_target_pairs={{4,0},{6,2},{0,4},{2,6},{5,1},{7,3},{1,5},{3,7},{12,8},{14,10},{8,... | collective-permute-start | bytes 196616 | tf_op jit(solution)/shard_map/ppermute | solution.py:86
  8.5 0.3 %collective-permute-start = (bf16[2,64,256]{2,1,0:T(8,128)(2,1)S(1)}, bf16[2,64,256]{2,1,0:T(8,128)(2,1)S(1)}, u32[]{:S(2)}, u32[]{:S(2)}) collective-permute-start(bf16[2,64,256]{2,1,0:T(8,128)(2,1)S(1)} %factor.1.after_ref.refs_0_), channel_id=1, source_target_pairs={{2,0},{0,2},{6,4},{4,6},{3,1},{1,3},{7,5},{5,7},{10,8},{8,10},{14,... | collective-permute-start | bytes 196616 | tf_op jit(solution)/shard_map/ppermute | solution.py:87
  8.8 0.1 collective-permute-done.3.refs_4_
  8.9 2.8 %collective-permute-start.6 = (bf16[2,64,256]{2,1,0:T(8,128)(2,1)S(1)}, bf16[2,64,256]{2,1,0:T(8,128)(2,1)S(1)}, u32[]{:S(2)}, u32[]{:S(2)}) collective-permute-start(bf16[2,64,256]{2,1,0:T(8,128)(2,1)S(1)} %collective-permute-done.3.refs_4_), channel_id=1, source_target_pairs={{24,0},{25,1},{16,8},{17,9},{8,16},{9,17},{0,24},{1,25},{26,2},{27... | collective-permute-start | bytes 196616 | tf_op jit(solution)/shard_map/ppermute | solution.py:200
  11.7 1.9 %collective-permute-start.5 = (bf16[2,64,256]{2,1,0:T(8,128)(2,1)S(1)}, bf16[2,64,256]{2,1,0:T(8,128)(2,1)S(1)}, u32[]{:S(2)}, u32[]{:S(2)}) collective-permute-start(bf16[2,64,256]{2,1,0:T(8,128)(2,1)S(1)} %collective-permute-done.3.refs_4_), channel_id=1, source_target_pairs={{8,0},{17,1},{0,8},{25,9},{24,16},{1,17},{16,24},{9,25},{10,2},{19... | collective-permute-start | bytes 196616 | tf_op jit(solution)/shard_map/ppermute | solution.py:200
  13.6 1.5 %collective-permute-start.4 = (bf16[2,64,256]{2,1,0:T(8,128)(2,1)S(1)}, bf16[2,64,256]{2,1,0:T(8,128)(2,1)S(1)}, u32[]{:S(2)}, u32[]{:S(2)}) collective-permute-start(bf16[2,64,256]{2,1,0:T(8,128)(2,1)S(1)} %collective-permute-done.3.refs_4_), channel_id=1, source_target_pairs={{16,0},{9,1},{24,8},{1,9},{0,16},{25,17},{8,24},{17,25},{18,2},{11... | collective-permute-start | bytes 196616 | tf_op jit(solution)/shard_map/ppermute | solution.py:200
  15.1 0.0 collective-permute-done.1.refs_2_
  15.1 0.0 collective-permute-start.7
  15.1 0.0 collective-permute-done.refs_1_
  15.1 0.1 collective-permute-start.2
  15.2 0.0 collective-permute-done.6.refs_7_
  15.2 0.5 %collective-permute-start.10 = (bf16[2,64,256]{2,1,0:T(8,128)(2,1)S(1)}, bf16[2,64,256]{2,1,0:T(8,128)(2,1)S(1)}, u32[]{:S(2)}, u32[]{:S(2)}) collective-permute-start(bf16[2,64,256]{2,1,0:T(8,128)(2,1)S(1)} %collective-permute-done.6.refs_7_), channel_id=1, source_target_pairs={{1,0},{0,1},{3,2},{2,3},{5,4},{4,5},{7,6},{6,7},{9,8},{8,9},{11,10... | collective-permute-start | bytes 196616 | tf_op jit(solution)/shard_map/ppermute | solution.py:204
  15.7 0.9 %collective-permute-done.5.refs_6_ = bf16[2,64,256]{2,1,0:T(8,128)(2,1)S(1)} collective-permute-done((bf16[2,64,256]{2,1,0:T(8,128)(2,1)S(1)}, bf16[2,64,256]{2,1,0:T(8,128)(2,1)S(1)}, u32[]{:S(2)}, u32[]{:S(2)}) %collective-permute-start.5) | collective-permute-done | bytes 65568 | tf_op jit(solution)/shard_map/ppermute | solution.py:200
  16.5 0.0 collective-permute-start.9
  16.6 1.3 %collective-permute-done.4.refs_5_ = bf16[2,64,256]{2,1,0:T(8,128)(2,1)S(1)} collective-permute-done((bf16[2,64,256]{2,1,0:T(8,128)(2,1)S(1)}, bf16[2,64,256]{2,1,0:T(8,128)(2,1)S(1)}, u32[]{:S(2)}, u32[]{:S(2)}) %collective-permute-start.4) | collective-permute-done | bytes 65568 | tf_op jit(solution)/shard_map/ppermute | solution.py:200
  17.9 0.0 collective-permute-start.8
  17.9 0.0 collective-permute-done.7.refs_8_
  17.9 1.7 %collective-permute-done.2.refs_3_ = bf16[2,64,256]{2,1,0:T(8,128)(2,1)S(1)} collective-permute-done((bf16[2,64,256]{2,1,0:T(8,128)(2,1)S(1)}, bf16[2,64,256]{2,1,0:T(8,128)(2,1)S(1)}, u32[]{:S(2)}, u32[]{:S(2)}) %collective-permute-start.2) | collective-permute-done | bytes 65568 | tf_op jit(solution)/shard_map/ppermute | solution.py:88
  19.6 0.0 collective-permute-done.10.refs_11_
  19.6 0.0 collective-permute-done.9.refs_10_
  19.6 0.0 collective-permute-done.8.refs_9_
  19.6 1.9 %update.1 = f32[4096,128]{1,0:T(8,128)} custom-call(bf16[2,64,256]{2,1,0:T(8,128)(2,1)S(1)} %factor.1.after_ref.refs_0_, bf16[2,64,256]{2,1,0:T(8,128)(2,1)S(1)} %collective-permute-done.refs_1_, bf16[2,64,256]{2,1,0:T(8,128)(2,1)S(1)} %collective-permute-done.1.refs_2_, bf16[2,64,256]{2,1,0:T(8,128)(2,1)S(1)} %collective-permute-done.2.refs_3_, ...), custom_call_target="tpu_custom_call" | custom-call | tf_op jit(solution)/shard_map/update/pallas_call | solution.py:163
Async XLA Ops:
  1.4 7.4 %collective-permute-start.3 = (bf16[2,64,256]{2,1,0:T(8,128)(2,1)S(1)}, bf16[2,64,256]{2,1,0:T(8,128)(2,1)S(1)}, u32[]{:S(2)}, u32[]{:S(2)}) collective-permute-start(bf16[2,64,256]{2,1,0:T(8,128)(2,1)S(1)} %factor.1.after_ref.refs_0_), channel_id=1, source_target_pairs={{0,24},{2,8},{4,16},{6,0},{8,26},{10,18},{12,2},{14,10},{16,20},{1... | collective-permute-start | bytes 196616 | tf_op jit(solution)/shard_map/ppermute | solution.py:187
  7.0 8.1 %collective-permute-start.1 = (bf16[2,64,256]{2,1,0:T(8,128)(2,1)S(1)}, bf16[2,64,256]{2,1,0:T(8,128)(2,1)S(1)}, u32[]{:S(2)}, u32[]{:S(2)}) collective-permute-start(bf16[2,64,256]{2,1,0:T(8,128)(2,1)S(1)} %factor.1.after_ref.refs_0_), channel_id=1, source_target_pairs={{4,0},{6,2},{0,4},{2,6},{5,1},{7,3},{1,5},{3,7},{12,8},{14,10},{8,... | collective-permute-start | bytes 196616 | tf_op jit(solution)/shard_map/ppermute | solution.py:86
  8.5 6.6 %collective-permute-start = (bf16[2,64,256]{2,1,0:T(8,128)(2,1)S(1)}, bf16[2,64,256]{2,1,0:T(8,128)(2,1)S(1)}, u32[]{:S(2)}, u32[]{:S(2)}) collective-permute-start(bf16[2,64,256]{2,1,0:T(8,128)(2,1)S(1)} %factor.1.after_ref.refs_0_), channel_id=1, source_target_pairs={{2,0},{0,2},{6,4},{4,6},{3,1},{1,3},{7,5},{5,7},{10,8},{8,10},{14,... | collective-permute-start | bytes 196616 | tf_op jit(solution)/shard_map/ppermute | solution.py:87
  8.9 6.3 %collective-permute-start.6 = (bf16[2,64,256]{2,1,0:T(8,128)(2,1)S(1)}, bf16[2,64,256]{2,1,0:T(8,128)(2,1)S(1)}, u32[]{:S(2)}, u32[]{:S(2)}) collective-permute-start(bf16[2,64,256]{2,1,0:T(8,128)(2,1)S(1)} %collective-permute-done.3.refs_4_), channel_id=1, source_target_pairs={{24,0},{25,1},{16,8},{17,9},{8,16},{9,17},{0,24},{1,25},{26,2},{27... | collective-permute-start | bytes 196616 | tf_op jit(solution)/shard_map/ppermute | solution.py:200
  11.7 4.8 %collective-permute-start.5 = (bf16[2,64,256]{2,1,0:T(8,128)(2,1)S(1)}, bf16[2,64,256]{2,1,0:T(8,128)(2,1)S(1)}, u32[]{:S(2)}, u32[]{:S(2)}) collective-permute-start(bf16[2,64,256]{2,1,0:T(8,128)(2,1)S(1)} %collective-permute-done.3.refs_4_), channel_id=1, source_target_pairs={{8,0},{17,1},{0,8},{25,9},{24,16},{1,17},{16,24},{9,25},{10,2},{19... | collective-permute-start | bytes 196616 | tf_op jit(solution)/shard_map/ppermute | solution.py:200
  13.6 4.3 %collective-permute-start.4 = (bf16[2,64,256]{2,1,0:T(8,128)(2,1)S(1)}, bf16[2,64,256]{2,1,0:T(8,128)(2,1)S(1)}, u32[]{:S(2)}, u32[]{:S(2)}) collective-permute-start(bf16[2,64,256]{2,1,0:T(8,128)(2,1)S(1)} %collective-permute-done.3.refs_4_), channel_id=1, source_target_pairs={{16,0},{9,1},{24,8},{1,9},{0,16},{25,17},{8,24},{17,25},{18,2},{11... | collective-permute-start | bytes 196616 | tf_op jit(solution)/shard_map/ppermute | solution.py:200
  15.1 2.8 %collective-permute-start.7 = (bf16[2,64,256]{2,1,0:T(8,128)(2,1)S(1)}, bf16[2,64,256]{2,1,0:T(8,128)(2,1)S(1)}, u32[]{:S(2)}, u32[]{:S(2)}) collective-permute-start(bf16[2,64,256]{2,1,0:T(8,128)(2,1)S(1)} %collective-permute-done.3.refs_4_), channel_id=1, source_target_pairs={{1,0},{0,1},{3,2},{2,3},{5,4},{4,5},{7,6},{6,7},{9,8},{8,9},{11,10... | collective-permute-start | bytes 196616 | tf_op jit(solution)/shard_map/ppermute | solution.py:204
  15.1 4.5 %collective-permute-start.2 = (bf16[2,64,256]{2,1,0:T(8,128)(2,1)S(1)}, bf16[2,64,256]{2,1,0:T(8,128)(2,1)S(1)}, u32[]{:S(2)}, u32[]{:S(2)}) collective-permute-start(bf16[2,64,256]{2,1,0:T(8,128)(2,1)S(1)} %collective-permute-done.1.refs_2_), channel_id=1, source_target_pairs={{2,0},{0,2},{6,4},{4,6},{3,1},{1,3},{7,5},{5,7},{10,8},{8,10},{14,... | collective-permute-start | bytes 196616 | tf_op jit(solution)/shard_map/ppermute | solution.py:88
  15.2 4.4 %collective-permute-start.10 = (bf16[2,64,256]{2,1,0:T(8,128)(2,1)S(1)}, bf16[2,64,256]{2,1,0:T(8,128)(2,1)S(1)}, u32[]{:S(2)}, u32[]{:S(2)}) collective-permute-start(bf16[2,64,256]{2,1,0:T(8,128)(2,1)S(1)} %collective-permute-done.6.refs_7_), channel_id=1, source_target_pairs={{1,0},{0,1},{3,2},{2,3},{5,4},{4,5},{7,6},{6,7},{9,8},{8,9},{11,10... | collective-permute-start | bytes 196616 | tf_op jit(solution)/shard_map/ppermute | solution.py:204
  16.5 3.0 %collective-permute-start.9 = (bf16[2,64,256]{2,1,0:T(8,128)(2,1)S(1)}, bf16[2,64,256]{2,1,0:T(8,128)(2,1)S(1)}, u32[]{:S(2)}, u32[]{:S(2)}) collective-permute-start(bf16[2,64,256]{2,1,0:T(8,128)(2,1)S(1)} %collective-permute-done.5.refs_6_), channel_id=1, source_target_pairs={{1,0},{0,1},{3,2},{2,3},{5,4},{4,5},{7,6},{6,7},{9,8},{8,9},{11,10... | collective-permute-start | bytes 196616 | tf_op jit(solution)/shard_map/ppermute | solution.py:204
  17.9 1.7 %collective-permute-start.8 = (bf16[2,64,256]{2,1,0:T(8,128)(2,1)S(1)}, bf16[2,64,256]{2,1,0:T(8,128)(2,1)S(1)}, u32[]{:S(2)}, u32[]{:S(2)}) collective-permute-start(bf16[2,64,256]{2,1,0:T(8,128)(2,1)S(1)} %collective-permute-done.4.refs_5_), channel_id=1, source_target_pairs={{1,0},{0,1},{3,2},{2,3},{5,4},{4,5},{7,6},{6,7},{9,8},{8,9},{11,10... | collective-permute-start | bytes 196616 | tf_op jit(solution)/shard_map/ppermute | solution.py:204

commit v11 on v9

--- a/solution.py
+++ b/solution.py
@@ -59,7 +59,7 @@
 
 def plane_slots(count):
     if count == 4:
-        return ((3, 1, 2, 0), (3, 2, 0, 1), (2, 3, 1, 0), (3, 1, 2, 0))
+        return ((3, 0, 1, 2), (3, 2, 1, 0), (0, 2, 1, 3), (3, 1, 2, 0))
     return tuple(tuple(count - 1 - b for b in range(count)) for _ in range(count))
 
 
@@ -110,8 +110,8 @@
 
 
 def update_kernel(pieces, layers, half, tile, tile_rows, col_tiles, *refs):
-    row_refs = refs[:pieces]
-    col_refs = refs[pieces : pieces * (1 + layers)]
+    col_refs = refs[: pieces * layers]
+    row_refs = refs[pieces * layers : pieces * (1 + layers)]
     share_ref, out_ref, row_buf, col_buf, out_buf, out_sems = refs[pieces * (1 + layers) :]
     r, c, layer = (lax.axis_index(axis) for axis in AXES)
     slots = plane_slots(pieces)
@@ -167,7 +167,7 @@
         ],
         compiler_params=pltpu.CompilerParams(vmem_limit_bytes=VMEM_BYTES),
         name="update",
-    )(*row_pieces, *col_pieces, share)
+    )(*col_pieces, *row_pieces, share)
     return result.reshape(half, 1, tile, col_tiles, 1, tile)
 
 
@@ -187,10 +187,11 @@
     plane = [moved]
     for step in plane_steps(count)[1:]:
         plane.append(lax.ppermute(moved, "row", [(partner(a, step, count), a) for a in range(count)]))
+    first, plane[-1] = lax.optimization_barrier((moved, plane[-1]))
     others = []
     for shift in range(1, layers):
         pairs = [((l + shift) % layers, l) for l in range(layers)]
-        others += [lax.ppermute(piece, "layer", pairs) for piece in plane]
+        others += [lax.ppermute(piece, "layer", pairs) for piece in [first] + plane[1:]]
     return update_trailing(line, plane + others, share, half, layers, tile, col_tiles)
 
 

time: 21.6 us -> 21.5 us (level)
  waiting for transfers between devices: 4.02 us -> 1.74 us
  starting transfers between devices: 12.5 us -> 14.5 us
    ppermute x3, starting transfers between devices: 6.17 us -> 4.01 us  [per_device(): lax.ppermute(moved, 'row', [(partner(a, step, count), a) for a in range(c...]
    ppermute x1, starting transfers between devices: 0.31 us -> 2.3 us  [gather_line(): near = lax.ppermute(factor, 'col', [(b ^ 1, b) for b in range(count)])]
    ppermute x1, starting transfers between devices: 0.07 us -> 2.02 us  [gather_line(): both = lax.ppermute(far, 'col', [(b ^ 1, b) for b in range(count)])]
    ppermute x3, waiting for transfers between devices: 2.21 us -> 0.72 us  [per_device(): lax.ppermute(moved, 'row', [(partner(a, step, count), a) for a in range(c...]
    ppermute x1, waiting for transfers between devices: 1.71 us -> 0.76 us  [gather_line(): both = lax.ppermute(far, 'col', [(b ^ 1, b) for b in range(count)])]
    ppermute x4, starting transfers between devices: 0.5 us -> 0.75 us  [per_device(): lax.ppermute(piece, 'layer', pairs)]
    ppermute x4, waiting for transfers between devices: 0.01 us -> 0.25 us  [per_device(): lax.ppermute(piece, 'layer', pairs)]
  transfers between devices with their start and end apart: 11 -> 11, of which waited for: 4 -> 4; matrix products, arithmetic and copies ran while one was open for 0% -> 0% of each run, Pallas kernels for 7% -> 8%
where the time goes in v11:
time: 21.5 us; the launch traced here: 21.2 us
  starting transfers between devices  14.5 us (67%)
  Pallas kernels  4.9 us (23%)
  waiting for transfers between devices  1.74 us (8%)
    ppermute x3, starting transfers between devices, per_device(): lax.ppermute(moved, 'row', [(partner(a, step, count), a) for a in range(c...  4.01 us
    ppermute x1, starting transfers between devices, per_device(): lax.ppermute(factor, ('row', 'col'), [(a * count + b, slots[a][b] * count...  3.94 us
    ppermute x1, starting transfers between devices, gather_line(): near = lax.ppermute(factor, 'col', [(b ^ 1, b) for b in range(count)])  2.3 us
    ppermute x1, starting transfers between devices, gather_line(): both = lax.ppermute(far, 'col', [(b ^ 1, b) for b in range(count)])  2.02 us
    pallas_call x1, Pallas kernels, update_trailing(): pl.pallas_call(body, out_shape=jax.ShapeDtypeStruct(share.shape, jnp.floa...  1.87 us
    pallas_call x1, Pallas kernels, load_share(): pl.pallas_call(load_kernel, out_shape=jax.ShapeDtypeStruct((rows, LANES),...  1.6 us
    ppermute x1, starting transfers between devices, gather_line(): far = lax.ppermute(factor, 'col', [(b ^ 2, b) for b in range(count)])  1.47 us
    pallas_call x1, Pallas kernels, make_factor(): pl.pallas_call(factor_kernel, out_shape=jax.ShapeDtypeStruct((half, tile_...  1.44 us
  transfers between devices with their start and end apart: 11, of which 4 were waited for; matrix products, arithmetic and copies ran while one was open for 0% of the time, Pallas kernels for 8%

profile of v11, /device:TPU:0, one launch (start us, length us, event | category | flops | bytes accessed | tf_op | source)
XLA Modules:
  0.0 21.2 jit_solution(10264306487433268477)
XLA Ops:
  0.0 1.4 %factor.1.after_ref.refs_8_ = bf16[2,64,256]{2,1,0:T(8,128)(2,1)S(1)} custom-call(f32[4,1,64,256]{3,2,1,0:T(8,128)} %panel_ref.1, f32[256,256]{1,0:T(8,128)} %inverse_ref.1), custom_call_target="tpu_custom_call" | custom-call | tf_op jit(solution)/shard_map/factor/pallas_call | solution.py:41
  1.4 3.9 %collective-permute-start = (bf16[2,64,256]{2,1,0:T(8,128)(2,1)S(1)}, bf16[2,64,256]{2,1,0:T(8,128)(2,1)S(1)}, u32[]{:S(2)}, u32[]{:S(2)}) collective-permute-start(bf16[2,64,256]{2,1,0:T(8,128)(2,1)S(1)} %factor.1.after_ref.refs_8_), channel_id=1, source_target_pairs={{0,24},{2,0},{4,8},{6,16},{8,26},{10,18},{12,10},{14,2},{16,4},{18... | collective-permute-start | bytes 196616 | tf_op jit(solution)/shard_map/ppermute | solution.py:181
  5.4 1.6 %load_share.1.refs_12_ = f32[4096,128]{1,0:T(8,128)S(1)} custom-call(bf16[2,64,256]{2,1,0:T(8,128)(2,1)S(1)} %factor.1.after_ref.refs_8_, f32[8192,128]{1,0:T(8,128)} %bitcast.2), custom_call_target="tpu_custom_call" | custom-call | bytes 4194304 | tf_op jit(solution)/shard_map/load_share/pallas_call | solution.py:100
  7.0 1.5 %collective-permute-start.9 = (bf16[2,64,256]{2,1,0:T(8,128)(2,1)S(1)}, bf16[2,64,256]{2,1,0:T(8,128)(2,1)S(1)}, u32[]{:S(2)}, u32[]{:S(2)}) collective-permute-start(bf16[2,64,256]{2,1,0:T(8,128)(2,1)S(1)} %factor.1.after_ref.refs_8_), channel_id=1, source_target_pairs={{4,0},{6,2},{0,4},{2,6},{5,1},{7,3},{1,5},{3,7},{12,8},{14,10},{8,... | collective-permute-start | bytes 196616 | tf_op jit(solution)/shard_map/ppermute | solution.py:84
  8.5 0.0 collective-permute-done.refs_0_
  8.5 2.7 %collective-permute-start.3 = (bf16[2,64,256]{2,1,0:T(8,128)(2,1)S(1)}, bf16[2,64,256]{2,1,0:T(8,128)(2,1)S(1)}, u32[]{:S(2)}, u32[]{:S(2)}) collective-permute-start(bf16[2,64,256]{2,1,0:T(8,128)(2,1)S(1)} %collective-permute-done.refs_0_), channel_id=1, source_target_pairs={{24,0},{16,8},{8,16},{0,24},{25,1},{17,9},{9,17},{1,25},{26,2},{18... | collective-permute-start | bytes 196616 | tf_op jit(solution)/shard_map/ppermute | solution.py:189
  11.2 2.3 %collective-permute-start.8 = (bf16[2,64,256]{2,1,0:T(8,128)(2,1)S(1)}, bf16[2,64,256]{2,1,0:T(8,128)(2,1)S(1)}, u32[]{:S(2)}, u32[]{:S(2)}) collective-permute-start(bf16[2,64,256]{2,1,0:T(8,128)(2,1)S(1)} %factor.1.after_ref.refs_8_), channel_id=1, source_target_pairs={{2,0},{0,2},{6,4},{4,6},{3,1},{1,3},{7,5},{5,7},{10,8},{8,10},{14,... | collective-permute-start | bytes 196616 | tf_op jit(solution)/shard_map/ppermute | solution.py:85
  13.5 0.3 %collective-permute-start.2 = (bf16[2,64,256]{2,1,0:T(8,128)(2,1)S(1)}, bf16[2,64,256]{2,1,0:T(8,128)(2,1)S(1)}, u32[]{:S(2)}, u32[]{:S(2)}) collective-permute-start(bf16[2,64,256]{2,1,0:T(8,128)(2,1)S(1)} %collective-permute-done.refs_0_), channel_id=1, source_target_pairs={{8,0},{0,8},{24,16},{16,24},{9,1},{1,9},{25,17},{17,25},{10,2},{2,... | collective-permute-start | bytes 196616 | tf_op jit(solution)/shard_map/ppermute | solution.py:189
  13.8 1.0 %collective-permute-start.1 = (bf16[2,64,256]{2,1,0:T(8,128)(2,1)S(1)}, bf16[2,64,256]{2,1,0:T(8,128)(2,1)S(1)}, u32[]{:S(2)}, u32[]{:S(2)}) collective-permute-start(bf16[2,64,256]{2,1,0:T(8,128)(2,1)S(1)} %collective-permute-done.refs_0_), channel_id=1, source_target_pairs={{16,0},{24,8},{0,16},{8,24},{17,1},{25,9},{1,17},{9,25},{18,2},{26... | collective-permute-start | bytes 196616 | tf_op jit(solution)/shard_map/ppermute | solution.py:189
  14.8 0.0 collective-permute-done.9.refs_10_
  14.8 2.0 %collective-permute-start.10 = (bf16[2,64,256]{2,1,0:T(8,128)(2,1)S(1)}, bf16[2,64,256]{2,1,0:T(8,128)(2,1)S(1)}, u32[]{:S(2)}, u32[]{:S(2)}) collective-permute-start(bf16[2,64,256]{2,1,0:T(8,128)(2,1)S(1)} %collective-permute-done.9.refs_10_), channel_id=1, source_target_pairs={{2,0},{0,2},{6,4},{4,6},{3,1},{1,3},{7,5},{5,7},{10,8},{8,10},{14,... | collective-permute-start | bytes 196616 | tf_op jit(solution)/shard_map/ppermute | solution.py:86
  16.8 0.0 collective-permute-done.3.refs_3_
  16.8 0.0 collective-permute-start.4
  16.8 0.0 collective-permute-done.8.refs_9_
  16.8 0.5 %collective-permute-start.7 = (bf16[2,64,256]{2,1,0:T(8,128)(2,1)S(1)}, bf16[2,64,256]{2,1,0:T(8,128)(2,1)S(1)}, u32[]{:S(2)}, u32[]{:S(2)}) collective-permute-start(bf16[2,64,256]{2,1,0:T(8,128)(2,1)S(1)} %collective-permute-done.3.refs_3_), channel_id=1, source_target_pairs={{1,0},{0,1},{3,2},{2,3},{5,4},{4,5},{7,6},{6,7},{9,8},{8,9},{11,10... | collective-permute-start | bytes 196616 | tf_op jit(solution)/shard_map/ppermute | solution.py:194
  17.3 0.4 %collective-permute-done.2.refs_2_ = bf16[2,64,256]{2,1,0:T(8,128)(2,1)S(1)} collective-permute-done((bf16[2,64,256]{2,1,0:T(8,128)(2,1)S(1)}, bf16[2,64,256]{2,1,0:T(8,128)(2,1)S(1)}, u32[]{:S(2)}, u32[]{:S(2)}) %collective-permute-start.2) | collective-permute-done | bytes 65568 | tf_op jit(solution)/shard_map/ppermute | solution.py:189
  17.8 0.0 collective-permute-start.6
  17.8 0.3 %collective-permute-done.1.refs_1_ = bf16[2,64,256]{2,1,0:T(8,128)(2,1)S(1)} collective-permute-done((bf16[2,64,256]{2,1,0:T(8,128)(2,1)S(1)}, bf16[2,64,256]{2,1,0:T(8,128)(2,1)S(1)}, u32[]{:S(2)}, u32[]{:S(2)}) %collective-permute-start.1) | collective-permute-done | bytes 65568 | tf_op jit(solution)/shard_map/ppermute | solution.py:189
  18.0 0.2 %collective-permute-start.5 = (bf16[2,64,256]{2,1,0:T(8,128)(2,1)S(1)}, bf16[2,64,256]{2,1,0:T(8,128)(2,1)S(1)}, u32[]{:S(2)}, u32[]{:S(2)}) collective-permute-start(bf16[2,64,256]{2,1,0:T(8,128)(2,1)S(1)} %collective-permute-done.1.refs_1_), channel_id=1, source_target_pairs={{1,0},{0,1},{3,2},{2,3},{5,4},{4,5},{7,6},{6,7},{9,8},{8,9},{11,10... | collective-permute-start | bytes 196616 | tf_op jit(solution)/shard_map/ppermute | solution.py:194
  18.3 0.8 %collective-permute-done.10.refs_11_ = bf16[2,64,256]{2,1,0:T(8,128)(2,1)S(1)} collective-permute-done((bf16[2,64,256]{2,1,0:T(8,128)(2,1)S(1)}, bf16[2,64,256]{2,1,0:T(8,128)(2,1)S(1)}, u32[]{:S(2)}, u32[]{:S(2)}) %collective-permute-start.10) | collective-permute-done | bytes 65568 | tf_op jit(solution)/shard_map/ppermute | solution.py:86
  19.1 0.0 collective-permute-done.4.refs_4_
  19.1 0.0 collective-permute-done.7.refs_7_
  19.1 0.0 collective-permute-done.6.refs_6_
  19.1 0.2 %collective-permute-done.5.refs_5_ = bf16[2,64,256]{2,1,0:T(8,128)(2,1)S(1)} collective-permute-done((bf16[2,64,256]{2,1,0:T(8,128)(2,1)S(1)}, bf16[2,64,256]{2,1,0:T(8,128)(2,1)S(1)}, u32[]{:S(2)}, u32[]{:S(2)}) %collective-permute-start.5) | collective-permute-done | bytes 65568 | tf_op jit(solution)/shard_map/ppermute | solution.py:194
  19.3 1.9 %update.1 = f32[4096,128]{1,0:T(8,128)} custom-call(bf16[2,64,256]{2,1,0:T(8,128)(2,1)S(1)} %collective-permute-done.refs_0_, bf16[2,64,256]{2,1,0:T(8,128)(2,1)S(1)} %collective-permute-done.1.refs_1_, bf16[2,64,256]{2,1,0:T(8,128)(2,1)S(1)} %collective-permute-done.2.refs_2_, bf16[2,64,256]{2,1,0:T(8,128)(2,1)S(1)} %collective-permute-done.3.refs_3_, ...), custom_call_target="tpu_custom_call" | custom-call | tf_op jit(solution)/shard_map/update/pallas_call | solution.py:157
Async XLA Ops:
  1.4 7.0 %collective-permute-start = (bf16[2,64,256]{2,1,0:T(8,128)(2,1)S(1)}, bf16[2,64,256]{2,1,0:T(8,128)(2,1)S(1)}, u32[]{:S(2)}, u32[]{:S(2)}) collective-permute-start(bf16[2,64,256]{2,1,0:T(8,128)(2,1)S(1)} %factor.1.after_ref.refs_8_), channel_id=1, source_target_pairs={{0,24},{2,0},{4,8},{6,16},{8,26},{10,18},{12,10},{14,2},{16,4},{18... | collective-permute-start | bytes 196616 | tf_op jit(solution)/shard_map/ppermute | solution.py:181
  7.0 7.8 %collective-permute-start.9 = (bf16[2,64,256]{2,1,0:T(8,128)(2,1)S(1)}, bf16[2,64,256]{2,1,0:T(8,128)(2,1)S(1)}, u32[]{:S(2)}, u32[]{:S(2)}) collective-permute-start(bf16[2,64,256]{2,1,0:T(8,128)(2,1)S(1)} %factor.1.after_ref.refs_8_), channel_id=1, source_target_pairs={{4,0},{6,2},{0,4},{2,6},{5,1},{7,3},{1,5},{3,7},{12,8},{14,10},{8,... | collective-permute-start | bytes 196616 | tf_op jit(solution)/shard_map/ppermute | solution.py:84
  8.5 8.3 %collective-permute-start.3 = (bf16[2,64,256]{2,1,0:T(8,128)(2,1)S(1)}, bf16[2,64,256]{2,1,0:T(8,128)(2,1)S(1)}, u32[]{:S(2)}, u32[]{:S(2)}) collective-permute-start(bf16[2,64,256]{2,1,0:T(8,128)(2,1)S(1)} %collective-permute-done.refs_0_), channel_id=1, source_target_pairs={{24,0},{16,8},{8,16},{0,24},{25,1},{17,9},{9,17},{1,25},{26,2},{18... | collective-permute-start | bytes 196616 | tf_op jit(solution)/shard_map/ppermute | solution.py:189
  11.2 5.6 %collective-permute-start.8 = (bf16[2,64,256]{2,1,0:T(8,128)(2,1)S(1)}, bf16[2,64,256]{2,1,0:T(8,128)(2,1)S(1)}, u32[]{:S(2)}, u32[]{:S(2)}) collective-permute-start(bf16[2,64,256]{2,1,0:T(8,128)(2,1)S(1)} %factor.1.after_ref.refs_8_), channel_id=1, source_target_pairs={{2,0},{0,2},{6,4},{4,6},{3,1},{1,3},{7,5},{5,7},{10,8},{8,10},{14,... | collective-permute-start | bytes 196616 | tf_op jit(solution)/shard_map/ppermute | solution.py:85
  13.5 4.3 %collective-permute-start.2 = (bf16[2,64,256]{2,1,0:T(8,128)(2,1)S(1)}, bf16[2,64,256]{2,1,0:T(8,128)(2,1)S(1)}, u32[]{:S(2)}, u32[]{:S(2)}) collective-permute-start(bf16[2,64,256]{2,1,0:T(8,128)(2,1)S(1)} %collective-permute-done.refs_0_), channel_id=1, source_target_pairs={{8,0},{0,8},{24,16},{16,24},{9,1},{1,9},{25,17},{17,25},{10,2},{2,... | collective-permute-start | bytes 196616 | tf_op jit(solution)/shard_map/ppermute | solution.py:189
  13.8 4.3 %collective-permute-start.1 = (bf16[2,64,256]{2,1,0:T(8,128)(2,1)S(1)}, bf16[2,64,256]{2,1,0:T(8,128)(2,1)S(1)}, u32[]{:S(2)}, u32[]{:S(2)}) collective-permute-start(bf16[2,64,256]{2,1,0:T(8,128)(2,1)S(1)} %collective-permute-done.refs_0_), channel_id=1, source_target_pairs={{16,0},{24,8},{0,16},{8,24},{17,1},{25,9},{1,17},{9,25},{18,2},{26... | collective-permute-start | bytes 196616 | tf_op jit(solution)/shard_map/ppermute | solution.py:189
  14.8 4.3 %collective-permute-start.10 = (bf16[2,64,256]{2,1,0:T(8,128)(2,1)S(1)}, bf16[2,64,256]{2,1,0:T(8,128)(2,1)S(1)}, u32[]{:S(2)}, u32[]{:S(2)}) collective-permute-start(bf16[2,64,256]{2,1,0:T(8,128)(2,1)S(1)} %collective-permute-done.9.refs_10_), channel_id=1, source_target_pairs={{2,0},{0,2},{6,4},{4,6},{3,1},{1,3},{7,5},{5,7},{10,8},{8,10},{14,... | collective-permute-start | bytes 196616 | tf_op jit(solution)/shard_map/ppermute | solution.py:86
  16.8 2.2 %collective-permute-start.4 = (bf16[2,64,256]{2,1,0:T(8,128)(2,1)S(1)}, bf16[2,64,256]{2,1,0:T(8,128)(2,1)S(1)}, u32[]{:S(2)}, u32[]{:S(2)}) collective-permute-start(bf16[2,64,256]{2,1,0:T(8,128)(2,1)S(1)} %collective-permute-done.refs_0_), channel_id=1, source_target_pairs={{1,0},{0,1},{3,2},{2,3},{5,4},{4,5},{7,6},{6,7},{9,8},{8,9},{11,10... | collective-permute-start | bytes 196616 | tf_op jit(solution)/shard_map/ppermute | solution.py:194
  16.8 2.2 %collective-permute-start.7 = (bf16[2,64,256]{2,1,0:T(8,128)(2,1)S(1)}, bf16[2,64,256]{2,1,0:T(8,128)(2,1)S(1)}, u32[]{:S(2)}, u32[]{:S(2)}) collective-permute-start(bf16[2,64,256]{2,1,0:T(8,128)(2,1)S(1)} %collective-permute-done.3.refs_3_), channel_id=1, source_target_pairs={{1,0},{0,1},{3,2},{2,3},{5,4},{4,5},{7,6},{6,7},{9,8},{8,9},{11,10... | collective-permute-start | bytes 196616 | tf_op jit(solution)/shard_map/ppermute | solution.py:194
  17.8 1.3 %collective-permute-start.6 = (bf16[2,64,256]{2,1,0:T(8,128)(2,1)S(1)}, bf16[2,64,256]{2,1,0:T(8,128)(2,1)S(1)}, u32[]{:S(2)}, u32[]{:S(2)}) collective-permute-start(bf16[2,64,256]{2,1,0:T(8,128)(2,1)S(1)} %collective-permute-done.2.refs_2_), channel_id=1, source_target_pairs={{1,0},{0,1},{3,2},{2,3},{5,4},{4,5},{7,6},{6,7},{9,8},{8,9},{11,10... | collective-permute-start | bytes 196616 | tf_op jit(solution)/shard_map/ppermute | solution.py:194
  18.0 1.3 %collective-permute-start.5 = (bf16[2,64,256]{2,1,0:T(8,128)(2,1)S(1)}, bf16[2,64,256]{2,1,0:T(8,128)(2,1)S(1)}, u32[]{:S(2)}, u32[]{:S(2)}) collective-permute-start(bf16[2,64,256]{2,1,0:T(8,128)(2,1)S(1)} %collective-permute-done.1.refs_1_), channel_id=1, source_target_pairs={{1,0},{0,1},{3,2},{2,3},{5,4},{4,5},{7,6},{6,7},{9,8},{8,9},{11,10... | collective-permute-start | bytes 196616 | tf_op jit(solution)/shard_map/ppermute | solution.py:194

commit v12 on v9

--- a/solution.py
+++ b/solution.py
@@ -59,7 +59,7 @@
 
 def plane_slots(count):
     if count == 4:
-        return ((3, 1, 2, 0), (3, 2, 0, 1), (2, 3, 1, 0), (3, 1, 2, 0))
+        return ((3, 0, 1, 2), (3, 2, 1, 0), (0, 2, 1, 3), (3, 1, 2, 0))
     return tuple(tuple(count - 1 - b for b in range(count)) for _ in range(count))
 
 

time: 21.6 us -> 21.1 us (0.977)
  starting transfers between devices: 12.5 us -> 11.5 us
  waiting for transfers between devices: 4.02 us -> 4.43 us
    ppermute x3, starting transfers between devices: 6.17 us -> 4.56 us  [per_device(): lax.ppermute(moved, 'row', [(partner(a, step, count), a) for a in range(c...]
    ppermute x1, starting transfers between devices: 0.31 us -> 1.49 us  [gather_line(): near = lax.ppermute(factor, 'col', [(b ^ 1, b) for b in range(count)])]
    ppermute x3, waiting for transfers between devices: 2.21 us -> 2.79 us  [per_device(): lax.ppermute(moved, 'row', [(partner(a, step, count), a) for a in range(c...]
    ppermute x4, starting transfers between devices: 0.5 us -> 0.01 us  [per_device(): others += [lax.ppermute(piece, 'layer', pairs) for piece in plane]]
  transfers between devices with their start and end apart: 11 -> 11, of which waited for: 4 -> 4; matrix products, arithmetic and copies ran while one was open for 0% -> 0% of each run, Pallas kernels for 7% -> 8%
where the time goes in v12:
time: 21.1 us; the launch traced here: 20.9 us
  starting transfers between devices  11.5 us (55%)
  Pallas kernels  4.91 us (23%)
  waiting for transfers between devices  4.43 us (21%)
    ppermute x3, starting transfers between devices, per_device(): lax.ppermute(moved, 'row', [(partner(a, step, count), a) for a in range(c...  4.56 us
    ppermute x1, starting transfers between devices, per_device(): lax.ppermute(factor, ('row', 'col'), [(a * count + b, slots[a][b] * count...  3.94 us
    ppermute x3, waiting for transfers between devices, per_device(): lax.ppermute(moved, 'row', [(partner(a, step, count), a) for a in range(c...  2.79 us
    pallas_call x1, Pallas kernels, update_trailing(): pl.pallas_call(body, out_shape=jax.ShapeDtypeStruct(share.shape, jnp.floa...  1.87 us
    ppermute x1, waiting for transfers between devices, gather_line(): both = lax.ppermute(far, 'col', [(b ^ 1, b) for b in range(count)])  1.62 us
    pallas_call x1, Pallas kernels, load_share(): pl.pallas_call(load_kernel, out_shape=jax.ShapeDtypeStruct((rows, LANES),...  1.6 us
    ppermute x1, starting transfers between devices, gather_line(): near = lax.ppermute(factor, 'col', [(b ^ 1, b) for b in range(count)])  1.49 us
    ppermute x1, starting transfers between devices, gather_line(): far = lax.ppermute(factor, 'col', [(b ^ 2, b) for b in range(count)])  1.47 us
  transfers between devices with their start and end apart: 11, of which 4 were waited for; matrix products, arithmetic and copies ran while one was open for 0% of the time, Pallas kernels for 8%

profile of v12, /device:TPU:0, one launch (start us, length us, event | category | flops | bytes accessed | tf_op | source)
XLA Modules:
  0.0 20.9 jit_solution(9483819113387073337)
XLA Ops:
  0.0 1.4 %factor.1.after_ref.refs_0_ = bf16[2,64,256]{2,1,0:T(8,128)(2,1)S(1)} custom-call(f32[4,1,64,256]{3,2,1,0:T(8,128)} %panel_ref.1, f32[256,256]{1,0:T(8,128)} %inverse_ref.1), custom_call_target="tpu_custom_call" | custom-call | tf_op jit(solution)/shard_map/factor/pallas_call | solution.py:41
  1.4 3.9 %collective-permute-start.3 = (bf16[2,64,256]{2,1,0:T(8,128)(2,1)S(1)}, bf16[2,64,256]{2,1,0:T(8,128)(2,1)S(1)}, u32[]{:S(2)}, u32[]{:S(2)}) collective-permute-start(bf16[2,64,256]{2,1,0:T(8,128)(2,1)S(1)} %factor.1.after_ref.refs_0_), channel_id=1, source_target_pairs={{0,24},{2,0},{4,8},{6,16},{8,26},{10,18},{12,10},{14,2},{16,4},{18... | collective-permute-start | bytes 196616 | tf_op jit(solution)/shard_map/ppermute | solution.py:181
  5.4 1.6 %load_share.1.refs_12_ = f32[4096,128]{1,0:T(8,128)S(1)} custom-call(bf16[2,64,256]{2,1,0:T(8,128)(2,1)S(1)} %factor.1.after_ref.refs_0_, f32[8192,128]{1,0:T(8,128)} %bitcast.2), custom_call_target="tpu_custom_call" | custom-call | bytes 4194304 | tf_op jit(solution)/shard_map/load_share/pallas_call | solution.py:100
  7.0 1.5 %collective-permute-start.1 = (bf16[2,64,256]{2,1,0:T(8,128)(2,1)S(1)}, bf16[2,64,256]{2,1,0:T(8,128)(2,1)S(1)}, u32[]{:S(2)}, u32[]{:S(2)}) collective-permute-start(bf16[2,64,256]{2,1,0:T(8,128)(2,1)S(1)} %factor.1.after_ref.refs_0_), channel_id=1, source_target_pairs={{4,0},{6,2},{0,4},{2,6},{5,1},{7,3},{1,5},{3,7},{12,8},{14,10},{8,... | collective-permute-start | bytes 196616 | tf_op jit(solution)/shard_map/ppermute | solution.py:84
  8.5 1.5 %collective-permute-start = (bf16[2,64,256]{2,1,0:T(8,128)(2,1)S(1)}, bf16[2,64,256]{2,1,0:T(8,128)(2,1)S(1)}, u32[]{:S(2)}, u32[]{:S(2)}) collective-permute-start(bf16[2,64,256]{2,1,0:T(8,128)(2,1)S(1)} %factor.1.after_ref.refs_0_), channel_id=1, source_target_pairs={{2,0},{0,2},{6,4},{4,6},{3,1},{1,3},{7,5},{5,7},{10,8},{8,10},{14,... | collective-permute-start | bytes 196616 | tf_op jit(solution)/shard_map/ppermute | solution.py:85
  10.0 0.0 collective-permute-done.3.refs_4_
  10.0 1.7 %collective-permute-start.6 = (bf16[2,64,256]{2,1,0:T(8,128)(2,1)S(1)}, bf16[2,64,256]{2,1,0:T(8,128)(2,1)S(1)}, u32[]{:S(2)}, u32[]{:S(2)}) collective-permute-start(bf16[2,64,256]{2,1,0:T(8,128)(2,1)S(1)} %collective-permute-done.3.refs_4_), channel_id=1, source_target_pairs={{24,0},{16,8},{8,16},{0,24},{25,1},{17,9},{9,17},{1,25},{26,2},{18... | collective-permute-start | bytes 196616 | tf_op jit(solution)/shard_map/ppermute | solution.py:189
  11.7 1.4 %collective-permute-start.5 = (bf16[2,64,256]{2,1,0:T(8,128)(2,1)S(1)}, bf16[2,64,256]{2,1,0:T(8,128)(2,1)S(1)}, u32[]{:S(2)}, u32[]{:S(2)}) collective-permute-start(bf16[2,64,256]{2,1,0:T(8,128)(2,1)S(1)} %collective-permute-done.3.refs_4_), channel_id=1, source_target_pairs={{8,0},{0,8},{24,16},{16,24},{9,1},{1,9},{25,17},{17,25},{10,2},{2,... | collective-permute-start | bytes 196616 | tf_op jit(solution)/shard_map/ppermute | solution.py:189
  13.1 1.4 %collective-permute-start.4 = (bf16[2,64,256]{2,1,0:T(8,128)(2,1)S(1)}, bf16[2,64,256]{2,1,0:T(8,128)(2,1)S(1)}, u32[]{:S(2)}, u32[]{:S(2)}) collective-permute-start(bf16[2,64,256]{2,1,0:T(8,128)(2,1)S(1)} %collective-permute-done.3.refs_4_), channel_id=1, source_target_pairs={{16,0},{24,8},{0,16},{8,24},{17,1},{25,9},{1,17},{9,25},{18,2},{26... | collective-permute-start | bytes 196616 | tf_op jit(solution)/shard_map/ppermute | solution.py:189
  14.5 0.0 collective-permute-done.1.refs_2_
  14.5 0.0 collective-permute-start.7
  14.5 0.0 collective-permute-done.refs_1_
  14.5 0.1 collective-permute-start.2
  14.6 0.6 %collective-permute-done.6.refs_7_ = bf16[2,64,256]{2,1,0:T(8,128)(2,1)S(1)} collective-permute-done((bf16[2,64,256]{2,1,0:T(8,128)(2,1)S(1)}, bf16[2,64,256]{2,1,0:T(8,128)(2,1)S(1)}, u32[]{:S(2)}, u32[]{:S(2)}) %collective-permute-start.6) | collective-permute-done | bytes 65568 | tf_op jit(solution)/shard_map/ppermute | solution.py:189
  15.2 0.0 collective-permute-start.10
  15.2 0.8 %collective-permute-done.5.refs_6_ = bf16[2,64,256]{2,1,0:T(8,128)(2,1)S(1)} collective-permute-done((bf16[2,64,256]{2,1,0:T(8,128)(2,1)S(1)}, bf16[2,64,256]{2,1,0:T(8,128)(2,1)S(1)}, u32[]{:S(2)}, u32[]{:S(2)}) %collective-permute-start.5) | collective-permute-done | bytes 65568 | tf_op jit(solution)/shard_map/ppermute | solution.py:189
  16.1 0.0 collective-permute-start.9
  16.1 1.3 %collective-permute-done.4.refs_5_ = bf16[2,64,256]{2,1,0:T(8,128)(2,1)S(1)} collective-permute-done((bf16[2,64,256]{2,1,0:T(8,128)(2,1)S(1)}, bf16[2,64,256]{2,1,0:T(8,128)(2,1)S(1)}, u32[]{:S(2)}, u32[]{:S(2)}) %collective-permute-start.4) | collective-permute-done | bytes 65568 | tf_op jit(solution)/shard_map/ppermute | solution.py:189
  17.4 0.0 collective-permute-start.8
  17.4 0.0 collective-permute-done.7.refs_8_
  17.4 1.6 %collective-permute-done.2.refs_3_ = bf16[2,64,256]{2,1,0:T(8,128)(2,1)S(1)} collective-permute-done((bf16[2,64,256]{2,1,0:T(8,128)(2,1)S(1)}, bf16[2,64,256]{2,1,0:T(8,128)(2,1)S(1)}, u32[]{:S(2)}, u32[]{:S(2)}) %collective-permute-start.2) | collective-permute-done | bytes 65568 | tf_op jit(solution)/shard_map/ppermute | solution.py:86
  19.0 0.0 collective-permute-done.10.refs_11_
  19.0 0.0 collective-permute-done.9.refs_10_
  19.0 0.0 collective-permute-done.8.refs_9_
  19.1 1.9 %update.1 = f32[4096,128]{1,0:T(8,128)} custom-call(bf16[2,64,256]{2,1,0:T(8,128)(2,1)S(1)} %factor.1.after_ref.refs_0_, bf16[2,64,256]{2,1,0:T(8,128)(2,1)S(1)} %collective-permute-done.refs_1_, bf16[2,64,256]{2,1,0:T(8,128)(2,1)S(1)} %collective-permute-done.1.refs_2_, bf16[2,64,256]{2,1,0:T(8,128)(2,1)S(1)} %collective-permute-done.2.refs_3_, ...), custom_call_target="tpu_custom_call" | custom-call | tf_op jit(solution)/shard_map/update/pallas_call | solution.py:157
Async XLA Ops:
  1.4 8.5 %collective-permute-start.3 = (bf16[2,64,256]{2,1,0:T(8,128)(2,1)S(1)}, bf16[2,64,256]{2,1,0:T(8,128)(2,1)S(1)}, u32[]{:S(2)}, u32[]{:S(2)}) collective-permute-start(bf16[2,64,256]{2,1,0:T(8,128)(2,1)S(1)} %factor.1.after_ref.refs_0_), channel_id=1, source_target_pairs={{0,24},{2,0},{4,8},{6,16},{8,26},{10,18},{12,10},{14,2},{16,4},{18... | collective-permute-start | bytes 196616 | tf_op jit(solution)/shard_map/ppermute | solution.py:181
  7.0 7.5 %collective-permute-start.1 = (bf16[2,64,256]{2,1,0:T(8,128)(2,1)S(1)}, bf16[2,64,256]{2,1,0:T(8,128)(2,1)S(1)}, u32[]{:S(2)}, u32[]{:S(2)}) collective-permute-start(bf16[2,64,256]{2,1,0:T(8,128)(2,1)S(1)} %factor.1.after_ref.refs_0_), channel_id=1, source_target_pairs={{4,0},{6,2},{0,4},{2,6},{5,1},{7,3},{1,5},{3,7},{12,8},{14,10},{8,... | collective-permute-start | bytes 196616 | tf_op jit(solution)/shard_map/ppermute | solution.py:84
  8.5 6.1 %collective-permute-start = (bf16[2,64,256]{2,1,0:T(8,128)(2,1)S(1)}, bf16[2,64,256]{2,1,0:T(8,128)(2,1)S(1)}, u32[]{:S(2)}, u32[]{:S(2)}) collective-permute-start(bf16[2,64,256]{2,1,0:T(8,128)(2,1)S(1)} %factor.1.after_ref.refs_0_), channel_id=1, source_target_pairs={{2,0},{0,2},{6,4},{4,6},{3,1},{1,3},{7,5},{5,7},{10,8},{8,10},{14,... | collective-permute-start | bytes 196616 | tf_op jit(solution)/shard_map/ppermute | solution.py:85
  10.0 5.3 %collective-permute-start.6 = (bf16[2,64,256]{2,1,0:T(8,128)(2,1)S(1)}, bf16[2,64,256]{2,1,0:T(8,128)(2,1)S(1)}, u32[]{:S(2)}, u32[]{:S(2)}) collective-permute-start(bf16[2,64,256]{2,1,0:T(8,128)(2,1)S(1)} %collective-permute-done.3.refs_4_), channel_id=1, source_target_pairs={{24,0},{16,8},{8,16},{0,24},{25,1},{17,9},{9,17},{1,25},{26,2},{18... | collective-permute-start | bytes 196616 | tf_op jit(solution)/shard_map/ppermute | solution.py:189
  11.7 4.4 %collective-permute-start.5 = (bf16[2,64,256]{2,1,0:T(8,128)(2,1)S(1)}, bf16[2,64,256]{2,1,0:T(8,128)(2,1)S(1)}, u32[]{:S(2)}, u32[]{:S(2)}) collective-permute-start(bf16[2,64,256]{2,1,0:T(8,128)(2,1)S(1)} %collective-permute-done.3.refs_4_), channel_id=1, source_target_pairs={{8,0},{0,8},{24,16},{16,24},{9,1},{1,9},{25,17},{17,25},{10,2},{2,... | collective-permute-start | bytes 196616 | tf_op jit(solution)/shard_map/ppermute | solution.py:189
  13.1 4.3 %collective-permute-start.4 = (bf16[2,64,256]{2,1,0:T(8,128)(2,1)S(1)}, bf16[2,64,256]{2,1,0:T(8,128)(2,1)S(1)}, u32[]{:S(2)}, u32[]{:S(2)}) collective-permute-start(bf16[2,64,256]{2,1,0:T(8,128)(2,1)S(1)} %collective-permute-done.3.refs_4_), channel_id=1, source_target_pairs={{16,0},{24,8},{0,16},{8,24},{17,1},{25,9},{1,17},{9,25},{18,2},{26... | collective-permute-start | bytes 196616 | tf_op jit(solution)/shard_map/ppermute | solution.py:189
  14.5 2.9 %collective-permute-start.7 = (bf16[2,64,256]{2,1,0:T(8,128)(2,1)S(1)}, bf16[2,64,256]{2,1,0:T(8,128)(2,1)S(1)}, u32[]{:S(2)}, u32[]{:S(2)}) collective-permute-start(bf16[2,64,256]{2,1,0:T(8,128)(2,1)S(1)} %collective-permute-done.3.refs_4_), channel_id=1, source_target_pairs={{1,0},{0,1},{3,2},{2,3},{5,4},{4,5},{7,6},{6,7},{9,8},{8,9},{11,10... | collective-permute-start | bytes 196616 | tf_op jit(solution)/shard_map/ppermute | solution.py:193
  14.5 4.5 %collective-permute-start.2 = (bf16[2,64,256]{2,1,0:T(8,128)(2,1)S(1)}, bf16[2,64,256]{2,1,0:T(8,128)(2,1)S(1)}, u32[]{:S(2)}, u32[]{:S(2)}) collective-permute-start(bf16[2,64,256]{2,1,0:T(8,128)(2,1)S(1)} %collective-permute-done.1.refs_2_), channel_id=1, source_target_pairs={{2,0},{0,2},{6,4},{4,6},{3,1},{1,3},{7,5},{5,7},{10,8},{8,10},{14,... | collective-permute-start | bytes 196616 | tf_op jit(solution)/shard_map/ppermute | solution.py:86
  15.2 3.8 %collective-permute-start.10 = (bf16[2,64,256]{2,1,0:T(8,128)(2,1)S(1)}, bf16[2,64,256]{2,1,0:T(8,128)(2,1)S(1)}, u32[]{:S(2)}, u32[]{:S(2)}) collective-permute-start(bf16[2,64,256]{2,1,0:T(8,128)(2,1)S(1)} %collective-permute-done.6.refs_7_), channel_id=1, source_target_pairs={{1,0},{0,1},{3,2},{2,3},{5,4},{4,5},{7,6},{6,7},{9,8},{8,9},{11,10... | collective-permute-start | bytes 196616 | tf_op jit(solution)/shard_map/ppermute | solution.py:193
  16.1 3.0 %collective-permute-start.9 = (bf16[2,64,256]{2,1,0:T(8,128)(2,1)S(1)}, bf16[2,64,256]{2,1,0:T(8,128)(2,1)S(1)}, u32[]{:S(2)}, u32[]{:S(2)}) collective-permute-start(bf16[2,64,256]{2,1,0:T(8,128)(2,1)S(1)} %collective-permute-done.5.refs_6_), channel_id=1, source_target_pairs={{1,0},{0,1},{3,2},{2,3},{5,4},{4,5},{7,6},{6,7},{9,8},{8,9},{11,10... | collective-permute-start | bytes 196616 | tf_op jit(solution)/shard_map/ppermute | solution.py:193
  17.4 1.6 %collective-permute-start.8 = (bf16[2,64,256]{2,1,0:T(8,128)(2,1)S(1)}, bf16[2,64,256]{2,1,0:T(8,128)(2,1)S(1)}, u32[]{:S(2)}, u32[]{:S(2)}) collective-permute-start(bf16[2,64,256]{2,1,0:T(8,128)(2,1)S(1)} %collective-permute-done.4.refs_5_), channel_id=1, source_target_pairs={{1,0},{0,1},{3,2},{2,3},{5,4},{4,5},{7,6},{6,7},{9,8},{8,9},{11,10... | collective-permute-start | bytes 196616 | tf_op jit(solution)/shard_map/ppermute | solution.py:193

commit v13 on v12

--- a/solution.py
+++ b/solution.py
@@ -75,14 +75,14 @@
     return slab
 
 
-def gather_line(factor, count):
+def gather_line(factor, late_factor, count):
     if count != 4:
         line = [factor]
         for step in range(1, count):
             line.append(lax.ppermute(factor, "col", [(partner(b, step, count), b) for b in range(count)]))
         return line
-    far = lax.ppermute(factor, "col", [(b ^ 2, b) for b in range(count)])
     near = lax.ppermute(factor, "col", [(b ^ 1, b) for b in range(count)])
+    far = lax.ppermute(late_factor, "col", [(b ^ 2, b) for b in range(count)])
     both = lax.ppermute(far, "col", [(b ^ 1, b) for b in range(count)])
     return [factor, near, far, both]
 
@@ -183,7 +183,7 @@
     )
     share = load_share(factor, trailing.reshape(-1, LANES), layers)
     loaded_factor, share = lax.optimization_barrier((factor, share))
-    line = gather_line(loaded_factor, count)
+    line = gather_line(factor, loaded_factor, count)
     plane = [moved]
     for step in plane_steps(count)[1:]:
         plane.append(lax.ppermute(moved, "row", [(partner(a, step, count), a) for a in range(count)]))

time: 21.1 us -> 21.3 us (level)
  the two profiles are of different devices: /device:TPU:0 before, /device:TPU:25 now
where the time goes in v13:
time: 21.3 us; the launch traced here: 21.2 us
  starting transfers between devices  15.3 us (72%)
  Pallas kernels  4.9 us (23%)
  waiting for transfers between devices  0.91 us (4%)
    ppermute x4, starting transfers between devices, per_device(): others += [lax.ppermute(piece, 'layer', pairs) for piece in plane]  9.22 us
    ppermute x3, starting transfers between devices, per_device(): lax.ppermute(moved, 'row', [(partner(a, step, count), a) for a in range(c...  3.61 us
    pallas_call x1, Pallas kernels, update_trailing(): pl.pallas_call(body, out_shape=jax.ShapeDtypeStruct(share.shape, jnp.floa...  1.86 us
    pallas_call x1, Pallas kernels, load_share(): pl.pallas_call(load_kernel, out_shape=jax.ShapeDtypeStruct((rows, LANES),...  1.6 us
    pallas_call x1, Pallas kernels, make_factor(): pl.pallas_call(factor_kernel, out_shape=jax.ShapeDtypeStruct((half, tile_...  1.44 us
    ppermute x1, starting transfers between devices, gather_line(): far = lax.ppermute(late_factor, 'col', [(b ^ 2, b) for b in range(count)])  1.3 us
    ppermute x1, starting transfers between devices, per_device(): lax.ppermute(factor, ('row', 'col'), [(a * count + b, slots[a][b] * count...  0.95 us
    ppermute x4, waiting for transfers between devices, per_device(): others += [lax.ppermute(piece, 'layer', pairs) for piece in plane]  0.89 us
  transfers between devices with their start and end apart: 11, of which 1 were waited for; matrix products, arithmetic and copies ran while one was open for 0% of the time, Pallas kernels for 8%

profile of v13, /device:TPU:25, one launch (start us, length us, event | category | flops | bytes accessed | tf_op | source)
XLA Modules:
  0.0 21.2 jit_solution(10263186518435936135)
XLA Ops:
  0.0 1.4 %factor.1.after_ref.refs_0_ = bf16[2,64,256]{2,1,0:T(8,128)(2,1)S(1)} custom-call(f32[4,1,64,256]{3,2,1,0:T(8,128)} %panel_ref.1, f32[256,256]{1,0:T(8,128)} %inverse_ref.1), custom_call_target="tpu_custom_call" | custom-call | tf_op jit(solution)/shard_map/factor/pallas_call | solution.py:41
  1.4 1.0 %collective-permute-start.3 = (bf16[2,64,256]{2,1,0:T(8,128)(2,1)S(1)}, bf16[2,64,256]{2,1,0:T(8,128)(2,1)S(1)}, u32[]{:S(2)}, u32[]{:S(2)}) collective-permute-start(bf16[2,64,256]{2,1,0:T(8,128)(2,1)S(1)} %factor.1.after_ref.refs_0_), channel_id=1, source_target_pairs={{0,24},{2,0},{4,8},{6,16},{8,26},{10,18},{12,10},{14,2},{16,4},{18... | collective-permute-start | bytes 196616 | tf_op jit(solution)/shard_map/ppermute | solution.py:181
  2.4 0.3 %collective-permute-start = (bf16[2,64,256]{2,1,0:T(8,128)(2,1)S(1)}, bf16[2,64,256]{2,1,0:T(8,128)(2,1)S(1)}, u32[]{:S(2)}, u32[]{:S(2)}) collective-permute-start(bf16[2,64,256]{2,1,0:T(8,128)(2,1)S(1)} %factor.1.after_ref.refs_0_), channel_id=1, source_target_pairs={{2,0},{0,2},{6,4},{4,6},{3,1},{1,3},{7,5},{5,7},{10,8},{8,10},{14,... | collective-permute-start | bytes 196616 | tf_op jit(solution)/shard_map/ppermute | solution.py:84
  2.7 1.6 %load_share.1.refs_12_ = f32[4096,128]{1,0:T(8,128)S(1)} custom-call(bf16[2,64,256]{2,1,0:T(8,128)(2,1)S(1)} %factor.1.after_ref.refs_0_, f32[8192,128]{1,0:T(8,128)} %bitcast.2), custom_call_target="tpu_custom_call" | custom-call | bytes 4194304 | tf_op jit(solution)/shard_map/load_share/pallas_call | solution.py:100
  4.3 1.3 %collective-permute-start.1 = (bf16[2,64,256]{2,1,0:T(8,128)(2,1)S(1)}, bf16[2,64,256]{2,1,0:T(8,128)(2,1)S(1)}, u32[]{:S(2)}, u32[]{:S(2)}) collective-permute-start(bf16[2,64,256]{2,1,0:T(8,128)(2,1)S(1)} %factor.1.after_ref.refs_0_), channel_id=1, source_target_pairs={{4,0},{6,2},{0,4},{2,6},{5,1},{7,3},{1,5},{3,7},{12,8},{14,10},{8,... | collective-permute-start | bytes 196616 | tf_op jit(solution)/shard_map/ppermute | solution.py:85
  5.6 0.0 collective-permute-done.3.refs_4_
  5.6 3.3 %collective-permute-start.6 = (bf16[2,64,256]{2,1,0:T(8,128)(2,1)S(1)}, bf16[2,64,256]{2,1,0:T(8,128)(2,1)S(1)}, u32[]{:S(2)}, u32[]{:S(2)}) collective-permute-start(bf16[2,64,256]{2,1,0:T(8,128)(2,1)S(1)} %collective-permute-done.3.refs_4_), channel_id=1, source_target_pairs={{24,0},{16,8},{8,16},{0,24},{25,1},{17,9},{9,17},{1,25},{26,2},{18... | collective-permute-start | bytes 196616 | tf_op jit(solution)/shard_map/ppermute | solution.py:189
  8.9 0.0 collective-permute-start.5
  8.9 0.3 %collective-permute-start.4 = (bf16[2,64,256]{2,1,0:T(8,128)(2,1)S(1)}, bf16[2,64,256]{2,1,0:T(8,128)(2,1)S(1)}, u32[]{:S(2)}, u32[]{:S(2)}) collective-permute-start(bf16[2,64,256]{2,1,0:T(8,128)(2,1)S(1)} %collective-permute-done.3.refs_4_), channel_id=1, source_target_pairs={{16,0},{24,8},{0,16},{8,24},{17,1},{25,9},{1,17},{9,25},{18,2},{26... | collective-permute-start | bytes 196616 | tf_op jit(solution)/shard_map/ppermute | solution.py:189
  9.2 0.0 collective-permute-done.refs_1_
  9.2 5.0 %collective-permute-start.7 = (bf16[2,64,256]{2,1,0:T(8,128)(2,1)S(1)}, bf16[2,64,256]{2,1,0:T(8,128)(2,1)S(1)}, u32[]{:S(2)}, u32[]{:S(2)}) collective-permute-start(bf16[2,64,256]{2,1,0:T(8,128)(2,1)S(1)} %collective-permute-done.3.refs_4_), channel_id=1, source_target_pairs={{1,0},{0,1},{3,2},{2,3},{5,4},{4,5},{7,6},{6,7},{9,8},{8,9},{11,10... | collective-permute-start | bytes 196616 | tf_op jit(solution)/shard_map/ppermute | solution.py:193
  14.2 0.0 collective-permute-done.1.refs_2_
  14.2 0.0 collective-permute-start.2
  14.2 0.0 collective-permute-done.6.refs_7_
  14.2 0.2 collective-permute-start.10
  14.3 0.0 collective-permute-done.5.refs_6_
  14.3 2.8 %collective-permute-start.9 = (bf16[2,64,256]{2,1,0:T(8,128)(2,1)S(1)}, bf16[2,64,256]{2,1,0:T(8,128)(2,1)S(1)}, u32[]{:S(2)}, u32[]{:S(2)}) collective-permute-start(bf16[2,64,256]{2,1,0:T(8,128)(2,1)S(1)} %collective-permute-done.5.refs_6_), channel_id=1, source_target_pairs={{1,0},{0,1},{3,2},{2,3},{5,4},{4,5},{7,6},{6,7},{9,8},{8,9},{11,10... | collective-permute-start | bytes 196616 | tf_op jit(solution)/shard_map/ppermute | solution.py:193
  17.1 0.0 collective-permute-done.4.refs_5_
  17.1 1.3 %collective-permute-start.8 = (bf16[2,64,256]{2,1,0:T(8,128)(2,1)S(1)}, bf16[2,64,256]{2,1,0:T(8,128)(2,1)S(1)}, u32[]{:S(2)}, u32[]{:S(2)}) collective-permute-start(bf16[2,64,256]{2,1,0:T(8,128)(2,1)S(1)} %collective-permute-done.4.refs_5_), channel_id=1, source_target_pairs={{1,0},{0,1},{3,2},{2,3},{5,4},{4,5},{7,6},{6,7},{9,8},{8,9},{11,10... | collective-permute-start | bytes 196616 | tf_op jit(solution)/shard_map/ppermute | solution.py:193
  18.4 0.0 collective-permute-done.7.refs_8_
  18.4 0.0 collective-permute-done.2.refs_3_
  18.4 0.0 collective-permute-done.10.refs_11_
  18.4 0.0 collective-permute-done.9.refs_10_
  18.4 0.9 %collective-permute-done.8.refs_9_ = bf16[2,64,256]{2,1,0:T(8,128)(2,1)S(1)} collective-permute-done((bf16[2,64,256]{2,1,0:T(8,128)(2,1)S(1)}, bf16[2,64,256]{2,1,0:T(8,128)(2,1)S(1)}, u32[]{:S(2)}, u32[]{:S(2)}) %collective-permute-start.8) | collective-permute-done | bytes 65568 | tf_op jit(solution)/shard_map/ppermute | solution.py:193
  19.3 1.9 %update.1 = f32[4096,128]{1,0:T(8,128)} custom-call(bf16[2,64,256]{2,1,0:T(8,128)(2,1)S(1)} %factor.1.after_ref.refs_0_, bf16[2,64,256]{2,1,0:T(8,128)(2,1)S(1)} %collective-permute-done.refs_1_, bf16[2,64,256]{2,1,0:T(8,128)(2,1)S(1)} %collective-permute-done.1.refs_2_, bf16[2,64,256]{2,1,0:T(8,128)(2,1)S(1)} %collective-permute-done.2.refs_3_, ...), custom_call_target="tpu_custom_call" | custom-call | tf_op jit(solution)/shard_map/update/pallas_call | solution.py:157
Async XLA Ops:
  1.4 4.1 %collective-permute-start.3 = (bf16[2,64,256]{2,1,0:T(8,128)(2,1)S(1)}, bf16[2,64,256]{2,1,0:T(8,128)(2,1)S(1)}, u32[]{:S(2)}, u32[]{:S(2)}) collective-permute-start(bf16[2,64,256]{2,1,0:T(8,128)(2,1)S(1)} %factor.1.after_ref.refs_0_), channel_id=1, source_target_pairs={{0,24},{2,0},{4,8},{6,16},{8,26},{10,18},{12,10},{14,2},{16,4},{18... | collective-permute-start | bytes 196616 | tf_op jit(solution)/shard_map/ppermute | solution.py:181
  2.4 6.8 %collective-permute-start = (bf16[2,64,256]{2,1,0:T(8,128)(2,1)S(1)}, bf16[2,64,256]{2,1,0:T(8,128)(2,1)S(1)}, u32[]{:S(2)}, u32[]{:S(2)}) collective-permute-start(bf16[2,64,256]{2,1,0:T(8,128)(2,1)S(1)} %factor.1.after_ref.refs_0_), channel_id=1, source_target_pairs={{2,0},{0,2},{6,4},{4,6},{3,1},{1,3},{7,5},{5,7},{10,8},{8,10},{14,... | collective-permute-start | bytes 196616 | tf_op jit(solution)/shard_map/ppermute | solution.py:84
  4.3 9.9 %collective-permute-start.1 = (bf16[2,64,256]{2,1,0:T(8,128)(2,1)S(1)}, bf16[2,64,256]{2,1,0:T(8,128)(2,1)S(1)}, u32[]{:S(2)}, u32[]{:S(2)}) collective-permute-start(bf16[2,64,256]{2,1,0:T(8,128)(2,1)S(1)} %factor.1.after_ref.refs_0_), channel_id=1, source_target_pairs={{4,0},{6,2},{0,4},{2,6},{5,1},{7,3},{1,5},{3,7},{12,8},{14,10},{8,... | collective-permute-start | bytes 196616 | tf_op jit(solution)/shard_map/ppermute | solution.py:85
  5.6 8.6 %collective-permute-start.6 = (bf16[2,64,256]{2,1,0:T(8,128)(2,1)S(1)}, bf16[2,64,256]{2,1,0:T(8,128)(2,1)S(1)}, u32[]{:S(2)}, u32[]{:S(2)}) collective-permute-start(bf16[2,64,256]{2,1,0:T(8,128)(2,1)S(1)} %collective-permute-done.3.refs_4_), channel_id=1, source_target_pairs={{24,0},{16,8},{8,16},{0,24},{25,1},{17,9},{9,17},{1,25},{26,2},{18... | collective-permute-start | bytes 196616 | tf_op jit(solution)/shard_map/ppermute | solution.py:189
  8.9 5.4 %collective-permute-start.5 = (bf16[2,64,256]{2,1,0:T(8,128)(2,1)S(1)}, bf16[2,64,256]{2,1,0:T(8,128)(2,1)S(1)}, u32[]{:S(2)}, u32[]{:S(2)}) collective-permute-start(bf16[2,64,256]{2,1,0:T(8,128)(2,1)S(1)} %collective-permute-done.3.refs_4_), channel_id=1, source_target_pairs={{8,0},{0,8},{24,16},{16,24},{9,1},{1,9},{25,17},{17,25},{10,2},{2,... | collective-permute-start | bytes 196616 | tf_op jit(solution)/shard_map/ppermute | solution.py:189
  8.9 8.2 %collective-permute-start.4 = (bf16[2,64,256]{2,1,0:T(8,128)(2,1)S(1)}, bf16[2,64,256]{2,1,0:T(8,128)(2,1)S(1)}, u32[]{:S(2)}, u32[]{:S(2)}) collective-permute-start(bf16[2,64,256]{2,1,0:T(8,128)(2,1)S(1)} %collective-permute-done.3.refs_4_), channel_id=1, source_target_pairs={{16,0},{24,8},{0,16},{8,24},{17,1},{25,9},{1,17},{9,25},{18,2},{26... | collective-permute-start | bytes 196616 | tf_op jit(solution)/shard_map/ppermute | solution.py:189
  9.2 9.2 %collective-permute-start.7 = (bf16[2,64,256]{2,1,0:T(8,128)(2,1)S(1)}, bf16[2,64,256]{2,1,0:T(8,128)(2,1)S(1)}, u32[]{:S(2)}, u32[]{:S(2)}) collective-permute-start(bf16[2,64,256]{2,1,0:T(8,128)(2,1)S(1)} %collective-permute-done.3.refs_4_), channel_id=1, source_target_pairs={{1,0},{0,1},{3,2},{2,3},{5,4},{4,5},{7,6},{6,7},{9,8},{8,9},{11,10... | collective-permute-start | bytes 196616 | tf_op jit(solution)/shard_map/ppermute | solution.py:193
  14.2 4.3 %collective-permute-start.2 = (bf16[2,64,256]{2,1,0:T(8,128)(2,1)S(1)}, bf16[2,64,256]{2,1,0:T(8,128)(2,1)S(1)}, u32[]{:S(2)}, u32[]{:S(2)}) collective-permute-start(bf16[2,64,256]{2,1,0:T(8,128)(2,1)S(1)} %collective-permute-done.1.refs_2_), channel_id=1, source_target_pairs={{2,0},{0,2},{6,4},{4,6},{3,1},{1,3},{7,5},{5,7},{10,8},{8,10},{14,... | collective-permute-start | bytes 196616 | tf_op jit(solution)/shard_map/ppermute | solution.py:86
  14.2 4.3 %collective-permute-start.10 = (bf16[2,64,256]{2,1,0:T(8,128)(2,1)S(1)}, bf16[2,64,256]{2,1,0:T(8,128)(2,1)S(1)}, u32[]{:S(2)}, u32[]{:S(2)}) collective-permute-start(bf16[2,64,256]{2,1,0:T(8,128)(2,1)S(1)} %collective-permute-done.6.refs_7_), channel_id=1, source_target_pairs={{1,0},{0,1},{3,2},{2,3},{5,4},{4,5},{7,6},{6,7},{9,8},{8,9},{11,10... | collective-permute-start | bytes 196616 | tf_op jit(solution)/shard_map/ppermute | solution.py:193
  14.3 4.1 %collective-permute-start.9 = (bf16[2,64,256]{2,1,0:T(8,128)(2,1)S(1)}, bf16[2,64,256]{2,1,0:T(8,128)(2,1)S(1)}, u32[]{:S(2)}, u32[]{:S(2)}) collective-permute-start(bf16[2,64,256]{2,1,0:T(8,128)(2,1)S(1)} %collective-permute-done.5.refs_6_), channel_id=1, source_target_pairs={{1,0},{0,1},{3,2},{2,3},{5,4},{4,5},{7,6},{6,7},{9,8},{8,9},{11,10... | collective-permute-start | bytes 196616 | tf_op jit(solution)/shard_map/ppermute | solution.py:193
  17.1 2.2 %collective-permute-start.8 = (bf16[2,64,256]{2,1,0:T(8,128)(2,1)S(1)}, bf16[2,64,256]{2,1,0:T(8,128)(2,1)S(1)}, u32[]{:S(2)}, u32[]{:S(2)}) collective-permute-start(bf16[2,64,256]{2,1,0:T(8,128)(2,1)S(1)} %collective-permute-done.4.refs_5_), channel_id=1, source_target_pairs={{1,0},{0,1},{3,2},{2,3},{5,4},{4,5},{7,6},{6,7},{9,8},{8,9},{11,10... | collective-permute-start | bytes 196616 | tf_op jit(solution)/shard_map/ppermute | solution.py:193

commit v14 on v13

--- a/solution.py
+++ b/solution.py
@@ -59,7 +59,7 @@
 
 def plane_slots(count):
     if count == 4:
-        return ((3, 0, 1, 2), (3, 2, 1, 0), (0, 2, 1, 3), (3, 1, 2, 0))
+        return ((3, 0, 1, 2), (3, 2, 1, 0), (0, 2, 1, 3), (3, 2, 1, 0))
     return tuple(tuple(count - 1 - b for b in range(count)) for _ in range(count))
 
 

time: 21.3 us -> 20.8 us (0.977)
  the two profiles are of different devices: /device:TPU:25 before, /device:TPU:0 now
where the time goes in v14:
time: 20.8 us; the launch traced here: 20.6 us
  starting transfers between devices  11.4 us (55%)
  Pallas kernels  4.89 us (24%)
  waiting for transfers between devices  4.31 us (21%)
    ppermute x1, starting transfers between devices, per_device(): lax.ppermute(factor, ('row', 'col'), [(a * count + b, slots[a][b] * count...  3.94 us
    ppermute x3, starting transfers between devices, per_device(): lax.ppermute(moved, 'row', [(partner(a, step, count), a) for a in range(c...  3.49 us
    ppermute x3, waiting for transfers between devices, per_device(): lax.ppermute(moved, 'row', [(partner(a, step, count), a) for a in range(c...  3.05 us
    ppermute x1, starting transfers between devices, gather_line(): far = lax.ppermute(late_factor, 'col', [(b ^ 2, b) for b in range(count)])  2.96 us
    pallas_call x1, Pallas kernels, update_trailing(): pl.pallas_call(body, out_shape=jax.ShapeDtypeStruct(share.shape, jnp.floa...  1.86 us
    pallas_call x1, Pallas kernels, load_share(): pl.pallas_call(load_kernel, out_shape=jax.ShapeDtypeStruct((rows, LANES),...  1.6 us
    pallas_call x1, Pallas kernels, make_factor(): pl.pallas_call(factor_kernel, out_shape=jax.ShapeDtypeStruct((half, tile_...  1.44 us
    ppermute x1, starting transfers between devices, gather_line(): both = lax.ppermute(far, 'col', [(b ^ 1, b) for b in range(count)])  0.95 us
  transfers between devices with their start and end apart: 11, of which 5 were waited for; matrix products, arithmetic and copies ran while one was open for 0% of the time, Pallas kernels for 8%

profile of v14, /device:TPU:0, one launch (start us, length us, event | category | flops | bytes accessed | tf_op | source)
XLA Modules:
  0.0 20.6 jit_solution(13041478963108410971)
XLA Ops:
  0.0 1.4 %factor.1.after_ref.refs_0_ = bf16[2,64,256]{2,1,0:T(8,128)(2,1)S(1)} custom-call(f32[4,1,64,256]{3,2,1,0:T(8,128)} %panel_ref.1, f32[256,256]{1,0:T(8,128)} %inverse_ref.1), custom_call_target="tpu_custom_call" | custom-call | tf_op jit(solution)/shard_map/factor/pallas_call | solution.py:41
  1.4 3.9 %collective-permute-start.3 = (bf16[2,64,256]{2,1,0:T(8,128)(2,1)S(1)}, bf16[2,64,256]{2,1,0:T(8,128)(2,1)S(1)}, u32[]{:S(2)}, u32[]{:S(2)}) collective-permute-start(bf16[2,64,256]{2,1,0:T(8,128)(2,1)S(1)} %factor.1.after_ref.refs_0_), channel_id=1, source_target_pairs={{0,24},{2,0},{4,8},{6,16},{8,26},{10,18},{12,10},{14,2},{16,4},{18... | collective-permute-start | bytes 196616 | tf_op jit(solution)/shard_map/ppermute | solution.py:181
  5.4 0.0 collective-permute-start
  5.4 1.6 %load_share.1.refs_12_ = f32[4096,128]{1,0:T(8,128)S(1)} custom-call(bf16[2,64,256]{2,1,0:T(8,128)(2,1)S(1)} %factor.1.after_ref.refs_0_, f32[8192,128]{1,0:T(8,128)} %bitcast.2), custom_call_target="tpu_custom_call" | custom-call | bytes 4194304 | tf_op jit(solution)/shard_map/load_share/pallas_call | solution.py:100
  7.0 3.0 %collective-permute-start.1 = (bf16[2,64,256]{2,1,0:T(8,128)(2,1)S(1)}, bf16[2,64,256]{2,1,0:T(8,128)(2,1)S(1)}, u32[]{:S(2)}, u32[]{:S(2)}) collective-permute-start(bf16[2,64,256]{2,1,0:T(8,128)(2,1)S(1)} %factor.1.after_ref.refs_0_), channel_id=1, source_target_pairs={{4,0},{6,2},{0,4},{2,6},{5,1},{7,3},{1,5},{3,7},{12,8},{14,10},{8,... | collective-permute-start | bytes 196616 | tf_op jit(solution)/shard_map/ppermute | solution.py:85
  10.0 0.0 collective-permute-done.3.refs_4_
  10.0 1.7 %collective-permute-start.6 = (bf16[2,64,256]{2,1,0:T(8,128)(2,1)S(1)}, bf16[2,64,256]{2,1,0:T(8,128)(2,1)S(1)}, u32[]{:S(2)}, u32[]{:S(2)}) collective-permute-start(bf16[2,64,256]{2,1,0:T(8,128)(2,1)S(1)} %collective-permute-done.3.refs_4_), channel_id=1, source_target_pairs={{24,0},{16,8},{8,16},{0,24},{25,1},{17,9},{9,17},{1,25},{26,2},{18... | collective-permute-start | bytes 196616 | tf_op jit(solution)/shard_map/ppermute | solution.py:189
  11.7 1.5 %collective-permute-start.5 = (bf16[2,64,256]{2,1,0:T(8,128)(2,1)S(1)}, bf16[2,64,256]{2,1,0:T(8,128)(2,1)S(1)}, u32[]{:S(2)}, u32[]{:S(2)}) collective-permute-start(bf16[2,64,256]{2,1,0:T(8,128)(2,1)S(1)} %collective-permute-done.3.refs_4_), channel_id=1, source_target_pairs={{8,0},{0,8},{24,16},{16,24},{9,1},{1,9},{25,17},{17,25},{10,2},{2,... | collective-permute-start | bytes 196616 | tf_op jit(solution)/shard_map/ppermute | solution.py:189
  13.2 0.2 %collective-permute-start.4 = (bf16[2,64,256]{2,1,0:T(8,128)(2,1)S(1)}, bf16[2,64,256]{2,1,0:T(8,128)(2,1)S(1)}, u32[]{:S(2)}, u32[]{:S(2)}) collective-permute-start(bf16[2,64,256]{2,1,0:T(8,128)(2,1)S(1)} %collective-permute-done.3.refs_4_), channel_id=1, source_target_pairs={{16,0},{24,8},{0,16},{8,24},{17,1},{25,9},{1,17},{9,25},{18,2},{26... | collective-permute-start | bytes 196616 | tf_op jit(solution)/shard_map/ppermute | solution.py:189
  13.5 0.0 collective-permute-done.refs_1_
  13.5 0.0 collective-permute-start.7
  13.5 0.0 collective-permute-done.1.refs_2_
  13.5 1.0 %collective-permute-start.2 = (bf16[2,64,256]{2,1,0:T(8,128)(2,1)S(1)}, bf16[2,64,256]{2,1,0:T(8,128)(2,1)S(1)}, u32[]{:S(2)}, u32[]{:S(2)}) collective-permute-start(bf16[2,64,256]{2,1,0:T(8,128)(2,1)S(1)} %collective-permute-done.1.refs_2_), channel_id=1, source_target_pairs={{2,0},{0,2},{6,4},{4,6},{3,1},{1,3},{7,5},{5,7},{10,8},{8,10},{14,... | collective-permute-start | bytes 196616 | tf_op jit(solution)/shard_map/ppermute | solution.py:86
  14.4 0.8 %collective-permute-done.6.refs_7_ = bf16[2,64,256]{2,1,0:T(8,128)(2,1)S(1)} collective-permute-done((bf16[2,64,256]{2,1,0:T(8,128)(2,1)S(1)}, bf16[2,64,256]{2,1,0:T(8,128)(2,1)S(1)}, u32[]{:S(2)}, u32[]{:S(2)}) %collective-permute-start.6) | collective-permute-done | bytes 65568 | tf_op jit(solution)/shard_map/ppermute | solution.py:189
  15.2 0.0 collective-permute-start.10
  15.2 0.9 %collective-permute-done.5.refs_6_ = bf16[2,64,256]{2,1,0:T(8,128)(2,1)S(1)} collective-permute-done((bf16[2,64,256]{2,1,0:T(8,128)(2,1)S(1)}, bf16[2,64,256]{2,1,0:T(8,128)(2,1)S(1)}, u32[]{:S(2)}, u32[]{:S(2)}) %collective-permute-start.5) | collective-permute-done | bytes 65568 | tf_op jit(solution)/shard_map/ppermute | solution.py:189
  16.2 0.0 collective-permute-start.9
  16.2 1.3 %collective-permute-done.4.refs_5_ = bf16[2,64,256]{2,1,0:T(8,128)(2,1)S(1)} collective-permute-done((bf16[2,64,256]{2,1,0:T(8,128)(2,1)S(1)}, bf16[2,64,256]{2,1,0:T(8,128)(2,1)S(1)}, u32[]{:S(2)}, u32[]{:S(2)}) %collective-permute-start.4) | collective-permute-done | bytes 65568 | tf_op jit(solution)/shard_map/ppermute | solution.py:189
  17.5 0.0 collective-permute-start.8
  17.5 0.0 collective-permute-done.7.refs_8_
  17.5 0.5 %collective-permute-done.2.refs_3_ = bf16[2,64,256]{2,1,0:T(8,128)(2,1)S(1)} collective-permute-done((bf16[2,64,256]{2,1,0:T(8,128)(2,1)S(1)}, bf16[2,64,256]{2,1,0:T(8,128)(2,1)S(1)}, u32[]{:S(2)}, u32[]{:S(2)}) %collective-permute-start.2) | collective-permute-done | bytes 65568 | tf_op jit(solution)/shard_map/ppermute | solution.py:86
  18.0 0.0 collective-permute-done.10.refs_11_
  18.0 0.0 collective-permute-done.9.refs_10_
  18.0 0.8 %collective-permute-done.8.refs_9_ = bf16[2,64,256]{2,1,0:T(8,128)(2,1)S(1)} collective-permute-done((bf16[2,64,256]{2,1,0:T(8,128)(2,1)S(1)}, bf16[2,64,256]{2,1,0:T(8,128)(2,1)S(1)}, u32[]{:S(2)}, u32[]{:S(2)}) %collective-permute-start.8) | collective-permute-done | bytes 65568 | tf_op jit(solution)/shard_map/ppermute | solution.py:193
  18.7 1.9 %update.1 = f32[4096,128]{1,0:T(8,128)} custom-call(bf16[2,64,256]{2,1,0:T(8,128)(2,1)S(1)} %factor.1.after_ref.refs_0_, bf16[2,64,256]{2,1,0:T(8,128)(2,1)S(1)} %collective-permute-done.refs_1_, bf16[2,64,256]{2,1,0:T(8,128)(2,1)S(1)} %collective-permute-done.1.refs_2_, bf16[2,64,256]{2,1,0:T(8,128)(2,1)S(1)} %collective-permute-done.2.refs_3_, ...), custom_call_target="tpu_custom_call" | custom-call | tf_op jit(solution)/shard_map/update/pallas_call | solution.py:157
Async XLA Ops:
  1.4 8.5 %collective-permute-start.3 = (bf16[2,64,256]{2,1,0:T(8,128)(2,1)S(1)}, bf16[2,64,256]{2,1,0:T(8,128)(2,1)S(1)}, u32[]{:S(2)}, u32[]{:S(2)}) collective-permute-start(bf16[2,64,256]{2,1,0:T(8,128)(2,1)S(1)} %factor.1.after_ref.refs_0_), channel_id=1, source_target_pairs={{0,24},{2,0},{4,8},{6,16},{8,26},{10,18},{12,10},{14,2},{16,4},{18... | collective-permute-start | bytes 196616 | tf_op jit(solution)/shard_map/ppermute | solution.py:181
  5.4 8.1 %collective-permute-start = (bf16[2,64,256]{2,1,0:T(8,128)(2,1)S(1)}, bf16[2,64,256]{2,1,0:T(8,128)(2,1)S(1)}, u32[]{:S(2)}, u32[]{:S(2)}) collective-permute-start(bf16[2,64,256]{2,1,0:T(8,128)(2,1)S(1)} %factor.1.after_ref.refs_0_), channel_id=1, source_target_pairs={{2,0},{0,2},{6,4},{4,6},{3,1},{1,3},{7,5},{5,7},{10,8},{8,10},{14,... | collective-permute-start | bytes 196616 | tf_op jit(solution)/shard_map/ppermute | solution.py:84
  7.0 6.5 %collective-permute-start.1 = (bf16[2,64,256]{2,1,0:T(8,128)(2,1)S(1)}, bf16[2,64,256]{2,1,0:T(8,128)(2,1)S(1)}, u32[]{:S(2)}, u32[]{:S(2)}) collective-permute-start(bf16[2,64,256]{2,1,0:T(8,128)(2,1)S(1)} %factor.1.after_ref.refs_0_), channel_id=1, source_target_pairs={{4,0},{6,2},{0,4},{2,6},{5,1},{7,3},{1,5},{3,7},{12,8},{14,10},{8,... | collective-permute-start | bytes 196616 | tf_op jit(solution)/shard_map/ppermute | solution.py:85
  10.0 5.3 %collective-permute-start.6 = (bf16[2,64,256]{2,1,0:T(8,128)(2,1)S(1)}, bf16[2,64,256]{2,1,0:T(8,128)(2,1)S(1)}, u32[]{:S(2)}, u32[]{:S(2)}) collective-permute-start(bf16[2,64,256]{2,1,0:T(8,128)(2,1)S(1)} %collective-permute-done.3.refs_4_), channel_id=1, source_target_pairs={{24,0},{16,8},{8,16},{0,24},{25,1},{17,9},{9,17},{1,25},{26,2},{18... | collective-permute-start | bytes 196616 | tf_op jit(solution)/shard_map/ppermute | solution.py:189
  11.7 4.4 %collective-permute-start.5 = (bf16[2,64,256]{2,1,0:T(8,128)(2,1)S(1)}, bf16[2,64,256]{2,1,0:T(8,128)(2,1)S(1)}, u32[]{:S(2)}, u32[]{:S(2)}) collective-permute-start(bf16[2,64,256]{2,1,0:T(8,128)(2,1)S(1)} %collective-permute-done.3.refs_4_), channel_id=1, source_target_pairs={{8,0},{0,8},{24,16},{16,24},{9,1},{1,9},{25,17},{17,25},{10,2},{2,... | collective-permute-start | bytes 196616 | tf_op jit(solution)/shard_map/ppermute | solution.py:189
  13.2 4.3 %collective-permute-start.4 = (bf16[2,64,256]{2,1,0:T(8,128)(2,1)S(1)}, bf16[2,64,256]{2,1,0:T(8,128)(2,1)S(1)}, u32[]{:S(2)}, u32[]{:S(2)}) collective-permute-start(bf16[2,64,256]{2,1,0:T(8,128)(2,1)S(1)} %collective-permute-done.3.refs_4_), channel_id=1, source_target_pairs={{16,0},{24,8},{0,16},{8,24},{17,1},{25,9},{1,17},{9,25},{18,2},{26... | collective-permute-start | bytes 196616 | tf_op jit(solution)/shard_map/ppermute | solution.py:189
  13.5 4.0 %collective-permute-start.7 = (bf16[2,64,256]{2,1,0:T(8,128)(2,1)S(1)}, bf16[2,64,256]{2,1,0:T(8,128)(2,1)S(1)}, u32[]{:S(2)}, u32[]{:S(2)}) collective-permute-start(bf16[2,64,256]{2,1,0:T(8,128)(2,1)S(1)} %collective-permute-done.3.refs_4_), channel_id=1, source_target_pairs={{1,0},{0,1},{3,2},{2,3},{5,4},{4,5},{7,6},{6,7},{9,8},{8,9},{11,10... | collective-permute-start | bytes 196616 | tf_op jit(solution)/shard_map/ppermute | solution.py:193
  13.5 4.5 %collective-permute-start.2 = (bf16[2,64,256]{2,1,0:T(8,128)(2,1)S(1)}, bf16[2,64,256]{2,1,0:T(8,128)(2,1)S(1)}, u32[]{:S(2)}, u32[]{:S(2)}) collective-permute-start(bf16[2,64,256]{2,1,0:T(8,128)(2,1)S(1)} %collective-permute-done.1.refs_2_), channel_id=1, source_target_pairs={{2,0},{0,2},{6,4},{4,6},{3,1},{1,3},{7,5},{5,7},{10,8},{8,10},{14,... | collective-permute-start | bytes 196616 | tf_op jit(solution)/shard_map/ppermute | solution.py:86
  15.2 2.7 %collective-permute-start.10 = (bf16[2,64,256]{2,1,0:T(8,128)(2,1)S(1)}, bf16[2,64,256]{2,1,0:T(8,128)(2,1)S(1)}, u32[]{:S(2)}, u32[]{:S(2)}) collective-permute-start(bf16[2,64,256]{2,1,0:T(8,128)(2,1)S(1)} %collective-permute-done.6.refs_7_), channel_id=1, source_target_pairs={{1,0},{0,1},{3,2},{2,3},{5,4},{4,5},{7,6},{6,7},{9,8},{8,9},{11,10... | collective-permute-start | bytes 196616 | tf_op jit(solution)/shard_map/ppermute | solution.py:193
  16.2 1.8 %collective-permute-start.9 = (bf16[2,64,256]{2,1,0:T(8,128)(2,1)S(1)}, bf16[2,64,256]{2,1,0:T(8,128)(2,1)S(1)}, u32[]{:S(2)}, u32[]{:S(2)}) collective-permute-start(bf16[2,64,256]{2,1,0:T(8,128)(2,1)S(1)} %collective-permute-done.5.refs_6_), channel_id=1, source_target_pairs={{1,0},{0,1},{3,2},{2,3},{5,4},{4,5},{7,6},{6,7},{9,8},{8,9},{11,10... | collective-permute-start | bytes 196616 | tf_op jit(solution)/shard_map/ppermute | solution.py:193
  17.5 1.3 %collective-permute-start.8 = (bf16[2,64,256]{2,1,0:T(8,128)(2,1)S(1)}, bf16[2,64,256]{2,1,0:T(8,128)(2,1)S(1)}, u32[]{:S(2)}, u32[]{:S(2)}) collective-permute-start(bf16[2,64,256]{2,1,0:T(8,128)(2,1)S(1)} %collective-permute-done.4.refs_5_), channel_id=1, source_target_pairs={{1,0},{0,1},{3,2},{2,3},{5,4},{4,5},{7,6},{6,7},{9,8},{8,9},{11,10... | collective-permute-start | bytes 196616 | tf_op jit(solution)/shard_map/ppermute | solution.py:193

commit v15 on v14

--- a/solution.py
+++ b/solution.py
@@ -6,7 +6,7 @@
 from jax.sharding import PartitionSpec as P
 
 LANES = 128
-CHUNK_ROWS = 128
+CHUNK_ROWS = 256
 VMEM_BYTES = 24 * 1024 * 1024
 LOAD_VMEM_BYTES = 52000 * 1024
 FACTOR_VMEM_BYTES = 55040 * 1024
@@ -68,6 +68,10 @@
 
 
 def slab_of(slots, plane, place):
+    if len(slots) == 4:
+        packed = sum(row.index(p) << 2 * (4 * at + p) for at, row in enumerate(slots) for p in range(4))
+        packed -= (packed >> 31) << 32
+        return (jnp.int32(packed) >> (2 * (4 * plane + place))) & 3
     slab = jnp.int32(0)
     for at, row in enumerate(slots):
         for b, slot in enumerate(row):

time: 20.8 us -> 20.7 us (level)
  no operation moved by 1% of the time
where the time goes in v15:
time: 20.7 us; the launch traced here: 20.6 us
  starting transfers between devices  11.4 us (55%)
  Pallas kernels  4.86 us (23%)
  waiting for transfers between devices  4.31 us (21%)
    ppermute x1, starting transfers between devices, per_device(): lax.ppermute(factor, ('row', 'col'), [(a * count + b, slots[a][b] * count...  3.94 us
    ppermute x3, starting transfers between devices, per_device(): lax.ppermute(moved, 'row', [(partner(a, step, count), a) for a in range(c...  3.49 us
    ppermute x3, waiting for transfers between devices, per_device(): lax.ppermute(moved, 'row', [(partner(a, step, count), a) for a in range(c...  3.05 us
    ppermute x1, starting transfers between devices, gather_line(): far = lax.ppermute(late_factor, 'col', [(b ^ 2, b) for b in range(count)])  2.96 us
    pallas_call x1, Pallas kernels, update_trailing(): pl.pallas_call(body, out_shape=jax.ShapeDtypeStruct(share.shape, jnp.floa...  1.82 us
    pallas_call x1, Pallas kernels, load_share(): pl.pallas_call(load_kernel, out_shape=jax.ShapeDtypeStruct((rows, LANES),...  1.6 us
    pallas_call x1, Pallas kernels, make_factor(): pl.pallas_call(factor_kernel, out_shape=jax.ShapeDtypeStruct((half, tile_...  1.44 us
    ppermute x1, starting transfers between devices, gather_line(): both = lax.ppermute(far, 'col', [(b ^ 1, b) for b in range(count)])  0.95 us
  transfers between devices with their start and end apart: 11, of which 5 were waited for; matrix products, arithmetic and copies ran while one was open for 0% of the time, Pallas kernels for 8%

profile of v15, /device:TPU:0, one launch (start us, length us, event | category | flops | bytes accessed | tf_op | source)
XLA Modules:
  0.0 20.6 jit_solution(9526431625828047535)
XLA Ops:
  0.0 1.4 %factor.1.after_ref.refs_0_ = bf16[2,64,256]{2,1,0:T(8,128)(2,1)S(1)} custom-call(f32[4,1,64,256]{3,2,1,0:T(8,128)} %panel_ref.1, f32[256,256]{1,0:T(8,128)} %inverse_ref.1), custom_call_target="tpu_custom_call" | custom-call | tf_op jit(solution)/shard_map/factor/pallas_call | solution.py:41
  1.4 3.9 %collective-permute-start.3 = (bf16[2,64,256]{2,1,0:T(8,128)(2,1)S(1)}, bf16[2,64,256]{2,1,0:T(8,128)(2,1)S(1)}, u32[]{:S(2)}, u32[]{:S(2)}) collective-permute-start(bf16[2,64,256]{2,1,0:T(8,128)(2,1)S(1)} %factor.1.after_ref.refs_0_), channel_id=1, source_target_pairs={{0,24},{2,0},{4,8},{6,16},{8,26},{10,18},{12,10},{14,2},{16,4},{18... | collective-permute-start | bytes 196616 | tf_op jit(solution)/shard_map/ppermute | solution.py:185
  5.4 0.0 collective-permute-start
  5.4 1.6 %load_share.1.refs_12_ = f32[4096,128]{1,0:T(8,128)S(1)} custom-call(bf16[2,64,256]{2,1,0:T(8,128)(2,1)S(1)} %factor.1.after_ref.refs_0_, f32[8192,128]{1,0:T(8,128)} %bitcast.2), custom_call_target="tpu_custom_call" | custom-call | bytes 4194304 | tf_op jit(solution)/shard_map/load_share/pallas_call | solution.py:104
  7.0 3.0 %collective-permute-start.1 = (bf16[2,64,256]{2,1,0:T(8,128)(2,1)S(1)}, bf16[2,64,256]{2,1,0:T(8,128)(2,1)S(1)}, u32[]{:S(2)}, u32[]{:S(2)}) collective-permute-start(bf16[2,64,256]{2,1,0:T(8,128)(2,1)S(1)} %factor.1.after_ref.refs_0_), channel_id=1, source_target_pairs={{4,0},{6,2},{0,4},{2,6},{5,1},{7,3},{1,5},{3,7},{12,8},{14,10},{8,... | collective-permute-start | bytes 196616 | tf_op jit(solution)/shard_map/ppermute | solution.py:89
  10.0 0.0 collective-permute-done.3.refs_4_
  10.0 1.7 %collective-permute-start.6 = (bf16[2,64,256]{2,1,0:T(8,128)(2,1)S(1)}, bf16[2,64,256]{2,1,0:T(8,128)(2,1)S(1)}, u32[]{:S(2)}, u32[]{:S(2)}) collective-permute-start(bf16[2,64,256]{2,1,0:T(8,128)(2,1)S(1)} %collective-permute-done.3.refs_4_), channel_id=1, source_target_pairs={{24,0},{16,8},{8,16},{0,24},{25,1},{17,9},{9,17},{1,25},{26,2},{18... | collective-permute-start | bytes 196616 | tf_op jit(solution)/shard_map/ppermute | solution.py:193
  11.7 1.5 %collective-permute-start.5 = (bf16[2,64,256]{2,1,0:T(8,128)(2,1)S(1)}, bf16[2,64,256]{2,1,0:T(8,128)(2,1)S(1)}, u32[]{:S(2)}, u32[]{:S(2)}) collective-permute-start(bf16[2,64,256]{2,1,0:T(8,128)(2,1)S(1)} %collective-permute-done.3.refs_4_), channel_id=1, source_target_pairs={{8,0},{0,8},{24,16},{16,24},{9,1},{1,9},{25,17},{17,25},{10,2},{2,... | collective-permute-start | bytes 196616 | tf_op jit(solution)/shard_map/ppermute | solution.py:193
  13.2 0.2 %collective-permute-start.4 = (bf16[2,64,256]{2,1,0:T(8,128)(2,1)S(1)}, bf16[2,64,256]{2,1,0:T(8,128)(2,1)S(1)}, u32[]{:S(2)}, u32[]{:S(2)}) collective-permute-start(bf16[2,64,256]{2,1,0:T(8,128)(2,1)S(1)} %collective-permute-done.3.refs_4_), channel_id=1, source_target_pairs={{16,0},{24,8},{0,16},{8,24},{17,1},{25,9},{1,17},{9,25},{18,2},{26... | collective-permute-start | bytes 196616 | tf_op jit(solution)/shard_map/ppermute | solution.py:193
  13.5 0.0 collective-permute-done.refs_1_
  13.5 0.0 collective-permute-start.7
  13.5 0.0 collective-permute-done.1.refs_2_
  13.5 1.0 %collective-permute-start.2 = (bf16[2,64,256]{2,1,0:T(8,128)(2,1)S(1)}, bf16[2,64,256]{2,1,0:T(8,128)(2,1)S(1)}, u32[]{:S(2)}, u32[]{:S(2)}) collective-permute-start(bf16[2,64,256]{2,1,0:T(8,128)(2,1)S(1)} %collective-permute-done.1.refs_2_), channel_id=1, source_target_pairs={{2,0},{0,2},{6,4},{4,6},{3,1},{1,3},{7,5},{5,7},{10,8},{8,10},{14,... | collective-permute-start | bytes 196616 | tf_op jit(solution)/shard_map/ppermute | solution.py:90
  14.4 0.8 %collective-permute-done.6.refs_7_ = bf16[2,64,256]{2,1,0:T(8,128)(2,1)S(1)} collective-permute-done((bf16[2,64,256]{2,1,0:T(8,128)(2,1)S(1)}, bf16[2,64,256]{2,1,0:T(8,128)(2,1)S(1)}, u32[]{:S(2)}, u32[]{:S(2)}) %collective-permute-start.6) | collective-permute-done | bytes 65568 | tf_op jit(solution)/shard_map/ppermute | solution.py:193
  15.2 0.0 collective-permute-start.10
  15.2 0.9 %collective-permute-done.5.refs_6_ = bf16[2,64,256]{2,1,0:T(8,128)(2,1)S(1)} collective-permute-done((bf16[2,64,256]{2,1,0:T(8,128)(2,1)S(1)}, bf16[2,64,256]{2,1,0:T(8,128)(2,1)S(1)}, u32[]{:S(2)}, u32[]{:S(2)}) %collective-permute-start.5) | collective-permute-done | bytes 65568 | tf_op jit(solution)/shard_map/ppermute | solution.py:193
  16.2 0.0 collective-permute-start.9
  16.2 1.3 %collective-permute-done.4.refs_5_ = bf16[2,64,256]{2,1,0:T(8,128)(2,1)S(1)} collective-permute-done((bf16[2,64,256]{2,1,0:T(8,128)(2,1)S(1)}, bf16[2,64,256]{2,1,0:T(8,128)(2,1)S(1)}, u32[]{:S(2)}, u32[]{:S(2)}) %collective-permute-start.4) | collective-permute-done | bytes 65568 | tf_op jit(solution)/shard_map/ppermute | solution.py:193
  17.5 0.0 collective-permute-start.8
  17.5 0.0 collective-permute-done.7.refs_8_
  17.5 0.5 %collective-permute-done.2.refs_3_ = bf16[2,64,256]{2,1,0:T(8,128)(2,1)S(1)} collective-permute-done((bf16[2,64,256]{2,1,0:T(8,128)(2,1)S(1)}, bf16[2,64,256]{2,1,0:T(8,128)(2,1)S(1)}, u32[]{:S(2)}, u32[]{:S(2)}) %collective-permute-start.2) | collective-permute-done | bytes 65568 | tf_op jit(solution)/shard_map/ppermute | solution.py:90
  18.0 0.0 collective-permute-done.10.refs_11_
  18.0 0.0 collective-permute-done.9.refs_10_
  18.0 0.8 %collective-permute-done.8.refs_9_ = bf16[2,64,256]{2,1,0:T(8,128)(2,1)S(1)} collective-permute-done((bf16[2,64,256]{2,1,0:T(8,128)(2,1)S(1)}, bf16[2,64,256]{2,1,0:T(8,128)(2,1)S(1)}, u32[]{:S(2)}, u32[]{:S(2)}) %collective-permute-start.8) | collective-permute-done | bytes 65568 | tf_op jit(solution)/shard_map/ppermute | solution.py:197
  18.7 1.8 %update.1 = f32[4096,128]{1,0:T(8,128)} custom-call(bf16[2,64,256]{2,1,0:T(8,128)(2,1)S(1)} %factor.1.after_ref.refs_0_, bf16[2,64,256]{2,1,0:T(8,128)(2,1)S(1)} %collective-permute-done.refs_1_, bf16[2,64,256]{2,1,0:T(8,128)(2,1)S(1)} %collective-permute-done.1.refs_2_, bf16[2,64,256]{2,1,0:T(8,128)(2,1)S(1)} %collective-permute-done.2.refs_3_, ...), custom_call_target="tpu_custom_call" | custom-call | tf_op jit(solution)/shard_map/update/pallas_call | solution.py:161
Async XLA Ops:
  1.4 8.5 %collective-permute-start.3 = (bf16[2,64,256]{2,1,0:T(8,128)(2,1)S(1)}, bf16[2,64,256]{2,1,0:T(8,128)(2,1)S(1)}, u32[]{:S(2)}, u32[]{:S(2)}) collective-permute-start(bf16[2,64,256]{2,1,0:T(8,128)(2,1)S(1)} %factor.1.after_ref.refs_0_), channel_id=1, source_target_pairs={{0,24},{2,0},{4,8},{6,16},{8,26},{10,18},{12,10},{14,2},{16,4},{18... | collective-permute-start | bytes 196616 | tf_op jit(solution)/shard_map/ppermute | solution.py:185
  5.4 8.1 %collective-permute-start = (bf16[2,64,256]{2,1,0:T(8,128)(2,1)S(1)}, bf16[2,64,256]{2,1,0:T(8,128)(2,1)S(1)}, u32[]{:S(2)}, u32[]{:S(2)}) collective-permute-start(bf16[2,64,256]{2,1,0:T(8,128)(2,1)S(1)} %factor.1.after_ref.refs_0_), channel_id=1, source_target_pairs={{2,0},{0,2},{6,4},{4,6},{3,1},{1,3},{7,5},{5,7},{10,8},{8,10},{14,... | collective-permute-start | bytes 196616 | tf_op jit(solution)/shard_map/ppermute | solution.py:88
  7.0 6.5 %collective-permute-start.1 = (bf16[2,64,256]{2,1,0:T(8,128)(2,1)S(1)}, bf16[2,64,256]{2,1,0:T(8,128)(2,1)S(1)}, u32[]{:S(2)}, u32[]{:S(2)}) collective-permute-start(bf16[2,64,256]{2,1,0:T(8,128)(2,1)S(1)} %factor.1.after_ref.refs_0_), channel_id=1, source_target_pairs={{4,0},{6,2},{0,4},{2,6},{5,1},{7,3},{1,5},{3,7},{12,8},{14,10},{8,... | collective-permute-start | bytes 196616 | tf_op jit(solution)/shard_map/ppermute | solution.py:89
  10.0 5.3 %collective-permute-start.6 = (bf16[2,64,256]{2,1,0:T(8,128)(2,1)S(1)}, bf16[2,64,256]{2,1,0:T(8,128)(2,1)S(1)}, u32[]{:S(2)}, u32[]{:S(2)}) collective-permute-start(bf16[2,64,256]{2,1,0:T(8,128)(2,1)S(1)} %collective-permute-done.3.refs_4_), channel_id=1, source_target_pairs={{24,0},{16,8},{8,16},{0,24},{25,1},{17,9},{9,17},{1,25},{26,2},{18... | collective-permute-start | bytes 196616 | tf_op jit(solution)/shard_map/ppermute | solution.py:193
  11.7 4.4 %collective-permute-start.5 = (bf16[2,64,256]{2,1,0:T(8,128)(2,1)S(1)}, bf16[2,64,256]{2,1,0:T(8,128)(2,1)S(1)}, u32[]{:S(2)}, u32[]{:S(2)}) collective-permute-start(bf16[2,64,256]{2,1,0:T(8,128)(2,1)S(1)} %collective-permute-done.3.refs_4_), channel_id=1, source_target_pairs={{8,0},{0,8},{24,16},{16,24},{9,1},{1,9},{25,17},{17,25},{10,2},{2,... | collective-permute-start | bytes 196616 | tf_op jit(solution)/shard_map/ppermute | solution.py:193
  13.2 4.3 %collective-permute-start.4 = (bf16[2,64,256]{2,1,0:T(8,128)(2,1)S(1)}, bf16[2,64,256]{2,1,0:T(8,128)(2,1)S(1)}, u32[]{:S(2)}, u32[]{:S(2)}) collective-permute-start(bf16[2,64,256]{2,1,0:T(8,128)(2,1)S(1)} %collective-permute-done.3.refs_4_), channel_id=1, source_target_pairs={{16,0},{24,8},{0,16},{8,24},{17,1},{25,9},{1,17},{9,25},{18,2},{26... | collective-permute-start | bytes 196616 | tf_op jit(solution)/shard_map/ppermute | solution.py:193
  13.5 4.0 %collective-permute-start.7 = (bf16[2,64,256]{2,1,0:T(8,128)(2,1)S(1)}, bf16[2,64,256]{2,1,0:T(8,128)(2,1)S(1)}, u32[]{:S(2)}, u32[]{:S(2)}) collective-permute-start(bf16[2,64,256]{2,1,0:T(8,128)(2,1)S(1)} %collective-permute-done.3.refs_4_), channel_id=1, source_target_pairs={{1,0},{0,1},{3,2},{2,3},{5,4},{4,5},{7,6},{6,7},{9,8},{8,9},{11,10... | collective-permute-start | bytes 196616 | tf_op jit(solution)/shard_map/ppermute | solution.py:197
  13.5 4.5 %collective-permute-start.2 = (bf16[2,64,256]{2,1,0:T(8,128)(2,1)S(1)}, bf16[2,64,256]{2,1,0:T(8,128)(2,1)S(1)}, u32[]{:S(2)}, u32[]{:S(2)}) collective-permute-start(bf16[2,64,256]{2,1,0:T(8,128)(2,1)S(1)} %collective-permute-done.1.refs_2_), channel_id=1, source_target_pairs={{2,0},{0,2},{6,4},{4,6},{3,1},{1,3},{7,5},{5,7},{10,8},{8,10},{14,... | collective-permute-start | bytes 196616 | tf_op jit(solution)/shard_map/ppermute | solution.py:90
  15.2 2.7 %collective-permute-start.10 = (bf16[2,64,256]{2,1,0:T(8,128)(2,1)S(1)}, bf16[2,64,256]{2,1,0:T(8,128)(2,1)S(1)}, u32[]{:S(2)}, u32[]{:S(2)}) collective-permute-start(bf16[2,64,256]{2,1,0:T(8,128)(2,1)S(1)} %collective-permute-done.6.refs_7_), channel_id=1, source_target_pairs={{1,0},{0,1},{3,2},{2,3},{5,4},{4,5},{7,6},{6,7},{9,8},{8,9},{11,10... | collective-permute-start | bytes 196616 | tf_op jit(solution)/shard_map/ppermute | solution.py:197
  16.2 1.8 %collective-permute-start.9 = (bf16[2,64,256]{2,1,0:T(8,128)(2,1)S(1)}, bf16[2,64,256]{2,1,0:T(8,128)(2,1)S(1)}, u32[]{:S(2)}, u32[]{:S(2)}) collective-permute-start(bf16[2,64,256]{2,1,0:T(8,128)(2,1)S(1)} %collective-permute-done.5.refs_6_), channel_id=1, source_target_pairs={{1,0},{0,1},{3,2},{2,3},{5,4},{4,5},{7,6},{6,7},{9,8},{8,9},{11,10... | collective-permute-start | bytes 196616 | tf_op jit(solution)/shard_map/ppermute | solution.py:197
  17.5 1.3 %collective-permute-start.8 = (bf16[2,64,256]{2,1,0:T(8,128)(2,1)S(1)}, bf16[2,64,256]{2,1,0:T(8,128)(2,1)S(1)}, u32[]{:S(2)}, u32[]{:S(2)}) collective-permute-start(bf16[2,64,256]{2,1,0:T(8,128)(2,1)S(1)} %collective-permute-done.4.refs_5_), channel_id=1, source_target_pairs={{1,0},{0,1},{3,2},{2,3},{5,4},{4,5},{7,6},{6,7},{9,8},{8,9},{11,10... | collective-permute-start | bytes 196616 | tf_op jit(solution)/shard_map/ppermute | solution.py:197

commit v16 on v15

--- a/solution.py
+++ b/solution.py
@@ -85,7 +85,10 @@
         for step in range(1, count):
             line.append(lax.ppermute(factor, "col", [(partner(b, step, count), b) for b in range(count)]))
         return line
-    near = lax.ppermute(factor, "col", [(b ^ 1, b) for b in range(count)])
+    sources = {(r, c): (r ^ 1, c) if r == c else (r, c ^ 1) for r in range(count) for c in range(count)}
+    near = lax.ppermute(
+        factor, ("row", "col"), [(a * count + b, r * count + c) for (r, c), (a, b) in sources.items()]
+    )
     far = lax.ppermute(late_factor, "col", [(b ^ 2, b) for b in range(count)])
     both = lax.ppermute(far, "col", [(b ^ 1, b) for b in range(count)])
     return [factor, near, far, both]
@@ -130,6 +133,12 @@
             owner = lax.rem(layer + shift, layers)
             for k in range(half):
                 col_buf[owner * half + k, pl.ds(col_at, tile_rows), :] = col_refs[shift * pieces + step][k]
+    if pieces == 4:
+
+        @pl.when(r == c)
+        def _():
+            row_buf[...] = col_buf[pl.ds(layer * half, half)]
+
     chunks = half * (tile // CHUNK_ROWS)
     chunk_lines = CHUNK_ROWS * per_row
     stores = []

time: 20.7 us -> 20.7 us (level)
  no operation moved by 1% of the time
where the time goes in v16:
time: 20.7 us; the launch traced here: 20.5 us
  starting transfers between devices  11.4 us (55%)
  Pallas kernels  4.88 us (24%)
  waiting for transfers between devices  4.26 us (21%)
    ppermute x1, starting transfers between devices, per_device(): lax.ppermute(factor, ('row', 'col'), [(a * count + b, slots[a][b] * count...  3.94 us
    ppermute x3, starting transfers between devices, per_device(): lax.ppermute(moved, 'row', [(partner(a, step, count), a) for a in range(c...  3.49 us
    ppermute x3, waiting for transfers between devices, per_device(): lax.ppermute(moved, 'row', [(partner(a, step, count), a) for a in range(c...  3 us
    ppermute x1, starting transfers between devices, gather_line(): far = lax.ppermute(late_factor, 'col', [(b ^ 2, b) for b in range(count)])  2.96 us
    pallas_call x1, Pallas kernels, update_trailing(): pl.pallas_call(body, out_shape=jax.ShapeDtypeStruct(share.shape, jnp.floa...  1.85 us
    pallas_call x1, Pallas kernels, load_share(): pl.pallas_call(load_kernel, out_shape=jax.ShapeDtypeStruct((rows, LANES),...  1.6 us
    pallas_call x1, Pallas kernels, make_factor(): pl.pallas_call(factor_kernel, out_shape=jax.ShapeDtypeStruct((half, tile_...  1.44 us
    ppermute x1, starting transfers between devices, gather_line(): both = lax.ppermute(far, 'col', [(b ^ 1, b) for b in range(count)])  0.95 us
  transfers between devices with their start and end apart: 11, of which 5 were waited for; matrix products, arithmetic and copies ran while one was open for 0% of the time, Pallas kernels for 8%

profile of v16, /device:TPU:0, one launch (start us, length us, event | category | flops | bytes accessed | tf_op | source)
XLA Modules:
  0.0 20.5 jit_solution(661866814158440159)
XLA Ops:
  0.0 1.4 %factor.1.after_ref.refs_0_ = bf16[2,64,256]{2,1,0:T(8,128)(2,1)S(1)} custom-call(f32[4,1,64,256]{3,2,1,0:T(8,128)} %panel_ref.1, f32[256,256]{1,0:T(8,128)} %inverse_ref.1), custom_call_target="tpu_custom_call" | custom-call | tf_op jit(solution)/shard_map/factor/pallas_call | solution.py:41
  1.4 3.9 %collective-permute-start.3 = (bf16[2,64,256]{2,1,0:T(8,128)(2,1)S(1)}, bf16[2,64,256]{2,1,0:T(8,128)(2,1)S(1)}, u32[]{:S(2)}, u32[]{:S(2)}) collective-permute-start(bf16[2,64,256]{2,1,0:T(8,128)(2,1)S(1)} %factor.1.after_ref.refs_0_), channel_id=1, source_target_pairs={{0,24},{2,0},{4,8},{6,16},{8,26},{10,18},{12,10},{14,2},{16,4},{18... | collective-permute-start | bytes 196616 | tf_op jit(solution)/shard_map/ppermute | solution.py:194
  5.4 0.0 collective-permute-start
  5.4 1.6 %load_share.1.refs_12_ = f32[4096,128]{1,0:T(8,128)S(1)} custom-call(bf16[2,64,256]{2,1,0:T(8,128)(2,1)S(1)} %factor.1.after_ref.refs_0_, f32[8192,128]{1,0:T(8,128)} %bitcast.2), custom_call_target="tpu_custom_call" | custom-call | bytes 4194304 | tf_op jit(solution)/shard_map/load_share/pallas_call | solution.py:107
  7.0 3.0 %collective-permute-start.1 = (bf16[2,64,256]{2,1,0:T(8,128)(2,1)S(1)}, bf16[2,64,256]{2,1,0:T(8,128)(2,1)S(1)}, u32[]{:S(2)}, u32[]{:S(2)}) collective-permute-start(bf16[2,64,256]{2,1,0:T(8,128)(2,1)S(1)} %factor.1.after_ref.refs_0_), channel_id=1, source_target_pairs={{4,0},{6,2},{0,4},{2,6},{5,1},{7,3},{1,5},{3,7},{12,8},{14,10},{8,... | collective-permute-start | bytes 196616 | tf_op jit(solution)/shard_map/ppermute | solution.py:92
  10.0 0.0 collective-permute-done.3.refs_4_
  10.0 1.7 %collective-permute-start.6 = (bf16[2,64,256]{2,1,0:T(8,128)(2,1)S(1)}, bf16[2,64,256]{2,1,0:T(8,128)(2,1)S(1)}, u32[]{:S(2)}, u32[]{:S(2)}) collective-permute-start(bf16[2,64,256]{2,1,0:T(8,128)(2,1)S(1)} %collective-permute-done.3.refs_4_), channel_id=1, source_target_pairs={{24,0},{16,8},{8,16},{0,24},{25,1},{17,9},{9,17},{1,25},{26,2},{18... | collective-permute-start | bytes 196616 | tf_op jit(solution)/shard_map/ppermute | solution.py:202
  11.6 1.5 %collective-permute-start.5 = (bf16[2,64,256]{2,1,0:T(8,128)(2,1)S(1)}, bf16[2,64,256]{2,1,0:T(8,128)(2,1)S(1)}, u32[]{:S(2)}, u32[]{:S(2)}) collective-permute-start(bf16[2,64,256]{2,1,0:T(8,128)(2,1)S(1)} %collective-permute-done.3.refs_4_), channel_id=1, source_target_pairs={{8,0},{0,8},{24,16},{16,24},{9,1},{1,9},{25,17},{17,25},{10,2},{2,... | collective-permute-start | bytes 196616 | tf_op jit(solution)/shard_map/ppermute | solution.py:202
  13.2 0.3 %collective-permute-start.4 = (bf16[2,64,256]{2,1,0:T(8,128)(2,1)S(1)}, bf16[2,64,256]{2,1,0:T(8,128)(2,1)S(1)}, u32[]{:S(2)}, u32[]{:S(2)}) collective-permute-start(bf16[2,64,256]{2,1,0:T(8,128)(2,1)S(1)} %collective-permute-done.3.refs_4_), channel_id=1, source_target_pairs={{16,0},{24,8},{0,16},{8,24},{17,1},{25,9},{1,17},{9,25},{18,2},{26... | collective-permute-start | bytes 196616 | tf_op jit(solution)/shard_map/ppermute | solution.py:202
  13.5 0.0 collective-permute-done.refs_1_
  13.5 0.0 collective-permute-start.7
  13.5 0.0 collective-permute-done.1.refs_2_
  13.5 1.0 %collective-permute-start.2 = (bf16[2,64,256]{2,1,0:T(8,128)(2,1)S(1)}, bf16[2,64,256]{2,1,0:T(8,128)(2,1)S(1)}, u32[]{:S(2)}, u32[]{:S(2)}) collective-permute-start(bf16[2,64,256]{2,1,0:T(8,128)(2,1)S(1)} %collective-permute-done.1.refs_2_), channel_id=1, source_target_pairs={{2,0},{0,2},{6,4},{4,6},{3,1},{1,3},{7,5},{5,7},{10,8},{8,10},{14,... | collective-permute-start | bytes 196616 | tf_op jit(solution)/shard_map/ppermute | solution.py:93
  14.4 0.8 %collective-permute-done.6.refs_7_ = bf16[2,64,256]{2,1,0:T(8,128)(2,1)S(1)} collective-permute-done((bf16[2,64,256]{2,1,0:T(8,128)(2,1)S(1)}, bf16[2,64,256]{2,1,0:T(8,128)(2,1)S(1)}, u32[]{:S(2)}, u32[]{:S(2)}) %collective-permute-start.6) | collective-permute-done | bytes 65568 | tf_op jit(solution)/shard_map/ppermute | solution.py:202
  15.2 0.0 collective-permute-start.10
  15.2 0.9 %collective-permute-done.5.refs_6_ = bf16[2,64,256]{2,1,0:T(8,128)(2,1)S(1)} collective-permute-done((bf16[2,64,256]{2,1,0:T(8,128)(2,1)S(1)}, bf16[2,64,256]{2,1,0:T(8,128)(2,1)S(1)}, u32[]{:S(2)}, u32[]{:S(2)}) %collective-permute-start.5) | collective-permute-done | bytes 65568 | tf_op jit(solution)/shard_map/ppermute | solution.py:202
  16.1 0.0 collective-permute-start.9
  16.1 1.3 %collective-permute-done.4.refs_5_ = bf16[2,64,256]{2,1,0:T(8,128)(2,1)S(1)} collective-permute-done((bf16[2,64,256]{2,1,0:T(8,128)(2,1)S(1)}, bf16[2,64,256]{2,1,0:T(8,128)(2,1)S(1)}, u32[]{:S(2)}, u32[]{:S(2)}) %collective-permute-start.4) | collective-permute-done | bytes 65568 | tf_op jit(solution)/shard_map/ppermute | solution.py:202
  17.4 0.0 collective-permute-start.8
  17.4 0.0 collective-permute-done.7.refs_8_
  17.4 0.5 %collective-permute-done.2.refs_3_ = bf16[2,64,256]{2,1,0:T(8,128)(2,1)S(1)} collective-permute-done((bf16[2,64,256]{2,1,0:T(8,128)(2,1)S(1)}, bf16[2,64,256]{2,1,0:T(8,128)(2,1)S(1)}, u32[]{:S(2)}, u32[]{:S(2)}) %collective-permute-start.2) | collective-permute-done | bytes 65568 | tf_op jit(solution)/shard_map/ppermute | solution.py:93
  18.0 0.0 collective-permute-done.10.refs_11_
  18.0 0.0 collective-permute-done.9.refs_10_
  18.0 0.7 %collective-permute-done.8.refs_9_ = bf16[2,64,256]{2,1,0:T(8,128)(2,1)S(1)} collective-permute-done((bf16[2,64,256]{2,1,0:T(8,128)(2,1)S(1)}, bf16[2,64,256]{2,1,0:T(8,128)(2,1)S(1)}, u32[]{:S(2)}, u32[]{:S(2)}) %collective-permute-start.8) | collective-permute-done | bytes 65568 | tf_op jit(solution)/shard_map/ppermute | solution.py:206
  18.7 1.8 %update.1 = f32[4096,128]{1,0:T(8,128)} custom-call(bf16[2,64,256]{2,1,0:T(8,128)(2,1)S(1)} %factor.1.after_ref.refs_0_, bf16[2,64,256]{2,1,0:T(8,128)(2,1)S(1)} %collective-permute-done.refs_1_, bf16[2,64,256]{2,1,0:T(8,128)(2,1)S(1)} %collective-permute-done.1.refs_2_, bf16[2,64,256]{2,1,0:T(8,128)(2,1)S(1)} %collective-permute-done.2.refs_3_, ...), custom_call_target="tpu_custom_call" | custom-call | tf_op jit(solution)/shard_map/update/pallas_call | solution.py:170
Async XLA Ops:
  1.4 8.5 %collective-permute-start.3 = (bf16[2,64,256]{2,1,0:T(8,128)(2,1)S(1)}, bf16[2,64,256]{2,1,0:T(8,128)(2,1)S(1)}, u32[]{:S(2)}, u32[]{:S(2)}) collective-permute-start(bf16[2,64,256]{2,1,0:T(8,128)(2,1)S(1)} %factor.1.after_ref.refs_0_), channel_id=1, source_target_pairs={{0,24},{2,0},{4,8},{6,16},{8,26},{10,18},{12,10},{14,2},{16,4},{18... | collective-permute-start | bytes 196616 | tf_op jit(solution)/shard_map/ppermute | solution.py:194
  5.4 8.1 %collective-permute-start = (bf16[2,64,256]{2,1,0:T(8,128)(2,1)S(1)}, bf16[2,64,256]{2,1,0:T(8,128)(2,1)S(1)}, u32[]{:S(2)}, u32[]{:S(2)}) collective-permute-start(bf16[2,64,256]{2,1,0:T(8,128)(2,1)S(1)} %factor.1.after_ref.refs_0_), channel_id=1, source_target_pairs={{8,0},{0,2},{6,4},{4,6},{10,8},{2,10},{14,12},{12,14},{18,16},{16,... | collective-permute-start | bytes 196616 | tf_op jit(solution)/shard_map/ppermute | solution.py:89
  7.0 6.5 %collective-permute-start.1 = (bf16[2,64,256]{2,1,0:T(8,128)(2,1)S(1)}, bf16[2,64,256]{2,1,0:T(8,128)(2,1)S(1)}, u32[]{:S(2)}, u32[]{:S(2)}) collective-permute-start(bf16[2,64,256]{2,1,0:T(8,128)(2,1)S(1)} %factor.1.after_ref.refs_0_), channel_id=1, source_target_pairs={{4,0},{6,2},{0,4},{2,6},{5,1},{7,3},{1,5},{3,7},{12,8},{14,10},{8,... | collective-permute-start | bytes 196616 | tf_op jit(solution)/shard_map/ppermute | solution.py:92
  10.0 5.3 %collective-permute-start.6 = (bf16[2,64,256]{2,1,0:T(8,128)(2,1)S(1)}, bf16[2,64,256]{2,1,0:T(8,128)(2,1)S(1)}, u32[]{:S(2)}, u32[]{:S(2)}) collective-permute-start(bf16[2,64,256]{2,1,0:T(8,128)(2,1)S(1)} %collective-permute-done.3.refs_4_), channel_id=1, source_target_pairs={{24,0},{16,8},{8,16},{0,24},{25,1},{17,9},{9,17},{1,25},{26,2},{18... | collective-permute-start | bytes 196616 | tf_op jit(solution)/shard_map/ppermute | solution.py:202
  11.6 4.5 %collective-permute-start.5 = (bf16[2,64,256]{2,1,0:T(8,128)(2,1)S(1)}, bf16[2,64,256]{2,1,0:T(8,128)(2,1)S(1)}, u32[]{:S(2)}, u32[]{:S(2)}) collective-permute-start(bf16[2,64,256]{2,1,0:T(8,128)(2,1)S(1)} %collective-permute-done.3.refs_4_), channel_id=1, source_target_pairs={{8,0},{0,8},{24,16},{16,24},{9,1},{1,9},{25,17},{17,25},{10,2},{2,... | collective-permute-start | bytes 196616 | tf_op jit(solution)/shard_map/ppermute | solution.py:202
  13.2 4.3 %collective-permute-start.4 = (bf16[2,64,256]{2,1,0:T(8,128)(2,1)S(1)}, bf16[2,64,256]{2,1,0:T(8,128)(2,1)S(1)}, u32[]{:S(2)}, u32[]{:S(2)}) collective-permute-start(bf16[2,64,256]{2,1,0:T(8,128)(2,1)S(1)} %collective-permute-done.3.refs_4_), channel_id=1, source_target_pairs={{16,0},{24,8},{0,16},{8,24},{17,1},{25,9},{1,17},{9,25},{18,2},{26... | collective-permute-start | bytes 196616 | tf_op jit(solution)/shard_map/ppermute | solution.py:202
  13.5 4.0 %collective-permute-start.7 = (bf16[2,64,256]{2,1,0:T(8,128)(2,1)S(1)}, bf16[2,64,256]{2,1,0:T(8,128)(2,1)S(1)}, u32[]{:S(2)}, u32[]{:S(2)}) collective-permute-start(bf16[2,64,256]{2,1,0:T(8,128)(2,1)S(1)} %collective-permute-done.3.refs_4_), channel_id=1, source_target_pairs={{1,0},{0,1},{3,2},{2,3},{5,4},{4,5},{7,6},{6,7},{9,8},{8,9},{11,10... | collective-permute-start | bytes 196616 | tf_op jit(solution)/shard_map/ppermute | solution.py:206
  13.5 4.5 %collective-permute-start.2 = (bf16[2,64,256]{2,1,0:T(8,128)(2,1)S(1)}, bf16[2,64,256]{2,1,0:T(8,128)(2,1)S(1)}, u32[]{:S(2)}, u32[]{:S(2)}) collective-permute-start(bf16[2,64,256]{2,1,0:T(8,128)(2,1)S(1)} %collective-permute-done.1.refs_2_), channel_id=1, source_target_pairs={{2,0},{0,2},{6,4},{4,6},{3,1},{1,3},{7,5},{5,7},{10,8},{8,10},{14,... | collective-permute-start | bytes 196616 | tf_op jit(solution)/shard_map/ppermute | solution.py:93
  15.2 2.7 %collective-permute-start.10 = (bf16[2,64,256]{2,1,0:T(8,128)(2,1)S(1)}, bf16[2,64,256]{2,1,0:T(8,128)(2,1)S(1)}, u32[]{:S(2)}, u32[]{:S(2)}) collective-permute-start(bf16[2,64,256]{2,1,0:T(8,128)(2,1)S(1)} %collective-permute-done.6.refs_7_), channel_id=1, source_target_pairs={{1,0},{0,1},{3,2},{2,3},{5,4},{4,5},{7,6},{6,7},{9,8},{8,9},{11,10... | collective-permute-start | bytes 196616 | tf_op jit(solution)/shard_map/ppermute | solution.py:206
  16.1 1.9 %collective-permute-start.9 = (bf16[2,64,256]{2,1,0:T(8,128)(2,1)S(1)}, bf16[2,64,256]{2,1,0:T(8,128)(2,1)S(1)}, u32[]{:S(2)}, u32[]{:S(2)}) collective-permute-start(bf16[2,64,256]{2,1,0:T(8,128)(2,1)S(1)} %collective-permute-done.5.refs_6_), channel_id=1, source_target_pairs={{1,0},{0,1},{3,2},{2,3},{5,4},{4,5},{7,6},{6,7},{9,8},{8,9},{11,10... | collective-permute-start | bytes 196616 | tf_op jit(solution)/shard_map/ppermute | solution.py:206
  17.4 1.3 %collective-permute-start.8 = (bf16[2,64,256]{2,1,0:T(8,128)(2,1)S(1)}, bf16[2,64,256]{2,1,0:T(8,128)(2,1)S(1)}, u32[]{:S(2)}, u32[]{:S(2)}) collective-permute-start(bf16[2,64,256]{2,1,0:T(8,128)(2,1)S(1)} %collective-permute-done.4.refs_5_), channel_id=1, source_target_pairs={{1,0},{0,1},{3,2},{2,3},{5,4},{4,5},{7,6},{6,7},{9,8},{8,9},{11,10... | collective-permute-start | bytes 196616 | tf_op jit(solution)/shard_map/ppermute | solution.py:206

commit v17 on v16

--- a/solution.py
+++ b/solution.py
@@ -11,6 +11,14 @@
 LOAD_VMEM_BYTES = 52000 * 1024
 FACTOR_VMEM_BYTES = 55040 * 1024
 AXES = ("row", "col", "layer")
+
+
+def split(x):
+    parts = []
+    for _ in range(3):
+        parts.append(x.astype(jnp.bfloat16))
+        x = x - parts[-1].astype(jnp.float32)
+    return parts
 
 
 def factor_kernel(panel_ref, inverse_ref, factor_ref, panel_buf, inverse_buf, sems):
@@ -26,13 +34,20 @@
         copy.start()
     for copy in copies:
         copy.wait()
-    product = lax.dot_general(
-        panel_buf[...].reshape(half * tile_rows, width),
-        inverse_buf[...],
-        (((1,), (1,)), ((), ())),
-        precision=lax.Precision.HIGHEST,
-        preferred_element_type=jnp.float32,
-    )
+    rows = half * tile_rows
+    panel = split(panel_buf[...].reshape(rows, width))
+    inverse = split(inverse_buf[...])
+
+    def times(parts, part):
+        return lax.dot_general(
+            jnp.concatenate(parts, axis=0), part, (((1,), (1,)), ((), ())), preferred_element_type=jnp.float32
+        )
+
+    high = times(panel, inverse[0])
+    middle = times(panel[:2], inverse[1])
+    low = times(panel[:1], inverse[2])
+    product = (low + middle[rows:]) + high[2 * rows :]
+    product = (product + (middle[:rows] + high[rows : 2 * rows])) + high[:rows]
     factor_ref[...] = product.astype(jnp.bfloat16).reshape(factor_ref.shape)
 
 
@@ -63,8 +78,10 @@
     return tuple(tuple(count - 1 - b for b in range(count)) for _ in range(count))
 
 
-def plane_steps(count):
-    return (0, 2, 1, 3) if count == 4 else tuple(range(count))
+def plane_mates(count, plane):
+    if count == 4:
+        return (0, 1, 2, 3) if plane == 0 else (0, 2, 1, 3)
+    return tuple(range(count))
 
 
 def slab_of(slots, plane, place):
@@ -123,9 +140,10 @@
     r, c, layer = (lax.axis_index(axis) for axis in AXES)
     slots = plane_slots(pieces)
     per_row = col_tiles * tile // LANES
-    for step, plane_step in enumerate(plane_steps(pieces)):
+    for step in range(pieces):
+        mate = jnp.where(c == 0, plane_mates(pieces, 0)[step], plane_mates(pieces, 1)[step])
         row_at = pl.multiple_of(partner(c, step, pieces) * tile_rows, tile_rows)
-        slab = slab_of(slots, c, partner(r, plane_step, pieces))
+        slab = slab_of(slots, c, partner(r, mate, pieces))
         col_at = pl.multiple_of(slab * tile_rows, tile_rows)
         for k in range(half):
             row_buf[k, pl.ds(row_at, tile_rows), :] = row_refs[step][k]
@@ -198,8 +216,13 @@
     loaded_factor, share = lax.optimization_barrier((factor, share))
     line = gather_line(factor, loaded_factor, count)
     plane = [moved]
-    for step in plane_steps(count)[1:]:
-        plane.append(lax.ppermute(moved, "row", [(partner(a, step, count), a) for a in range(count)]))
+    for step in range(1, count):
+        pairs = [
+            (partner(a, plane_mates(count, b)[step], count) * count + b, a * count + b)
+            for a in range(count)
+            for b in range(count)
+        ]
+        plane.append(lax.ppermute(moved, ("row", "col"), pairs))
     others = []
     for shift in range(1, layers):
         pairs = [((l + shift) % layers, l) for l in range(layers)]

time: 20.7 us -> 20.1 us (0.971)
  waiting for transfers between devices: 4.26 us -> 3.79 us
    ppermute x3, waiting for transfers between devices: 3 us -> 2.54 us  [per_device(): plane.append(lax.ppermute(moved, ('row', 'col'), pairs))]
    ppermute x4, waiting for transfers between devices: 0.71 us -> 0.25 us  [per_device(): others += [lax.ppermute(piece, 'layer', pairs) for piece in plane]]
    ppermute x1, waiting for transfers between devices: 0.54 us -> 1 us  [gather_line(): both = lax.ppermute(far, 'col', [(b ^ 1, b) for b in range(count)])]
where the time goes in v17:
time: 20.1 us; the launch traced here: 20 us
  starting transfers between devices  11.4 us (57%)
  Pallas kernels  4.79 us (24%)
  waiting for transfers between devices  3.79 us (19%)
    ppermute x1, starting transfers between devices, per_device(): lax.ppermute(factor, ('row', 'col'), [(a * count + b, slots[a][b] * count...  3.95 us
    ppermute x3, starting transfers between devices, per_device(): plane.append(lax.ppermute(moved, ('row', 'col'), pairs))  3.49 us
    ppermute x1, starting transfers between devices, gather_line(): far = lax.ppermute(late_factor, 'col', [(b ^ 2, b) for b in range(count)])  2.96 us
    ppermute x3, waiting for transfers between devices, per_device(): plane.append(lax.ppermute(moved, ('row', 'col'), pairs))  2.54 us
    pallas_call x1, Pallas kernels, update_trailing(): pl.pallas_call(body, out_shape=jax.ShapeDtypeStruct(share.shape, jnp.floa...  1.85 us
    pallas_call x1, Pallas kernels, load_share(): pl.pallas_call(load_kernel, out_shape=jax.ShapeDtypeStruct((rows, LANES),...  1.6 us
    pallas_call x1, Pallas kernels, make_factor(): pl.pallas_call(factor_kernel, out_shape=jax.ShapeDtypeStruct((half, tile_...  1.34 us
    ppermute x1, waiting for transfers between devices, gather_line(): both = lax.ppermute(far, 'col', [(b ^ 1, b) for b in range(count)])  1 us
  transfers between devices with their start and end apart: 11, of which 5 were waited for; matrix products, arithmetic and copies ran while one was open for 0% of the time, Pallas kernels for 8%

profile of v17, /device:TPU:0, one launch (start us, length us, event | category | flops | bytes accessed | tf_op | source)
XLA Modules:
  0.0 20.0 jit_solution(6916172514489460047)
XLA Ops:
  0.0 1.3 %factor.1.after_ref.refs_0_ = bf16[2,64,256]{2,1,0:T(8,128)(2,1)S(1)} custom-call(f32[4,1,64,256]{3,2,1,0:T(8,128)} %panel_ref.1, f32[256,256]{1,0:T(8,128)} %inverse_ref.1), custom_call_target="tpu_custom_call" | custom-call | tf_op jit(solution)/shard_map/factor/pallas_call | solution.py:56
  1.4 3.9 %collective-permute-start.3 = (bf16[2,64,256]{2,1,0:T(8,128)(2,1)S(1)}, bf16[2,64,256]{2,1,0:T(8,128)(2,1)S(1)}, u32[]{:S(2)}, u32[]{:S(2)}) collective-permute-start(bf16[2,64,256]{2,1,0:T(8,128)(2,1)S(1)} %factor.1.after_ref.refs_0_), channel_id=1, source_target_pairs={{0,24},{2,0},{4,8},{6,16},{8,26},{10,18},{12,10},{14,2},{16,4},{18... | collective-permute-start | bytes 196616 | tf_op jit(solution)/shard_map/ppermute | solution.py:212
  5.3 0.0 collective-permute-start
  5.3 1.6 %load_share.1.refs_12_ = f32[4096,128]{1,0:T(8,128)S(1)} custom-call(bf16[2,64,256]{2,1,0:T(8,128)(2,1)S(1)} %factor.1.after_ref.refs_0_, f32[8192,128]{1,0:T(8,128)} %bitcast.2), custom_call_target="tpu_custom_call" | custom-call | bytes 4194304 | tf_op jit(solution)/shard_map/load_share/pallas_call | solution.py:124
  6.9 3.0 %collective-permute-start.1 = (bf16[2,64,256]{2,1,0:T(8,128)(2,1)S(1)}, bf16[2,64,256]{2,1,0:T(8,128)(2,1)S(1)}, u32[]{:S(2)}, u32[]{:S(2)}) collective-permute-start(bf16[2,64,256]{2,1,0:T(8,128)(2,1)S(1)} %factor.1.after_ref.refs_0_), channel_id=1, source_target_pairs={{4,0},{6,2},{0,4},{2,6},{5,1},{7,3},{1,5},{3,7},{12,8},{14,10},{8,... | collective-permute-start | bytes 196616 | tf_op jit(solution)/shard_map/ppermute | solution.py:109
  9.9 0.0 collective-permute-done.3.refs_4_
  9.9 1.7 %collective-permute-start.6 = (bf16[2,64,256]{2,1,0:T(8,128)(2,1)S(1)}, bf16[2,64,256]{2,1,0:T(8,128)(2,1)S(1)}, u32[]{:S(2)}, u32[]{:S(2)}) collective-permute-start(bf16[2,64,256]{2,1,0:T(8,128)(2,1)S(1)} %collective-permute-done.3.refs_4_), channel_id=1, source_target_pairs={{24,0},{26,2},{28,4},{30,6},{16,8},{18,10},{20,12},{22,14},{8,16},... | collective-permute-start | bytes 196616 | tf_op jit(solution)/shard_map/ppermute | solution.py:225
  11.5 1.1 %collective-permute-start.5 = (bf16[2,64,256]{2,1,0:T(8,128)(2,1)S(1)}, bf16[2,64,256]{2,1,0:T(8,128)(2,1)S(1)}, u32[]{:S(2)}, u32[]{:S(2)}) collective-permute-start(bf16[2,64,256]{2,1,0:T(8,128)(2,1)S(1)} %collective-permute-done.3.refs_4_), channel_id=1, source_target_pairs={{16,0},{10,2},{12,4},{14,6},{24,8},{2,10},{4,12},{6,14},{0,16},{26... | collective-permute-start | bytes 196616 | tf_op jit(solution)/shard_map/ppermute | solution.py:225
  12.6 0.8 %collective-permute-start.4 = (bf16[2,64,256]{2,1,0:T(8,128)(2,1)S(1)}, bf16[2,64,256]{2,1,0:T(8,128)(2,1)S(1)}, u32[]{:S(2)}, u32[]{:S(2)}) collective-permute-start(bf16[2,64,256]{2,1,0:T(8,128)(2,1)S(1)} %collective-permute-done.3.refs_4_), channel_id=1, source_target_pairs={{8,0},{18,2},{20,4},{22,6},{0,8},{26,10},{28,12},{30,14},{24,16},{... | collective-permute-start | bytes 196616 | tf_op jit(solution)/shard_map/ppermute | solution.py:225
  13.4 0.0 collective-permute-done.refs_1_
  13.4 0.0 collective-permute-start.7
  13.4 0.0 collective-permute-done.1.refs_2_
  13.4 1.0 %collective-permute-start.2 = (bf16[2,64,256]{2,1,0:T(8,128)(2,1)S(1)}, bf16[2,64,256]{2,1,0:T(8,128)(2,1)S(1)}, u32[]{:S(2)}, u32[]{:S(2)}) collective-permute-start(bf16[2,64,256]{2,1,0:T(8,128)(2,1)S(1)} %collective-permute-done.1.refs_2_), channel_id=1, source_target_pairs={{2,0},{0,2},{6,4},{4,6},{3,1},{1,3},{7,5},{5,7},{10,8},{8,10},{14,... | collective-permute-start | bytes 196616 | tf_op jit(solution)/shard_map/ppermute | solution.py:110
  14.3 1.2 %collective-permute-done.6.refs_7_ = bf16[2,64,256]{2,1,0:T(8,128)(2,1)S(1)} collective-permute-done((bf16[2,64,256]{2,1,0:T(8,128)(2,1)S(1)}, bf16[2,64,256]{2,1,0:T(8,128)(2,1)S(1)}, u32[]{:S(2)}, u32[]{:S(2)}) %collective-permute-start.6) | collective-permute-done | bytes 65568 | tf_op jit(solution)/shard_map/ppermute | solution.py:225
  15.5 0.0 collective-permute-start.10
  15.5 0.6 %collective-permute-done.5.refs_6_ = bf16[2,64,256]{2,1,0:T(8,128)(2,1)S(1)} collective-permute-done((bf16[2,64,256]{2,1,0:T(8,128)(2,1)S(1)}, bf16[2,64,256]{2,1,0:T(8,128)(2,1)S(1)}, u32[]{:S(2)}, u32[]{:S(2)}) %collective-permute-start.5) | collective-permute-done | bytes 65568 | tf_op jit(solution)/shard_map/ppermute | solution.py:225
  16.1 0.0 collective-permute-start.9
  16.1 0.8 %collective-permute-done.4.refs_5_ = bf16[2,64,256]{2,1,0:T(8,128)(2,1)S(1)} collective-permute-done((bf16[2,64,256]{2,1,0:T(8,128)(2,1)S(1)}, bf16[2,64,256]{2,1,0:T(8,128)(2,1)S(1)}, u32[]{:S(2)}, u32[]{:S(2)}) %collective-permute-start.4) | collective-permute-done | bytes 65568 | tf_op jit(solution)/shard_map/ppermute | solution.py:225
  16.9 0.0 collective-permute-start.8
  16.9 0.0 collective-permute-done.7.refs_8_
  16.9 1.0 %collective-permute-done.2.refs_3_ = bf16[2,64,256]{2,1,0:T(8,128)(2,1)S(1)} collective-permute-done((bf16[2,64,256]{2,1,0:T(8,128)(2,1)S(1)}, bf16[2,64,256]{2,1,0:T(8,128)(2,1)S(1)}, u32[]{:S(2)}, u32[]{:S(2)}) %collective-permute-start.2) | collective-permute-done | bytes 65568 | tf_op jit(solution)/shard_map/ppermute | solution.py:110
  17.9 0.0 collective-permute-done.10.refs_11_
  17.9 0.0 collective-permute-done.9.refs_10_
  17.9 0.2 %collective-permute-done.8.refs_9_ = bf16[2,64,256]{2,1,0:T(8,128)(2,1)S(1)} collective-permute-done((bf16[2,64,256]{2,1,0:T(8,128)(2,1)S(1)}, bf16[2,64,256]{2,1,0:T(8,128)(2,1)S(1)}, u32[]{:S(2)}, u32[]{:S(2)}) %collective-permute-start.8) | collective-permute-done | bytes 65568 | tf_op jit(solution)/shard_map/ppermute | solution.py:229
  18.1 1.9 %update.1 = f32[4096,128]{1,0:T(8,128)} custom-call(bf16[2,64,256]{2,1,0:T(8,128)(2,1)S(1)} %factor.1.after_ref.refs_0_, bf16[2,64,256]{2,1,0:T(8,128)(2,1)S(1)} %collective-permute-done.refs_1_, bf16[2,64,256]{2,1,0:T(8,128)(2,1)S(1)} %collective-permute-done.1.refs_2_, bf16[2,64,256]{2,1,0:T(8,128)(2,1)S(1)} %collective-permute-done.2.refs_3_, ...), custom_call_target="tpu_custom_call" | custom-call | tf_op jit(solution)/shard_map/update/pallas_call | solution.py:188
Async XLA Ops:
  1.4 8.5 %collective-permute-start.3 = (bf16[2,64,256]{2,1,0:T(8,128)(2,1)S(1)}, bf16[2,64,256]{2,1,0:T(8,128)(2,1)S(1)}, u32[]{:S(2)}, u32[]{:S(2)}) collective-permute-start(bf16[2,64,256]{2,1,0:T(8,128)(2,1)S(1)} %factor.1.after_ref.refs_0_), channel_id=1, source_target_pairs={{0,24},{2,0},{4,8},{6,16},{8,26},{10,18},{12,10},{14,2},{16,4},{18... | collective-permute-start | bytes 196616 | tf_op jit(solution)/shard_map/ppermute | solution.py:212
  5.3 8.1 %collective-permute-start = (bf16[2,64,256]{2,1,0:T(8,128)(2,1)S(1)}, bf16[2,64,256]{2,1,0:T(8,128)(2,1)S(1)}, u32[]{:S(2)}, u32[]{:S(2)}) collective-permute-start(bf16[2,64,256]{2,1,0:T(8,128)(2,1)S(1)} %factor.1.after_ref.refs_0_), channel_id=1, source_target_pairs={{8,0},{0,2},{6,4},{4,6},{10,8},{2,10},{14,12},{12,14},{18,16},{16,... | collective-permute-start | bytes 196616 | tf_op jit(solution)/shard_map/ppermute | solution.py:106
  6.9 6.5 %collective-permute-start.1 = (bf16[2,64,256]{2,1,0:T(8,128)(2,1)S(1)}, bf16[2,64,256]{2,1,0:T(8,128)(2,1)S(1)}, u32[]{:S(2)}, u32[]{:S(2)}) collective-permute-start(bf16[2,64,256]{2,1,0:T(8,128)(2,1)S(1)} %factor.1.after_ref.refs_0_), channel_id=1, source_target_pairs={{4,0},{6,2},{0,4},{2,6},{5,1},{7,3},{1,5},{3,7},{12,8},{14,10},{8,... | collective-permute-start | bytes 196616 | tf_op jit(solution)/shard_map/ppermute | solution.py:109
  9.9 5.7 %collective-permute-start.6 = (bf16[2,64,256]{2,1,0:T(8,128)(2,1)S(1)}, bf16[2,64,256]{2,1,0:T(8,128)(2,1)S(1)}, u32[]{:S(2)}, u32[]{:S(2)}) collective-permute-start(bf16[2,64,256]{2,1,0:T(8,128)(2,1)S(1)} %collective-permute-done.3.refs_4_), channel_id=1, source_target_pairs={{24,0},{26,2},{28,4},{30,6},{16,8},{18,10},{20,12},{22,14},{8,16},... | collective-permute-start | bytes 196616 | tf_op jit(solution)/shard_map/ppermute | solution.py:225
  11.5 4.6 %collective-permute-start.5 = (bf16[2,64,256]{2,1,0:T(8,128)(2,1)S(1)}, bf16[2,64,256]{2,1,0:T(8,128)(2,1)S(1)}, u32[]{:S(2)}, u32[]{:S(2)}) collective-permute-start(bf16[2,64,256]{2,1,0:T(8,128)(2,1)S(1)} %collective-permute-done.3.refs_4_), channel_id=1, source_target_pairs={{16,0},{10,2},{12,4},{14,6},{24,8},{2,10},{4,12},{6,14},{0,16},{26... | collective-permute-start | bytes 196616 | tf_op jit(solution)/shard_map/ppermute | solution.py:225
  12.6 4.3 %collective-permute-start.4 = (bf16[2,64,256]{2,1,0:T(8,128)(2,1)S(1)}, bf16[2,64,256]{2,1,0:T(8,128)(2,1)S(1)}, u32[]{:S(2)}, u32[]{:S(2)}) collective-permute-start(bf16[2,64,256]{2,1,0:T(8,128)(2,1)S(1)} %collective-permute-done.3.refs_4_), channel_id=1, source_target_pairs={{8,0},{18,2},{20,4},{22,6},{0,8},{26,10},{28,12},{30,14},{24,16},{... | collective-permute-start | bytes 196616 | tf_op jit(solution)/shard_map/ppermute | solution.py:225
  13.4 3.5 %collective-permute-start.7 = (bf16[2,64,256]{2,1,0:T(8,128)(2,1)S(1)}, bf16[2,64,256]{2,1,0:T(8,128)(2,1)S(1)}, u32[]{:S(2)}, u32[]{:S(2)}) collective-permute-start(bf16[2,64,256]{2,1,0:T(8,128)(2,1)S(1)} %collective-permute-done.3.refs_4_), channel_id=1, source_target_pairs={{1,0},{0,1},{3,2},{2,3},{5,4},{4,5},{7,6},{6,7},{9,8},{8,9},{11,10... | collective-permute-start | bytes 196616 | tf_op jit(solution)/shard_map/ppermute | solution.py:229
  13.4 4.5 %collective-permute-start.2 = (bf16[2,64,256]{2,1,0:T(8,128)(2,1)S(1)}, bf16[2,64,256]{2,1,0:T(8,128)(2,1)S(1)}, u32[]{:S(2)}, u32[]{:S(2)}) collective-permute-start(bf16[2,64,256]{2,1,0:T(8,128)(2,1)S(1)} %collective-permute-done.1.refs_2_), channel_id=1, source_target_pairs={{2,0},{0,2},{6,4},{4,6},{3,1},{1,3},{7,5},{5,7},{10,8},{8,10},{14,... | collective-permute-start | bytes 196616 | tf_op jit(solution)/shard_map/ppermute | solution.py:110
  15.5 2.3 %collective-permute-start.10 = (bf16[2,64,256]{2,1,0:T(8,128)(2,1)S(1)}, bf16[2,64,256]{2,1,0:T(8,128)(2,1)S(1)}, u32[]{:S(2)}, u32[]{:S(2)}) collective-permute-start(bf16[2,64,256]{2,1,0:T(8,128)(2,1)S(1)} %collective-permute-done.6.refs_7_), channel_id=1, source_target_pairs={{1,0},{0,1},{3,2},{2,3},{5,4},{4,5},{7,6},{6,7},{9,8},{8,9},{11,10... | collective-permute-start | bytes 196616 | tf_op jit(solution)/shard_map/ppermute | solution.py:229
  16.1 1.8 %collective-permute-start.9 = (bf16[2,64,256]{2,1,0:T(8,128)(2,1)S(1)}, bf16[2,64,256]{2,1,0:T(8,128)(2,1)S(1)}, u32[]{:S(2)}, u32[]{:S(2)}) collective-permute-start(bf16[2,64,256]{2,1,0:T(8,128)(2,1)S(1)} %collective-permute-done.5.refs_6_), channel_id=1, source_target_pairs={{1,0},{0,1},{3,2},{2,3},{5,4},{4,5},{7,6},{6,7},{9,8},{8,9},{11,10... | collective-permute-start | bytes 196616 | tf_op jit(solution)/shard_map/ppermute | solution.py:229
  16.9 1.3 %collective-permute-start.8 = (bf16[2,64,256]{2,1,0:T(8,128)(2,1)S(1)}, bf16[2,64,256]{2,1,0:T(8,128)(2,1)S(1)}, u32[]{:S(2)}, u32[]{:S(2)}) collective-permute-start(bf16[2,64,256]{2,1,0:T(8,128)(2,1)S(1)} %collective-permute-done.4.refs_5_), channel_id=1, source_target_pairs={{1,0},{0,1},{3,2},{2,3},{5,4},{4,5},{7,6},{6,7},{9,8},{8,9},{11,10... | collective-permute-start | bytes 196616 | tf_op jit(solution)/shard_map/ppermute | solution.py:229

commit v18 on v17

--- a/solution.py
+++ b/solution.py
@@ -6,7 +6,6 @@
 from jax.sharding import PartitionSpec as P
 
 LANES = 128
-CHUNK_ROWS = 256
 VMEM_BYTES = 24 * 1024 * 1024
 LOAD_VMEM_BYTES = 52000 * 1024
 FACTOR_VMEM_BYTES = 55040 * 1024
@@ -133,73 +132,132 @@
     )(after, lines)
 
 
-def update_kernel(pieces, layers, half, tile, tile_rows, col_tiles, *refs):
-    row_refs = refs[:pieces]
-    col_refs = refs[pieces : pieces * (1 + layers)]
-    share_ref, out_ref, row_buf, col_buf, out_buf, out_sems = refs[pieces * (1 + layers) :]
+def fill_columns(columns_ref, pieces, slots, r, c, owner):
+    half, tile_rows, _ = pieces[0].shape
+    tile = tile_rows * len(pieces)
+    for step, piece in enumerate(pieces):
+        mate = jnp.where(c == 0, plane_mates(len(pieces), 0)[step], plane_mates(len(pieces), 1)[step])
+        slab = slab_of(slots, c, partner(r, mate, len(pieces)))
+        for k in range(half):
+            at = pl.multiple_of(k * tile + slab * tile_rows, tile_rows)
+            columns_ref[pl.ds(at, tile_rows), :] = piece[k]
+
+
+def subtract_product(share_ref, rows, columns, tile, first_row, first_line, per_row):
+    half, tile_rows, width = rows.shape
+    product = lax.dot_general(
+        rows.reshape(half * tile_rows, width),
+        columns,
+        (((1,), (1,)), ((), ())),
+        preferred_element_type=jnp.float32,
+    )
+    for k in range(half):
+        for part in range(product.shape[1] // LANES):
+            start = (k * tile + first_row) * per_row + first_line + part
+            at = pl.ds(start, tile_rows, stride=per_row)
+            share_ref[at, :] -= product[k * tile_rows : (k + 1) * tile_rows, part * LANES : (part + 1) * LANES]
+
+
+def begin_kernel(pieces, layers, tile, *refs):
+    column_refs, row_refs, rest = refs[:pieces], refs[pieces : 2 * pieces - 1], refs[2 * pieces - 1 :]
+    _, share_ref, columns_ref, near_ref = rest
     r, c, layer = (lax.axis_index(axis) for axis in AXES)
-    slots = plane_slots(pieces)
-    per_row = col_tiles * tile // LANES
-    for step in range(pieces):
-        mate = jnp.where(c == 0, plane_mates(pieces, 0)[step], plane_mates(pieces, 1)[step])
-        row_at = pl.multiple_of(partner(c, step, pieces) * tile_rows, tile_rows)
-        slab = slab_of(slots, c, partner(r, mate, pieces))
-        col_at = pl.multiple_of(slab * tile_rows, tile_rows)
-        for k in range(half):
-            row_buf[k, pl.ds(row_at, tile_rows), :] = row_refs[step][k]
-        for shift in range(layers):
-            owner = lax.rem(layer + shift, layers)
-            for k in range(half):
-                col_buf[owner * half + k, pl.ds(col_at, tile_rows), :] = col_refs[shift * pieces + step][k]
+    half, tile_rows, _ = row_refs[0].shape
+    own_lines = half * tile // LANES
+    fill_columns(columns_ref, column_refs, plane_slots(pieces), r, c, layer)
+    near_ref[...] = row_refs[1][...]
+    near_at = pl.multiple_of(partner(c, 1, pieces) * tile_rows, tile_rows)
     if pieces == 4:
 
         @pl.when(r == c)
         def _():
-            row_buf[...] = col_buf[pl.ds(layer * half, half)]
-
-    chunks = half * (tile // CHUNK_ROWS)
-    chunk_lines = CHUNK_ROWS * per_row
+            for k in range(half):
+                near_ref[k] = columns_ref[pl.ds(k * tile + near_at, tile_rows), :]
+
+    for step, row_ref in enumerate((row_refs[0], near_ref, *row_refs[2:])):
+        first_row = partner(c, step, pieces) * tile_rows
+        subtract_product(
+            share_ref, row_ref[...], columns_ref[...], tile, first_row, layer * own_lines, layers * own_lines
+        )
+
+
+def begin_update(column_pieces, row_pieces, share, layers, tile):
+    pieces = len(column_pieces)
+    half, _, width = row_pieces[0].shape
+
+    def body(*refs):
+        begin_kernel(pieces, layers, tile, *refs)
+
+    return pl.pallas_call(
+        body,
+        out_shape=[
+            jax.ShapeDtypeStruct(share.shape, jnp.float32),
+            jax.ShapeDtypeStruct((half * tile, width), jnp.bfloat16),
+            jax.ShapeDtypeStruct(row_pieces[0].shape, jnp.bfloat16),
+        ],
+        in_specs=[pl.BlockSpec(memory_space=pltpu.VMEM)] * (2 * pieces),
+        out_specs=[pl.BlockSpec(memory_space=pltpu.VMEM)] * 3,
+        input_output_aliases={2 * pieces - 1: 0},
+        compiler_params=pltpu.CompilerParams(vmem_limit_bytes=VMEM_BYTES),
+        name="begin_update",
+    )(*column_pieces, *row_pieces, share)
+
+
+def end_kernel(pieces, layers, tile, *refs):
+    others = pieces * (layers - 1)
+    column_refs, row_refs, rest = refs[:others], refs[others : others + pieces], refs[others + pieces :]
+    own_ref, _, out_ref, share_ref, columns_buf, sems = rest
+    r, c, layer = (lax.axis_index(axis) for axis in AXES)
+    half, tile_rows, _ = row_refs[0].shape
+    own_lines = half * tile // LANES
+    per_row = layers * own_lines
+    owners = [lax.rem(layer + shift, layers) for shift in range(1, layers)]
+    for at, owner in enumerate(owners):
+        fill_columns(
+            columns_buf.at[at], column_refs[at * pieces : (at + 1) * pieces], plane_slots(pieces), r, c, owner
+        )
     stores = []
-    for chunk in range(chunks):
-        k, first_row = divmod(chunk * CHUNK_ROWS, tile)
-        update = lax.dot_general(
-            row_buf[k, first_row : first_row + CHUNK_ROWS, :],
-            col_buf[...].reshape(col_tiles * tile, -1),
-            (((1,), (1,)), ((), ())),
-            preferred_element_type=jnp.float32,
-        )
-        written = pl.ds(chunk * chunk_lines, chunk_lines)
-        out_buf[written, :] = share_ref[written, :] - update.reshape(chunk_lines, LANES)
-        store = pltpu.make_async_copy(out_buf.at[written], out_ref.at[written], out_sems.at[chunk])
-        store.start()
-        stores.append(store)
+    for step, row_ref in enumerate(row_refs):
+        first_row = partner(c, step, pieces) * tile_rows
+        rows = row_ref[...]
+        for at, owner in enumerate(owners):
+            subtract_product(share_ref, rows, columns_buf[at], tile, first_row, owner * own_lines, per_row)
+        if step == pieces - 1:
+            subtract_product(share_ref, rows, own_ref[...], tile, first_row, layer * own_lines, per_row)
+        for k in range(half):
+            lines = tile_rows * per_row
+            start = pl.multiple_of((k * tile + first_row) * per_row, lines)
+            store = pltpu.make_async_copy(
+                share_ref.at[pl.ds(start, lines)], out_ref.at[pl.ds(start, lines)], sems.at[step * half + k]
+            )
+            store.start()
+            stores.append(store)
     for store in stores:
         store.wait()
 
 
-def update_trailing(row_pieces, col_pieces, share, half, layers, tile, col_tiles):
+def end_update(column_pieces, row_pieces, own_columns, share, layers, tile):
     pieces = len(row_pieces)
-    tile_rows = row_pieces[0].shape[1]
-    width = row_pieces[0].shape[2]
+    half = row_pieces[0].shape[0]
+    operands = (*column_pieces, *row_pieces, own_columns, share)
 
     def body(*refs):
-        update_kernel(pieces, layers, half, tile, tile_rows, col_tiles, *refs)
-
-    result = pl.pallas_call(
+        end_kernel(pieces, layers, tile, *refs)
+
+    result, _ = pl.pallas_call(
         body,
-        out_shape=jax.ShapeDtypeStruct(share.shape, jnp.float32),
-        in_specs=[pl.BlockSpec(memory_space=pltpu.VMEM)] * (pieces * (1 + layers) + 1),
-        out_specs=pl.BlockSpec(memory_space=pltpu.HBM),
+        out_shape=[jax.ShapeDtypeStruct(share.shape, jnp.float32)] * 2,
+        in_specs=[pl.BlockSpec(memory_space=pltpu.VMEM)] * len(operands),
+        out_specs=[pl.BlockSpec(memory_space=pltpu.HBM), pl.BlockSpec(memory_space=pltpu.VMEM)],
         scratch_shapes=[
-            pltpu.VMEM((half, tile, width), jnp.bfloat16),
-            pltpu.VMEM((half * layers, tile, width), jnp.bfloat16),
-            pltpu.VMEM(share.shape, jnp.float32),
-            pltpu.SemaphoreType.DMA((half * (tile // CHUNK_ROWS),)),
+            pltpu.VMEM((layers - 1, *own_columns.shape), jnp.bfloat16),
+            pltpu.SemaphoreType.DMA((half * pieces,)),
         ],
+        input_output_aliases={len(operands) - 1: 1},
         compiler_params=pltpu.CompilerParams(vmem_limit_bytes=VMEM_BYTES),
-        name="update",
-    )(*row_pieces, *col_pieces, share)
-    return result.reshape(half, 1, tile, col_tiles, 1, tile)
+        name="end_update",
+    )(*operands)
+    return result
 
 
 def per_device(trailing, panel, inverse_factor):
@@ -227,7 +285,10 @@
     for shift in range(1, layers):
         pairs = [((l + shift) % layers, l) for l in range(layers)]
         others += [lax.ppermute(piece, "layer", pairs) for piece in plane]
-    return update_trailing(line, plane + others, share, half, layers, tile, col_tiles)
+    share, own_columns, near = begin_update(plane, line[:-1], share, layers, tile)
+    rows = [line[0], near, *line[2:]]
+    result = end_update(others, rows, own_columns, share, layers, tile)
+    return result.reshape(half, 1, tile, col_tiles, 1, tile)
 
 
 def solution(mesh):

time: 20.1 us -> 20 us (level)
  waiting for transfers between devices: 3.79 us -> 3.3 us
  Pallas kernels: 4.79 us -> 5.1 us
    ppermute x1, waiting for transfers between devices: 1 us -> 0.5 us  [gather_line(): both = lax.ppermute(far, 'col', [(b ^ 1, b) for b in range(count)])]
    pallas_call x1 -> x2, Pallas kernels: 1.85 us -> 2.16 us  [the longest x1 1.68 us: end_update(): pl.pallas_call(body, out_shape=[jax.ShapeDtypeStruct(share.shape, jnp.flo...]
  transfers between devices with their start and end apart: 11 -> 11, of which waited for: 5 -> 5; matrix products, arithmetic and copies ran while one was open for 0% -> 0% of each run, Pallas kernels for 8% -> 11%
where the time goes in v18:
time: 20 us; the launch traced here: 19.8 us
  starting transfers between devices  11.4 us (57%)
  Pallas kernels  5.1 us (25%)
  waiting for transfers between devices  3.3 us (16%)
    ppermute x1, starting transfers between devices, per_device(): lax.ppermute(factor, ('row', 'col'), [(a * count + b, slots[a][b] * count...  3.95 us
    ppermute x3, starting transfers between devices, per_device(): plane.append(lax.ppermute(moved, ('row', 'col'), pairs))  3.49 us
    ppermute x1, starting transfers between devices, gather_line(): far = lax.ppermute(late_factor, 'col', [(b ^ 2, b) for b in range(count)])  2.96 us
    ppermute x3, waiting for transfers between devices, per_device(): plane.append(lax.ppermute(moved, ('row', 'col'), pairs))  2.54 us
    pallas_call x1, Pallas kernels, end_update(): pl.pallas_call(body, out_shape=[jax.ShapeDtypeStruct(share.shape, jnp.flo...  1.68 us
    pallas_call x1, Pallas kernels, load_share(): pl.pallas_call(load_kernel, out_shape=jax.ShapeDtypeStruct((rows, LANES),...  1.6 us
    pallas_call x1, Pallas kernels, make_factor(): pl.pallas_call(factor_kernel, out_shape=jax.ShapeDtypeStruct((half, tile_...  1.34 us
    ppermute x1, starting transfers between devices, gather_line(): both = lax.ppermute(far, 'col', [(b ^ 1, b) for b in range(count)])  0.96 us
  transfers between devices with their start and end apart: 11, of which 5 were waited for; matrix products, arithmetic and copies ran while one was open for 0% of the time, Pallas kernels for 11%

profile of v18, /device:TPU:0, one launch (start us, length us, event | category | flops | bytes accessed | tf_op | source)
XLA Modules:
  0.0 19.8 jit_solution(8249456590093958763)
XLA Ops:
  0.0 1.3 %factor.1.after_ref.refs_4_ = bf16[2,64,256]{2,1,0:T(8,128)(2,1)S(1)} custom-call(f32[4,1,64,256]{3,2,1,0:T(8,128)} %panel_ref.1, f32[256,256]{1,0:T(8,128)} %inverse_ref.1), custom_call_target="tpu_custom_call" | custom-call | tf_op jit(solution)/shard_map/factor/pallas_call | solution.py:55
  1.4 3.9 %collective-permute-start = (bf16[2,64,256]{2,1,0:T(8,128)(2,1)S(1)}, bf16[2,64,256]{2,1,0:T(8,128)(2,1)S(1)}, u32[]{:S(2)}, u32[]{:S(2)}) collective-permute-start(bf16[2,64,256]{2,1,0:T(8,128)(2,1)S(1)} %factor.1.after_ref.refs_4_), channel_id=1, source_target_pairs={{0,24},{2,0},{4,8},{6,16},{8,26},{10,18},{12,10},{14,2},{16,4},{18... | collective-permute-start | bytes 196616 | tf_op jit(solution)/shard_map/ppermute | solution.py:270
  5.3 0.0 collective-permute-start.8
  5.3 1.6 %load_share.1.refs_7_ = f32[4096,128]{1,0:T(8,128)S(1)} custom-call(bf16[2,64,256]{2,1,0:T(8,128)(2,1)S(1)} %factor.1.after_ref.refs_4_, f32[8192,128]{1,0:T(8,128)} %bitcast.2), custom_call_target="tpu_custom_call" | custom-call | bytes 4194304 | tf_op jit(solution)/shard_map/load_share/pallas_call | solution.py:123
  6.9 3.0 %collective-permute-start.9 = (bf16[2,64,256]{2,1,0:T(8,128)(2,1)S(1)}, bf16[2,64,256]{2,1,0:T(8,128)(2,1)S(1)}, u32[]{:S(2)}, u32[]{:S(2)}) collective-permute-start(bf16[2,64,256]{2,1,0:T(8,128)(2,1)S(1)} %factor.1.after_ref.refs_4_), channel_id=1, source_target_pairs={{4,0},{6,2},{0,4},{2,6},{5,1},{7,3},{1,5},{3,7},{12,8},{14,10},{8,... | collective-permute-start | bytes 196616 | tf_op jit(solution)/shard_map/ppermute | solution.py:108
  9.9 0.0 collective-permute-done.refs_0_
  9.9 1.7 %collective-permute-start.6 = (bf16[2,64,256]{2,1,0:T(8,128)(2,1)S(1)}, bf16[2,64,256]{2,1,0:T(8,128)(2,1)S(1)}, u32[]{:S(2)}, u32[]{:S(2)}) collective-permute-start(bf16[2,64,256]{2,1,0:T(8,128)(2,1)S(1)} %collective-permute-done.refs_0_), channel_id=1, source_target_pairs={{24,0},{26,2},{28,4},{30,6},{16,8},{18,10},{20,12},{22,14},{8,16},... | collective-permute-start | bytes 196616 | tf_op jit(solution)/shard_map/ppermute | solution.py:283
  11.5 1.1 %collective-permute-start.4 = (bf16[2,64,256]{2,1,0:T(8,128)(2,1)S(1)}, bf16[2,64,256]{2,1,0:T(8,128)(2,1)S(1)}, u32[]{:S(2)}, u32[]{:S(2)}) collective-permute-start(bf16[2,64,256]{2,1,0:T(8,128)(2,1)S(1)} %collective-permute-done.refs_0_), channel_id=1, source_target_pairs={{16,0},{10,2},{12,4},{14,6},{24,8},{2,10},{4,12},{6,14},{0,16},{26... | collective-permute-start | bytes 196616 | tf_op jit(solution)/shard_map/ppermute | solution.py:283
  12.6 0.8 %collective-permute-start.2 = (bf16[2,64,256]{2,1,0:T(8,128)(2,1)S(1)}, bf16[2,64,256]{2,1,0:T(8,128)(2,1)S(1)}, u32[]{:S(2)}, u32[]{:S(2)}) collective-permute-start(bf16[2,64,256]{2,1,0:T(8,128)(2,1)S(1)} %collective-permute-done.refs_0_), channel_id=1, source_target_pairs={{8,0},{18,2},{20,4},{22,6},{0,8},{26,10},{28,12},{30,14},{24,16},{... | collective-permute-start | bytes 196616 | tf_op jit(solution)/shard_map/ppermute | solution.py:283
  13.4 0.0 collective-permute-done.8.refs_5_
  13.4 0.0 collective-permute-start.1
  13.4 0.0 collective-permute-done.9.refs_6_
  13.4 1.0 %collective-permute-start.10 = (bf16[2,64,256]{2,1,0:T(8,128)(2,1)S(1)}, bf16[2,64,256]{2,1,0:T(8,128)(2,1)S(1)}, u32[]{:S(2)}, u32[]{:S(2)}) collective-permute-start(bf16[2,64,256]{2,1,0:T(8,128)(2,1)S(1)} %collective-permute-done.9.refs_6_), channel_id=1, source_target_pairs={{2,0},{0,2},{6,4},{4,6},{3,1},{1,3},{7,5},{5,7},{10,8},{8,10},{14,... | collective-permute-start | bytes 196616 | tf_op jit(solution)/shard_map/ppermute | solution.py:109
  14.3 1.2 %collective-permute-done.6.refs_3_ = bf16[2,64,256]{2,1,0:T(8,128)(2,1)S(1)} collective-permute-done((bf16[2,64,256]{2,1,0:T(8,128)(2,1)S(1)}, bf16[2,64,256]{2,1,0:T(8,128)(2,1)S(1)}, u32[]{:S(2)}, u32[]{:S(2)}) %collective-permute-start.6) | collective-permute-done | bytes 65568 | tf_op jit(solution)/shard_map/ppermute | solution.py:283
  15.5 0.0 collective-permute-start.7
  15.5 0.6 %collective-permute-done.4.refs_2_ = bf16[2,64,256]{2,1,0:T(8,128)(2,1)S(1)} collective-permute-done((bf16[2,64,256]{2,1,0:T(8,128)(2,1)S(1)}, bf16[2,64,256]{2,1,0:T(8,128)(2,1)S(1)}, u32[]{:S(2)}, u32[]{:S(2)}) %collective-permute-start.4) | collective-permute-done | bytes 65568 | tf_op jit(solution)/shard_map/ppermute | solution.py:283
  16.1 0.0 collective-permute-start.5
  16.1 0.8 %collective-permute-done.2.refs_1_ = bf16[2,64,256]{2,1,0:T(8,128)(2,1)S(1)} collective-permute-done((bf16[2,64,256]{2,1,0:T(8,128)(2,1)S(1)}, bf16[2,64,256]{2,1,0:T(8,128)(2,1)S(1)}, u32[]{:S(2)}, u32[]{:S(2)}) %collective-permute-start.2) | collective-permute-done | bytes 65568 | tf_op jit(solution)/shard_map/ppermute | solution.py:283
  16.9 0.0 collective-permute-start.3
  16.9 0.5 %begin_update.1 = (f32[4096,128]{1,0:T(8,128)S(1)}, bf16[512,256]{1,0:T(8,128)(2,1)S(1)}, bf16[2,64,256]{2,1,0:T(8,128)(2,1)S(1)}) custom-call(bf16[2,64,256]{2,1,0:T(8,128)(2,1)S(1)} %collective-permute-done.refs_0_, bf16[2,64,256]{2,1,0:T(8,128)(2,1)S(1)} %collective-permute-done.2.refs_1_, ...), custom_call_target="tpu_custom_call", output_to_operand_aliasing={{0}: (7, {})} | custom-call | tf_op jit(solution)/shard_map/begin_update/pallas_call | solution.py:191
  17.4 0.0 collective-permute-done.1.refs_0_
  17.4 0.5 %collective-permute-done.10.refs_7_ = bf16[2,64,256]{2,1,0:T(8,128)(2,1)S(1)} collective-permute-done((bf16[2,64,256]{2,1,0:T(8,128)(2,1)S(1)}, bf16[2,64,256]{2,1,0:T(8,128)(2,1)S(1)}, u32[]{:S(2)}, u32[]{:S(2)}) %collective-permute-start.10) | collective-permute-done | bytes 65568 | tf_op jit(solution)/shard_map/ppermute | solution.py:109
  17.9 0.0 collective-permute-done.7.refs_3_
  17.9 0.0 collective-permute-done.5.refs_2_
  17.9 0.2 %collective-permute-done.3.refs_1_ = bf16[2,64,256]{2,1,0:T(8,128)(2,1)S(1)} collective-permute-done((bf16[2,64,256]{2,1,0:T(8,128)(2,1)S(1)}, bf16[2,64,256]{2,1,0:T(8,128)(2,1)S(1)}, u32[]{:S(2)}, u32[]{:S(2)}) %collective-permute-start.3) | collective-permute-done | bytes 65568 | tf_op jit(solution)/shard_map/ppermute | solution.py:287
  18.1 1.7 %end_update.1 = (f32[4096,128]{1,0:T(8,128)}, f32[4096,128]{1,0:T(8,128)S(1)}) custom-call(bf16[2,64,256]{2,1,0:T(8,128)(2,1)S(1)} %collective-permute-done.1.refs_0_, bf16[2,64,256]{2,1,0:T(8,128)(2,1)S(1)} %collective-permute-done.3.refs_1_, bf16[2,64,256]{2,1,0:T(8,128)(2,1)S(1)} %collective-permute-done.5.refs_2_, ...), custom_call_target="tpu_custom_call", output_to_operand_aliasing={{1}: (9, {})} | custom-call | tf_op jit(solution)/shard_map/end_update/pallas_call | solution.py:247
Async XLA Ops:
  1.4 8.5 %collective-permute-start = (bf16[2,64,256]{2,1,0:T(8,128)(2,1)S(1)}, bf16[2,64,256]{2,1,0:T(8,128)(2,1)S(1)}, u32[]{:S(2)}, u32[]{:S(2)}) collective-permute-start(bf16[2,64,256]{2,1,0:T(8,128)(2,1)S(1)} %factor.1.after_ref.refs_4_), channel_id=1, source_target_pairs={{0,24},{2,0},{4,8},{6,16},{8,26},{10,18},{12,10},{14,2},{16,4},{18... | collective-permute-start | bytes 196616 | tf_op jit(solution)/shard_map/ppermute | solution.py:270
  5.3 8.1 %collective-permute-start.8 = (bf16[2,64,256]{2,1,0:T(8,128)(2,1)S(1)}, bf16[2,64,256]{2,1,0:T(8,128)(2,1)S(1)}, u32[]{:S(2)}, u32[]{:S(2)}) collective-permute-start(bf16[2,64,256]{2,1,0:T(8,128)(2,1)S(1)} %factor.1.after_ref.refs_4_), channel_id=1, source_target_pairs={{8,0},{0,2},{6,4},{4,6},{10,8},{2,10},{14,12},{12,14},{18,16},{16,... | collective-permute-start | bytes 196616 | tf_op jit(solution)/shard_map/ppermute | solution.py:105
  6.9 6.5 %collective-permute-start.9 = (bf16[2,64,256]{2,1,0:T(8,128)(2,1)S(1)}, bf16[2,64,256]{2,1,0:T(8,128)(2,1)S(1)}, u32[]{:S(2)}, u32[]{:S(2)}) collective-permute-start(bf16[2,64,256]{2,1,0:T(8,128)(2,1)S(1)} %factor.1.after_ref.refs_4_), channel_id=1, source_target_pairs={{4,0},{6,2},{0,4},{2,6},{5,1},{7,3},{1,5},{3,7},{12,8},{14,10},{8,... | collective-permute-start | bytes 196616 | tf_op jit(solution)/shard_map/ppermute | solution.py:108
  9.9 5.7 %collective-permute-start.6 = (bf16[2,64,256]{2,1,0:T(8,128)(2,1)S(1)}, bf16[2,64,256]{2,1,0:T(8,128)(2,1)S(1)}, u32[]{:S(2)}, u32[]{:S(2)}) collective-permute-start(bf16[2,64,256]{2,1,0:T(8,128)(2,1)S(1)} %collective-permute-done.refs_0_), channel_id=1, source_target_pairs={{24,0},{26,2},{28,4},{30,6},{16,8},{18,10},{20,12},{22,14},{8,16},... | collective-permute-start | bytes 196616 | tf_op jit(solution)/shard_map/ppermute | solution.py:283
  11.5 4.6 %collective-permute-start.4 = (bf16[2,64,256]{2,1,0:T(8,128)(2,1)S(1)}, bf16[2,64,256]{2,1,0:T(8,128)(2,1)S(1)}, u32[]{:S(2)}, u32[]{:S(2)}) collective-permute-start(bf16[2,64,256]{2,1,0:T(8,128)(2,1)S(1)} %collective-permute-done.refs_0_), channel_id=1, source_target_pairs={{16,0},{10,2},{12,4},{14,6},{24,8},{2,10},{4,12},{6,14},{0,16},{26... | collective-permute-start | bytes 196616 | tf_op jit(solution)/shard_map/ppermute | solution.py:283
  12.6 4.3 %collective-permute-start.2 = (bf16[2,64,256]{2,1,0:T(8,128)(2,1)S(1)}, bf16[2,64,256]{2,1,0:T(8,128)(2,1)S(1)}, u32[]{:S(2)}, u32[]{:S(2)}) collective-permute-start(bf16[2,64,256]{2,1,0:T(8,128)(2,1)S(1)} %collective-permute-done.refs_0_), channel_id=1, source_target_pairs={{8,0},{18,2},{20,4},{22,6},{0,8},{26,10},{28,12},{30,14},{24,16},{... | collective-permute-start | bytes 196616 | tf_op jit(solution)/shard_map/ppermute | solution.py:283
  13.4 4.0 %collective-permute-start.1 = (bf16[2,64,256]{2,1,0:T(8,128)(2,1)S(1)}, bf16[2,64,256]{2,1,0:T(8,128)(2,1)S(1)}, u32[]{:S(2)}, u32[]{:S(2)}) collective-permute-start(bf16[2,64,256]{2,1,0:T(8,128)(2,1)S(1)} %collective-permute-done.refs_0_), channel_id=1, source_target_pairs={{1,0},{0,1},{3,2},{2,3},{5,4},{4,5},{7,6},{6,7},{9,8},{8,9},{11,10... | collective-permute-start | bytes 196616 | tf_op jit(solution)/shard_map/ppermute | solution.py:287
  13.4 4.5 %collective-permute-start.10 = (bf16[2,64,256]{2,1,0:T(8,128)(2,1)S(1)}, bf16[2,64,256]{2,1,0:T(8,128)(2,1)S(1)}, u32[]{:S(2)}, u32[]{:S(2)}) collective-permute-start(bf16[2,64,256]{2,1,0:T(8,128)(2,1)S(1)} %collective-permute-done.9.refs_6_), channel_id=1, source_target_pairs={{2,0},{0,2},{6,4},{4,6},{3,1},{1,3},{7,5},{5,7},{10,8},{8,10},{14,... | collective-permute-start | bytes 196616 | tf_op jit(solution)/shard_map/ppermute | solution.py:109
  15.5 2.3 %collective-permute-start.7 = (bf16[2,64,256]{2,1,0:T(8,128)(2,1)S(1)}, bf16[2,64,256]{2,1,0:T(8,128)(2,1)S(1)}, u32[]{:S(2)}, u32[]{:S(2)}) collective-permute-start(bf16[2,64,256]{2,1,0:T(8,128)(2,1)S(1)} %collective-permute-done.6.refs_3_), channel_id=1, source_target_pairs={{1,0},{0,1},{3,2},{2,3},{5,4},{4,5},{7,6},{6,7},{9,8},{8,9},{11,10... | collective-permute-start | bytes 196616 | tf_op jit(solution)/shard_map/ppermute | solution.py:287
  16.1 1.8 %collective-permute-start.5 = (bf16[2,64,256]{2,1,0:T(8,128)(2,1)S(1)}, bf16[2,64,256]{2,1,0:T(8,128)(2,1)S(1)}, u32[]{:S(2)}, u32[]{:S(2)}) collective-permute-start(bf16[2,64,256]{2,1,0:T(8,128)(2,1)S(1)} %collective-permute-done.4.refs_2_), channel_id=1, source_target_pairs={{1,0},{0,1},{3,2},{2,3},{5,4},{4,5},{7,6},{6,7},{9,8},{8,9},{11,10... | collective-permute-start | bytes 196616 | tf_op jit(solution)/shard_map/ppermute | solution.py:287
  16.9 1.3 %collective-permute-start.3 = (bf16[2,64,256]{2,1,0:T(8,128)(2,1)S(1)}, bf16[2,64,256]{2,1,0:T(8,128)(2,1)S(1)}, u32[]{:S(2)}, u32[]{:S(2)}) collective-permute-start(bf16[2,64,256]{2,1,0:T(8,128)(2,1)S(1)} %collective-permute-done.2.refs_1_), channel_id=1, source_target_pairs={{1,0},{0,1},{3,2},{2,3},{5,4},{4,5},{7,6},{6,7},{9,8},{8,9},{11,10... | collective-permute-start | bytes 196616 | tf_op jit(solution)/shard_map/ppermute | solution.py:287

commit v19 on v18

--- a/solution.py
+++ b/solution.py
@@ -73,7 +73,7 @@
 
 def plane_slots(count):
     if count == 4:
-        return ((3, 0, 1, 2), (3, 2, 1, 0), (0, 2, 1, 3), (3, 2, 1, 0))
+        return ((3, 0, 1, 2), (3, 2, 0, 1), (0, 2, 1, 3), (2, 3, 1, 0))
     return tuple(tuple(count - 1 - b for b in range(count)) for _ in range(count))
 
 
@@ -95,19 +95,31 @@
     return slab
 
 
-def gather_line(factor, late_factor, count):
+def line_steps(count):
+    return (0, 2, 1, 3) if count == 4 else tuple(range(count))
+
+
+def move(x, sources, count):
+    return lax.ppermute(x, ("row", "col"), [(a * count + b, r * count + c) for (r, c), (a, b) in sources.items()])
+
+
+def gather_line(factor, late_factor, moved, count):
     if count != 4:
         line = [factor]
         for step in range(1, count):
             line.append(lax.ppermute(factor, "col", [(partner(b, step, count), b) for b in range(count)]))
         return line
-    sources = {(r, c): (r ^ 1, c) if r == c else (r, c ^ 1) for r in range(count) for c in range(count)}
-    near = lax.ppermute(
-        factor, ("row", "col"), [(a * count + b, r * count + c) for (r, c), (a, b) in sources.items()]
-    )
-    far = lax.ppermute(late_factor, "col", [(b ^ 2, b) for b in range(count)])
-    both = lax.ppermute(far, "col", [(b ^ 1, b) for b in range(count)])
-    return [factor, near, far, both]
+    places = [(r, c) for r in range(count) for c in range(count)]
+    near = move(late_factor, {(r, c): (r ^ 1, c) if r == c else (r, c ^ 1) for r, c in places}, count)
+    far = move(late_factor, {(r, c): (r ^ 2, c) if r == c else (r, c ^ 2) for r, c in places}, count)
+    r, c = lax.axis_index("row"), lax.axis_index("col")
+    odd = r % 2 == 1
+    sent = jnp.where(~odd & (c == r ^ 3), near, far)
+    sent = jnp.where(odd & (c == r), moved, sent)
+    sent = jnp.where(~odd & (c == r ^ 1), late_factor, sent)
+    cycle = {0: 0, 2: 1, 3: 2, 1: 3}
+    last = move(sent, {(r, c): (r, c ^ 1) if r % 2 == 1 else (r, r ^ cycle[c ^ r]) for r, c in places}, count)
+    return [factor, far, near, last]
 
 
 def load_kernel(after_ref, lines_ref, share_ref, sem):
@@ -158,23 +170,30 @@
             share_ref[at, :] -= product[k * tile_rows : (k + 1) * tile_rows, part * LANES : (part + 1) * LANES]
 
 
+def take_rows(rows_ref, columns_ref, c, step, pieces):
+    half, tile_rows, _ = rows_ref.shape
+    for k in range(half):
+        at = pl.multiple_of((k * pieces + partner(c, step, pieces)) * tile_rows, tile_rows)
+        rows_ref[k] = columns_ref[pl.ds(at, tile_rows), :]
+
+
 def begin_kernel(pieces, layers, tile, *refs):
     column_refs, row_refs, rest = refs[:pieces], refs[pieces : 2 * pieces - 1], refs[2 * pieces - 1 :]
-    _, share_ref, columns_ref, near_ref = rest
+    _, share_ref, columns_ref, *line_refs = rest
     r, c, layer = (lax.axis_index(axis) for axis in AXES)
     half, tile_rows, _ = row_refs[0].shape
     own_lines = half * tile // LANES
     fill_columns(columns_ref, column_refs, plane_slots(pieces), r, c, layer)
-    near_ref[...] = row_refs[1][...]
-    near_at = pl.multiple_of(partner(c, 1, pieces) * tile_rows, tile_rows)
+    for line_ref, row_ref in zip(line_refs, row_refs[1:]):
+        line_ref[...] = row_ref[...]
     if pieces == 4:
 
         @pl.when(r == c)
         def _():
-            for k in range(half):
-                near_ref[k] = columns_ref[pl.ds(k * tile + near_at, tile_rows), :]
-
-    for step, row_ref in enumerate((row_refs[0], near_ref, *row_refs[2:])):
+            for step, line_ref in zip(line_steps(pieces)[1:], line_refs):
+                take_rows(line_ref, columns_ref, c, step, pieces)
+
+    for step, row_ref in zip(line_steps(pieces), (row_refs[0], *line_refs)):
         first_row = partner(c, step, pieces) * tile_rows
         subtract_product(
             share_ref, row_ref[...], columns_ref[...], tile, first_row, layer * own_lines, layers * own_lines
@@ -193,10 +212,10 @@
         out_shape=[
             jax.ShapeDtypeStruct(share.shape, jnp.float32),
             jax.ShapeDtypeStruct((half * tile, width), jnp.bfloat16),
-            jax.ShapeDtypeStruct(row_pieces[0].shape, jnp.bfloat16),
+            *[jax.ShapeDtypeStruct(row_pieces[0].shape, jnp.bfloat16)] * (pieces - 2),
         ],
         in_specs=[pl.BlockSpec(memory_space=pltpu.VMEM)] * (2 * pieces),
-        out_specs=[pl.BlockSpec(memory_space=pltpu.VMEM)] * 3,
+        out_specs=[pl.BlockSpec(memory_space=pltpu.VMEM)] * pieces,
         input_output_aliases={2 * pieces - 1: 0},
         compiler_params=pltpu.CompilerParams(vmem_limit_bytes=VMEM_BYTES),
         name="begin_update",
@@ -206,7 +225,7 @@
 def end_kernel(pieces, layers, tile, *refs):
     others = pieces * (layers - 1)
     column_refs, row_refs, rest = refs[:others], refs[others : others + pieces], refs[others + pieces :]
-    own_ref, _, out_ref, share_ref, columns_buf, sems = rest
+    own_ref, _, out_ref, share_ref, columns_buf, last_buf, sems = rest
     r, c, layer = (lax.axis_index(axis) for axis in AXES)
     half, tile_rows, _ = row_refs[0].shape
     own_lines = half * tile // LANES
@@ -216,19 +235,26 @@
         fill_columns(
             columns_buf.at[at], column_refs[at * pieces : (at + 1) * pieces], plane_slots(pieces), r, c, owner
         )
+    last_buf[...] = row_refs[-1][...]
+    if pieces == 4:
+
+        @pl.when(r == c)
+        def _():
+            take_rows(last_buf, own_ref, c, line_steps(pieces)[-1], pieces)
+
     stores = []
-    for step, row_ref in enumerate(row_refs):
-        first_row = partner(c, step, pieces) * tile_rows
+    for at_row, row_ref in enumerate((*row_refs[:-1], last_buf)):
+        first_row = partner(c, line_steps(pieces)[at_row], pieces) * tile_rows
         rows = row_ref[...]
         for at, owner in enumerate(owners):
             subtract_product(share_ref, rows, columns_buf[at], tile, first_row, owner * own_lines, per_row)
-        if step == pieces - 1:
+        if at_row == pieces - 1:
             subtract_product(share_ref, rows, own_ref[...], tile, first_row, layer * own_lines, per_row)
         for k in range(half):
             lines = tile_rows * per_row
             start = pl.multiple_of((k * tile + first_row) * per_row, lines)
             store = pltpu.make_async_copy(
-                share_ref.at[pl.ds(start, lines)], out_ref.at[pl.ds(start, lines)], sems.at[step * half + k]
+                share_ref.at[pl.ds(start, lines)], out_ref.at[pl.ds(start, lines)], sems.at[at_row * half + k]
             )
             store.start()
             stores.append(store)
@@ -251,6 +277,7 @@
         out_specs=[pl.BlockSpec(memory_space=pltpu.HBM), pl.BlockSpec(memory_space=pltpu.VMEM)],
         scratch_shapes=[
             pltpu.VMEM((layers - 1, *own_columns.shape), jnp.bfloat16),
+            pltpu.VMEM(row_pieces[0].shape, jnp.bfloat16),
             pltpu.SemaphoreType.DMA((half * pieces,)),
         ],
         input_output_aliases={len(operands) - 1: 1},
@@ -272,7 +299,7 @@
     )
     share = load_share(factor, trailing.reshape(-1, LANES), layers)
     loaded_factor, share = lax.optimization_barrier((factor, share))
-    line = gather_line(factor, loaded_factor, count)
+    line = gather_line(factor, loaded_factor, moved, count)
     plane = [moved]
     for step in range(1, count):
         pairs = [
@@ -285,8 +312,8 @@
     for shift in range(1, layers):
         pairs = [((l + shift) % layers, l) for l in range(layers)]
         others += [lax.ppermute(piece, "layer", pairs) for piece in plane]
-    share, own_columns, near = begin_update(plane, line[:-1], share, layers, tile)
-    rows = [line[0], near, *line[2:]]
+    share, own_columns, *rows = begin_update(plane, line[:-1], share, layers, tile)
+    rows = [line[0], *rows, line[-1]]
     result = end_update(others, rows, own_columns, share, layers, tile)
     return result.reshape(half, 1, tile, col_tiles, 1, tile)
 

time: 20 us -> 21.7 us (1.085)
  the two profiles are of different devices: /device:TPU:0 before, /device:TPU:4 now
where the time goes in v19:
time: 21.7 us; the launch traced here: 21.6 us
  starting transfers between devices  10.6 us (49%)
  waiting for transfers between devices  5.71 us (26%)
  Pallas kernels  5.11 us (24%)
    ppermute x3, waiting for transfers between devices, move(): lax.ppermute(x, ('row', 'col'), [(a * count + b, r * count + c) for (r, c...  3.54 us
    ppermute x3, starting transfers between devices, move(): lax.ppermute(x, ('row', 'col'), [(a * count + b, r * count + c) for (r, c...  3.49 us
    ppermute x3, starting transfers between devices, per_device(): plane.append(lax.ppermute(moved, ('row', 'col'), pairs))  3.49 us
    ppermute x1, starting transfers between devices, per_device(): lax.ppermute(factor, ('row', 'col'), [(a * count + b, slots[a][b] * count...  2.59 us
    ppermute x1, waiting for transfers between devices, per_device(): lax.ppermute(factor, ('row', 'col'), [(a * count + b, slots[a][b] * count...  2.16 us
    pallas_call x1, Pallas kernels, end_update(): pl.pallas_call(body, out_shape=[jax.ShapeDtypeStruct(share.shape, jnp.flo...  1.7 us
    pallas_call x1, Pallas kernels, load_share(): pl.pallas_call(load_kernel, out_shape=jax.ShapeDtypeStruct((rows, LANES),...  1.6 us
    pallas_call x1, Pallas kernels, make_factor(): pl.pallas_call(factor_kernel, out_shape=jax.ShapeDtypeStruct((half, tile_...  1.34 us
  transfers between devices with their start and end apart: 11, of which 2 were waited for; matrix products, arithmetic and copies ran while one was open for 0% of the time, Pallas kernels for 10%

profile of v19, /device:TPU:4, one launch (start us, length us, event | category | flops | bytes accessed | tf_op | source)
XLA Modules:
  0.0 21.6 jit_solution(15384419735541558484)
XLA Ops:
  0.0 1.3 %factor.1.after_ref.refs_4_ = bf16[2,64,256]{2,1,0:T(8,128)(2,1)S(1)} custom-call(f32[4,1,64,256]{3,2,1,0:T(8,128)} %panel_ref.1, f32[256,256]{1,0:T(8,128)} %inverse_ref.1), custom_call_target="tpu_custom_call" | custom-call | tf_op jit(solution)/shard_map/factor/pallas_call | solution.py:55
  1.4 2.6 %collective-permute-start = (bf16[2,64,256]{2,1,0:T(8,128)(2,1)S(1)}, bf16[2,64,256]{2,1,0:T(8,128)(2,1)S(1)}, u32[]{:S(2)}, u32[]{:S(2)}) collective-permute-start(bf16[2,64,256]{2,1,0:T(8,128)(2,1)S(1)} %factor.1.after_ref.refs_4_), channel_id=1, source_target_pairs={{0,24},{2,0},{4,8},{6,16},{8,26},{10,18},{12,2},{14,10},{16,4},{18... | collective-permute-start | bytes 196616 | tf_op jit(solution)/shard_map/ppermute | solution.py:297
  3.9 1.6 %load_share.1.refs_7_ = f32[4096,128]{1,0:T(8,128)S(1)} custom-call(bf16[2,64,256]{2,1,0:T(8,128)(2,1)S(1)} %factor.1.after_ref.refs_4_, f32[8192,128]{1,0:T(8,128)} %bitcast.2), custom_call_target="tpu_custom_call" | custom-call | bytes 4194304 | tf_op jit(solution)/shard_map/load_share/pallas_call | solution.py:135
  5.5 0.7 %collective-permute-start.9 = (bf16[2,64,256]{2,1,0:T(8,128)(2,1)S(1)}, bf16[2,64,256]{2,1,0:T(8,128)(2,1)S(1)}, u32[]{:S(2)}, u32[]{:S(2)}) collective-permute-start(bf16[2,64,256]{2,1,0:T(8,128)(2,1)S(1)} %factor.1.after_ref.refs_4_), channel_id=1, source_target_pairs={{8,0},{0,2},{6,4},{4,6},{10,8},{2,10},{14,12},{12,14},{18,16},{16,... | collective-permute-start | bytes 196616 | tf_op jit(solution)/shard_map/ppermute | solution.py:103
  6.2 0.0 collective-permute-start.8
  6.2 2.2 %collective-permute-done.refs_0_ = bf16[2,64,256]{2,1,0:T(8,128)(2,1)S(1)} collective-permute-done((bf16[2,64,256]{2,1,0:T(8,128)(2,1)S(1)}, bf16[2,64,256]{2,1,0:T(8,128)(2,1)S(1)}, u32[]{:S(2)}, u32[]{:S(2)}) %collective-permute-start) | collective-permute-done | bytes 65568 | tf_op jit(solution)/shard_map/ppermute | solution.py:297
  8.4 1.7 %collective-permute-start.6 = (bf16[2,64,256]{2,1,0:T(8,128)(2,1)S(1)}, bf16[2,64,256]{2,1,0:T(8,128)(2,1)S(1)}, u32[]{:S(2)}, u32[]{:S(2)}) collective-permute-start(bf16[2,64,256]{2,1,0:T(8,128)(2,1)S(1)} %collective-permute-done.refs_0_), channel_id=1, source_target_pairs={{24,0},{26,2},{28,4},{30,6},{16,8},{18,10},{20,12},{22,14},{8,16},... | collective-permute-start | bytes 196616 | tf_op jit(solution)/shard_map/ppermute | solution.py:310
  10.1 0.5 %collective-permute-start.4 = (bf16[2,64,256]{2,1,0:T(8,128)(2,1)S(1)}, bf16[2,64,256]{2,1,0:T(8,128)(2,1)S(1)}, u32[]{:S(2)}, u32[]{:S(2)}) collective-permute-start(bf16[2,64,256]{2,1,0:T(8,128)(2,1)S(1)} %collective-permute-done.refs_0_), channel_id=1, source_target_pairs={{16,0},{10,2},{12,4},{14,6},{24,8},{2,10},{4,12},{6,14},{0,16},{26... | collective-permute-start | bytes 196616 | tf_op jit(solution)/shard_map/ppermute | solution.py:310
  10.6 1.3 %collective-permute-start.2 = (bf16[2,64,256]{2,1,0:T(8,128)(2,1)S(1)}, bf16[2,64,256]{2,1,0:T(8,128)(2,1)S(1)}, u32[]{:S(2)}, u32[]{:S(2)}) collective-permute-start(bf16[2,64,256]{2,1,0:T(8,128)(2,1)S(1)} %collective-permute-done.refs_0_), channel_id=1, source_target_pairs={{8,0},{18,2},{20,4},{22,6},{0,8},{26,10},{28,12},{30,14},{24,16},{... | collective-permute-start | bytes 196616 | tf_op jit(solution)/shard_map/ppermute | solution.py:310
  11.9 0.0 collective-permute-done.9.refs_6_
  11.9 0.0 collective-permute-done.8.refs_5_
  11.9 2.8 %collective-permute-start.10 = (bf16[2,64,256]{2,1,0:T(8,128)(2,1)S(1)}, bf16[2,64,256]{2,1,0:T(8,128)(2,1)S(1)}, u32[]{:S(2)}, u32[]{:S(2)}) collective-permute-start(bf16[2,64,256]{2,1,0:T(8,128)(2,1)S(1)} %select_select_fusion), channel_id=1, source_target_pairs={{0,0},{6,2},{2,4},{4,6},{10,8},{8,10},{14,12},{12,14},{22,16},{16,... | collective-permute-start | bytes 196616 | tf_op jit(solution)/shard_map/ppermute | solution.py:103
  14.7 0.1 collective-permute-start.1
  14.8 0.0 collective-permute-done.6.refs_3_
  14.8 0.5 %collective-permute-start.7 = (bf16[2,64,256]{2,1,0:T(8,128)(2,1)S(1)}, bf16[2,64,256]{2,1,0:T(8,128)(2,1)S(1)}, u32[]{:S(2)}, u32[]{:S(2)}) collective-permute-start(bf16[2,64,256]{2,1,0:T(8,128)(2,1)S(1)} %collective-permute-done.6.refs_3_), channel_id=1, source_target_pairs={{1,0},{0,1},{3,2},{2,3},{5,4},{4,5},{7,6},{6,7},{9,8},{8,9},{11,10... | collective-permute-start | bytes 196616 | tf_op jit(solution)/shard_map/ppermute | solution.py:314
  15.3 0.0 collective-permute-done.4.refs_2_
  15.3 0.1 collective-permute-start.5
  15.4 0.0 collective-permute-done.2.refs_1_
  15.4 0.4 %collective-permute-start.3 = (bf16[2,64,256]{2,1,0:T(8,128)(2,1)S(1)}, bf16[2,64,256]{2,1,0:T(8,128)(2,1)S(1)}, u32[]{:S(2)}, u32[]{:S(2)}) collective-permute-start(bf16[2,64,256]{2,1,0:T(8,128)(2,1)S(1)} %collective-permute-done.2.refs_1_), channel_id=1, source_target_pairs={{1,0},{0,1},{3,2},{2,3},{5,4},{4,5},{7,6},{6,7},{9,8},{8,9},{11,10... | collective-permute-start | bytes 196616 | tf_op jit(solution)/shard_map/ppermute | solution.py:314
  15.8 0.5 %begin_update.1 = (f32[4096,128]{1,0:T(8,128)S(1)}, bf16[512,256]{1,0:T(8,128)(2,1)S(1)}, bf16[2,64,256]{2,1,0:T(8,128)(2,1)S(1)}, bf16[2,64,256]{2,1,0:T(8,128)(2,1)S(1)}) custom-call(bf16[2,64,256]{2,1,0:T(8,128)(2,1)S(1)} %collective-permute-done.refs_0_, bf16[2,64,256]{2,1,0:T(8,128)(2,1)S(1)} %collective-permute-done.2.refs_1_, ...), custom_call_target="tpu_custom_call", output_to_operand_aliasing={{0}: (7, {})} | custom-call | tf_op jit(solution)/shard_map/begin_update/pallas_call | solution.py:210
  16.3 0.0 collective-permute-done.1.refs_0_
  16.3 3.5 %collective-permute-done.10.refs_7_ = bf16[2,64,256]{2,1,0:T(8,128)(2,1)S(1)} collective-permute-done((bf16[2,64,256]{2,1,0:T(8,128)(2,1)S(1)}, bf16[2,64,256]{2,1,0:T(8,128)(2,1)S(1)}, u32[]{:S(2)}, u32[]{:S(2)}) %collective-permute-start.10) | collective-permute-done | bytes 65568 | tf_op jit(solution)/shard_map/ppermute | solution.py:103
  19.8 0.0 collective-permute-done.7.refs_3_
  19.8 0.0 collective-permute-done.5.refs_2_
  19.9 0.0 collective-permute-done.3.refs_1_
  19.9 1.7 %end_update.1 = (f32[4096,128]{1,0:T(8,128)}, f32[4096,128]{1,0:T(8,128)S(1)}) custom-call(bf16[2,64,256]{2,1,0:T(8,128)(2,1)S(1)} %collective-permute-done.1.refs_0_, bf16[2,64,256]{2,1,0:T(8,128)(2,1)S(1)} %collective-permute-done.3.refs_1_, bf16[2,64,256]{2,1,0:T(8,128)(2,1)S(1)} %collective-permute-done.5.refs_2_, ...), custom_call_target="tpu_custom_call", output_to_operand_aliasing={{1}: (9, {})} | custom-call | tf_op jit(solution)/shard_map/end_update/pallas_call | solution.py:273
  (1 shorter events, 0.0 us)
Async XLA Ops:
  1.4 7.0 %collective-permute-start = (bf16[2,64,256]{2,1,0:T(8,128)(2,1)S(1)}, bf16[2,64,256]{2,1,0:T(8,128)(2,1)S(1)}, u32[]{:S(2)}, u32[]{:S(2)}) collective-permute-start(bf16[2,64,256]{2,1,0:T(8,128)(2,1)S(1)} %factor.1.after_ref.refs_4_), channel_id=1, source_target_pairs={{0,24},{2,0},{4,8},{6,16},{8,26},{10,18},{12,2},{14,10},{16,4},{18... | collective-permute-start | bytes 196616 | tf_op jit(solution)/shard_map/ppermute | solution.py:297
  5.5 6.3 %collective-permute-start.9 = (bf16[2,64,256]{2,1,0:T(8,128)(2,1)S(1)}, bf16[2,64,256]{2,1,0:T(8,128)(2,1)S(1)}, u32[]{:S(2)}, u32[]{:S(2)}) collective-permute-start(bf16[2,64,256]{2,1,0:T(8,128)(2,1)S(1)} %factor.1.after_ref.refs_4_), channel_id=1, source_target_pairs={{8,0},{0,2},{6,4},{4,6},{10,8},{2,10},{14,12},{12,14},{18,16},{16,... | collective-permute-start | bytes 196616 | tf_op jit(solution)/shard_map/ppermute | solution.py:103
  6.2 5.7 %collective-permute-start.8 = (bf16[2,64,256]{2,1,0:T(8,128)(2,1)S(1)}, bf16[2,64,256]{2,1,0:T(8,128)(2,1)S(1)}, u32[]{:S(2)}, u32[]{:S(2)}) collective-permute-start(bf16[2,64,256]{2,1,0:T(8,128)(2,1)S(1)} %factor.1.after_ref.refs_4_), channel_id=1, source_target_pairs={{16,0},{6,2},{0,4},{2,6},{12,8},{26,10},{8,12},{10,14},{20,16},{22... | collective-permute-start | bytes 196616 | tf_op jit(solution)/shard_map/ppermute | solution.py:103
  8.4 6.4 %collective-permute-start.6 = (bf16[2,64,256]{2,1,0:T(8,128)(2,1)S(1)}, bf16[2,64,256]{2,1,0:T(8,128)(2,1)S(1)}, u32[]{:S(2)}, u32[]{:S(2)}) collective-permute-start(bf16[2,64,256]{2,1,0:T(8,128)(2,1)S(1)} %collective-permute-done.refs_0_), channel_id=1, source_target_pairs={{24,0},{26,2},{28,4},{30,6},{16,8},{18,10},{20,12},{22,14},{8,16},... | collective-permute-start | bytes 196616 | tf_op jit(solution)/shard_map/ppermute | solution.py:310
  10.1 5.2 %collective-permute-start.4 = (bf16[2,64,256]{2,1,0:T(8,128)(2,1)S(1)}, bf16[2,64,256]{2,1,0:T(8,128)(2,1)S(1)}, u32[]{:S(2)}, u32[]{:S(2)}) collective-permute-start(bf16[2,64,256]{2,1,0:T(8,128)(2,1)S(1)} %collective-permute-done.refs_0_), channel_id=1, source_target_pairs={{16,0},{10,2},{12,4},{14,6},{24,8},{2,10},{4,12},{6,14},{0,16},{26... | collective-permute-start | bytes 196616 | tf_op jit(solution)/shard_map/ppermute | solution.py:310
  10.6 4.8 %collective-permute-start.2 = (bf16[2,64,256]{2,1,0:T(8,128)(2,1)S(1)}, bf16[2,64,256]{2,1,0:T(8,128)(2,1)S(1)}, u32[]{:S(2)}, u32[]{:S(2)}) collective-permute-start(bf16[2,64,256]{2,1,0:T(8,128)(2,1)S(1)} %collective-permute-done.refs_0_), channel_id=1, source_target_pairs={{8,0},{18,2},{20,4},{22,6},{0,8},{26,10},{28,12},{30,14},{24,16},{... | collective-permute-start | bytes 196616 | tf_op jit(solution)/shard_map/ppermute | solution.py:310
  11.9 8.0 %collective-permute-start.10 = (bf16[2,64,256]{2,1,0:T(8,128)(2,1)S(1)}, bf16[2,64,256]{2,1,0:T(8,128)(2,1)S(1)}, u32[]{:S(2)}, u32[]{:S(2)}) collective-permute-start(bf16[2,64,256]{2,1,0:T(8,128)(2,1)S(1)} %select_select_fusion), channel_id=1, source_target_pairs={{0,0},{6,2},{2,4},{4,6},{10,8},{8,10},{14,12},{12,14},{22,16},{16,... | collective-permute-start | bytes 196616 | tf_op jit(solution)/shard_map/ppermute | solution.py:103
  14.7 1.6 %collective-permute-start.1 = (bf16[2,64,256]{2,1,0:T(8,128)(2,1)S(1)}, bf16[2,64,256]{2,1,0:T(8,128)(2,1)S(1)}, u32[]{:S(2)}, u32[]{:S(2)}) collective-permute-start(bf16[2,64,256]{2,1,0:T(8,128)(2,1)S(1)} %collective-permute-done.refs_0_), channel_id=1, source_target_pairs={{1,0},{0,1},{3,2},{2,3},{5,4},{4,5},{7,6},{6,7},{9,8},{8,9},{11,10... | collective-permute-start | bytes 196616 | tf_op jit(solution)/shard_map/ppermute | solution.py:314
  14.8 5.0 %collective-permute-start.7 = (bf16[2,64,256]{2,1,0:T(8,128)(2,1)S(1)}, bf16[2,64,256]{2,1,0:T(8,128)(2,1)S(1)}, u32[]{:S(2)}, u32[]{:S(2)}) collective-permute-start(bf16[2,64,256]{2,1,0:T(8,128)(2,1)S(1)} %collective-permute-done.6.refs_3_), channel_id=1, source_target_pairs={{1,0},{0,1},{3,2},{2,3},{5,4},{4,5},{7,6},{6,7},{9,8},{8,9},{11,10... | collective-permute-start | bytes 196616 | tf_op jit(solution)/shard_map/ppermute | solution.py:314
  15.3 4.5 %collective-permute-start.5 = (bf16[2,64,256]{2,1,0:T(8,128)(2,1)S(1)}, bf16[2,64,256]{2,1,0:T(8,128)(2,1)S(1)}, u32[]{:S(2)}, u32[]{:S(2)}) collective-permute-start(bf16[2,64,256]{2,1,0:T(8,128)(2,1)S(1)} %collective-permute-done.4.refs_2_), channel_id=1, source_target_pairs={{1,0},{0,1},{3,2},{2,3},{5,4},{4,5},{7,6},{6,7},{9,8},{8,9},{11,10... | collective-permute-start | bytes 196616 | tf_op jit(solution)/shard_map/ppermute | solution.py:314
  15.4 4.5 %collective-permute-start.3 = (bf16[2,64,256]{2,1,0:T(8,128)(2,1)S(1)}, bf16[2,64,256]{2,1,0:T(8,128)(2,1)S(1)}, u32[]{:S(2)}, u32[]{:S(2)}) collective-permute-start(bf16[2,64,256]{2,1,0:T(8,128)(2,1)S(1)} %collective-permute-done.2.refs_1_), channel_id=1, source_target_pairs={{1,0},{0,1},{3,2},{2,3},{5,4},{4,5},{7,6},{6,7},{9,8},{8,9},{11,10... | collective-permute-start | bytes 196616 | tf_op jit(solution)/shard_map/ppermute | solution.py:314

commit v20 on v19

--- a/solution.py
+++ b/solution.py
@@ -111,14 +111,11 @@
         return line
     places = [(r, c) for r in range(count) for c in range(count)]
     near = move(late_factor, {(r, c): (r ^ 1, c) if r == c else (r, c ^ 1) for r, c in places}, count)
-    far = move(late_factor, {(r, c): (r ^ 2, c) if r == c else (r, c ^ 2) for r, c in places}, count)
+    far = move(late_factor, {(r, c): (r ^ 2, c) if r == c and r % 2 == 1 else (r, c ^ 2) for r, c in places}, count)
     r, c = lax.axis_index("row"), lax.axis_index("col")
-    odd = r % 2 == 1
-    sent = jnp.where(~odd & (c == r ^ 3), near, far)
-    sent = jnp.where(odd & (c == r), moved, sent)
-    sent = jnp.where(~odd & (c == r ^ 1), late_factor, sent)
-    cycle = {0: 0, 2: 1, 3: 2, 1: 3}
-    last = move(sent, {(r, c): (r, c ^ 1) if r % 2 == 1 else (r, r ^ cycle[c ^ r]) for r, c in places}, count)
+    relayed = jnp.where((r == c) & (r % 2 == 1), moved, far)
+    relayed = jnp.where(r == c ^ 1, near, relayed)
+    last = move(relayed, {(r, c): (r, c ^ 1) for r, c in places}, count)
     return [factor, far, near, last]
 
 

time: 21.7 us -> 20.4 us (0.940)
  the two profiles are of different devices: /device:TPU:4 before, /device:TPU:0 now
where the time goes in v20:
time: 20.4 us; the launch traced here: 20.3 us
  starting transfers between devices  11.4 us (56%)
  Pallas kernels  5.13 us (25%)
  waiting for transfers between devices  3.69 us (18%)
    ppermute x1, starting transfers between devices, per_device(): lax.ppermute(factor, ('row', 'col'), [(a * count + b, slots[a][b] * count...  3.95 us
    ppermute x3, starting transfers between devices, move(): lax.ppermute(x, ('row', 'col'), [(a * count + b, r * count + c) for (r, c...  3.93 us
    ppermute x3, starting transfers between devices, per_device(): plane.append(lax.ppermute(moved, ('row', 'col'), pairs))  3.49 us
    ppermute x3, waiting for transfers between devices, per_device(): plane.append(lax.ppermute(moved, ('row', 'col'), pairs))  2.96 us
    pallas_call x1, Pallas kernels, end_update(): pl.pallas_call(body, out_shape=[jax.ShapeDtypeStruct(share.shape, jnp.flo...  1.7 us
    pallas_call x1, Pallas kernels, load_share(): pl.pallas_call(load_kernel, out_shape=jax.ShapeDtypeStruct((rows, LANES),...  1.6 us
    pallas_call x1, Pallas kernels, make_factor(): pl.pallas_call(factor_kernel, out_shape=jax.ShapeDtypeStruct((half, tile_...  1.34 us
    ppermute x4, waiting for transfers between devices, per_device(): others += [lax.ppermute(piece, 'layer', pairs) for piece in plane]  0.72 us
  transfers between devices with their start and end apart: 11, of which 4 were waited for; matrix products, arithmetic and copies ran while one was open for 0% of the time, Pallas kernels for 10%

profile of v20, /device:TPU:0, one launch (start us, length us, event | category | flops | bytes accessed | tf_op | source)
XLA Modules:
  0.0 20.3 jit_solution(2167955004286021664)
XLA Ops:
  0.0 1.3 %factor.1.after_ref.refs_4_ = bf16[2,64,256]{2,1,0:T(8,128)(2,1)S(1)} custom-call(f32[4,1,64,256]{3,2,1,0:T(8,128)} %panel_ref.1, f32[256,256]{1,0:T(8,128)} %inverse_ref.1), custom_call_target="tpu_custom_call" | custom-call | tf_op jit(solution)/shard_map/factor/pallas_call | solution.py:55
  1.4 3.9 %collective-permute-start = (bf16[2,64,256]{2,1,0:T(8,128)(2,1)S(1)}, bf16[2,64,256]{2,1,0:T(8,128)(2,1)S(1)}, u32[]{:S(2)}, u32[]{:S(2)}) collective-permute-start(bf16[2,64,256]{2,1,0:T(8,128)(2,1)S(1)} %factor.1.after_ref.refs_4_), channel_id=1, source_target_pairs={{0,24},{2,0},{4,8},{6,16},{8,26},{10,18},{12,2},{14,10},{16,4},{18... | collective-permute-start | bytes 196616 | tf_op jit(solution)/shard_map/ppermute | solution.py:294
  5.3 1.6 %load_share.1.refs_7_ = f32[4096,128]{1,0:T(8,128)S(1)} custom-call(bf16[2,64,256]{2,1,0:T(8,128)(2,1)S(1)} %factor.1.after_ref.refs_4_, f32[8192,128]{1,0:T(8,128)} %bitcast.2), custom_call_target="tpu_custom_call" | custom-call | bytes 4194304 | tf_op jit(solution)/shard_map/load_share/pallas_call | solution.py:132
  6.9 0.1 collective-permute-start.9
  7.0 2.9 %collective-permute-start.8 = (bf16[2,64,256]{2,1,0:T(8,128)(2,1)S(1)}, bf16[2,64,256]{2,1,0:T(8,128)(2,1)S(1)}, u32[]{:S(2)}, u32[]{:S(2)}) collective-permute-start(bf16[2,64,256]{2,1,0:T(8,128)(2,1)S(1)} %factor.1.after_ref.refs_4_), channel_id=1, source_target_pairs={{4,0},{6,2},{0,4},{2,6},{12,8},{26,10},{8,12},{10,14},{20,16},{22,... | collective-permute-start | bytes 196616 | tf_op jit(solution)/shard_map/ppermute | solution.py:103
  9.8 0.0 collective-permute-done.refs_0_
  9.9 1.7 %collective-permute-start.6 = (bf16[2,64,256]{2,1,0:T(8,128)(2,1)S(1)}, bf16[2,64,256]{2,1,0:T(8,128)(2,1)S(1)}, u32[]{:S(2)}, u32[]{:S(2)}) collective-permute-start(bf16[2,64,256]{2,1,0:T(8,128)(2,1)S(1)} %collective-permute-done.refs_0_), channel_id=1, source_target_pairs={{24,0},{26,2},{28,4},{30,6},{16,8},{18,10},{20,12},{22,14},{8,16},... | collective-permute-start | bytes 196616 | tf_op jit(solution)/shard_map/ppermute | solution.py:307
  11.5 1.6 %collective-permute-start.4 = (bf16[2,64,256]{2,1,0:T(8,128)(2,1)S(1)}, bf16[2,64,256]{2,1,0:T(8,128)(2,1)S(1)}, u32[]{:S(2)}, u32[]{:S(2)}) collective-permute-start(bf16[2,64,256]{2,1,0:T(8,128)(2,1)S(1)} %collective-permute-done.refs_0_), channel_id=1, source_target_pairs={{16,0},{10,2},{12,4},{14,6},{24,8},{2,10},{4,12},{6,14},{0,16},{26... | collective-permute-start | bytes 196616 | tf_op jit(solution)/shard_map/ppermute | solution.py:307
  13.1 0.3 %collective-permute-start.2 = (bf16[2,64,256]{2,1,0:T(8,128)(2,1)S(1)}, bf16[2,64,256]{2,1,0:T(8,128)(2,1)S(1)}, u32[]{:S(2)}, u32[]{:S(2)}) collective-permute-start(bf16[2,64,256]{2,1,0:T(8,128)(2,1)S(1)} %collective-permute-done.refs_0_), channel_id=1, source_target_pairs={{8,0},{18,2},{20,4},{22,6},{0,8},{26,10},{28,12},{30,14},{24,16},{... | collective-permute-start | bytes 196616 | tf_op jit(solution)/shard_map/ppermute | solution.py:307
  13.3 0.0 collective-permute-done.9.refs_6_
  13.3 0.0 collective-permute-done.8.refs_5_
  13.4 1.0 %collective-permute-start.10 = (bf16[2,64,256]{2,1,0:T(8,128)(2,1)S(1)}, bf16[2,64,256]{2,1,0:T(8,128)(2,1)S(1)}, u32[]{:S(2)}, u32[]{:S(2)}) collective-permute-start(bf16[2,64,256]{2,1,0:T(8,128)(2,1)S(1)} %select_select_fusion), channel_id=1, source_target_pairs={{2,0},{0,2},{6,4},{4,6},{10,8},{8,10},{14,12},{12,14},{18,16},{16,... | collective-permute-start | bytes 196616 | tf_op jit(solution)/shard_map/ppermute | solution.py:103
  14.4 0.0 collective-permute-start.1
  14.4 1.1 %collective-permute-done.6.refs_3_ = bf16[2,64,256]{2,1,0:T(8,128)(2,1)S(1)} collective-permute-done((bf16[2,64,256]{2,1,0:T(8,128)(2,1)S(1)}, bf16[2,64,256]{2,1,0:T(8,128)(2,1)S(1)}, u32[]{:S(2)}, u32[]{:S(2)}) %collective-permute-start.6) | collective-permute-done | bytes 65568 | tf_op jit(solution)/shard_map/ppermute | solution.py:307
  15.5 0.0 collective-permute-start.7
  15.5 0.6 %collective-permute-done.4.refs_2_ = bf16[2,64,256]{2,1,0:T(8,128)(2,1)S(1)} collective-permute-done((bf16[2,64,256]{2,1,0:T(8,128)(2,1)S(1)}, bf16[2,64,256]{2,1,0:T(8,128)(2,1)S(1)}, u32[]{:S(2)}, u32[]{:S(2)}) %collective-permute-start.4) | collective-permute-done | bytes 65568 | tf_op jit(solution)/shard_map/ppermute | solution.py:307
  16.1 0.0 collective-permute-start.5
  16.1 1.2 %collective-permute-done.2.refs_1_ = bf16[2,64,256]{2,1,0:T(8,128)(2,1)S(1)} collective-permute-done((bf16[2,64,256]{2,1,0:T(8,128)(2,1)S(1)}, bf16[2,64,256]{2,1,0:T(8,128)(2,1)S(1)}, u32[]{:S(2)}, u32[]{:S(2)}) %collective-permute-start.2) | collective-permute-done | bytes 65568 | tf_op jit(solution)/shard_map/ppermute | solution.py:307
  17.3 0.0 collective-permute-start.3
  17.3 0.5 %begin_update.1 = (f32[4096,128]{1,0:T(8,128)S(1)}, bf16[512,256]{1,0:T(8,128)(2,1)S(1)}, bf16[2,64,256]{2,1,0:T(8,128)(2,1)S(1)}, bf16[2,64,256]{2,1,0:T(8,128)(2,1)S(1)}) custom-call(bf16[2,64,256]{2,1,0:T(8,128)(2,1)S(1)} %collective-permute-done.refs_0_, bf16[2,64,256]{2,1,0:T(8,128)(2,1)S(1)} %collective-permute-done.2.refs_1_, ...), custom_call_target="tpu_custom_call", output_to_operand_aliasing={{0}: (7, {})} | custom-call | tf_op jit(solution)/shard_map/begin_update/pallas_call | solution.py:207
  17.8 0.0 collective-permute-done.1.refs_0_
  17.8 0.0 collective-permute-done.10.refs_7_
  17.9 0.0 collective-permute-done.7.refs_3_
  17.9 0.0 collective-permute-done.5.refs_2_
  17.9 0.7 %collective-permute-done.3.refs_1_ = bf16[2,64,256]{2,1,0:T(8,128)(2,1)S(1)} collective-permute-done((bf16[2,64,256]{2,1,0:T(8,128)(2,1)S(1)}, bf16[2,64,256]{2,1,0:T(8,128)(2,1)S(1)}, u32[]{:S(2)}, u32[]{:S(2)}) %collective-permute-start.3) | collective-permute-done | bytes 65568 | tf_op jit(solution)/shard_map/ppermute | solution.py:311
  18.6 1.7 %end_update.1 = (f32[4096,128]{1,0:T(8,128)}, f32[4096,128]{1,0:T(8,128)S(1)}) custom-call(bf16[2,64,256]{2,1,0:T(8,128)(2,1)S(1)} %collective-permute-done.1.refs_0_, bf16[2,64,256]{2,1,0:T(8,128)(2,1)S(1)} %collective-permute-done.3.refs_1_, bf16[2,64,256]{2,1,0:T(8,128)(2,1)S(1)} %collective-permute-done.5.refs_2_, ...), custom_call_target="tpu_custom_call", output_to_operand_aliasing={{1}: (9, {})} | custom-call | tf_op jit(solution)/shard_map/end_update/pallas_call | solution.py:270
  (1 shorter events, 0.0 us)
Async XLA Ops:
  1.4 8.5 %collective-permute-start = (bf16[2,64,256]{2,1,0:T(8,128)(2,1)S(1)}, bf16[2,64,256]{2,1,0:T(8,128)(2,1)S(1)}, u32[]{:S(2)}, u32[]{:S(2)}) collective-permute-start(bf16[2,64,256]{2,1,0:T(8,128)(2,1)S(1)} %factor.1.after_ref.refs_4_), channel_id=1, source_target_pairs={{0,24},{2,0},{4,8},{6,16},{8,26},{10,18},{12,2},{14,10},{16,4},{18... | collective-permute-start | bytes 196616 | tf_op jit(solution)/shard_map/ppermute | solution.py:294
  6.9 6.4 %collective-permute-start.9 = (bf16[2,64,256]{2,1,0:T(8,128)(2,1)S(1)}, bf16[2,64,256]{2,1,0:T(8,128)(2,1)S(1)}, u32[]{:S(2)}, u32[]{:S(2)}) collective-permute-start(bf16[2,64,256]{2,1,0:T(8,128)(2,1)S(1)} %factor.1.after_ref.refs_4_), channel_id=1, source_target_pairs={{8,0},{0,2},{6,4},{4,6},{10,8},{2,10},{14,12},{12,14},{18,16},{16,... | collective-permute-start | bytes 196616 | tf_op jit(solution)/shard_map/ppermute | solution.py:103
  7.0 6.4 %collective-permute-start.8 = (bf16[2,64,256]{2,1,0:T(8,128)(2,1)S(1)}, bf16[2,64,256]{2,1,0:T(8,128)(2,1)S(1)}, u32[]{:S(2)}, u32[]{:S(2)}) collective-permute-start(bf16[2,64,256]{2,1,0:T(8,128)(2,1)S(1)} %factor.1.after_ref.refs_4_), channel_id=1, source_target_pairs={{4,0},{6,2},{0,4},{2,6},{12,8},{26,10},{8,12},{10,14},{20,16},{22,... | collective-permute-start | bytes 196616 | tf_op jit(solution)/shard_map/ppermute | solution.py:103
  9.9 5.7 %collective-permute-start.6 = (bf16[2,64,256]{2,1,0:T(8,128)(2,1)S(1)}, bf16[2,64,256]{2,1,0:T(8,128)(2,1)S(1)}, u32[]{:S(2)}, u32[]{:S(2)}) collective-permute-start(bf16[2,64,256]{2,1,0:T(8,128)(2,1)S(1)} %collective-permute-done.refs_0_), channel_id=1, source_target_pairs={{24,0},{26,2},{28,4},{30,6},{16,8},{18,10},{20,12},{22,14},{8,16},... | collective-permute-start | bytes 196616 | tf_op jit(solution)/shard_map/ppermute | solution.py:307
  11.5 4.6 %collective-permute-start.4 = (bf16[2,64,256]{2,1,0:T(8,128)(2,1)S(1)}, bf16[2,64,256]{2,1,0:T(8,128)(2,1)S(1)}, u32[]{:S(2)}, u32[]{:S(2)}) collective-permute-start(bf16[2,64,256]{2,1,0:T(8,128)(2,1)S(1)} %collective-permute-done.refs_0_), channel_id=1, source_target_pairs={{16,0},{10,2},{12,4},{14,6},{24,8},{2,10},{4,12},{6,14},{0,16},{26... | collective-permute-start | bytes 196616 | tf_op jit(solution)/shard_map/ppermute | solution.py:307
  13.1 4.3 %collective-permute-start.2 = (bf16[2,64,256]{2,1,0:T(8,128)(2,1)S(1)}, bf16[2,64,256]{2,1,0:T(8,128)(2,1)S(1)}, u32[]{:S(2)}, u32[]{:S(2)}) collective-permute-start(bf16[2,64,256]{2,1,0:T(8,128)(2,1)S(1)} %collective-permute-done.refs_0_), channel_id=1, source_target_pairs={{8,0},{18,2},{20,4},{22,6},{0,8},{26,10},{28,12},{30,14},{24,16},{... | collective-permute-start | bytes 196616 | tf_op jit(solution)/shard_map/ppermute | solution.py:307
  13.4 4.5 %collective-permute-start.10 = (bf16[2,64,256]{2,1,0:T(8,128)(2,1)S(1)}, bf16[2,64,256]{2,1,0:T(8,128)(2,1)S(1)}, u32[]{:S(2)}, u32[]{:S(2)}) collective-permute-start(bf16[2,64,256]{2,1,0:T(8,128)(2,1)S(1)} %select_select_fusion), channel_id=1, source_target_pairs={{2,0},{0,2},{6,4},{4,6},{10,8},{8,10},{14,12},{12,14},{18,16},{16,... | collective-permute-start | bytes 196616 | tf_op jit(solution)/shard_map/ppermute | solution.py:103
  14.4 3.5 %collective-permute-start.1 = (bf16[2,64,256]{2,1,0:T(8,128)(2,1)S(1)}, bf16[2,64,256]{2,1,0:T(8,128)(2,1)S(1)}, u32[]{:S(2)}, u32[]{:S(2)}) collective-permute-start(bf16[2,64,256]{2,1,0:T(8,128)(2,1)S(1)} %collective-permute-done.refs_0_), channel_id=1, source_target_pairs={{1,0},{0,1},{3,2},{2,3},{5,4},{4,5},{7,6},{6,7},{9,8},{8,9},{11,10... | collective-permute-start | bytes 196616 | tf_op jit(solution)/shard_map/ppermute | solution.py:311
  15.5 2.3 %collective-permute-start.7 = (bf16[2,64,256]{2,1,0:T(8,128)(2,1)S(1)}, bf16[2,64,256]{2,1,0:T(8,128)(2,1)S(1)}, u32[]{:S(2)}, u32[]{:S(2)}) collective-permute-start(bf16[2,64,256]{2,1,0:T(8,128)(2,1)S(1)} %collective-permute-done.6.refs_3_), channel_id=1, source_target_pairs={{1,0},{0,1},{3,2},{2,3},{5,4},{4,5},{7,6},{6,7},{9,8},{8,9},{11,10... | collective-permute-start | bytes 196616 | tf_op jit(solution)/shard_map/ppermute | solution.py:311
  16.1 1.8 %collective-permute-start.5 = (bf16[2,64,256]{2,1,0:T(8,128)(2,1)S(1)}, bf16[2,64,256]{2,1,0:T(8,128)(2,1)S(1)}, u32[]{:S(2)}, u32[]{:S(2)}) collective-permute-start(bf16[2,64,256]{2,1,0:T(8,128)(2,1)S(1)} %collective-permute-done.4.refs_2_), channel_id=1, source_target_pairs={{1,0},{0,1},{3,2},{2,3},{5,4},{4,5},{7,6},{6,7},{9,8},{8,9},{11,10... | collective-permute-start | bytes 196616 | tf_op jit(solution)/shard_map/ppermute | solution.py:311
  17.3 1.3 %collective-permute-start.3 = (bf16[2,64,256]{2,1,0:T(8,128)(2,1)S(1)}, bf16[2,64,256]{2,1,0:T(8,128)(2,1)S(1)}, u32[]{:S(2)}, u32[]{:S(2)}) collective-permute-start(bf16[2,64,256]{2,1,0:T(8,128)(2,1)S(1)} %collective-permute-done.2.refs_1_), channel_id=1, source_target_pairs={{1,0},{0,1},{3,2},{2,3},{5,4},{4,5},{7,6},{6,7},{9,8},{8,9},{11,10... | collective-permute-start | bytes 196616 | tf_op jit(solution)/shard_map/ppermute | solution.py:311

commit v21 on v20

--- a/solution.py
+++ b/solution.py
@@ -73,13 +73,13 @@
 
 def plane_slots(count):
     if count == 4:
-        return ((3, 0, 1, 2), (3, 2, 0, 1), (0, 2, 1, 3), (2, 3, 1, 0))
+        return ((3, 0, 1, 2), (3, 0, 2, 1), (0, 2, 1, 3), (2, 3, 1, 0))
     return tuple(tuple(count - 1 - b for b in range(count)) for _ in range(count))
 
 
 def plane_mates(count, plane):
     if count == 4:
-        return (0, 1, 2, 3) if plane == 0 else (0, 2, 1, 3)
+        return ((0, 3, 1, 2), (0, 1, 2, 3), (0, 2, 1, 3), (0, 2, 1, 3))[plane]
     return tuple(range(count))
 
 
@@ -145,7 +145,9 @@
     half, tile_rows, _ = pieces[0].shape
     tile = tile_rows * len(pieces)
     for step, piece in enumerate(pieces):
-        mate = jnp.where(c == 0, plane_mates(len(pieces), 0)[step], plane_mates(len(pieces), 1)[step])
+        mate = jnp.int32(plane_mates(len(pieces), 0)[step])
+        for plane in range(1, len(pieces) if len(pieces) == 4 else 1):
+            mate = jnp.where(c == plane, plane_mates(len(pieces), plane)[step], mate)
         slab = slab_of(slots, c, partner(r, mate, len(pieces)))
         for k in range(half):
             at = pl.multiple_of(k * tile + slab * tile_rows, tile_rows)
@@ -299,12 +301,15 @@
     line = gather_line(factor, loaded_factor, moved, count)
     plane = [moved]
     for step in range(1, count):
-        pairs = [
-            (partner(a, plane_mates(count, b)[step], count) * count + b, a * count + b)
-            for a in range(count)
-            for b in range(count)
-        ]
-        plane.append(lax.ppermute(moved, ("row", "col"), pairs))
+        sources = {
+            (r, c): (partner(r, plane_mates(count, c)[step], count), c) for r in range(count) for c in range(count)
+        }
+        if count == 4 and step == 1:
+            sources[0, 0], sources[1, 1] = (0, 1), (3, 0)
+        plane.append(move(moved, sources, count))
+    if count == 4:
+        r, c = lax.axis_index("row"), lax.axis_index("col")
+        plane[1] = jnp.where((r == c) & (r < 2), factor, plane[1])
     others = []
     for shift in range(1, layers):
         pairs = [((l + shift) % layers, l) for l in range(layers)]

time: 20.4 us -> 19.6 us (0.961)
  waiting for transfers between devices: 3.69 us -> 2.4 us
  starting transfers between devices: 11.4 us -> 11.8 us
    ppermute x3 -> x0, starting transfers between devices: 3.49 us -> none  [per_device(): plane.append(lax.ppermute(moved, ('row', 'col'), pairs))]
    ppermute x3 -> x6, starting transfers between devices: 3.93 us -> 7.25 us  [move(): lax.ppermute(x, ('row', 'col'), [(a * count + b, r * count + c) for (r, c...]
    ppermute x3 -> x0, waiting for transfers between devices: 2.96 us -> none  [per_device(): plane.append(lax.ppermute(moved, ('row', 'col'), pairs))]
    ppermute x3 -> x6, waiting for transfers between devices: 0.01 us -> 2.38 us  [move(): lax.ppermute(x, ('row', 'col'), [(a * count + b, r * count + c) for (r, c...]
    ppermute x4, waiting for transfers between devices: 0.72 us -> 0.01 us  [per_device(): others += [lax.ppermute(piece, 'layer', pairs) for piece in plane]]
    ppermute x4, starting transfers between devices: 0.01 us -> 0.59 us  [per_device(): others += [lax.ppermute(piece, 'layer', pairs) for piece in plane]]
  transfers between devices with their start and end apart: 11 -> 11, of which waited for: 4 -> 3; matrix products, arithmetic and copies ran while one was open for 0% -> 0% of each run, Pallas kernels for 10% -> 11%
where the time goes in v21:
time: 19.6 us; the launch traced here: 19.4 us
  starting transfers between devices  11.8 us (60%)
  Pallas kernels  5.14 us (26%)
  waiting for transfers between devices  2.4 us (12%)
    ppermute x6, starting transfers between devices, move(): lax.ppermute(x, ('row', 'col'), [(a * count + b, r * count + c) for (r, c...  7.25 us
    ppermute x1, starting transfers between devices, per_device(): lax.ppermute(factor, ('row', 'col'), [(a * count + b, slots[a][b] * count...  3.95 us
    ppermute x6, waiting for transfers between devices, move(): lax.ppermute(x, ('row', 'col'), [(a * count + b, r * count + c) for (r, c...  2.38 us
    pallas_call x1, Pallas kernels, end_update(): pl.pallas_call(body, out_shape=[jax.ShapeDtypeStruct(share.shape, jnp.flo...  1.7 us
    pallas_call x1, Pallas kernels, load_share(): pl.pallas_call(load_kernel, out_shape=jax.ShapeDtypeStruct((rows, LANES),...  1.6 us
    pallas_call x1, Pallas kernels, make_factor(): pl.pallas_call(factor_kernel, out_shape=jax.ShapeDtypeStruct((half, tile_...  1.34 us
    ppermute x4, starting transfers between devices, per_device(): others += [lax.ppermute(piece, 'layer', pairs) for piece in plane]  0.59 us
    pallas_call x1, Pallas kernels, begin_update(): pl.pallas_call(body, out_shape=[jax.ShapeDtypeStruct(share.shape, jnp.flo...  0.5 us
  transfers between devices with their start and end apart: 11, of which 3 were waited for; matrix products, arithmetic and copies ran while one was open for 0% of the time, Pallas kernels for 11%

profile of v21, /device:TPU:0, one launch (start us, length us, event | category | flops | bytes accessed | tf_op | source)
XLA Modules:
  0.0 19.4 jit_solution(14822774255833509994)
XLA Ops:
  0.0 1.3 %factor.1.after_ref.refs_4_ = bf16[2,64,256]{2,1,0:T(8,128)(2,1)S(1)} custom-call(f32[4,1,64,256]{3,2,1,0:T(8,128)} %panel_ref.1, f32[256,256]{1,0:T(8,128)} %inverse_ref.1), custom_call_target="tpu_custom_call" | custom-call | tf_op jit(solution)/shard_map/factor/pallas_call | solution.py:55
  1.4 3.9 %collective-permute-start = (bf16[2,64,256]{2,1,0:T(8,128)(2,1)S(1)}, bf16[2,64,256]{2,1,0:T(8,128)(2,1)S(1)}, u32[]{:S(2)}, u32[]{:S(2)}) collective-permute-start(bf16[2,64,256]{2,1,0:T(8,128)(2,1)S(1)} %factor.1.after_ref.refs_4_), channel_id=1, source_target_pairs={{0,24},{2,0},{4,8},{6,16},{8,26},{10,2},{12,18},{14,10},{16,4},{18... | collective-permute-start | bytes 196616 | tf_op jit(solution)/shard_map/ppermute | solution.py:296
  5.3 1.6 %load_share.1.refs_7_ = f32[4096,128]{1,0:T(8,128)S(1)} custom-call(bf16[2,64,256]{2,1,0:T(8,128)(2,1)S(1)} %factor.1.after_ref.refs_4_, f32[8192,128]{1,0:T(8,128)} %bitcast.2), custom_call_target="tpu_custom_call" | custom-call | bytes 4194304 | tf_op jit(solution)/shard_map/load_share/pallas_call | solution.py:132
  6.9 0.1 collective-permute-start.9
  7.0 2.9 %collective-permute-start.8 = (bf16[2,64,256]{2,1,0:T(8,128)(2,1)S(1)}, bf16[2,64,256]{2,1,0:T(8,128)(2,1)S(1)}, u32[]{:S(2)}, u32[]{:S(2)}) collective-permute-start(bf16[2,64,256]{2,1,0:T(8,128)(2,1)S(1)} %factor.1.after_ref.refs_4_), channel_id=1, source_target_pairs={{4,0},{6,2},{0,4},{2,6},{12,8},{26,10},{8,12},{10,14},{20,16},{22,... | collective-permute-start | bytes 196616 | tf_op jit(solution)/shard_map/ppermute | solution.py:103
  9.8 0.0 collective-permute-done.refs_0_
  9.9 1.7 %collective-permute-start.6 = (bf16[2,64,256]{2,1,0:T(8,128)(2,1)S(1)}, bf16[2,64,256]{2,1,0:T(8,128)(2,1)S(1)}, u32[]{:S(2)}, u32[]{:S(2)}) collective-permute-start(bf16[2,64,256]{2,1,0:T(8,128)(2,1)S(1)} %collective-permute-done.refs_0_), channel_id=1, source_target_pairs={{16,0},{26,2},{28,4},{30,6},{24,8},{18,10},{20,12},{22,14},{0,16},... | collective-permute-start | bytes 196616 | tf_op jit(solution)/shard_map/ppermute | solution.py:103
  11.6 0.5 %collective-permute-start.4 = (bf16[2,64,256]{2,1,0:T(8,128)(2,1)S(1)}, bf16[2,64,256]{2,1,0:T(8,128)(2,1)S(1)}, u32[]{:S(2)}, u32[]{:S(2)}) collective-permute-start(bf16[2,64,256]{2,1,0:T(8,128)(2,1)S(1)} %collective-permute-done.refs_0_), channel_id=1, source_target_pairs={{8,0},{18,2},{12,4},{14,6},{0,8},{26,10},{4,12},{6,14},{24,16},{2,... | collective-permute-start | bytes 196616 | tf_op jit(solution)/shard_map/ppermute | solution.py:103
  12.1 1.3 %collective-permute-start.2 = (bf16[2,64,256]{2,1,0:T(8,128)(2,1)S(1)}, bf16[2,64,256]{2,1,0:T(8,128)(2,1)S(1)}, u32[]{:S(2)}, u32[]{:S(2)}) collective-permute-start(bf16[2,64,256]{2,1,0:T(8,128)(2,1)S(1)} %collective-permute-done.refs_0_), channel_id=1, source_target_pairs={{2,0},{10,2},{20,4},{22,6},{16,8},{24,10},{28,12},{30,14},{8,16},{... | collective-permute-start | bytes 196616 | tf_op jit(solution)/shard_map/ppermute | solution.py:103
  13.3 0.0 collective-permute-done.9.refs_6_
  13.3 0.0 collective-permute-done.8.refs_5_
  13.4 0.8 %collective-permute-start.10 = (bf16[2,64,256]{2,1,0:T(8,128)(2,1)S(1)}, bf16[2,64,256]{2,1,0:T(8,128)(2,1)S(1)}, u32[]{:S(2)}, u32[]{:S(2)}) collective-permute-start(bf16[2,64,256]{2,1,0:T(8,128)(2,1)S(1)} %select_select_fusion), channel_id=1, source_target_pairs={{2,0},{0,2},{6,4},{4,6},{10,8},{8,10},{14,12},{12,14},{18,16},{16,... | collective-permute-start | bytes 196616 | tf_op jit(solution)/shard_map/ppermute | solution.py:103
  14.2 0.0 collective-permute-start.1
  14.2 0.0 collective-permute-done.6.refs_3_
  14.2 0.5 %collective-permute-start.7 = (bf16[2,64,256]{2,1,0:T(8,128)(2,1)S(1)}, bf16[2,64,256]{2,1,0:T(8,128)(2,1)S(1)}, u32[]{:S(2)}, u32[]{:S(2)}) collective-permute-start(bf16[2,64,256]{2,1,0:T(8,128)(2,1)S(1)} %collective-permute-done.6.refs_3_), channel_id=1, source_target_pairs={{1,0},{0,1},{3,2},{2,3},{5,4},{4,5},{7,6},{6,7},{9,8},{8,9},{11,10... | collective-permute-start | bytes 196616 | tf_op jit(solution)/shard_map/ppermute | solution.py:316
  14.7 1.1 %collective-permute-done.4.refs_2_ = bf16[2,64,256]{2,1,0:T(8,128)(2,1)S(1)} collective-permute-done((bf16[2,64,256]{2,1,0:T(8,128)(2,1)S(1)}, bf16[2,64,256]{2,1,0:T(8,128)(2,1)S(1)}, u32[]{:S(2)}, u32[]{:S(2)}) %collective-permute-start.4) | collective-permute-done | bytes 65568 | tf_op jit(solution)/shard_map/ppermute | solution.py:103
  15.8 0.0 collective-permute-start.5
  15.8 0.5 %collective-permute-done.2 = bf16[2,64,256]{2,1,0:T(8,128)(2,1)S(1)} collective-permute-done((bf16[2,64,256]{2,1,0:T(8,128)(2,1)S(1)}, bf16[2,64,256]{2,1,0:T(8,128)(2,1)S(1)}, u32[]{:S(2)}, u32[]{:S(2)}) %collective-permute-start.2) | collective-permute-done | bytes 65568 | tf_op jit(solution)/shard_map/ppermute | solution.py:103
  16.4 0.1 collective-permute-start.3
  16.4 0.5 %begin_update.1 = (f32[4096,128]{1,0:T(8,128)S(1)}, bf16[512,256]{1,0:T(8,128)(2,1)S(1)}, bf16[2,64,256]{2,1,0:T(8,128)(2,1)S(1)}, bf16[2,64,256]{2,1,0:T(8,128)(2,1)S(1)}) custom-call(bf16[2,64,256]{2,1,0:T(8,128)(2,1)S(1)} %collective-permute-done.refs_0_, bf16[2,64,256]{2,1,0:T(8,128)(2,1)S(1)} %broadcast_select_fusion.refs_1_, ...), custom_call_target="tpu_custom_call", output_to_operand_aliasing={{0}: (7, {})} | custom-call | tf_op jit(solution)/shard_map/begin_update/pallas_call | solution.py:209
  16.9 0.0 collective-permute-done.1.refs_0_
  17.0 0.7 %collective-permute-done.10.refs_7_ = bf16[2,64,256]{2,1,0:T(8,128)(2,1)S(1)} collective-permute-done((bf16[2,64,256]{2,1,0:T(8,128)(2,1)S(1)}, bf16[2,64,256]{2,1,0:T(8,128)(2,1)S(1)}, u32[]{:S(2)}, u32[]{:S(2)}) %collective-permute-start.10) | collective-permute-done | bytes 65568 | tf_op jit(solution)/shard_map/ppermute | solution.py:103
  17.7 0.0 collective-permute-done.7.refs_3_
  17.7 0.0 collective-permute-done.5.refs_2_
  17.7 0.0 collective-permute-done.3.refs_1_
  17.7 1.7 %end_update.1 = (f32[4096,128]{1,0:T(8,128)}, f32[4096,128]{1,0:T(8,128)S(1)}) custom-call(bf16[2,64,256]{2,1,0:T(8,128)(2,1)S(1)} %collective-permute-done.1.refs_0_, bf16[2,64,256]{2,1,0:T(8,128)(2,1)S(1)} %collective-permute-done.3.refs_1_, bf16[2,64,256]{2,1,0:T(8,128)(2,1)S(1)} %collective-permute-done.5.refs_2_, ...), custom_call_target="tpu_custom_call", output_to_operand_aliasing={{1}: (9, {})} | custom-call | tf_op jit(solution)/shard_map/end_update/pallas_call | solution.py:272
  (2 shorter events, 0.0 us)
Async XLA Ops:
  1.4 8.5 %collective-permute-start = (bf16[2,64,256]{2,1,0:T(8,128)(2,1)S(1)}, bf16[2,64,256]{2,1,0:T(8,128)(2,1)S(1)}, u32[]{:S(2)}, u32[]{:S(2)}) collective-permute-start(bf16[2,64,256]{2,1,0:T(8,128)(2,1)S(1)} %factor.1.after_ref.refs_4_), channel_id=1, source_target_pairs={{0,24},{2,0},{4,8},{6,16},{8,26},{10,2},{12,18},{14,10},{16,4},{18... | collective-permute-start | bytes 196616 | tf_op jit(solution)/shard_map/ppermute | solution.py:296
  6.9 6.4 %collective-permute-start.9 = (bf16[2,64,256]{2,1,0:T(8,128)(2,1)S(1)}, bf16[2,64,256]{2,1,0:T(8,128)(2,1)S(1)}, u32[]{:S(2)}, u32[]{:S(2)}) collective-permute-start(bf16[2,64,256]{2,1,0:T(8,128)(2,1)S(1)} %factor.1.after_ref.refs_4_), channel_id=1, source_target_pairs={{8,0},{0,2},{6,4},{4,6},{10,8},{2,10},{14,12},{12,14},{18,16},{16,... | collective-permute-start | bytes 196616 | tf_op jit(solution)/shard_map/ppermute | solution.py:103
  7.0 6.4 %collective-permute-start.8 = (bf16[2,64,256]{2,1,0:T(8,128)(2,1)S(1)}, bf16[2,64,256]{2,1,0:T(8,128)(2,1)S(1)}, u32[]{:S(2)}, u32[]{:S(2)}) collective-permute-start(bf16[2,64,256]{2,1,0:T(8,128)(2,1)S(1)} %factor.1.after_ref.refs_4_), channel_id=1, source_target_pairs={{4,0},{6,2},{0,4},{2,6},{12,8},{26,10},{8,12},{10,14},{20,16},{22,... | collective-permute-start | bytes 196616 | tf_op jit(solution)/shard_map/ppermute | solution.py:103
  9.9 4.3 %collective-permute-start.6 = (bf16[2,64,256]{2,1,0:T(8,128)(2,1)S(1)}, bf16[2,64,256]{2,1,0:T(8,128)(2,1)S(1)}, u32[]{:S(2)}, u32[]{:S(2)}) collective-permute-start(bf16[2,64,256]{2,1,0:T(8,128)(2,1)S(1)} %collective-permute-done.refs_0_), channel_id=1, source_target_pairs={{16,0},{26,2},{28,4},{30,6},{24,8},{18,10},{20,12},{22,14},{0,16},... | collective-permute-start | bytes 196616 | tf_op jit(solution)/shard_map/ppermute | solution.py:103
  11.6 4.3 %collective-permute-start.4 = (bf16[2,64,256]{2,1,0:T(8,128)(2,1)S(1)}, bf16[2,64,256]{2,1,0:T(8,128)(2,1)S(1)}, u32[]{:S(2)}, u32[]{:S(2)}) collective-permute-start(bf16[2,64,256]{2,1,0:T(8,128)(2,1)S(1)} %collective-permute-done.refs_0_), channel_id=1, source_target_pairs={{8,0},{18,2},{12,4},{14,6},{0,8},{26,10},{4,12},{6,14},{24,16},{2,... | collective-permute-start | bytes 196616 | tf_op jit(solution)/shard_map/ppermute | solution.py:103
  12.1 4.3 %collective-permute-start.2 = (bf16[2,64,256]{2,1,0:T(8,128)(2,1)S(1)}, bf16[2,64,256]{2,1,0:T(8,128)(2,1)S(1)}, u32[]{:S(2)}, u32[]{:S(2)}) collective-permute-start(bf16[2,64,256]{2,1,0:T(8,128)(2,1)S(1)} %collective-permute-done.refs_0_), channel_id=1, source_target_pairs={{2,0},{10,2},{20,4},{22,6},{16,8},{24,10},{28,12},{30,14},{8,16},{... | collective-permute-start | bytes 196616 | tf_op jit(solution)/shard_map/ppermute | solution.py:103
  13.4 4.3 %collective-permute-start.10 = (bf16[2,64,256]{2,1,0:T(8,128)(2,1)S(1)}, bf16[2,64,256]{2,1,0:T(8,128)(2,1)S(1)}, u32[]{:S(2)}, u32[]{:S(2)}) collective-permute-start(bf16[2,64,256]{2,1,0:T(8,128)(2,1)S(1)} %select_select_fusion), channel_id=1, source_target_pairs={{2,0},{0,2},{6,4},{4,6},{10,8},{8,10},{14,12},{12,14},{18,16},{16,... | collective-permute-start | bytes 196616 | tf_op jit(solution)/shard_map/ppermute | solution.py:103
  14.2 2.8 %collective-permute-start.1 = (bf16[2,64,256]{2,1,0:T(8,128)(2,1)S(1)}, bf16[2,64,256]{2,1,0:T(8,128)(2,1)S(1)}, u32[]{:S(2)}, u32[]{:S(2)}) collective-permute-start(bf16[2,64,256]{2,1,0:T(8,128)(2,1)S(1)} %collective-permute-done.refs_0_), channel_id=1, source_target_pairs={{1,0},{0,1},{3,2},{2,3},{5,4},{4,5},{7,6},{6,7},{9,8},{8,9},{11,10... | collective-permute-start | bytes 196616 | tf_op jit(solution)/shard_map/ppermute | solution.py:316
  14.2 3.5 %collective-permute-start.7 = (bf16[2,64,256]{2,1,0:T(8,128)(2,1)S(1)}, bf16[2,64,256]{2,1,0:T(8,128)(2,1)S(1)}, u32[]{:S(2)}, u32[]{:S(2)}) collective-permute-start(bf16[2,64,256]{2,1,0:T(8,128)(2,1)S(1)} %collective-permute-done.6.refs_3_), channel_id=1, source_target_pairs={{1,0},{0,1},{3,2},{2,3},{5,4},{4,5},{7,6},{6,7},{9,8},{8,9},{11,10... | collective-permute-start | bytes 196616 | tf_op jit(solution)/shard_map/ppermute | solution.py:316
  15.8 1.9 %collective-permute-start.5 = (bf16[2,64,256]{2,1,0:T(8,128)(2,1)S(1)}, bf16[2,64,256]{2,1,0:T(8,128)(2,1)S(1)}, u32[]{:S(2)}, u32[]{:S(2)}) collective-permute-start(bf16[2,64,256]{2,1,0:T(8,128)(2,1)S(1)} %collective-permute-done.4.refs_2_), channel_id=1, source_target_pairs={{1,0},{0,1},{3,2},{2,3},{5,4},{4,5},{7,6},{6,7},{9,8},{8,9},{11,10... | collective-permute-start | bytes 196616 | tf_op jit(solution)/shard_map/ppermute | solution.py:316
  16.4 1.4 %collective-permute-start.3 = (bf16[2,64,256]{2,1,0:T(8,128)(2,1)S(1)}, bf16[2,64,256]{2,1,0:T(8,128)(2,1)S(1)}, u32[]{:S(2)}, u32[]{:S(2)}) collective-permute-start(bf16[2,64,256]{2,1,0:T(8,128)(2,1)S(1)} %broadcast_select_fusion.refs_1_), channel_id=1, source_target_pairs={{1,0},{0,1},{3,2},{2,3},{5,4},{4,5},{7,6},{6,7},{9,8},{8,9},{11,10... | collective-permute-start | bytes 196616 | tf_op jit(solution)/shard_map/ppermute | solution.py:316

commit v22 on v21

--- a/solution.py
+++ b/solution.py
@@ -119,19 +119,22 @@
     return [factor, far, near, last]
 
 
-def load_kernel(after_ref, lines_ref, share_ref, sem):
-    rows = share_ref.shape[0]
+def load_kernel(rows, after_ref, lines_ref, share_ref, sem):
     layer = lax.axis_index("layer")
-    load = pltpu.make_async_copy(lines_ref.at[pl.ds(layer * rows, rows)], share_ref, sem)
+    load = pltpu.make_async_copy(lines_ref.at[pl.ds(layer * rows, rows)], share_ref.at[pl.ds(0, rows)], sem)
     load.start()
     load.wait()
 
 
-def load_share(after, lines, layers):
+def load_share(after, lines, layers, per_row):
     rows = lines.shape[0] // layers
+
+    def body(*refs):
+        load_kernel(rows, *refs)
+
     return pl.pallas_call(
-        load_kernel,
-        out_shape=jax.ShapeDtypeStruct((rows, LANES), jnp.float32),
+        body,
+        out_shape=jax.ShapeDtypeStruct((rows + per_row, LANES), jnp.float32),
         in_specs=[pl.BlockSpec(memory_space=pl.ANY), pl.BlockSpec(memory_space=pltpu.HBM)],
         out_specs=pl.BlockSpec(memory_space=pltpu.VMEM),
         scratch_shapes=[pltpu.SemaphoreType.DMA],
@@ -264,6 +267,7 @@
 def end_update(column_pieces, row_pieces, own_columns, share, layers, tile):
     pieces = len(row_pieces)
     half = row_pieces[0].shape[0]
+    per_row = layers * own_columns.shape[0] // LANES
     operands = (*column_pieces, *row_pieces, own_columns, share)
 
     def body(*refs):
@@ -271,7 +275,10 @@
 
     result, _ = pl.pallas_call(
         body,
-        out_shape=[jax.ShapeDtypeStruct(share.shape, jnp.float32)] * 2,
+        out_shape=[
+            jax.ShapeDtypeStruct((half * pieces * row_pieces[0].shape[1] * per_row, LANES), jnp.float32),
+            jax.ShapeDtypeStruct(share.shape, jnp.float32),
+        ],
         in_specs=[pl.BlockSpec(memory_space=pltpu.VMEM)] * len(operands),
         out_specs=[pl.BlockSpec(memory_space=pltpu.HBM), pl.BlockSpec(memory_space=pltpu.VMEM)],
         scratch_shapes=[
@@ -296,7 +303,7 @@
     moved = lax.ppermute(
         factor, ("row", "col"), [(a * count + b, slots[a][b] * count + a) for a in range(count) for b in range(count)]
     )
-    share = load_share(factor, trailing.reshape(-1, LANES), layers)
+    share = load_share(factor, trailing.reshape(-1, LANES), layers, col_tiles * tile // LANES)
     loaded_factor, share = lax.optimization_barrier((factor, share))
     line = gather_line(factor, loaded_factor, moved, count)
     plane = [moved]

time: 19.6 us -> 19.6 us (level)
  no operation moved by 1% of the time
where the time goes in v22:
time: 19.6 us; the launch traced here: 19.4 us
  starting transfers between devices  11.8 us (60%)
  Pallas kernels  5.14 us (26%)
  waiting for transfers between devices  2.4 us (12%)
    ppermute x6, starting transfers between devices, move(): lax.ppermute(x, ('row', 'col'), [(a * count + b, r * count + c) for (r, c...  7.25 us
    ppermute x1, starting transfers between devices, per_device(): lax.ppermute(factor, ('row', 'col'), [(a * count + b, slots[a][b] * count...  3.95 us
    ppermute x6, waiting for transfers between devices, move(): lax.ppermute(x, ('row', 'col'), [(a * count + b, r * count + c) for (r, c...  2.38 us
    pallas_call x1, Pallas kernels, end_update(): pl.pallas_call(body, out_shape=[jax.ShapeDtypeStruct((half * pieces * row...  1.7 us
    pallas_call x1, Pallas kernels, load_share(): pl.pallas_call(body, out_shape=jax.ShapeDtypeStruct((rows + per_row, LANE...  1.6 us
    pallas_call x1, Pallas kernels, make_factor(): pl.pallas_call(factor_kernel, out_shape=jax.ShapeDtypeStruct((half, tile_...  1.34 us
    ppermute x4, starting transfers between devices, per_device(): others += [lax.ppermute(piece, 'layer', pairs) for piece in plane]  0.59 us
    pallas_call x1, Pallas kernels, begin_update(): pl.pallas_call(body, out_shape=[jax.ShapeDtypeStruct(share.shape, jnp.flo...  0.5 us
  transfers between devices with their start and end apart: 11, of which 3 were waited for; matrix products, arithmetic and copies ran while one was open for 0% of the time, Pallas kernels for 11%

profile of v22, /device:TPU:0, one launch (start us, length us, event | category | flops | bytes accessed | tf_op | source)
XLA Modules:
  0.0 19.4 jit_solution(10098567946335511167)
XLA Ops:
  0.0 1.3 %factor.1.refs_0_.refs_4_ = bf16[2,64,256]{2,1,0:T(8,128)(2,1)S(1)} custom-call(f32[4,1,64,256]{3,2,1,0:T(8,128)} %panel_ref.1, f32[256,256]{1,0:T(8,128)} %inverse_ref.1), custom_call_target="tpu_custom_call" | custom-call | tf_op jit(solution)/shard_map/factor/pallas_call | solution.py:55
  1.4 3.9 %collective-permute-start = (bf16[2,64,256]{2,1,0:T(8,128)(2,1)S(1)}, bf16[2,64,256]{2,1,0:T(8,128)(2,1)S(1)}, u32[]{:S(2)}, u32[]{:S(2)}) collective-permute-start(bf16[2,64,256]{2,1,0:T(8,128)(2,1)S(1)} %factor.1.refs_0_.refs_4_), channel_id=1, source_target_pairs={{0,24},{2,0},{4,8},{6,16},{8,26},{10,2},{12,18},{14,10},{16,4},{18... | collective-permute-start | bytes 196616 | tf_op jit(solution)/shard_map/ppermute | solution.py:303
  5.3 1.6 %load_share.1.refs_7_ = f32[4104,128]{1,0:T(8,128)S(1)} custom-call(bf16[2,64,256]{2,1,0:T(8,128)(2,1)S(1)} %factor.1.refs_0_.refs_4_, f32[8192,128]{1,0:T(8,128)} %bitcast.2), custom_call_target="tpu_custom_call" | custom-call | bytes 4194304 | tf_op jit(solution)/shard_map/load_share/pallas_call | solution.py:135
  6.9 0.1 collective-permute-start.9
  7.0 2.9 %collective-permute-start.8 = (bf16[2,64,256]{2,1,0:T(8,128)(2,1)S(1)}, bf16[2,64,256]{2,1,0:T(8,128)(2,1)S(1)}, u32[]{:S(2)}, u32[]{:S(2)}) collective-permute-start(bf16[2,64,256]{2,1,0:T(8,128)(2,1)S(1)} %factor.1.refs_0_.refs_4_), channel_id=1, source_target_pairs={{4,0},{6,2},{0,4},{2,6},{12,8},{26,10},{8,12},{10,14},{20,16},{22,... | collective-permute-start | bytes 196616 | tf_op jit(solution)/shard_map/ppermute | solution.py:103
  9.8 0.0 collective-permute-done.refs_0_
  9.9 1.7 %collective-permute-start.6 = (bf16[2,64,256]{2,1,0:T(8,128)(2,1)S(1)}, bf16[2,64,256]{2,1,0:T(8,128)(2,1)S(1)}, u32[]{:S(2)}, u32[]{:S(2)}) collective-permute-start(bf16[2,64,256]{2,1,0:T(8,128)(2,1)S(1)} %collective-permute-done.refs_0_), channel_id=1, source_target_pairs={{16,0},{26,2},{28,4},{30,6},{24,8},{18,10},{20,12},{22,14},{0,16},... | collective-permute-start | bytes 196616 | tf_op jit(solution)/shard_map/ppermute | solution.py:103
  11.6 0.5 %collective-permute-start.4 = (bf16[2,64,256]{2,1,0:T(8,128)(2,1)S(1)}, bf16[2,64,256]{2,1,0:T(8,128)(2,1)S(1)}, u32[]{:S(2)}, u32[]{:S(2)}) collective-permute-start(bf16[2,64,256]{2,1,0:T(8,128)(2,1)S(1)} %collective-permute-done.refs_0_), channel_id=1, source_target_pairs={{8,0},{18,2},{12,4},{14,6},{0,8},{26,10},{4,12},{6,14},{24,16},{2,... | collective-permute-start | bytes 196616 | tf_op jit(solution)/shard_map/ppermute | solution.py:103
  12.1 1.3 %collective-permute-start.2 = (bf16[2,64,256]{2,1,0:T(8,128)(2,1)S(1)}, bf16[2,64,256]{2,1,0:T(8,128)(2,1)S(1)}, u32[]{:S(2)}, u32[]{:S(2)}) collective-permute-start(bf16[2,64,256]{2,1,0:T(8,128)(2,1)S(1)} %collective-permute-done.refs_0_), channel_id=1, source_target_pairs={{2,0},{10,2},{20,4},{22,6},{16,8},{24,10},{28,12},{30,14},{8,16},{... | collective-permute-start | bytes 196616 | tf_op jit(solution)/shard_map/ppermute | solution.py:103
  13.3 0.0 collective-permute-done.9.refs_6_
  13.3 0.0 collective-permute-done.8.refs_5_
  13.4 0.8 %collective-permute-start.10 = (bf16[2,64,256]{2,1,0:T(8,128)(2,1)S(1)}, bf16[2,64,256]{2,1,0:T(8,128)(2,1)S(1)}, u32[]{:S(2)}, u32[]{:S(2)}) collective-permute-start(bf16[2,64,256]{2,1,0:T(8,128)(2,1)S(1)} %select_select_fusion), channel_id=1, source_target_pairs={{2,0},{0,2},{6,4},{4,6},{10,8},{8,10},{14,12},{12,14},{18,16},{16,... | collective-permute-start | bytes 196616 | tf_op jit(solution)/shard_map/ppermute | solution.py:103
  14.2 0.0 collective-permute-start.1
  14.2 0.0 collective-permute-done.6.refs_3_
  14.2 0.5 %collective-permute-start.7 = (bf16[2,64,256]{2,1,0:T(8,128)(2,1)S(1)}, bf16[2,64,256]{2,1,0:T(8,128)(2,1)S(1)}, u32[]{:S(2)}, u32[]{:S(2)}) collective-permute-start(bf16[2,64,256]{2,1,0:T(8,128)(2,1)S(1)} %collective-permute-done.6.refs_3_), channel_id=1, source_target_pairs={{1,0},{0,1},{3,2},{2,3},{5,4},{4,5},{7,6},{6,7},{9,8},{8,9},{11,10... | collective-permute-start | bytes 196616 | tf_op jit(solution)/shard_map/ppermute | solution.py:323
  14.7 1.1 %collective-permute-done.4.refs_2_ = bf16[2,64,256]{2,1,0:T(8,128)(2,1)S(1)} collective-permute-done((bf16[2,64,256]{2,1,0:T(8,128)(2,1)S(1)}, bf16[2,64,256]{2,1,0:T(8,128)(2,1)S(1)}, u32[]{:S(2)}, u32[]{:S(2)}) %collective-permute-start.4) | collective-permute-done | bytes 65568 | tf_op jit(solution)/shard_map/ppermute | solution.py:103
  15.8 0.0 collective-permute-start.5
  15.8 0.5 %collective-permute-done.2 = bf16[2,64,256]{2,1,0:T(8,128)(2,1)S(1)} collective-permute-done((bf16[2,64,256]{2,1,0:T(8,128)(2,1)S(1)}, bf16[2,64,256]{2,1,0:T(8,128)(2,1)S(1)}, u32[]{:S(2)}, u32[]{:S(2)}) %collective-permute-start.2) | collective-permute-done | bytes 65568 | tf_op jit(solution)/shard_map/ppermute | solution.py:103
  16.4 0.1 collective-permute-start.3
  16.4 0.5 %begin_update.1 = (f32[4104,128]{1,0:T(8,128)S(1)}, bf16[512,256]{1,0:T(8,128)(2,1)S(1)}, bf16[2,64,256]{2,1,0:T(8,128)(2,1)S(1)}, bf16[2,64,256]{2,1,0:T(8,128)(2,1)S(1)}) custom-call(bf16[2,64,256]{2,1,0:T(8,128)(2,1)S(1)} %collective-permute-done.refs_0_, bf16[2,64,256]{2,1,0:T(8,128)(2,1)S(1)} %broadcast_select_fusion.refs_1_, ...), custom_call_target="tpu_custom_call", output_to_operand_aliasing={{0}: (7, {})} | custom-call | tf_op jit(solution)/shard_map/begin_update/pallas_call | solution.py:212
  16.9 0.0 collective-permute-done.1.refs_0_
  17.0 0.7 %collective-permute-done.10.refs_7_ = bf16[2,64,256]{2,1,0:T(8,128)(2,1)S(1)} collective-permute-done((bf16[2,64,256]{2,1,0:T(8,128)(2,1)S(1)}, bf16[2,64,256]{2,1,0:T(8,128)(2,1)S(1)}, u32[]{:S(2)}, u32[]{:S(2)}) %collective-permute-start.10) | collective-permute-done | bytes 65568 | tf_op jit(solution)/shard_map/ppermute | solution.py:103
  17.7 0.0 collective-permute-done.7.refs_3_
  17.7 0.0 collective-permute-done.5.refs_2_
  17.7 0.0 collective-permute-done.3.refs_1_
  17.7 1.7 %end_update.1 = (f32[4096,128]{1,0:T(8,128)}, f32[4104,128]{1,0:T(8,128)S(1)}) custom-call(bf16[2,64,256]{2,1,0:T(8,128)(2,1)S(1)} %collective-permute-done.1.refs_0_, bf16[2,64,256]{2,1,0:T(8,128)(2,1)S(1)} %collective-permute-done.3.refs_1_, bf16[2,64,256]{2,1,0:T(8,128)(2,1)S(1)} %collective-permute-done.5.refs_2_, ...), custom_call_target="tpu_custom_call", output_to_operand_aliasing={{1}: (9, {})} | custom-call | tf_op jit(solution)/shard_map/end_update/pallas_call | solution.py:276
  (2 shorter events, 0.0 us)
Async XLA Ops:
  1.4 8.5 %collective-permute-start = (bf16[2,64,256]{2,1,0:T(8,128)(2,1)S(1)}, bf16[2,64,256]{2,1,0:T(8,128)(2,1)S(1)}, u32[]{:S(2)}, u32[]{:S(2)}) collective-permute-start(bf16[2,64,256]{2,1,0:T(8,128)(2,1)S(1)} %factor.1.refs_0_.refs_4_), channel_id=1, source_target_pairs={{0,24},{2,0},{4,8},{6,16},{8,26},{10,2},{12,18},{14,10},{16,4},{18... | collective-permute-start | bytes 196616 | tf_op jit(solution)/shard_map/ppermute | solution.py:303
  6.9 6.4 %collective-permute-start.9 = (bf16[2,64,256]{2,1,0:T(8,128)(2,1)S(1)}, bf16[2,64,256]{2,1,0:T(8,128)(2,1)S(1)}, u32[]{:S(2)}, u32[]{:S(2)}) collective-permute-start(bf16[2,64,256]{2,1,0:T(8,128)(2,1)S(1)} %factor.1.refs_0_.refs_4_), channel_id=1, source_target_pairs={{8,0},{0,2},{6,4},{4,6},{10,8},{2,10},{14,12},{12,14},{18,16},{16,... | collective-permute-start | bytes 196616 | tf_op jit(solution)/shard_map/ppermute | solution.py:103
  7.0 6.4 %collective-permute-start.8 = (bf16[2,64,256]{2,1,0:T(8,128)(2,1)S(1)}, bf16[2,64,256]{2,1,0:T(8,128)(2,1)S(1)}, u32[]{:S(2)}, u32[]{:S(2)}) collective-permute-start(bf16[2,64,256]{2,1,0:T(8,128)(2,1)S(1)} %factor.1.refs_0_.refs_4_), channel_id=1, source_target_pairs={{4,0},{6,2},{0,4},{2,6},{12,8},{26,10},{8,12},{10,14},{20,16},{22,... | collective-permute-start | bytes 196616 | tf_op jit(solution)/shard_map/ppermute | solution.py:103
  9.9 4.3 %collective-permute-start.6 = (bf16[2,64,256]{2,1,0:T(8,128)(2,1)S(1)}, bf16[2,64,256]{2,1,0:T(8,128)(2,1)S(1)}, u32[]{:S(2)}, u32[]{:S(2)}) collective-permute-start(bf16[2,64,256]{2,1,0:T(8,128)(2,1)S(1)} %collective-permute-done.refs_0_), channel_id=1, source_target_pairs={{16,0},{26,2},{28,4},{30,6},{24,8},{18,10},{20,12},{22,14},{0,16},... | collective-permute-start | bytes 196616 | tf_op jit(solution)/shard_map/ppermute | solution.py:103
  11.6 4.3 %collective-permute-start.4 = (bf16[2,64,256]{2,1,0:T(8,128)(2,1)S(1)}, bf16[2,64,256]{2,1,0:T(8,128)(2,1)S(1)}, u32[]{:S(2)}, u32[]{:S(2)}) collective-permute-start(bf16[2,64,256]{2,1,0:T(8,128)(2,1)S(1)} %collective-permute-done.refs_0_), channel_id=1, source_target_pairs={{8,0},{18,2},{12,4},{14,6},{0,8},{26,10},{4,12},{6,14},{24,16},{2,... | collective-permute-start | bytes 196616 | tf_op jit(solution)/shard_map/ppermute | solution.py:103
  12.1 4.3 %collective-permute-start.2 = (bf16[2,64,256]{2,1,0:T(8,128)(2,1)S(1)}, bf16[2,64,256]{2,1,0:T(8,128)(2,1)S(1)}, u32[]{:S(2)}, u32[]{:S(2)}) collective-permute-start(bf16[2,64,256]{2,1,0:T(8,128)(2,1)S(1)} %collective-permute-done.refs_0_), channel_id=1, source_target_pairs={{2,0},{10,2},{20,4},{22,6},{16,8},{24,10},{28,12},{30,14},{8,16},{... | collective-permute-start | bytes 196616 | tf_op jit(solution)/shard_map/ppermute | solution.py:103
  13.4 4.3 %collective-permute-start.10 = (bf16[2,64,256]{2,1,0:T(8,128)(2,1)S(1)}, bf16[2,64,256]{2,1,0:T(8,128)(2,1)S(1)}, u32[]{:S(2)}, u32[]{:S(2)}) collective-permute-start(bf16[2,64,256]{2,1,0:T(8,128)(2,1)S(1)} %select_select_fusion), channel_id=1, source_target_pairs={{2,0},{0,2},{6,4},{4,6},{10,8},{8,10},{14,12},{12,14},{18,16},{16,... | collective-permute-start | bytes 196616 | tf_op jit(solution)/shard_map/ppermute | solution.py:103
  14.2 2.8 %collective-permute-start.1 = (bf16[2,64,256]{2,1,0:T(8,128)(2,1)S(1)}, bf16[2,64,256]{2,1,0:T(8,128)(2,1)S(1)}, u32[]{:S(2)}, u32[]{:S(2)}) collective-permute-start(bf16[2,64,256]{2,1,0:T(8,128)(2,1)S(1)} %collective-permute-done.refs_0_), channel_id=1, source_target_pairs={{1,0},{0,1},{3,2},{2,3},{5,4},{4,5},{7,6},{6,7},{9,8},{8,9},{11,10... | collective-permute-start | bytes 196616 | tf_op jit(solution)/shard_map/ppermute | solution.py:323
  14.2 3.5 %collective-permute-start.7 = (bf16[2,64,256]{2,1,0:T(8,128)(2,1)S(1)}, bf16[2,64,256]{2,1,0:T(8,128)(2,1)S(1)}, u32[]{:S(2)}, u32[]{:S(2)}) collective-permute-start(bf16[2,64,256]{2,1,0:T(8,128)(2,1)S(1)} %collective-permute-done.6.refs_3_), channel_id=1, source_target_pairs={{1,0},{0,1},{3,2},{2,3},{5,4},{4,5},{7,6},{6,7},{9,8},{8,9},{11,10... | collective-permute-start | bytes 196616 | tf_op jit(solution)/shard_map/ppermute | solution.py:323
  15.8 1.9 %collective-permute-start.5 = (bf16[2,64,256]{2,1,0:T(8,128)(2,1)S(1)}, bf16[2,64,256]{2,1,0:T(8,128)(2,1)S(1)}, u32[]{:S(2)}, u32[]{:S(2)}) collective-permute-start(bf16[2,64,256]{2,1,0:T(8,128)(2,1)S(1)} %collective-permute-done.4.refs_2_), channel_id=1, source_target_pairs={{1,0},{0,1},{3,2},{2,3},{5,4},{4,5},{7,6},{6,7},{9,8},{8,9},{11,10... | collective-permute-start | bytes 196616 | tf_op jit(solution)/shard_map/ppermute | solution.py:323
  16.4 1.4 %collective-permute-start.3 = (bf16[2,64,256]{2,1,0:T(8,128)(2,1)S(1)}, bf16[2,64,256]{2,1,0:T(8,128)(2,1)S(1)}, u32[]{:S(2)}, u32[]{:S(2)}) collective-permute-start(bf16[2,64,256]{2,1,0:T(8,128)(2,1)S(1)} %broadcast_select_fusion.refs_1_), channel_id=1, source_target_pairs={{1,0},{0,1},{3,2},{2,3},{5,4},{4,5},{7,6},{6,7},{9,8},{8,9},{11,10... | collective-permute-start | bytes 196616 | tf_op jit(solution)/shard_map/ppermute | solution.py:323

commit v23 on v22

--- a/solution.py
+++ b/solution.py
@@ -95,28 +95,20 @@
     return slab
 
 
-def line_steps(count):
-    return (0, 2, 1, 3) if count == 4 else tuple(range(count))
+def early_late(count):
+    return ((0, 2), (1, 3)) if count == 4 else (tuple(range(count - 1)), (count - 1,))
 
 
 def move(x, sources, count):
     return lax.ppermute(x, ("row", "col"), [(a * count + b, r * count + c) for (r, c), (a, b) in sources.items()])
 
 
-def gather_line(factor, late_factor, moved, count):
-    if count != 4:
-        line = [factor]
-        for step in range(1, count):
-            line.append(lax.ppermute(factor, "col", [(partner(b, step, count), b) for b in range(count)]))
-        return line
-    places = [(r, c) for r in range(count) for c in range(count)]
-    near = move(late_factor, {(r, c): (r ^ 1, c) if r == c else (r, c ^ 1) for r, c in places}, count)
-    far = move(late_factor, {(r, c): (r ^ 2, c) if r == c and r % 2 == 1 else (r, c ^ 2) for r, c in places}, count)
-    r, c = lax.axis_index("row"), lax.axis_index("col")
-    relayed = jnp.where((r == c) & (r % 2 == 1), moved, far)
-    relayed = jnp.where(r == c ^ 1, near, relayed)
-    last = move(relayed, {(r, c): (r, c ^ 1) for r, c in places}, count)
-    return [factor, far, near, last]
+def line_sources(step, count, kept):
+    return {
+        (r, c): (partner(r, step, count), c) if kept and r == c and r in kept else (r, partner(c, step, count))
+        for r in range(count)
+        for c in range(count)
+    }
 
 
 def load_kernel(rows, after_ref, lines_ref, share_ref, sem):
@@ -172,30 +164,29 @@
             share_ref[at, :] -= product[k * tile_rows : (k + 1) * tile_rows, part * LANES : (part + 1) * LANES]
 
 
-def take_rows(rows_ref, columns_ref, c, step, pieces):
-    half, tile_rows, _ = rows_ref.shape
-    for k in range(half):
-        at = pl.multiple_of((k * pieces + partner(c, step, pieces)) * tile_rows, tile_rows)
-        rows_ref[k] = columns_ref[pl.ds(at, tile_rows), :]
+def take_rows(rows_ref, piece_ref, columns_ref, r, c, step, pieces):
+    rows_ref[...] = piece_ref[...]
+    if pieces == 4:
+
+        @pl.when(r == c)
+        def _():
+            half, tile_rows, _ = rows_ref.shape
+            for k in range(half):
+                at = pl.multiple_of((k * pieces + partner(c, step, pieces)) * tile_rows, tile_rows)
+                rows_ref[k] = columns_ref[pl.ds(at, tile_rows), :]
 
 
 def begin_kernel(pieces, layers, tile, *refs):
-    column_refs, row_refs, rest = refs[:pieces], refs[pieces : 2 * pieces - 1], refs[2 * pieces - 1 :]
+    early, _ = early_late(pieces)
+    column_refs, row_refs, rest = refs[:pieces], refs[pieces : pieces + len(early)], refs[pieces + len(early) :]
     _, share_ref, columns_ref, *line_refs = rest
     r, c, layer = (lax.axis_index(axis) for axis in AXES)
     half, tile_rows, _ = row_refs[0].shape
     own_lines = half * tile // LANES
     fill_columns(columns_ref, column_refs, plane_slots(pieces), r, c, layer)
-    for line_ref, row_ref in zip(line_refs, row_refs[1:]):
-        line_ref[...] = row_ref[...]
-    if pieces == 4:
-
-        @pl.when(r == c)
-        def _():
-            for step, line_ref in zip(line_steps(pieces)[1:], line_refs):
-                take_rows(line_ref, columns_ref, c, step, pieces)
-
-    for step, row_ref in zip(line_steps(pieces), (row_refs[0], *line_refs)):
+    for step, line_ref, row_ref in zip(early[1:], line_refs, row_refs[1:]):
+        take_rows(line_ref, row_ref, columns_ref, r, c, step, pieces)
+    for step, row_ref in zip(early, (row_refs[0], *line_refs)):
         first_row = partner(c, step, pieces) * tile_rows
         subtract_product(
             share_ref, row_ref[...], columns_ref[...], tile, first_row, layer * own_lines, layers * own_lines
@@ -205,6 +196,7 @@
 def begin_update(column_pieces, row_pieces, share, layers, tile):
     pieces = len(column_pieces)
     half, _, width = row_pieces[0].shape
+    operands = (*column_pieces, *row_pieces, share)
 
     def body(*refs):
         begin_kernel(pieces, layers, tile, *refs)
@@ -214,20 +206,20 @@
         out_shape=[
             jax.ShapeDtypeStruct(share.shape, jnp.float32),
             jax.ShapeDtypeStruct((half * tile, width), jnp.bfloat16),
-            *[jax.ShapeDtypeStruct(row_pieces[0].shape, jnp.bfloat16)] * (pieces - 2),
+            *[jax.ShapeDtypeStruct(row_pieces[0].shape, jnp.bfloat16)] * (len(row_pieces) - 1),
         ],
-        in_specs=[pl.BlockSpec(memory_space=pltpu.VMEM)] * (2 * pieces),
-        out_specs=[pl.BlockSpec(memory_space=pltpu.VMEM)] * pieces,
-        input_output_aliases={2 * pieces - 1: 0},
+        in_specs=[pl.BlockSpec(memory_space=pltpu.VMEM)] * len(operands),
+        out_specs=[pl.BlockSpec(memory_space=pltpu.VMEM)] * (len(row_pieces) + 1),
+        input_output_aliases={len(operands) - 1: 0},
         compiler_params=pltpu.CompilerParams(vmem_limit_bytes=VMEM_BYTES),
         name="begin_update",
-    )(*column_pieces, *row_pieces, share)
+    )(*operands)
 
 
 def end_kernel(pieces, layers, tile, *refs):
     others = pieces * (layers - 1)
     column_refs, row_refs, rest = refs[:others], refs[others : others + pieces], refs[others + pieces :]
-    own_ref, _, out_ref, share_ref, columns_buf, last_buf, sems = rest
+    own_ref, _, out_ref, share_ref, columns_buf, late_buf, sems = rest
     r, c, layer = (lax.axis_index(axis) for axis in AXES)
     half, tile_rows, _ = row_refs[0].shape
     own_lines = half * tile // LANES
@@ -237,20 +229,17 @@
         fill_columns(
             columns_buf.at[at], column_refs[at * pieces : (at + 1) * pieces], plane_slots(pieces), r, c, owner
         )
-    last_buf[...] = row_refs[-1][...]
-    if pieces == 4:
-
-        @pl.when(r == c)
-        def _():
-            take_rows(last_buf, own_ref, c, line_steps(pieces)[-1], pieces)
-
+    early, late = early_late(pieces)
+    for at, step in enumerate(late):
+        take_rows(late_buf.at[at], row_refs[len(early) + at], own_ref, r, c, step, pieces)
     stores = []
-    for at_row, row_ref in enumerate((*row_refs[:-1], last_buf)):
-        first_row = partner(c, line_steps(pieces)[at_row], pieces) * tile_rows
-        rows = row_ref[...]
+    for at_row, step in enumerate(early + late):
+        first_row = partner(c, step, pieces) * tile_rows
+        is_late = at_row >= len(early)
+        rows = late_buf[at_row - len(early)] if is_late else row_refs[at_row][...]
         for at, owner in enumerate(owners):
             subtract_product(share_ref, rows, columns_buf[at], tile, first_row, owner * own_lines, per_row)
-        if at_row == pieces - 1:
+        if is_late:
             subtract_product(share_ref, rows, own_ref[...], tile, first_row, layer * own_lines, per_row)
         for k in range(half):
             lines = tile_rows * per_row
@@ -283,7 +272,7 @@
         out_specs=[pl.BlockSpec(memory_space=pltpu.HBM), pl.BlockSpec(memory_space=pltpu.VMEM)],
         scratch_shapes=[
             pltpu.VMEM((layers - 1, *own_columns.shape), jnp.bfloat16),
-            pltpu.VMEM(row_pieces[0].shape, jnp.bfloat16),
+            pltpu.VMEM((len(early_late(pieces)[1]), *row_pieces[0].shape), jnp.bfloat16),
             pltpu.SemaphoreType.DMA((half * pieces,)),
         ],
         input_output_aliases={len(operands) - 1: 1},
@@ -305,7 +294,11 @@
     )
     share = load_share(factor, trailing.reshape(-1, LANES), layers, col_tiles * tile // LANES)
     loaded_factor, share = lax.optimization_barrier((factor, share))
-    line = gather_line(factor, loaded_factor, moved, count)
+    if count == 4:
+        early = [factor, move(loaded_factor, line_sources(2, count, (1, 3)), count)]
+    else:
+        line = [move(loaded_factor, line_sources(step, count, ()), count) for step in range(1, count)]
+        early, late = [factor, *line[:-1]], line[-1:]
     plane = [moved]
     for step in range(1, count):
         sources = {
@@ -317,13 +310,16 @@
     if count == 4:
         r, c = lax.axis_index("row"), lax.axis_index("col")
         plane[1] = jnp.where((r == c) & (r < 2), factor, plane[1])
+        relayed = jnp.where((r == c) & (r % 2 == 1), moved, early[1])
+        last = move(relayed, line_sources(1, count, ()), count)
+        late_factor, plane[-1] = lax.optimization_barrier((factor, plane[-1]))
+        late = [move(late_factor, line_sources(1, count, range(count)), count), last]
     others = []
     for shift in range(1, layers):
         pairs = [((l + shift) % layers, l) for l in range(layers)]
         others += [lax.ppermute(piece, "layer", pairs) for piece in plane]
-    share, own_columns, *rows = begin_update(plane, line[:-1], share, layers, tile)
-    rows = [line[0], *rows, line[-1]]
-    result = end_update(others, rows, own_columns, share, layers, tile)
+    share, own_columns, *rows = begin_update(plane, early, share, layers, tile)
+    result = end_update(others, [factor, *rows, *late], own_columns, share, layers, tile)
     return result.reshape(half, 1, tile, col_tiles, 1, tile)
 
 

time: 19.6 us -> 22.2 us (1.13)
  starting transfers between devices: 11.8 us -> 14.6 us
    ppermute x6, starting transfers between devices: 7.25 us -> 9.85 us  [move(): lax.ppermute(x, ('row', 'col'), [(a * count + b, r * count + c) for (r, c...]
  transfers between devices with their start and end apart: 11 -> 11, of which waited for: 3 -> 3; matrix products, arithmetic and copies ran while one was open for 0% -> 0% of each run, Pallas kernels for 11% -> 9%
where the time goes in v23:
time: 22.2 us; the launch traced here: 22.1 us
  starting transfers between devices  14.6 us (66%)
  Pallas kernels  5.02 us (23%)
  waiting for transfers between devices  2.36 us (11%)
    ppermute x6, starting transfers between devices, move(): lax.ppermute(x, ('row', 'col'), [(a * count + b, r * count + c) for (r, c...  9.85 us
    ppermute x1, starting transfers between devices, per_device(): lax.ppermute(factor, ('row', 'col'), [(a * count + b, slots[a][b] * count...  3.95 us
    ppermute x6, waiting for transfers between devices, move(): lax.ppermute(x, ('row', 'col'), [(a * count + b, r * count + c) for (r, c...  2.35 us
    pallas_call x1, Pallas kernels, end_update(): pl.pallas_call(body, out_shape=[jax.ShapeDtypeStruct((half * pieces * row...  1.71 us
    pallas_call x1, Pallas kernels, load_share(): pl.pallas_call(body, out_shape=jax.ShapeDtypeStruct((rows + per_row, LANE...  1.6 us
    pallas_call x1, Pallas kernels, make_factor(): pl.pallas_call(factor_kernel, out_shape=jax.ShapeDtypeStruct((half, tile_...  1.34 us
    ppermute x4, starting transfers between devices, per_device(): others += [lax.ppermute(piece, 'layer', pairs) for piece in plane]  0.8 us
  transfers between devices with their start and end apart: 11, of which 3 were waited for; matrix products, arithmetic and copies ran while one was open for 0% of the time, Pallas kernels for 9%

profile of v23, /device:TPU:0, one launch (start us, length us, event | category | flops | bytes accessed | tf_op | source)
XLA Modules:
  0.0 22.1 jit_solution(15462363387742138817)
XLA Ops:
  0.0 1.3 %factor.1.refs_0_.refs_4_ = bf16[2,64,256]{2,1,0:T(8,128)(2,1)S(1)} custom-call(f32[4,1,64,256]{3,2,1,0:T(8,128)} %panel_ref.1, f32[256,256]{1,0:T(8,128)} %inverse_ref.1), custom_call_target="tpu_custom_call" | custom-call | tf_op jit(solution)/shard_map/factor/pallas_call | solution.py:55
  1.4 3.9 %collective-permute-start = (bf16[2,64,256]{2,1,0:T(8,128)(2,1)S(1)}, bf16[2,64,256]{2,1,0:T(8,128)(2,1)S(1)}, u32[]{:S(2)}, u32[]{:S(2)}) collective-permute-start(bf16[2,64,256]{2,1,0:T(8,128)(2,1)S(1)} %factor.1.refs_0_.refs_4_), channel_id=1, source_target_pairs={{0,24},{2,0},{4,8},{6,16},{8,26},{10,2},{12,18},{14,10},{16,4},{18... | collective-permute-start | bytes 196616 | tf_op jit(solution)/shard_map/ppermute | solution.py:292
  5.3 1.6 %load_share.1.refs_6_ = f32[4104,128]{1,0:T(8,128)S(1)} custom-call(bf16[2,64,256]{2,1,0:T(8,128)(2,1)S(1)} %factor.1.refs_0_.refs_4_, f32[8192,128]{1,0:T(8,128)} %bitcast.2), custom_call_target="tpu_custom_call" | custom-call | bytes 4194304 | tf_op jit(solution)/shard_map/load_share/pallas_call | solution.py:127
  6.9 1.5 %collective-permute-start.8 = (bf16[2,64,256]{2,1,0:T(8,128)(2,1)S(1)}, bf16[2,64,256]{2,1,0:T(8,128)(2,1)S(1)}, u32[]{:S(2)}, u32[]{:S(2)}) collective-permute-start(bf16[2,64,256]{2,1,0:T(8,128)(2,1)S(1)} %factor.1.refs_0_.refs_4_), channel_id=1, source_target_pairs={{4,0},{6,2},{0,4},{2,6},{12,8},{26,10},{8,12},{10,14},{20,16},{22,... | collective-permute-start | bytes 196616 | tf_op jit(solution)/shard_map/ppermute | solution.py:103
  8.4 0.0 collective-permute-done.refs_0_
  8.4 3.2 %collective-permute-start.6 = (bf16[2,64,256]{2,1,0:T(8,128)(2,1)S(1)}, bf16[2,64,256]{2,1,0:T(8,128)(2,1)S(1)}, u32[]{:S(2)}, u32[]{:S(2)}) collective-permute-start(bf16[2,64,256]{2,1,0:T(8,128)(2,1)S(1)} %collective-permute-done.refs_0_), channel_id=1, source_target_pairs={{16,0},{26,2},{28,4},{30,6},{24,8},{18,10},{20,12},{22,14},{0,16},... | collective-permute-start | bytes 196616 | tf_op jit(solution)/shard_map/ppermute | solution.py:103
  11.6 1.6 %collective-permute-start.4 = (bf16[2,64,256]{2,1,0:T(8,128)(2,1)S(1)}, bf16[2,64,256]{2,1,0:T(8,128)(2,1)S(1)}, u32[]{:S(2)}, u32[]{:S(2)}) collective-permute-start(bf16[2,64,256]{2,1,0:T(8,128)(2,1)S(1)} %collective-permute-done.refs_0_), channel_id=1, source_target_pairs={{8,0},{18,2},{12,4},{14,6},{0,8},{26,10},{4,12},{6,14},{24,16},{2,... | collective-permute-start | bytes 196616 | tf_op jit(solution)/shard_map/ppermute | solution.py:103
  13.2 1.5 %collective-permute-start.2 = (bf16[2,64,256]{2,1,0:T(8,128)(2,1)S(1)}, bf16[2,64,256]{2,1,0:T(8,128)(2,1)S(1)}, u32[]{:S(2)}, u32[]{:S(2)}) collective-permute-start(bf16[2,64,256]{2,1,0:T(8,128)(2,1)S(1)} %collective-permute-done.refs_0_), channel_id=1, source_target_pairs={{2,0},{10,2},{20,4},{22,6},{16,8},{24,10},{28,12},{30,14},{8,16},{... | collective-permute-start | bytes 196616 | tf_op jit(solution)/shard_map/ppermute | solution.py:103
  14.7 0.0 collective-permute-done.8.refs_5_
  14.7 0.6 %collective-permute-start.10 = (bf16[2,64,256]{2,1,0:T(8,128)(2,1)S(1)}, bf16[2,64,256]{2,1,0:T(8,128)(2,1)S(1)}, u32[]{:S(2)}, u32[]{:S(2)}) collective-permute-start(bf16[2,64,256]{2,1,0:T(8,128)(2,1)S(1)} %broadcast_select_fusion), channel_id=1, source_target_pairs={{2,0},{0,2},{6,4},{4,6},{10,8},{8,10},{14,12},{12,14},{18,16},{16,... | collective-permute-start | bytes 196616 | tf_op jit(solution)/shard_map/ppermute | solution.py:103
  15.3 0.0 collective-permute-start.1
  15.3 0.0 collective-permute-done.6.refs_3_
  15.3 1.5 %collective-permute-start.9 = (bf16[2,64,256]{2,1,0:T(8,128)(2,1)S(1)}, bf16[2,64,256]{2,1,0:T(8,128)(2,1)S(1)}, u32[]{:S(2)}, u32[]{:S(2)}) collective-permute-start(bf16[2,64,256]{2,1,0:T(8,128)(2,1)S(1)} %factor.1.refs_0_.refs_4_), channel_id=1, source_target_pairs={{8,0},{0,2},{6,4},{4,6},{10,8},{2,10},{14,12},{12,14},{18,16},{16,... | collective-permute-start | bytes 196616 | tf_op jit(solution)/shard_map/ppermute | solution.py:103
  16.8 0.0 collective-permute-done.4.refs_2_
  16.8 0.2 %collective-permute-start.7 = (bf16[2,64,256]{2,1,0:T(8,128)(2,1)S(1)}, bf16[2,64,256]{2,1,0:T(8,128)(2,1)S(1)}, u32[]{:S(2)}, u32[]{:S(2)}) collective-permute-start(bf16[2,64,256]{2,1,0:T(8,128)(2,1)S(1)} %collective-permute-done.6.refs_3_), channel_id=1, source_target_pairs={{1,0},{0,1},{3,2},{2,3},{5,4},{4,5},{7,6},{6,7},{9,8},{8,9},{11,10... | collective-permute-start | bytes 196616 | tf_op jit(solution)/shard_map/ppermute | solution.py:320
  17.0 0.5 %collective-permute-done.2 = bf16[2,64,256]{2,1,0:T(8,128)(2,1)S(1)} collective-permute-done((bf16[2,64,256]{2,1,0:T(8,128)(2,1)S(1)}, bf16[2,64,256]{2,1,0:T(8,128)(2,1)S(1)}, u32[]{:S(2)}, u32[]{:S(2)}) %collective-permute-start.2) | collective-permute-done | bytes 65568 | tf_op jit(solution)/shard_map/ppermute | solution.py:103
  17.5 0.0 collective-permute-start.5
  17.5 0.0 collective-permute-done.1.refs_0_
  17.5 0.6 %collective-permute-start.3 = (bf16[2,64,256]{2,1,0:T(8,128)(2,1)S(1)}, bf16[2,64,256]{2,1,0:T(8,128)(2,1)S(1)}, u32[]{:S(2)}, u32[]{:S(2)}) collective-permute-start(bf16[2,64,256]{2,1,0:T(8,128)(2,1)S(1)} %broadcast_select_fusion.1.refs_1_), channel_id=1, source_target_pairs={{1,0},{0,1},{3,2},{2,3},{5,4},{4,5},{7,6},{6,7},{9,8},{8,9},{11,10... | collective-permute-start | bytes 196616 | tf_op jit(solution)/shard_map/ppermute | solution.py:320
  18.1 0.4 %begin_update.1 = (f32[4104,128]{1,0:T(8,128)S(1)}, bf16[512,256]{1,0:T(8,128)(2,1)S(1)}, bf16[2,64,256]{2,1,0:T(8,128)(2,1)S(1)}) custom-call(bf16[2,64,256]{2,1,0:T(8,128)(2,1)S(1)} %collective-permute-done.refs_0_, bf16[2,64,256]{2,1,0:T(8,128)(2,1)S(1)} %broadcast_select_fusion.1.refs_1_, ...), custom_call_target="tpu_custom_call", output_to_operand_aliasing={{0}: (6, {})} | custom-call | tf_op jit(solution)/shard_map/begin_update/pallas_call | solution.py:204
  18.4 0.6 %collective-permute-done.10.refs_7_ = bf16[2,64,256]{2,1,0:T(8,128)(2,1)S(1)} collective-permute-done((bf16[2,64,256]{2,1,0:T(8,128)(2,1)S(1)}, bf16[2,64,256]{2,1,0:T(8,128)(2,1)S(1)}, u32[]{:S(2)}, u32[]{:S(2)}) %collective-permute-start.10) | collective-permute-done | bytes 65568 | tf_op jit(solution)/shard_map/ppermute | solution.py:103
  19.0 1.3 %collective-permute-done.9.refs_6_ = bf16[2,64,256]{2,1,0:T(8,128)(2,1)S(1)} collective-permute-done((bf16[2,64,256]{2,1,0:T(8,128)(2,1)S(1)}, bf16[2,64,256]{2,1,0:T(8,128)(2,1)S(1)}, u32[]{:S(2)}, u32[]{:S(2)}) %collective-permute-start.9) | collective-permute-done | bytes 65568 | tf_op jit(solution)/shard_map/ppermute | solution.py:103
  20.3 0.0 collective-permute-done.7.refs_3_
  20.3 0.0 collective-permute-done.5.refs_2_
  20.3 0.0 collective-permute-done.3.refs_1_
  20.3 1.7 %end_update.1 = (f32[4096,128]{1,0:T(8,128)}, f32[4104,128]{1,0:T(8,128)S(1)}) custom-call(bf16[2,64,256]{2,1,0:T(8,128)(2,1)S(1)} %collective-permute-done.1.refs_0_, bf16[2,64,256]{2,1,0:T(8,128)(2,1)S(1)} %collective-permute-done.3.refs_1_, bf16[2,64,256]{2,1,0:T(8,128)(2,1)S(1)} %collective-permute-done.5.refs_2_, ...), custom_call_target="tpu_custom_call", output_to_operand_aliasing={{1}: (9, {})} | custom-call | tf_op jit(solution)/shard_map/end_update/pallas_call | solution.py:265
  (2 shorter events, 0.0 us)
Async XLA Ops:
  1.4 7.0 %collective-permute-start = (bf16[2,64,256]{2,1,0:T(8,128)(2,1)S(1)}, bf16[2,64,256]{2,1,0:T(8,128)(2,1)S(1)}, u32[]{:S(2)}, u32[]{:S(2)}) collective-permute-start(bf16[2,64,256]{2,1,0:T(8,128)(2,1)S(1)} %factor.1.refs_0_.refs_4_), channel_id=1, source_target_pairs={{0,24},{2,0},{4,8},{6,16},{8,26},{10,2},{12,18},{14,10},{16,4},{18... | collective-permute-start | bytes 196616 | tf_op jit(solution)/shard_map/ppermute | solution.py:292
  6.9 7.8 %collective-permute-start.8 = (bf16[2,64,256]{2,1,0:T(8,128)(2,1)S(1)}, bf16[2,64,256]{2,1,0:T(8,128)(2,1)S(1)}, u32[]{:S(2)}, u32[]{:S(2)}) collective-permute-start(bf16[2,64,256]{2,1,0:T(8,128)(2,1)S(1)} %factor.1.refs_0_.refs_4_), channel_id=1, source_target_pairs={{4,0},{6,2},{0,4},{2,6},{12,8},{26,10},{8,12},{10,14},{20,16},{22,... | collective-permute-start | bytes 196616 | tf_op jit(solution)/shard_map/ppermute | solution.py:103
  8.4 7.0 %collective-permute-start.6 = (bf16[2,64,256]{2,1,0:T(8,128)(2,1)S(1)}, bf16[2,64,256]{2,1,0:T(8,128)(2,1)S(1)}, u32[]{:S(2)}, u32[]{:S(2)}) collective-permute-start(bf16[2,64,256]{2,1,0:T(8,128)(2,1)S(1)} %collective-permute-done.refs_0_), channel_id=1, source_target_pairs={{16,0},{26,2},{28,4},{30,6},{24,8},{18,10},{20,12},{22,14},{0,16},... | collective-permute-start | bytes 196616 | tf_op jit(solution)/shard_map/ppermute | solution.py:103
  11.6 5.2 %collective-permute-start.4 = (bf16[2,64,256]{2,1,0:T(8,128)(2,1)S(1)}, bf16[2,64,256]{2,1,0:T(8,128)(2,1)S(1)}, u32[]{:S(2)}, u32[]{:S(2)}) collective-permute-start(bf16[2,64,256]{2,1,0:T(8,128)(2,1)S(1)} %collective-permute-done.refs_0_), channel_id=1, source_target_pairs={{8,0},{18,2},{12,4},{14,6},{0,8},{26,10},{4,12},{6,14},{24,16},{2,... | collective-permute-start | bytes 196616 | tf_op jit(solution)/shard_map/ppermute | solution.py:103
  13.2 4.3 %collective-permute-start.2 = (bf16[2,64,256]{2,1,0:T(8,128)(2,1)S(1)}, bf16[2,64,256]{2,1,0:T(8,128)(2,1)S(1)}, u32[]{:S(2)}, u32[]{:S(2)}) collective-permute-start(bf16[2,64,256]{2,1,0:T(8,128)(2,1)S(1)} %collective-permute-done.refs_0_), channel_id=1, source_target_pairs={{2,0},{10,2},{20,4},{22,6},{16,8},{24,10},{28,12},{30,14},{8,16},{... | collective-permute-start | bytes 196616 | tf_op jit(solution)/shard_map/ppermute | solution.py:103
  14.7 4.3 %collective-permute-start.10 = (bf16[2,64,256]{2,1,0:T(8,128)(2,1)S(1)}, bf16[2,64,256]{2,1,0:T(8,128)(2,1)S(1)}, u32[]{:S(2)}, u32[]{:S(2)}) collective-permute-start(bf16[2,64,256]{2,1,0:T(8,128)(2,1)S(1)} %broadcast_select_fusion), channel_id=1, source_target_pairs={{2,0},{0,2},{6,4},{4,6},{10,8},{8,10},{14,12},{12,14},{18,16},{16,... | collective-permute-start | bytes 196616 | tf_op jit(solution)/shard_map/ppermute | solution.py:103
  15.3 2.2 %collective-permute-start.1 = (bf16[2,64,256]{2,1,0:T(8,128)(2,1)S(1)}, bf16[2,64,256]{2,1,0:T(8,128)(2,1)S(1)}, u32[]{:S(2)}, u32[]{:S(2)}) collective-permute-start(bf16[2,64,256]{2,1,0:T(8,128)(2,1)S(1)} %collective-permute-done.refs_0_), channel_id=1, source_target_pairs={{1,0},{0,1},{3,2},{2,3},{5,4},{4,5},{7,6},{6,7},{9,8},{8,9},{11,10... | collective-permute-start | bytes 196616 | tf_op jit(solution)/shard_map/ppermute | solution.py:320
  15.3 5.0 %collective-permute-start.9 = (bf16[2,64,256]{2,1,0:T(8,128)(2,1)S(1)}, bf16[2,64,256]{2,1,0:T(8,128)(2,1)S(1)}, u32[]{:S(2)}, u32[]{:S(2)}) collective-permute-start(bf16[2,64,256]{2,1,0:T(8,128)(2,1)S(1)} %factor.1.refs_0_.refs_4_), channel_id=1, source_target_pairs={{8,0},{0,2},{6,4},{4,6},{10,8},{2,10},{14,12},{12,14},{18,16},{16,... | collective-permute-start | bytes 196616 | tf_op jit(solution)/shard_map/ppermute | solution.py:103
  16.8 3.6 %collective-permute-start.7 = (bf16[2,64,256]{2,1,0:T(8,128)(2,1)S(1)}, bf16[2,64,256]{2,1,0:T(8,128)(2,1)S(1)}, u32[]{:S(2)}, u32[]{:S(2)}) collective-permute-start(bf16[2,64,256]{2,1,0:T(8,128)(2,1)S(1)} %collective-permute-done.6.refs_3_), channel_id=1, source_target_pairs={{1,0},{0,1},{3,2},{2,3},{5,4},{4,5},{7,6},{6,7},{9,8},{8,9},{11,10... | collective-permute-start | bytes 196616 | tf_op jit(solution)/shard_map/ppermute | solution.py:320
  17.5 2.9 %collective-permute-start.5 = (bf16[2,64,256]{2,1,0:T(8,128)(2,1)S(1)}, bf16[2,64,256]{2,1,0:T(8,128)(2,1)S(1)}, u32[]{:S(2)}, u32[]{:S(2)}) collective-permute-start(bf16[2,64,256]{2,1,0:T(8,128)(2,1)S(1)} %collective-permute-done.4.refs_2_), channel_id=1, source_target_pairs={{1,0},{0,1},{3,2},{2,3},{5,4},{4,5},{7,6},{6,7},{9,8},{8,9},{11,10... | collective-permute-start | bytes 196616 | tf_op jit(solution)/shard_map/ppermute | solution.py:320
  17.5 2.8 %collective-permute-start.3 = (bf16[2,64,256]{2,1,0:T(8,128)(2,1)S(1)}, bf16[2,64,256]{2,1,0:T(8,128)(2,1)S(1)}, u32[]{:S(2)}, u32[]{:S(2)}) collective-permute-start(bf16[2,64,256]{2,1,0:T(8,128)(2,1)S(1)} %broadcast_select_fusion.1.refs_1_), channel_id=1, source_target_pairs={{1,0},{0,1},{3,2},{2,3},{5,4},{4,5},{7,6},{6,7},{9,8},{8,9},{11,10... | collective-permute-start | bytes 196616 | tf_op jit(solution)/shard_map/ppermute | solution.py:320

commit v24 on v22

--- a/solution.py
+++ b/solution.py
@@ -181,10 +181,11 @@
 
 def begin_kernel(pieces, layers, tile, *refs):
     column_refs, row_refs, rest = refs[:pieces], refs[pieces : 2 * pieces - 1], refs[2 * pieces - 1 :]
-    _, share_ref, columns_ref, *line_refs = rest
+    loaded_ref, share_ref, columns_ref, *line_refs = rest
     r, c, layer = (lax.axis_index(axis) for axis in AXES)
     half, tile_rows, _ = row_refs[0].shape
     own_lines = half * tile // LANES
+    share_ref[...] = loaded_ref[...]
     fill_columns(columns_ref, column_refs, plane_slots(pieces), r, c, layer)
     for line_ref, row_ref in zip(line_refs, row_refs[1:]):
         line_ref[...] = row_ref[...]
@@ -227,7 +228,7 @@
 def end_kernel(pieces, layers, tile, *refs):
     others = pieces * (layers - 1)
     column_refs, row_refs, rest = refs[:others], refs[others : others + pieces], refs[others + pieces :]
-    own_ref, _, out_ref, share_ref, columns_buf, last_buf, sems = rest
+    own_ref, share_ref, out_ref, _, columns_buf, last_buf, sems = rest
     r, c, layer = (lax.axis_index(axis) for axis in AXES)
     half, tile_rows, _ = row_refs[0].shape
     own_lines = half * tile // LANES

time: 19.6 us -> 19.6 us (level)
  Pallas kernels: 5.14 us -> 5.4 us
  waiting for transfers between devices: 2.4 us -> 2.14 us
    pallas_call x1, Pallas kernels: 0.5 us -> 0.76 us  [begin_update(): pl.pallas_call(body, out_shape=[jax.ShapeDtypeStruct(share.shape, jnp.flo...]
    ppermute x6, waiting for transfers between devices: 2.38 us -> 2.12 us  [move(): lax.ppermute(x, ('row', 'col'), [(a * count + b, r * count + c) for (r, c...]
  transfers between devices with their start and end apart: 11 -> 11, of which waited for: 3 -> 3; matrix products, arithmetic and copies ran while one was open for 0% -> 0% of each run, Pallas kernels for 11% -> 12%
where the time goes in v24:
time: 19.6 us; the launch traced here: 19.4 us
  starting transfers between devices  11.8 us (60%)
  Pallas kernels  5.4 us (28%)
  waiting for transfers between devices  2.14 us (11%)
    ppermute x6, starting transfers between devices, move(): lax.ppermute(x, ('row', 'col'), [(a * count + b, r * count + c) for (r, c...  7.25 us
    ppermute x1, starting transfers between devices, per_device(): lax.ppermute(factor, ('row', 'col'), [(a * count + b, slots[a][b] * count...  3.95 us
    ppermute x6, waiting for transfers between devices, move(): lax.ppermute(x, ('row', 'col'), [(a * count + b, r * count + c) for (r, c...  2.12 us
    pallas_call x1, Pallas kernels, end_update(): pl.pallas_call(body, out_shape=[jax.ShapeDtypeStruct((half * pieces * row...  1.7 us
    pallas_call x1, Pallas kernels, load_share(): pl.pallas_call(body, out_shape=jax.ShapeDtypeStruct((rows + per_row, LANE...  1.6 us
    pallas_call x1, Pallas kernels, make_factor(): pl.pallas_call(factor_kernel, out_shape=jax.ShapeDtypeStruct((half, tile_...  1.34 us
    pallas_call x1, Pallas kernels, begin_update(): pl.pallas_call(body, out_shape=[jax.ShapeDtypeStruct(share.shape, jnp.flo...  0.76 us
    ppermute x4, starting transfers between devices, per_device(): others += [lax.ppermute(piece, 'layer', pairs) for piece in plane]  0.59 us
  transfers between devices with their start and end apart: 11, of which 3 were waited for; matrix products, arithmetic and copies ran while one was open for 0% of the time, Pallas kernels for 12%

profile of v24, /device:TPU:0, one launch (start us, length us, event | category | flops | bytes accessed | tf_op | source)
XLA Modules:
  0.0 19.4 jit_solution(2726640743355949163)
XLA Ops:
  0.0 1.3 %factor.1.refs_0_.refs_4_ = bf16[2,64,256]{2,1,0:T(8,128)(2,1)S(1)} custom-call(f32[4,1,64,256]{3,2,1,0:T(8,128)} %panel_ref.1, f32[256,256]{1,0:T(8,128)} %inverse_ref.1), custom_call_target="tpu_custom_call" | custom-call | tf_op jit(solution)/shard_map/factor/pallas_call | solution.py:55
  1.4 3.9 %collective-permute-start = (bf16[2,64,256]{2,1,0:T(8,128)(2,1)S(1)}, bf16[2,64,256]{2,1,0:T(8,128)(2,1)S(1)}, u32[]{:S(2)}, u32[]{:S(2)}) collective-permute-start(bf16[2,64,256]{2,1,0:T(8,128)(2,1)S(1)} %factor.1.refs_0_.refs_4_), channel_id=1, source_target_pairs={{0,24},{2,0},{4,8},{6,16},{8,26},{10,2},{12,18},{14,10},{16,4},{18... | collective-permute-start | bytes 196616 | tf_op jit(solution)/shard_map/ppermute | solution.py:304
  5.3 1.6 %load_share.1.refs_7_ = f32[4104,128]{1,0:T(8,128)S(1)} custom-call(bf16[2,64,256]{2,1,0:T(8,128)(2,1)S(1)} %factor.1.refs_0_.refs_4_, f32[8192,128]{1,0:T(8,128)} %bitcast.2), custom_call_target="tpu_custom_call" | custom-call | bytes 4194304 | tf_op jit(solution)/shard_map/load_share/pallas_call | solution.py:135
  6.9 0.1 collective-permute-start.9
  7.0 2.9 %collective-permute-start.8 = (bf16[2,64,256]{2,1,0:T(8,128)(2,1)S(1)}, bf16[2,64,256]{2,1,0:T(8,128)(2,1)S(1)}, u32[]{:S(2)}, u32[]{:S(2)}) collective-permute-start(bf16[2,64,256]{2,1,0:T(8,128)(2,1)S(1)} %factor.1.refs_0_.refs_4_), channel_id=1, source_target_pairs={{4,0},{6,2},{0,4},{2,6},{12,8},{26,10},{8,12},{10,14},{20,16},{22,... | collective-permute-start | bytes 196616 | tf_op jit(solution)/shard_map/ppermute | solution.py:103
  9.8 0.0 collective-permute-done.refs_0_
  9.9 1.7 %collective-permute-start.6 = (bf16[2,64,256]{2,1,0:T(8,128)(2,1)S(1)}, bf16[2,64,256]{2,1,0:T(8,128)(2,1)S(1)}, u32[]{:S(2)}, u32[]{:S(2)}) collective-permute-start(bf16[2,64,256]{2,1,0:T(8,128)(2,1)S(1)} %collective-permute-done.refs_0_), channel_id=1, source_target_pairs={{16,0},{26,2},{28,4},{30,6},{24,8},{18,10},{20,12},{22,14},{0,16},... | collective-permute-start | bytes 196616 | tf_op jit(solution)/shard_map/ppermute | solution.py:103
  11.6 0.5 %collective-permute-start.4 = (bf16[2,64,256]{2,1,0:T(8,128)(2,1)S(1)}, bf16[2,64,256]{2,1,0:T(8,128)(2,1)S(1)}, u32[]{:S(2)}, u32[]{:S(2)}) collective-permute-start(bf16[2,64,256]{2,1,0:T(8,128)(2,1)S(1)} %collective-permute-done.refs_0_), channel_id=1, source_target_pairs={{8,0},{18,2},{12,4},{14,6},{0,8},{26,10},{4,12},{6,14},{24,16},{2,... | collective-permute-start | bytes 196616 | tf_op jit(solution)/shard_map/ppermute | solution.py:103
  12.1 1.3 %collective-permute-start.2 = (bf16[2,64,256]{2,1,0:T(8,128)(2,1)S(1)}, bf16[2,64,256]{2,1,0:T(8,128)(2,1)S(1)}, u32[]{:S(2)}, u32[]{:S(2)}) collective-permute-start(bf16[2,64,256]{2,1,0:T(8,128)(2,1)S(1)} %collective-permute-done.refs_0_), channel_id=1, source_target_pairs={{2,0},{10,2},{20,4},{22,6},{16,8},{24,10},{28,12},{30,14},{8,16},{... | collective-permute-start | bytes 196616 | tf_op jit(solution)/shard_map/ppermute | solution.py:103
  13.3 0.0 collective-permute-done.9.refs_6_
  13.3 0.0 collective-permute-done.8.refs_5_
  13.4 0.8 %collective-permute-start.10 = (bf16[2,64,256]{2,1,0:T(8,128)(2,1)S(1)}, bf16[2,64,256]{2,1,0:T(8,128)(2,1)S(1)}, u32[]{:S(2)}, u32[]{:S(2)}) collective-permute-start(bf16[2,64,256]{2,1,0:T(8,128)(2,1)S(1)} %select_select_fusion), channel_id=1, source_target_pairs={{2,0},{0,2},{6,4},{4,6},{10,8},{8,10},{14,12},{12,14},{18,16},{16,... | collective-permute-start | bytes 196616 | tf_op jit(solution)/shard_map/ppermute | solution.py:103
  14.2 0.0 collective-permute-start.1
  14.2 0.0 collective-permute-done.6.refs_3_
  14.2 0.5 %collective-permute-start.7 = (bf16[2,64,256]{2,1,0:T(8,128)(2,1)S(1)}, bf16[2,64,256]{2,1,0:T(8,128)(2,1)S(1)}, u32[]{:S(2)}, u32[]{:S(2)}) collective-permute-start(bf16[2,64,256]{2,1,0:T(8,128)(2,1)S(1)} %collective-permute-done.6.refs_3_), channel_id=1, source_target_pairs={{1,0},{0,1},{3,2},{2,3},{5,4},{4,5},{7,6},{6,7},{9,8},{8,9},{11,10... | collective-permute-start | bytes 196616 | tf_op jit(solution)/shard_map/ppermute | solution.py:324
  14.7 1.1 %collective-permute-done.4.refs_2_ = bf16[2,64,256]{2,1,0:T(8,128)(2,1)S(1)} collective-permute-done((bf16[2,64,256]{2,1,0:T(8,128)(2,1)S(1)}, bf16[2,64,256]{2,1,0:T(8,128)(2,1)S(1)}, u32[]{:S(2)}, u32[]{:S(2)}) %collective-permute-start.4) | collective-permute-done | bytes 65568 | tf_op jit(solution)/shard_map/ppermute | solution.py:103
  15.8 0.0 collective-permute-start.5
  15.8 0.5 %collective-permute-done.2 = bf16[2,64,256]{2,1,0:T(8,128)(2,1)S(1)} collective-permute-done((bf16[2,64,256]{2,1,0:T(8,128)(2,1)S(1)}, bf16[2,64,256]{2,1,0:T(8,128)(2,1)S(1)}, u32[]{:S(2)}, u32[]{:S(2)}) %collective-permute-start.2) | collective-permute-done | bytes 65568 | tf_op jit(solution)/shard_map/ppermute | solution.py:103
  16.4 0.1 collective-permute-start.3
  16.4 0.8 %begin_update.1 = (f32[4104,128]{1,0:T(8,128)S(1)}, bf16[512,256]{1,0:T(8,128)(2,1)S(1)}, bf16[2,64,256]{2,1,0:T(8,128)(2,1)S(1)}, bf16[2,64,256]{2,1,0:T(8,128)(2,1)S(1)}) custom-call(bf16[2,64,256]{2,1,0:T(8,128)(2,1)S(1)} %collective-permute-done.refs_0_, bf16[2,64,256]{2,1,0:T(8,128)(2,1)S(1)} %broadcast_select_fusion.refs_1_, ...), custom_call_target="tpu_custom_call", output_to_operand_aliasing={{0}: (7, {})} | custom-call | tf_op jit(solution)/shard_map/begin_update/pallas_call | solution.py:213
  17.2 0.0 collective-permute-done.1.refs_0_
  17.2 0.5 %collective-permute-done.10.refs_7_ = bf16[2,64,256]{2,1,0:T(8,128)(2,1)S(1)} collective-permute-done((bf16[2,64,256]{2,1,0:T(8,128)(2,1)S(1)}, bf16[2,64,256]{2,1,0:T(8,128)(2,1)S(1)}, u32[]{:S(2)}, u32[]{:S(2)}) %collective-permute-start.10) | collective-permute-done | bytes 65568 | tf_op jit(solution)/shard_map/ppermute | solution.py:103
  17.7 0.0 collective-permute-done.7.refs_3_
  17.7 0.0 collective-permute-done.5.refs_2_
  17.7 0.0 collective-permute-done.3.refs_1_
  17.7 1.7 %end_update.1 = (f32[4096,128]{1,0:T(8,128)}, f32[4104,128]{1,0:T(8,128)S(1)}) custom-call(bf16[2,64,256]{2,1,0:T(8,128)(2,1)S(1)} %collective-permute-done.1.refs_0_, bf16[2,64,256]{2,1,0:T(8,128)(2,1)S(1)} %collective-permute-done.3.refs_1_, bf16[2,64,256]{2,1,0:T(8,128)(2,1)S(1)} %collective-permute-done.5.refs_2_, ...), custom_call_target="tpu_custom_call", output_to_operand_aliasing={{1}: (9, {})} | custom-call | tf_op jit(solution)/shard_map/end_update/pallas_call | solution.py:277
  (2 shorter events, 0.0 us)
Async XLA Ops:
  1.4 8.5 %collective-permute-start = (bf16[2,64,256]{2,1,0:T(8,128)(2,1)S(1)}, bf16[2,64,256]{2,1,0:T(8,128)(2,1)S(1)}, u32[]{:S(2)}, u32[]{:S(2)}) collective-permute-start(bf16[2,64,256]{2,1,0:T(8,128)(2,1)S(1)} %factor.1.refs_0_.refs_4_), channel_id=1, source_target_pairs={{0,24},{2,0},{4,8},{6,16},{8,26},{10,2},{12,18},{14,10},{16,4},{18... | collective-permute-start | bytes 196616 | tf_op jit(solution)/shard_map/ppermute | solution.py:304
  6.9 6.4 %collective-permute-start.9 = (bf16[2,64,256]{2,1,0:T(8,128)(2,1)S(1)}, bf16[2,64,256]{2,1,0:T(8,128)(2,1)S(1)}, u32[]{:S(2)}, u32[]{:S(2)}) collective-permute-start(bf16[2,64,256]{2,1,0:T(8,128)(2,1)S(1)} %factor.1.refs_0_.refs_4_), channel_id=1, source_target_pairs={{8,0},{0,2},{6,4},{4,6},{10,8},{2,10},{14,12},{12,14},{18,16},{16,... | collective-permute-start | bytes 196616 | tf_op jit(solution)/shard_map/ppermute | solution.py:103
  7.0 6.4 %collective-permute-start.8 = (bf16[2,64,256]{2,1,0:T(8,128)(2,1)S(1)}, bf16[2,64,256]{2,1,0:T(8,128)(2,1)S(1)}, u32[]{:S(2)}, u32[]{:S(2)}) collective-permute-start(bf16[2,64,256]{2,1,0:T(8,128)(2,1)S(1)} %factor.1.refs_0_.refs_4_), channel_id=1, source_target_pairs={{4,0},{6,2},{0,4},{2,6},{12,8},{26,10},{8,12},{10,14},{20,16},{22,... | collective-permute-start | bytes 196616 | tf_op jit(solution)/shard_map/ppermute | solution.py:103
  9.9 4.3 %collective-permute-start.6 = (bf16[2,64,256]{2,1,0:T(8,128)(2,1)S(1)}, bf16[2,64,256]{2,1,0:T(8,128)(2,1)S(1)}, u32[]{:S(2)}, u32[]{:S(2)}) collective-permute-start(bf16[2,64,256]{2,1,0:T(8,128)(2,1)S(1)} %collective-permute-done.refs_0_), channel_id=1, source_target_pairs={{16,0},{26,2},{28,4},{30,6},{24,8},{18,10},{20,12},{22,14},{0,16},... | collective-permute-start | bytes 196616 | tf_op jit(solution)/shard_map/ppermute | solution.py:103
  11.6 4.3 %collective-permute-start.4 = (bf16[2,64,256]{2,1,0:T(8,128)(2,1)S(1)}, bf16[2,64,256]{2,1,0:T(8,128)(2,1)S(1)}, u32[]{:S(2)}, u32[]{:S(2)}) collective-permute-start(bf16[2,64,256]{2,1,0:T(8,128)(2,1)S(1)} %collective-permute-done.refs_0_), channel_id=1, source_target_pairs={{8,0},{18,2},{12,4},{14,6},{0,8},{26,10},{4,12},{6,14},{24,16},{2,... | collective-permute-start | bytes 196616 | tf_op jit(solution)/shard_map/ppermute | solution.py:103
  12.1 4.3 %collective-permute-start.2 = (bf16[2,64,256]{2,1,0:T(8,128)(2,1)S(1)}, bf16[2,64,256]{2,1,0:T(8,128)(2,1)S(1)}, u32[]{:S(2)}, u32[]{:S(2)}) collective-permute-start(bf16[2,64,256]{2,1,0:T(8,128)(2,1)S(1)} %collective-permute-done.refs_0_), channel_id=1, source_target_pairs={{2,0},{10,2},{20,4},{22,6},{16,8},{24,10},{28,12},{30,14},{8,16},{... | collective-permute-start | bytes 196616 | tf_op jit(solution)/shard_map/ppermute | solution.py:103
  13.4 4.3 %collective-permute-start.10 = (bf16[2,64,256]{2,1,0:T(8,128)(2,1)S(1)}, bf16[2,64,256]{2,1,0:T(8,128)(2,1)S(1)}, u32[]{:S(2)}, u32[]{:S(2)}) collective-permute-start(bf16[2,64,256]{2,1,0:T(8,128)(2,1)S(1)} %select_select_fusion), channel_id=1, source_target_pairs={{2,0},{0,2},{6,4},{4,6},{10,8},{8,10},{14,12},{12,14},{18,16},{16,... | collective-permute-start | bytes 196616 | tf_op jit(solution)/shard_map/ppermute | solution.py:103
  14.2 3.0 %collective-permute-start.1 = (bf16[2,64,256]{2,1,0:T(8,128)(2,1)S(1)}, bf16[2,64,256]{2,1,0:T(8,128)(2,1)S(1)}, u32[]{:S(2)}, u32[]{:S(2)}) collective-permute-start(bf16[2,64,256]{2,1,0:T(8,128)(2,1)S(1)} %collective-permute-done.refs_0_), channel_id=1, source_target_pairs={{1,0},{0,1},{3,2},{2,3},{5,4},{4,5},{7,6},{6,7},{9,8},{8,9},{11,10... | collective-permute-start | bytes 196616 | tf_op jit(solution)/shard_map/ppermute | solution.py:324
  14.2 3.5 %collective-permute-start.7 = (bf16[2,64,256]{2,1,0:T(8,128)(2,1)S(1)}, bf16[2,64,256]{2,1,0:T(8,128)(2,1)S(1)}, u32[]{:S(2)}, u32[]{:S(2)}) collective-permute-start(bf16[2,64,256]{2,1,0:T(8,128)(2,1)S(1)} %collective-permute-done.6.refs_3_), channel_id=1, source_target_pairs={{1,0},{0,1},{3,2},{2,3},{5,4},{4,5},{7,6},{6,7},{9,8},{8,9},{11,10... | collective-permute-start | bytes 196616 | tf_op jit(solution)/shard_map/ppermute | solution.py:324
  15.8 1.9 %collective-permute-start.5 = (bf16[2,64,256]{2,1,0:T(8,128)(2,1)S(1)}, bf16[2,64,256]{2,1,0:T(8,128)(2,1)S(1)}, u32[]{:S(2)}, u32[]{:S(2)}) collective-permute-start(bf16[2,64,256]{2,1,0:T(8,128)(2,1)S(1)} %collective-permute-done.4.refs_2_), channel_id=1, source_target_pairs={{1,0},{0,1},{3,2},{2,3},{5,4},{4,5},{7,6},{6,7},{9,8},{8,9},{11,10... | collective-permute-start | bytes 196616 | tf_op jit(solution)/shard_map/ppermute | solution.py:324
  16.4 1.4 %collective-permute-start.3 = (bf16[2,64,256]{2,1,0:T(8,128)(2,1)S(1)}, bf16[2,64,256]{2,1,0:T(8,128)(2,1)S(1)}, u32[]{:S(2)}, u32[]{:S(2)}) collective-permute-start(bf16[2,64,256]{2,1,0:T(8,128)(2,1)S(1)} %broadcast_select_fusion.refs_1_), channel_id=1, source_target_pairs={{1,0},{0,1},{3,2},{2,3},{5,4},{4,5},{7,6},{6,7},{9,8},{8,9},{11,10... | collective-permute-start | bytes 196616 | tf_op jit(solution)/shard_map/ppermute | solution.py:324

commit v25 on v24

--- a/solution.py
+++ b/solution.py
@@ -73,7 +73,7 @@
 
 def plane_slots(count):
     if count == 4:
-        return ((3, 0, 1, 2), (3, 0, 2, 1), (0, 2, 1, 3), (2, 3, 1, 0))
+        return ((3, 0, 1, 2), (3, 0, 2, 1), (3, 2, 1, 0), (2, 3, 1, 0))
     return tuple(tuple(count - 1 - b for b in range(count)) for _ in range(count))
 
 

time: 19.6 us -> 19.6 us (level)
  no operation moved by 1% of the time
where the time goes in v25:
time: 19.6 us; the launch traced here: 19.4 us
  starting transfers between devices  11.8 us (60%)
  Pallas kernels  5.4 us (28%)
  waiting for transfers between devices  2.14 us (11%)
    ppermute x6, starting transfers between devices, move(): lax.ppermute(x, ('row', 'col'), [(a * count + b, r * count + c) for (r, c...  7.25 us
    ppermute x1, starting transfers between devices, per_device(): lax.ppermute(factor, ('row', 'col'), [(a * count + b, slots[a][b] * count...  3.95 us
    ppermute x6, waiting for transfers between devices, move(): lax.ppermute(x, ('row', 'col'), [(a * count + b, r * count + c) for (r, c...  2.12 us
    pallas_call x1, Pallas kernels, end_update(): pl.pallas_call(body, out_shape=[jax.ShapeDtypeStruct((half * pieces * row...  1.7 us
    pallas_call x1, Pallas kernels, load_share(): pl.pallas_call(body, out_shape=jax.ShapeDtypeStruct((rows + per_row, LANE...  1.6 us
    pallas_call x1, Pallas kernels, make_factor(): pl.pallas_call(factor_kernel, out_shape=jax.ShapeDtypeStruct((half, tile_...  1.34 us
    pallas_call x1, Pallas kernels, begin_update(): pl.pallas_call(body, out_shape=[jax.ShapeDtypeStruct(share.shape, jnp.flo...  0.76 us
    ppermute x4, starting transfers between devices, per_device(): others += [lax.ppermute(piece, 'layer', pairs) for piece in plane]  0.58 us
  transfers between devices with their start and end apart: 11, of which 3 were waited for; matrix products, arithmetic and copies ran while one was open for 0% of the time, Pallas kernels for 12%

profile of v25, /device:TPU:0, one launch (start us, length us, event | category | flops | bytes accessed | tf_op | source)
XLA Modules:
  0.0 19.4 jit_solution(2830375339628968699)
XLA Ops:
  0.0 1.3 %factor.1.refs_0_.refs_4_ = bf16[2,64,256]{2,1,0:T(8,128)(2,1)S(1)} custom-call(f32[4,1,64,256]{3,2,1,0:T(8,128)} %panel_ref.1, f32[256,256]{1,0:T(8,128)} %inverse_ref.1), custom_call_target="tpu_custom_call" | custom-call | tf_op jit(solution)/shard_map/factor/pallas_call | solution.py:55
  1.4 3.9 %collective-permute-start = (bf16[2,64,256]{2,1,0:T(8,128)(2,1)S(1)}, bf16[2,64,256]{2,1,0:T(8,128)(2,1)S(1)}, u32[]{:S(2)}, u32[]{:S(2)}) collective-permute-start(bf16[2,64,256]{2,1,0:T(8,128)(2,1)S(1)} %factor.1.refs_0_.refs_4_), channel_id=1, source_target_pairs={{0,24},{2,0},{4,8},{6,16},{8,26},{10,2},{12,18},{14,10},{16,28},{1... | collective-permute-start | bytes 196616 | tf_op jit(solution)/shard_map/ppermute | solution.py:304
  5.3 1.6 %load_share.1.refs_7_ = f32[4104,128]{1,0:T(8,128)S(1)} custom-call(bf16[2,64,256]{2,1,0:T(8,128)(2,1)S(1)} %factor.1.refs_0_.refs_4_, f32[8192,128]{1,0:T(8,128)} %bitcast.2), custom_call_target="tpu_custom_call" | custom-call | bytes 4194304 | tf_op jit(solution)/shard_map/load_share/pallas_call | solution.py:135
  6.9 0.1 collective-permute-start.9
  7.0 2.9 %collective-permute-start.8 = (bf16[2,64,256]{2,1,0:T(8,128)(2,1)S(1)}, bf16[2,64,256]{2,1,0:T(8,128)(2,1)S(1)}, u32[]{:S(2)}, u32[]{:S(2)}) collective-permute-start(bf16[2,64,256]{2,1,0:T(8,128)(2,1)S(1)} %factor.1.refs_0_.refs_4_), channel_id=1, source_target_pairs={{4,0},{6,2},{0,4},{2,6},{12,8},{26,10},{8,12},{10,14},{20,16},{22,... | collective-permute-start | bytes 196616 | tf_op jit(solution)/shard_map/ppermute | solution.py:103
  9.8 0.0 collective-permute-done.refs_0_
  9.9 1.5 %collective-permute-start.6 = (bf16[2,64,256]{2,1,0:T(8,128)(2,1)S(1)}, bf16[2,64,256]{2,1,0:T(8,128)(2,1)S(1)}, u32[]{:S(2)}, u32[]{:S(2)}) collective-permute-start(bf16[2,64,256]{2,1,0:T(8,128)(2,1)S(1)} %collective-permute-done.refs_0_), channel_id=1, source_target_pairs={{16,0},{26,2},{28,4},{30,6},{24,8},{18,10},{20,12},{22,14},{0,16},... | collective-permute-start | bytes 196616 | tf_op jit(solution)/shard_map/ppermute | solution.py:103
  11.3 0.7 %collective-permute-start.4 = (bf16[2,64,256]{2,1,0:T(8,128)(2,1)S(1)}, bf16[2,64,256]{2,1,0:T(8,128)(2,1)S(1)}, u32[]{:S(2)}, u32[]{:S(2)}) collective-permute-start(bf16[2,64,256]{2,1,0:T(8,128)(2,1)S(1)} %collective-permute-done.refs_0_), channel_id=1, source_target_pairs={{8,0},{18,2},{12,4},{14,6},{0,8},{26,10},{4,12},{6,14},{24,16},{2,... | collective-permute-start | bytes 196616 | tf_op jit(solution)/shard_map/ppermute | solution.py:103
  12.1 1.3 %collective-permute-start.2 = (bf16[2,64,256]{2,1,0:T(8,128)(2,1)S(1)}, bf16[2,64,256]{2,1,0:T(8,128)(2,1)S(1)}, u32[]{:S(2)}, u32[]{:S(2)}) collective-permute-start(bf16[2,64,256]{2,1,0:T(8,128)(2,1)S(1)} %collective-permute-done.refs_0_), channel_id=1, source_target_pairs={{2,0},{10,2},{20,4},{22,6},{16,8},{24,10},{28,12},{30,14},{8,16},{... | collective-permute-start | bytes 196616 | tf_op jit(solution)/shard_map/ppermute | solution.py:103
  13.3 0.0 collective-permute-done.9.refs_6_
  13.3 0.0 collective-permute-done.8.refs_5_
  13.4 0.8 %collective-permute-start.10 = (bf16[2,64,256]{2,1,0:T(8,128)(2,1)S(1)}, bf16[2,64,256]{2,1,0:T(8,128)(2,1)S(1)}, u32[]{:S(2)}, u32[]{:S(2)}) collective-permute-start(bf16[2,64,256]{2,1,0:T(8,128)(2,1)S(1)} %select_select_fusion), channel_id=1, source_target_pairs={{2,0},{0,2},{6,4},{4,6},{10,8},{8,10},{14,12},{12,14},{18,16},{16,... | collective-permute-start | bytes 196616 | tf_op jit(solution)/shard_map/ppermute | solution.py:103
  14.2 0.0 collective-permute-start.1
  14.2 0.0 collective-permute-done.6.refs_3_
  14.2 0.5 %collective-permute-start.7 = (bf16[2,64,256]{2,1,0:T(8,128)(2,1)S(1)}, bf16[2,64,256]{2,1,0:T(8,128)(2,1)S(1)}, u32[]{:S(2)}, u32[]{:S(2)}) collective-permute-start(bf16[2,64,256]{2,1,0:T(8,128)(2,1)S(1)} %collective-permute-done.6.refs_3_), channel_id=1, source_target_pairs={{1,0},{0,1},{3,2},{2,3},{5,4},{4,5},{7,6},{6,7},{9,8},{8,9},{11,10... | collective-permute-start | bytes 196616 | tf_op jit(solution)/shard_map/ppermute | solution.py:324
  14.7 0.9 %collective-permute-done.4.refs_2_ = bf16[2,64,256]{2,1,0:T(8,128)(2,1)S(1)} collective-permute-done((bf16[2,64,256]{2,1,0:T(8,128)(2,1)S(1)}, bf16[2,64,256]{2,1,0:T(8,128)(2,1)S(1)}, u32[]{:S(2)}, u32[]{:S(2)}) %collective-permute-start.4) | collective-permute-done | bytes 65568 | tf_op jit(solution)/shard_map/ppermute | solution.py:103
  15.6 0.0 collective-permute-start.5
  15.6 0.7 %collective-permute-done.2 = bf16[2,64,256]{2,1,0:T(8,128)(2,1)S(1)} collective-permute-done((bf16[2,64,256]{2,1,0:T(8,128)(2,1)S(1)}, bf16[2,64,256]{2,1,0:T(8,128)(2,1)S(1)}, u32[]{:S(2)}, u32[]{:S(2)}) %collective-permute-start.2) | collective-permute-done | bytes 65568 | tf_op jit(solution)/shard_map/ppermute | solution.py:103
  16.4 0.1 collective-permute-start.3
  16.4 0.8 %begin_update.1 = (f32[4104,128]{1,0:T(8,128)S(1)}, bf16[512,256]{1,0:T(8,128)(2,1)S(1)}, bf16[2,64,256]{2,1,0:T(8,128)(2,1)S(1)}, bf16[2,64,256]{2,1,0:T(8,128)(2,1)S(1)}) custom-call(bf16[2,64,256]{2,1,0:T(8,128)(2,1)S(1)} %collective-permute-done.refs_0_, bf16[2,64,256]{2,1,0:T(8,128)(2,1)S(1)} %broadcast_select_fusion.refs_1_, ...), custom_call_target="tpu_custom_call", output_to_operand_aliasing={{0}: (7, {})} | custom-call | tf_op jit(solution)/shard_map/begin_update/pallas_call | solution.py:213
  17.2 0.0 collective-permute-done.1.refs_0_
  17.2 0.5 %collective-permute-done.10.refs_7_ = bf16[2,64,256]{2,1,0:T(8,128)(2,1)S(1)} collective-permute-done((bf16[2,64,256]{2,1,0:T(8,128)(2,1)S(1)}, bf16[2,64,256]{2,1,0:T(8,128)(2,1)S(1)}, u32[]{:S(2)}, u32[]{:S(2)}) %collective-permute-start.10) | collective-permute-done | bytes 65568 | tf_op jit(solution)/shard_map/ppermute | solution.py:103
  17.7 0.0 collective-permute-done.7.refs_3_
  17.7 0.0 collective-permute-done.5.refs_2_
  17.7 0.0 collective-permute-done.3.refs_1_
  17.7 1.7 %end_update.1 = (f32[4096,128]{1,0:T(8,128)}, f32[4104,128]{1,0:T(8,128)S(1)}) custom-call(bf16[2,64,256]{2,1,0:T(8,128)(2,1)S(1)} %collective-permute-done.1.refs_0_, bf16[2,64,256]{2,1,0:T(8,128)(2,1)S(1)} %collective-permute-done.3.refs_1_, bf16[2,64,256]{2,1,0:T(8,128)(2,1)S(1)} %collective-permute-done.5.refs_2_, ...), custom_call_target="tpu_custom_call", output_to_operand_aliasing={{1}: (9, {})} | custom-call | tf_op jit(solution)/shard_map/end_update/pallas_call | solution.py:277
  (2 shorter events, 0.0 us)
Async XLA Ops:
  1.4 8.5 %collective-permute-start = (bf16[2,64,256]{2,1,0:T(8,128)(2,1)S(1)}, bf16[2,64,256]{2,1,0:T(8,128)(2,1)S(1)}, u32[]{:S(2)}, u32[]{:S(2)}) collective-permute-start(bf16[2,64,256]{2,1,0:T(8,128)(2,1)S(1)} %factor.1.refs_0_.refs_4_), channel_id=1, source_target_pairs={{0,24},{2,0},{4,8},{6,16},{8,26},{10,2},{12,18},{14,10},{16,28},{1... | collective-permute-start | bytes 196616 | tf_op jit(solution)/shard_map/ppermute | solution.py:304
  6.9 6.4 %collective-permute-start.9 = (bf16[2,64,256]{2,1,0:T(8,128)(2,1)S(1)}, bf16[2,64,256]{2,1,0:T(8,128)(2,1)S(1)}, u32[]{:S(2)}, u32[]{:S(2)}) collective-permute-start(bf16[2,64,256]{2,1,0:T(8,128)(2,1)S(1)} %factor.1.refs_0_.refs_4_), channel_id=1, source_target_pairs={{8,0},{0,2},{6,4},{4,6},{10,8},{2,10},{14,12},{12,14},{18,16},{16,... | collective-permute-start | bytes 196616 | tf_op jit(solution)/shard_map/ppermute | solution.py:103
  7.0 6.4 %collective-permute-start.8 = (bf16[2,64,256]{2,1,0:T(8,128)(2,1)S(1)}, bf16[2,64,256]{2,1,0:T(8,128)(2,1)S(1)}, u32[]{:S(2)}, u32[]{:S(2)}) collective-permute-start(bf16[2,64,256]{2,1,0:T(8,128)(2,1)S(1)} %factor.1.refs_0_.refs_4_), channel_id=1, source_target_pairs={{4,0},{6,2},{0,4},{2,6},{12,8},{26,10},{8,12},{10,14},{20,16},{22,... | collective-permute-start | bytes 196616 | tf_op jit(solution)/shard_map/ppermute | solution.py:103
  9.9 4.3 %collective-permute-start.6 = (bf16[2,64,256]{2,1,0:T(8,128)(2,1)S(1)}, bf16[2,64,256]{2,1,0:T(8,128)(2,1)S(1)}, u32[]{:S(2)}, u32[]{:S(2)}) collective-permute-start(bf16[2,64,256]{2,1,0:T(8,128)(2,1)S(1)} %collective-permute-done.refs_0_), channel_id=1, source_target_pairs={{16,0},{26,2},{28,4},{30,6},{24,8},{18,10},{20,12},{22,14},{0,16},... | collective-permute-start | bytes 196616 | tf_op jit(solution)/shard_map/ppermute | solution.py:103
  11.3 4.3 %collective-permute-start.4 = (bf16[2,64,256]{2,1,0:T(8,128)(2,1)S(1)}, bf16[2,64,256]{2,1,0:T(8,128)(2,1)S(1)}, u32[]{:S(2)}, u32[]{:S(2)}) collective-permute-start(bf16[2,64,256]{2,1,0:T(8,128)(2,1)S(1)} %collective-permute-done.refs_0_), channel_id=1, source_target_pairs={{8,0},{18,2},{12,4},{14,6},{0,8},{26,10},{4,12},{6,14},{24,16},{2,... | collective-permute-start | bytes 196616 | tf_op jit(solution)/shard_map/ppermute | solution.py:103
  12.1 4.3 %collective-permute-start.2 = (bf16[2,64,256]{2,1,0:T(8,128)(2,1)S(1)}, bf16[2,64,256]{2,1,0:T(8,128)(2,1)S(1)}, u32[]{:S(2)}, u32[]{:S(2)}) collective-permute-start(bf16[2,64,256]{2,1,0:T(8,128)(2,1)S(1)} %collective-permute-done.refs_0_), channel_id=1, source_target_pairs={{2,0},{10,2},{20,4},{22,6},{16,8},{24,10},{28,12},{30,14},{8,16},{... | collective-permute-start | bytes 196616 | tf_op jit(solution)/shard_map/ppermute | solution.py:103
  13.4 4.3 %collective-permute-start.10 = (bf16[2,64,256]{2,1,0:T(8,128)(2,1)S(1)}, bf16[2,64,256]{2,1,0:T(8,128)(2,1)S(1)}, u32[]{:S(2)}, u32[]{:S(2)}) collective-permute-start(bf16[2,64,256]{2,1,0:T(8,128)(2,1)S(1)} %select_select_fusion), channel_id=1, source_target_pairs={{2,0},{0,2},{6,4},{4,6},{10,8},{8,10},{14,12},{12,14},{18,16},{16,... | collective-permute-start | bytes 196616 | tf_op jit(solution)/shard_map/ppermute | solution.py:103
  14.2 3.0 %collective-permute-start.1 = (bf16[2,64,256]{2,1,0:T(8,128)(2,1)S(1)}, bf16[2,64,256]{2,1,0:T(8,128)(2,1)S(1)}, u32[]{:S(2)}, u32[]{:S(2)}) collective-permute-start(bf16[2,64,256]{2,1,0:T(8,128)(2,1)S(1)} %collective-permute-done.refs_0_), channel_id=1, source_target_pairs={{1,0},{0,1},{3,2},{2,3},{5,4},{4,5},{7,6},{6,7},{9,8},{8,9},{11,10... | collective-permute-start | bytes 196616 | tf_op jit(solution)/shard_map/ppermute | solution.py:324
  14.2 3.5 %collective-permute-start.7 = (bf16[2,64,256]{2,1,0:T(8,128)(2,1)S(1)}, bf16[2,64,256]{2,1,0:T(8,128)(2,1)S(1)}, u32[]{:S(2)}, u32[]{:S(2)}) collective-permute-start(bf16[2,64,256]{2,1,0:T(8,128)(2,1)S(1)} %collective-permute-done.6.refs_3_), channel_id=1, source_target_pairs={{1,0},{0,1},{3,2},{2,3},{5,4},{4,5},{7,6},{6,7},{9,8},{8,9},{11,10... | collective-permute-start | bytes 196616 | tf_op jit(solution)/shard_map/ppermute | solution.py:324
  15.6 2.1 %collective-permute-start.5 = (bf16[2,64,256]{2,1,0:T(8,128)(2,1)S(1)}, bf16[2,64,256]{2,1,0:T(8,128)(2,1)S(1)}, u32[]{:S(2)}, u32[]{:S(2)}) collective-permute-start(bf16[2,64,256]{2,1,0:T(8,128)(2,1)S(1)} %collective-permute-done.4.refs_2_), channel_id=1, source_target_pairs={{1,0},{0,1},{3,2},{2,3},{5,4},{4,5},{7,6},{6,7},{9,8},{8,9},{11,10... | collective-permute-start | bytes 196616 | tf_op jit(solution)/shard_map/ppermute | solution.py:324
  16.4 1.4 %collective-permute-start.3 = (bf16[2,64,256]{2,1,0:T(8,128)(2,1)S(1)}, bf16[2,64,256]{2,1,0:T(8,128)(2,1)S(1)}, u32[]{:S(2)}, u32[]{:S(2)}) collective-permute-start(bf16[2,64,256]{2,1,0:T(8,128)(2,1)S(1)} %broadcast_select_fusion.refs_1_), channel_id=1, source_target_pairs={{1,0},{0,1},{3,2},{2,3},{5,4},{4,5},{7,6},{6,7},{9,8},{8,9},{11,10... | collective-permute-start | bytes 196616 | tf_op jit(solution)/shard_map/ppermute | solution.py:324

commit v26 on v25

--- a/solution.py
+++ b/solution.py
@@ -95,8 +95,15 @@
     return slab
 
 
-def line_steps(count):
-    return (0, 2, 1, 3) if count == 4 else tuple(range(count))
+def line_steps(count, line):
+    if count == 4:
+        return (0, 3, 1, 2) if line == 0 else (0, 2, 1, 3)
+    return tuple(range(count))
+
+
+def steps_of(count, r):
+    pairs = zip(line_steps(count, 0), line_steps(count, 1))
+    return [first if first == other else jnp.where(r == 0, first, other) for first, other in pairs]
 
 
 def move(x, sources, count):
@@ -111,7 +118,10 @@
         return line
     places = [(r, c) for r in range(count) for c in range(count)]
     near = move(late_factor, {(r, c): (r ^ 1, c) if r == c else (r, c ^ 1) for r, c in places}, count)
-    far = move(late_factor, {(r, c): (r ^ 2, c) if r == c and r % 2 == 1 else (r, c ^ 2) for r, c in places}, count)
+    sources = {
+        (r, c): (r ^ 2, c) if r == c and r % 2 == 1 else (r, c ^ line_steps(count, r)[1]) for r, c in places
+    }
+    far = move(late_factor, sources, count)
     r, c = lax.axis_index("row"), lax.axis_index("col")
     relayed = jnp.where((r == c) & (r % 2 == 1), moved, far)
     relayed = jnp.where(r == c ^ 1, near, relayed)
@@ -193,10 +203,10 @@
 
         @pl.when(r == c)
         def _():
-            for step, line_ref in zip(line_steps(pieces)[1:], line_refs):
+            for step, line_ref in zip(steps_of(pieces, r)[1:], line_refs):
                 take_rows(line_ref, columns_ref, c, step, pieces)
 
-    for step, row_ref in zip(line_steps(pieces), (row_refs[0], *line_refs)):
+    for step, row_ref in zip(steps_of(pieces, r), (row_refs[0], *line_refs)):
         first_row = partner(c, step, pieces) * tile_rows
         subtract_product(
             share_ref, row_ref[...], columns_ref[...], tile, first_row, layer * own_lines, layers * own_lines
@@ -243,11 +253,11 @@
 
         @pl.when(r == c)
         def _():
-            take_rows(last_buf, own_ref, c, line_steps(pieces)[-1], pieces)
+            take_rows(last_buf, own_ref, c, steps_of(pieces, r)[-1], pieces)
 
     stores = []
     for at_row, row_ref in enumerate((*row_refs[:-1], last_buf)):
-        first_row = partner(c, line_steps(pieces)[at_row], pieces) * tile_rows
+        first_row = partner(c, steps_of(pieces, r)[at_row], pieces) * tile_rows
         rows = row_ref[...]
         for at, owner in enumerate(owners):
             subtract_product(share_ref, rows, columns_buf[at], tile, first_row, owner * own_lines, per_row)

time: 19.6 us -> 19.5 us (level)
  no operation moved by 1% of the time
where the time goes in v26:
time: 19.5 us; the launch traced here: 19.4 us
  starting transfers between devices  11.8 us (61%)
  Pallas kernels  5.4 us (28%)
  waiting for transfers between devices  2.11 us (11%)
    ppermute x6, starting transfers between devices, move(): lax.ppermute(x, ('row', 'col'), [(a * count + b, r * count + c) for (r, c...  7.25 us
    ppermute x1, starting transfers between devices, per_device(): lax.ppermute(factor, ('row', 'col'), [(a * count + b, slots[a][b] * count...  3.95 us
    ppermute x6, waiting for transfers between devices, move(): lax.ppermute(x, ('row', 'col'), [(a * count + b, r * count + c) for (r, c...  2.1 us
    pallas_call x1, Pallas kernels, end_update(): pl.pallas_call(body, out_shape=[jax.ShapeDtypeStruct((half * pieces * row...  1.7 us
    pallas_call x1, Pallas kernels, load_share(): pl.pallas_call(body, out_shape=jax.ShapeDtypeStruct((rows + per_row, LANE...  1.6 us
    pallas_call x1, Pallas kernels, make_factor(): pl.pallas_call(factor_kernel, out_shape=jax.ShapeDtypeStruct((half, tile_...  1.34 us
    pallas_call x1, Pallas kernels, begin_update(): pl.pallas_call(body, out_shape=[jax.ShapeDtypeStruct(share.shape, jnp.flo...  0.76 us
    ppermute x4, starting transfers between devices, per_device(): others += [lax.ppermute(piece, 'layer', pairs) for piece in plane]  0.58 us
  transfers between devices with their start and end apart: 11, of which 3 were waited for; matrix products, arithmetic and copies ran while one was open for 0% of the time, Pallas kernels for 12%

profile of v26, /device:TPU:0, one launch (start us, length us, event | category | flops | bytes accessed | tf_op | source)
XLA Modules:
  0.0 19.4 jit_solution(15211358526214876143)
XLA Ops:
  0.0 1.3 %factor.1.refs_0_.refs_4_ = bf16[2,64,256]{2,1,0:T(8,128)(2,1)S(1)} custom-call(f32[4,1,64,256]{3,2,1,0:T(8,128)} %panel_ref.1, f32[256,256]{1,0:T(8,128)} %inverse_ref.1), custom_call_target="tpu_custom_call" | custom-call | tf_op jit(solution)/shard_map/factor/pallas_call | solution.py:55
  1.4 3.9 %collective-permute-start = (bf16[2,64,256]{2,1,0:T(8,128)(2,1)S(1)}, bf16[2,64,256]{2,1,0:T(8,128)(2,1)S(1)}, u32[]{:S(2)}, u32[]{:S(2)}) collective-permute-start(bf16[2,64,256]{2,1,0:T(8,128)(2,1)S(1)} %factor.1.refs_0_.refs_4_), channel_id=1, source_target_pairs={{0,24},{2,0},{4,8},{6,16},{8,26},{10,2},{12,18},{14,10},{16,28},{1... | collective-permute-start | bytes 196616 | tf_op jit(solution)/shard_map/ppermute | solution.py:314
  5.3 1.6 %load_share.1.refs_7_ = f32[4104,128]{1,0:T(8,128)S(1)} custom-call(bf16[2,64,256]{2,1,0:T(8,128)(2,1)S(1)} %factor.1.refs_0_.refs_4_, f32[8192,128]{1,0:T(8,128)} %bitcast.2), custom_call_target="tpu_custom_call" | custom-call | bytes 4194304 | tf_op jit(solution)/shard_map/load_share/pallas_call | solution.py:145
  6.9 0.1 collective-permute-start.9
  7.0 2.9 %collective-permute-start.8 = (bf16[2,64,256]{2,1,0:T(8,128)(2,1)S(1)}, bf16[2,64,256]{2,1,0:T(8,128)(2,1)S(1)}, u32[]{:S(2)}, u32[]{:S(2)}) collective-permute-start(bf16[2,64,256]{2,1,0:T(8,128)(2,1)S(1)} %factor.1.refs_0_.refs_4_), channel_id=1, source_target_pairs={{6,0},{4,2},{2,4},{0,6},{12,8},{26,10},{8,12},{10,14},{20,16},{22,... | collective-permute-start | bytes 196616 | tf_op jit(solution)/shard_map/ppermute | solution.py:110
  9.8 0.0 collective-permute-done.refs_0_
  9.8 1.5 %collective-permute-start.6 = (bf16[2,64,256]{2,1,0:T(8,128)(2,1)S(1)}, bf16[2,64,256]{2,1,0:T(8,128)(2,1)S(1)}, u32[]{:S(2)}, u32[]{:S(2)}) collective-permute-start(bf16[2,64,256]{2,1,0:T(8,128)(2,1)S(1)} %collective-permute-done.refs_0_), channel_id=1, source_target_pairs={{16,0},{26,2},{28,4},{30,6},{24,8},{18,10},{20,12},{22,14},{0,16},... | collective-permute-start | bytes 196616 | tf_op jit(solution)/shard_map/ppermute | solution.py:110
  11.3 0.7 %collective-permute-start.4 = (bf16[2,64,256]{2,1,0:T(8,128)(2,1)S(1)}, bf16[2,64,256]{2,1,0:T(8,128)(2,1)S(1)}, u32[]{:S(2)}, u32[]{:S(2)}) collective-permute-start(bf16[2,64,256]{2,1,0:T(8,128)(2,1)S(1)} %collective-permute-done.refs_0_), channel_id=1, source_target_pairs={{8,0},{18,2},{12,4},{14,6},{0,8},{26,10},{4,12},{6,14},{24,16},{2,... | collective-permute-start | bytes 196616 | tf_op jit(solution)/shard_map/ppermute | solution.py:110
  12.1 1.2 %collective-permute-start.2 = (bf16[2,64,256]{2,1,0:T(8,128)(2,1)S(1)}, bf16[2,64,256]{2,1,0:T(8,128)(2,1)S(1)}, u32[]{:S(2)}, u32[]{:S(2)}) collective-permute-start(bf16[2,64,256]{2,1,0:T(8,128)(2,1)S(1)} %collective-permute-done.refs_0_), channel_id=1, source_target_pairs={{2,0},{10,2},{20,4},{22,6},{16,8},{24,10},{28,12},{30,14},{8,16},{... | collective-permute-start | bytes 196616 | tf_op jit(solution)/shard_map/ppermute | solution.py:110
  13.3 0.0 collective-permute-done.9.refs_6_
  13.3 0.0 collective-permute-done.8.refs_5_
  13.3 0.9 %collective-permute-start.10 = (bf16[2,64,256]{2,1,0:T(8,128)(2,1)S(1)}, bf16[2,64,256]{2,1,0:T(8,128)(2,1)S(1)}, u32[]{:S(2)}, u32[]{:S(2)}) collective-permute-start(bf16[2,64,256]{2,1,0:T(8,128)(2,1)S(1)} %select_select_fusion), channel_id=1, source_target_pairs={{2,0},{0,2},{6,4},{4,6},{10,8},{8,10},{14,12},{12,14},{18,16},{16,... | collective-permute-start | bytes 196616 | tf_op jit(solution)/shard_map/ppermute | solution.py:110
  14.2 0.0 collective-permute-start.1
  14.2 0.0 collective-permute-done.6.refs_3_
  14.2 0.5 %collective-permute-start.7 = (bf16[2,64,256]{2,1,0:T(8,128)(2,1)S(1)}, bf16[2,64,256]{2,1,0:T(8,128)(2,1)S(1)}, u32[]{:S(2)}, u32[]{:S(2)}) collective-permute-start(bf16[2,64,256]{2,1,0:T(8,128)(2,1)S(1)} %collective-permute-done.6.refs_3_), channel_id=1, source_target_pairs={{1,0},{0,1},{3,2},{2,3},{5,4},{4,5},{7,6},{6,7},{9,8},{8,9},{11,10... | collective-permute-start | bytes 196616 | tf_op jit(solution)/shard_map/ppermute | solution.py:334
  14.7 0.9 %collective-permute-done.4.refs_2_ = bf16[2,64,256]{2,1,0:T(8,128)(2,1)S(1)} collective-permute-done((bf16[2,64,256]{2,1,0:T(8,128)(2,1)S(1)}, bf16[2,64,256]{2,1,0:T(8,128)(2,1)S(1)}, u32[]{:S(2)}, u32[]{:S(2)}) %collective-permute-start.4) | collective-permute-done | bytes 65568 | tf_op jit(solution)/shard_map/ppermute | solution.py:110
  15.6 0.0 collective-permute-start.5
  15.6 0.7 %collective-permute-done.2 = bf16[2,64,256]{2,1,0:T(8,128)(2,1)S(1)} collective-permute-done((bf16[2,64,256]{2,1,0:T(8,128)(2,1)S(1)}, bf16[2,64,256]{2,1,0:T(8,128)(2,1)S(1)}, u32[]{:S(2)}, u32[]{:S(2)}) %collective-permute-start.2) | collective-permute-done | bytes 65568 | tf_op jit(solution)/shard_map/ppermute | solution.py:110
  16.4 0.1 collective-permute-start.3
  16.4 0.8 %begin_update.1 = (f32[4104,128]{1,0:T(8,128)S(1)}, bf16[512,256]{1,0:T(8,128)(2,1)S(1)}, bf16[2,64,256]{2,1,0:T(8,128)(2,1)S(1)}, bf16[2,64,256]{2,1,0:T(8,128)(2,1)S(1)}) custom-call(bf16[2,64,256]{2,1,0:T(8,128)(2,1)S(1)} %collective-permute-done.refs_0_, bf16[2,64,256]{2,1,0:T(8,128)(2,1)S(1)} %broadcast_select_fusion.refs_1_, ...), custom_call_target="tpu_custom_call", output_to_operand_aliasing={{0}: (7, {})} | custom-call | tf_op jit(solution)/shard_map/begin_update/pallas_call | solution.py:223
  17.2 0.0 collective-permute-done.1.refs_0_
  17.2 0.5 %collective-permute-done.10.refs_7_ = bf16[2,64,256]{2,1,0:T(8,128)(2,1)S(1)} collective-permute-done((bf16[2,64,256]{2,1,0:T(8,128)(2,1)S(1)}, bf16[2,64,256]{2,1,0:T(8,128)(2,1)S(1)}, u32[]{:S(2)}, u32[]{:S(2)}) %collective-permute-start.10) | collective-permute-done | bytes 65568 | tf_op jit(solution)/shard_map/ppermute | solution.py:110
  17.7 0.0 collective-permute-done.7.refs_3_
  17.7 0.0 collective-permute-done.5.refs_2_
  17.7 0.0 collective-permute-done.3.refs_1_
  17.7 1.7 %end_update.1 = (f32[4096,128]{1,0:T(8,128)}, f32[4104,128]{1,0:T(8,128)S(1)}) custom-call(bf16[2,64,256]{2,1,0:T(8,128)(2,1)S(1)} %collective-permute-done.1.refs_0_, bf16[2,64,256]{2,1,0:T(8,128)(2,1)S(1)} %collective-permute-done.3.refs_1_, bf16[2,64,256]{2,1,0:T(8,128)(2,1)S(1)} %collective-permute-done.5.refs_2_, ...), custom_call_target="tpu_custom_call", output_to_operand_aliasing={{1}: (9, {})} | custom-call | tf_op jit(solution)/shard_map/end_update/pallas_call | solution.py:287
  (2 shorter events, 0.0 us)
Async XLA Ops:
  1.4 8.5 %collective-permute-start = (bf16[2,64,256]{2,1,0:T(8,128)(2,1)S(1)}, bf16[2,64,256]{2,1,0:T(8,128)(2,1)S(1)}, u32[]{:S(2)}, u32[]{:S(2)}) collective-permute-start(bf16[2,64,256]{2,1,0:T(8,128)(2,1)S(1)} %factor.1.refs_0_.refs_4_), channel_id=1, source_target_pairs={{0,24},{2,0},{4,8},{6,16},{8,26},{10,2},{12,18},{14,10},{16,28},{1... | collective-permute-start | bytes 196616 | tf_op jit(solution)/shard_map/ppermute | solution.py:314
  6.9 6.4 %collective-permute-start.9 = (bf16[2,64,256]{2,1,0:T(8,128)(2,1)S(1)}, bf16[2,64,256]{2,1,0:T(8,128)(2,1)S(1)}, u32[]{:S(2)}, u32[]{:S(2)}) collective-permute-start(bf16[2,64,256]{2,1,0:T(8,128)(2,1)S(1)} %factor.1.refs_0_.refs_4_), channel_id=1, source_target_pairs={{8,0},{0,2},{6,4},{4,6},{10,8},{2,10},{14,12},{12,14},{18,16},{16,... | collective-permute-start | bytes 196616 | tf_op jit(solution)/shard_map/ppermute | solution.py:110
  7.0 6.4 %collective-permute-start.8 = (bf16[2,64,256]{2,1,0:T(8,128)(2,1)S(1)}, bf16[2,64,256]{2,1,0:T(8,128)(2,1)S(1)}, u32[]{:S(2)}, u32[]{:S(2)}) collective-permute-start(bf16[2,64,256]{2,1,0:T(8,128)(2,1)S(1)} %factor.1.refs_0_.refs_4_), channel_id=1, source_target_pairs={{6,0},{4,2},{2,4},{0,6},{12,8},{26,10},{8,12},{10,14},{20,16},{22,... | collective-permute-start | bytes 196616 | tf_op jit(solution)/shard_map/ppermute | solution.py:110
  9.8 4.4 %collective-permute-start.6 = (bf16[2,64,256]{2,1,0:T(8,128)(2,1)S(1)}, bf16[2,64,256]{2,1,0:T(8,128)(2,1)S(1)}, u32[]{:S(2)}, u32[]{:S(2)}) collective-permute-start(bf16[2,64,256]{2,1,0:T(8,128)(2,1)S(1)} %collective-permute-done.refs_0_), channel_id=1, source_target_pairs={{16,0},{26,2},{28,4},{30,6},{24,8},{18,10},{20,12},{22,14},{0,16},... | collective-permute-start | bytes 196616 | tf_op jit(solution)/shard_map/ppermute | solution.py:110
  11.3 4.3 %collective-permute-start.4 = (bf16[2,64,256]{2,1,0:T(8,128)(2,1)S(1)}, bf16[2,64,256]{2,1,0:T(8,128)(2,1)S(1)}, u32[]{:S(2)}, u32[]{:S(2)}) collective-permute-start(bf16[2,64,256]{2,1,0:T(8,128)(2,1)S(1)} %collective-permute-done.refs_0_), channel_id=1, source_target_pairs={{8,0},{18,2},{12,4},{14,6},{0,8},{26,10},{4,12},{6,14},{24,16},{2,... | collective-permute-start | bytes 196616 | tf_op jit(solution)/shard_map/ppermute | solution.py:110
  12.1 4.3 %collective-permute-start.2 = (bf16[2,64,256]{2,1,0:T(8,128)(2,1)S(1)}, bf16[2,64,256]{2,1,0:T(8,128)(2,1)S(1)}, u32[]{:S(2)}, u32[]{:S(2)}) collective-permute-start(bf16[2,64,256]{2,1,0:T(8,128)(2,1)S(1)} %collective-permute-done.refs_0_), channel_id=1, source_target_pairs={{2,0},{10,2},{20,4},{22,6},{16,8},{24,10},{28,12},{30,14},{8,16},{... | collective-permute-start | bytes 196616 | tf_op jit(solution)/shard_map/ppermute | solution.py:110
  13.3 4.3 %collective-permute-start.10 = (bf16[2,64,256]{2,1,0:T(8,128)(2,1)S(1)}, bf16[2,64,256]{2,1,0:T(8,128)(2,1)S(1)}, u32[]{:S(2)}, u32[]{:S(2)}) collective-permute-start(bf16[2,64,256]{2,1,0:T(8,128)(2,1)S(1)} %select_select_fusion), channel_id=1, source_target_pairs={{2,0},{0,2},{6,4},{4,6},{10,8},{8,10},{14,12},{12,14},{18,16},{16,... | collective-permute-start | bytes 196616 | tf_op jit(solution)/shard_map/ppermute | solution.py:110
  14.2 3.0 %collective-permute-start.1 = (bf16[2,64,256]{2,1,0:T(8,128)(2,1)S(1)}, bf16[2,64,256]{2,1,0:T(8,128)(2,1)S(1)}, u32[]{:S(2)}, u32[]{:S(2)}) collective-permute-start(bf16[2,64,256]{2,1,0:T(8,128)(2,1)S(1)} %collective-permute-done.refs_0_), channel_id=1, source_target_pairs={{1,0},{0,1},{3,2},{2,3},{5,4},{4,5},{7,6},{6,7},{9,8},{8,9},{11,10... | collective-permute-start | bytes 196616 | tf_op jit(solution)/shard_map/ppermute | solution.py:334
  14.2 3.5 %collective-permute-start.7 = (bf16[2,64,256]{2,1,0:T(8,128)(2,1)S(1)}, bf16[2,64,256]{2,1,0:T(8,128)(2,1)S(1)}, u32[]{:S(2)}, u32[]{:S(2)}) collective-permute-start(bf16[2,64,256]{2,1,0:T(8,128)(2,1)S(1)} %collective-permute-done.6.refs_3_), channel_id=1, source_target_pairs={{1,0},{0,1},{3,2},{2,3},{5,4},{4,5},{7,6},{6,7},{9,8},{8,9},{11,10... | collective-permute-start | bytes 196616 | tf_op jit(solution)/shard_map/ppermute | solution.py:334
  15.6 2.1 %collective-permute-start.5 = (bf16[2,64,256]{2,1,0:T(8,128)(2,1)S(1)}, bf16[2,64,256]{2,1,0:T(8,128)(2,1)S(1)}, u32[]{:S(2)}, u32[]{:S(2)}) collective-permute-start(bf16[2,64,256]{2,1,0:T(8,128)(2,1)S(1)} %collective-permute-done.4.refs_2_), channel_id=1, source_target_pairs={{1,0},{0,1},{3,2},{2,3},{5,4},{4,5},{7,6},{6,7},{9,8},{8,9},{11,10... | collective-permute-start | bytes 196616 | tf_op jit(solution)/shard_map/ppermute | solution.py:334
  16.4 1.3 %collective-permute-start.3 = (bf16[2,64,256]{2,1,0:T(8,128)(2,1)S(1)}, bf16[2,64,256]{2,1,0:T(8,128)(2,1)S(1)}, u32[]{:S(2)}, u32[]{:S(2)}) collective-permute-start(bf16[2,64,256]{2,1,0:T(8,128)(2,1)S(1)} %broadcast_select_fusion.refs_1_), channel_id=1, source_target_pairs={{1,0},{0,1},{3,2},{2,3},{5,4},{4,5},{7,6},{6,7},{9,8},{8,9},{11,10... | collective-permute-start | bytes 196616 | tf_op jit(solution)/shard_map/ppermute | solution.py:334

commit v27 on v25

--- a/solution.py
+++ b/solution.py
@@ -157,19 +157,21 @@
             columns_ref[pl.ds(at, tile_rows), :] = piece[k]
 
 
-def subtract_product(share_ref, rows, columns, tile, first_row, first_line, per_row):
+def product_of(rows, columns):
     half, tile_rows, width = rows.shape
-    product = lax.dot_general(
+    return lax.dot_general(
         rows.reshape(half * tile_rows, width),
         columns,
         (((1,), (1,)), ((), ())),
         preferred_element_type=jnp.float32,
     )
-    for k in range(half):
-        for part in range(product.shape[1] // LANES):
-            start = (k * tile + first_row) * per_row + first_line + part
-            at = pl.ds(start, tile_rows, stride=per_row)
-            share_ref[at, :] -= product[k * tile_rows : (k + 1) * tile_rows, part * LANES : (part + 1) * LANES]
+
+
+def subtract(share_ref, product, k, tile, tile_rows, first_row, first_line, per_row):
+    for part in range(product.shape[1] // LANES):
+        start = (k * tile + first_row) * per_row + first_line + part
+        at = pl.ds(start, tile_rows, stride=per_row)
+        share_ref[at, :] -= product[k * tile_rows : (k + 1) * tile_rows, part * LANES : (part + 1) * LANES]
 
 
 def take_rows(rows_ref, columns_ref, c, step, pieces):
@@ -198,9 +200,9 @@
 
     for step, row_ref in zip(line_steps(pieces), (row_refs[0], *line_refs)):
         first_row = partner(c, step, pieces) * tile_rows
-        subtract_product(
-            share_ref, row_ref[...], columns_ref[...], tile, first_row, layer * own_lines, layers * own_lines
-        )
+        product = product_of(row_ref[...], columns_ref[...])
+        for k in range(half):
+            subtract(share_ref, product, k, tile, tile_rows, first_row, layer * own_lines, layers * own_lines)
 
 
 def begin_update(column_pieces, row_pieces, share, layers, tile):
@@ -249,11 +251,12 @@
     for at_row, row_ref in enumerate((*row_refs[:-1], last_buf)):
         first_row = partner(c, line_steps(pieces)[at_row], pieces) * tile_rows
         rows = row_ref[...]
-        for at, owner in enumerate(owners):
-            subtract_product(share_ref, rows, columns_buf[at], tile, first_row, owner * own_lines, per_row)
+        products = [(product_of(rows, columns_buf[at]), owner) for at, owner in enumerate(owners)]
         if at_row == pieces - 1:
-            subtract_product(share_ref, rows, own_ref[...], tile, first_row, layer * own_lines, per_row)
+            products.append((product_of(rows, own_ref[...]), layer))
         for k in range(half):
+            for product, owner in products:
+                subtract(share_ref, product, k, tile, tile_rows, first_row, owner * own_lines, per_row)
             lines = tile_rows * per_row
             start = pl.multiple_of((k * tile + first_row) * per_row, lines)
             store = pltpu.make_async_copy(

time: 19.6 us -> 19.5 us (level)
  no operation moved by 1% of the time
where the time goes in v27:
time: 19.5 us; the launch traced here: 19.4 us
  starting transfers between devices  11.8 us (61%)
  Pallas kernels  5.36 us (27%)
  waiting for transfers between devices  2.14 us (11%)
    ppermute x6, starting transfers between devices, move(): lax.ppermute(x, ('row', 'col'), [(a * count + b, r * count + c) for (r, c...  7.25 us
    ppermute x1, starting transfers between devices, per_device(): lax.ppermute(factor, ('row', 'col'), [(a * count + b, slots[a][b] * count...  3.95 us
    ppermute x6, waiting for transfers between devices, move(): lax.ppermute(x, ('row', 'col'), [(a * count + b, r * count + c) for (r, c...  2.12 us
    pallas_call x1, Pallas kernels, end_update(): pl.pallas_call(body, out_shape=[jax.ShapeDtypeStruct((half * pieces * row...  1.66 us
    pallas_call x1, Pallas kernels, load_share(): pl.pallas_call(body, out_shape=jax.ShapeDtypeStruct((rows + per_row, LANE...  1.6 us
    pallas_call x1, Pallas kernels, make_factor(): pl.pallas_call(factor_kernel, out_shape=jax.ShapeDtypeStruct((half, tile_...  1.34 us
    pallas_call x1, Pallas kernels, begin_update(): pl.pallas_call(body, out_shape=[jax.ShapeDtypeStruct(share.shape, jnp.flo...  0.76 us
    ppermute x4, starting transfers between devices, per_device(): others += [lax.ppermute(piece, 'layer', pairs) for piece in plane]  0.58 us
  transfers between devices with their start and end apart: 11, of which 3 were waited for; matrix products, arithmetic and copies ran while one was open for 0% of the time, Pallas kernels for 12%

profile of v27, /device:TPU:0, one launch (start us, length us, event | category | flops | bytes accessed | tf_op | source)
XLA Modules:
  0.0 19.4 jit_solution(16711289305833830778)
XLA Ops:
  0.0 1.3 %factor.1.refs_0_.refs_4_ = bf16[2,64,256]{2,1,0:T(8,128)(2,1)S(1)} custom-call(f32[4,1,64,256]{3,2,1,0:T(8,128)} %panel_ref.1, f32[256,256]{1,0:T(8,128)} %inverse_ref.1), custom_call_target="tpu_custom_call" | custom-call | tf_op jit(solution)/shard_map/factor/pallas_call | solution.py:55
  1.4 3.9 %collective-permute-start = (bf16[2,64,256]{2,1,0:T(8,128)(2,1)S(1)}, bf16[2,64,256]{2,1,0:T(8,128)(2,1)S(1)}, u32[]{:S(2)}, u32[]{:S(2)}) collective-permute-start(bf16[2,64,256]{2,1,0:T(8,128)(2,1)S(1)} %factor.1.refs_0_.refs_4_), channel_id=1, source_target_pairs={{0,24},{2,0},{4,8},{6,16},{8,26},{10,2},{12,18},{14,10},{16,28},{1... | collective-permute-start | bytes 196616 | tf_op jit(solution)/shard_map/ppermute | solution.py:307
  5.3 1.6 %load_share.1.refs_7_ = f32[4104,128]{1,0:T(8,128)S(1)} custom-call(bf16[2,64,256]{2,1,0:T(8,128)(2,1)S(1)} %factor.1.refs_0_.refs_4_, f32[8192,128]{1,0:T(8,128)} %bitcast.2), custom_call_target="tpu_custom_call" | custom-call | bytes 4194304 | tf_op jit(solution)/shard_map/load_share/pallas_call | solution.py:135
  6.9 0.1 collective-permute-start.9
  7.0 2.9 %collective-permute-start.8 = (bf16[2,64,256]{2,1,0:T(8,128)(2,1)S(1)}, bf16[2,64,256]{2,1,0:T(8,128)(2,1)S(1)}, u32[]{:S(2)}, u32[]{:S(2)}) collective-permute-start(bf16[2,64,256]{2,1,0:T(8,128)(2,1)S(1)} %factor.1.refs_0_.refs_4_), channel_id=1, source_target_pairs={{4,0},{6,2},{0,4},{2,6},{12,8},{26,10},{8,12},{10,14},{20,16},{22,... | collective-permute-start | bytes 196616 | tf_op jit(solution)/shard_map/ppermute | solution.py:103
  9.8 0.0 collective-permute-done.refs_0_
  9.9 1.5 %collective-permute-start.6 = (bf16[2,64,256]{2,1,0:T(8,128)(2,1)S(1)}, bf16[2,64,256]{2,1,0:T(8,128)(2,1)S(1)}, u32[]{:S(2)}, u32[]{:S(2)}) collective-permute-start(bf16[2,64,256]{2,1,0:T(8,128)(2,1)S(1)} %collective-permute-done.refs_0_), channel_id=1, source_target_pairs={{16,0},{26,2},{28,4},{30,6},{24,8},{18,10},{20,12},{22,14},{0,16},... | collective-permute-start | bytes 196616 | tf_op jit(solution)/shard_map/ppermute | solution.py:103
  11.3 0.7 %collective-permute-start.4 = (bf16[2,64,256]{2,1,0:T(8,128)(2,1)S(1)}, bf16[2,64,256]{2,1,0:T(8,128)(2,1)S(1)}, u32[]{:S(2)}, u32[]{:S(2)}) collective-permute-start(bf16[2,64,256]{2,1,0:T(8,128)(2,1)S(1)} %collective-permute-done.refs_0_), channel_id=1, source_target_pairs={{8,0},{18,2},{12,4},{14,6},{0,8},{26,10},{4,12},{6,14},{24,16},{2,... | collective-permute-start | bytes 196616 | tf_op jit(solution)/shard_map/ppermute | solution.py:103
  12.1 1.3 %collective-permute-start.2 = (bf16[2,64,256]{2,1,0:T(8,128)(2,1)S(1)}, bf16[2,64,256]{2,1,0:T(8,128)(2,1)S(1)}, u32[]{:S(2)}, u32[]{:S(2)}) collective-permute-start(bf16[2,64,256]{2,1,0:T(8,128)(2,1)S(1)} %collective-permute-done.refs_0_), channel_id=1, source_target_pairs={{2,0},{10,2},{20,4},{22,6},{16,8},{24,10},{28,12},{30,14},{8,16},{... | collective-permute-start | bytes 196616 | tf_op jit(solution)/shard_map/ppermute | solution.py:103
  13.3 0.0 collective-permute-done.9.refs_6_
  13.3 0.0 collective-permute-done.8.refs_5_
  13.4 0.8 %collective-permute-start.10 = (bf16[2,64,256]{2,1,0:T(8,128)(2,1)S(1)}, bf16[2,64,256]{2,1,0:T(8,128)(2,1)S(1)}, u32[]{:S(2)}, u32[]{:S(2)}) collective-permute-start(bf16[2,64,256]{2,1,0:T(8,128)(2,1)S(1)} %select_select_fusion), channel_id=1, source_target_pairs={{2,0},{0,2},{6,4},{4,6},{10,8},{8,10},{14,12},{12,14},{18,16},{16,... | collective-permute-start | bytes 196616 | tf_op jit(solution)/shard_map/ppermute | solution.py:103
  14.2 0.0 collective-permute-start.1
  14.2 0.0 collective-permute-done.6.refs_3_
  14.2 0.5 %collective-permute-start.7 = (bf16[2,64,256]{2,1,0:T(8,128)(2,1)S(1)}, bf16[2,64,256]{2,1,0:T(8,128)(2,1)S(1)}, u32[]{:S(2)}, u32[]{:S(2)}) collective-permute-start(bf16[2,64,256]{2,1,0:T(8,128)(2,1)S(1)} %collective-permute-done.6.refs_3_), channel_id=1, source_target_pairs={{1,0},{0,1},{3,2},{2,3},{5,4},{4,5},{7,6},{6,7},{9,8},{8,9},{11,10... | collective-permute-start | bytes 196616 | tf_op jit(solution)/shard_map/ppermute | solution.py:327
  14.7 0.9 %collective-permute-done.4.refs_2_ = bf16[2,64,256]{2,1,0:T(8,128)(2,1)S(1)} collective-permute-done((bf16[2,64,256]{2,1,0:T(8,128)(2,1)S(1)}, bf16[2,64,256]{2,1,0:T(8,128)(2,1)S(1)}, u32[]{:S(2)}, u32[]{:S(2)}) %collective-permute-start.4) | collective-permute-done | bytes 65568 | tf_op jit(solution)/shard_map/ppermute | solution.py:103
  15.6 0.0 collective-permute-start.5
  15.6 0.7 %collective-permute-done.2 = bf16[2,64,256]{2,1,0:T(8,128)(2,1)S(1)} collective-permute-done((bf16[2,64,256]{2,1,0:T(8,128)(2,1)S(1)}, bf16[2,64,256]{2,1,0:T(8,128)(2,1)S(1)}, u32[]{:S(2)}, u32[]{:S(2)}) %collective-permute-start.2) | collective-permute-done | bytes 65568 | tf_op jit(solution)/shard_map/ppermute | solution.py:103
  16.4 0.1 collective-permute-start.3
  16.4 0.8 %begin_update.1 = (f32[4104,128]{1,0:T(8,128)S(1)}, bf16[512,256]{1,0:T(8,128)(2,1)S(1)}, bf16[2,64,256]{2,1,0:T(8,128)(2,1)S(1)}, bf16[2,64,256]{2,1,0:T(8,128)(2,1)S(1)}) custom-call(bf16[2,64,256]{2,1,0:T(8,128)(2,1)S(1)} %collective-permute-done.refs_0_, bf16[2,64,256]{2,1,0:T(8,128)(2,1)S(1)} %broadcast_select_fusion.refs_1_, ...), custom_call_target="tpu_custom_call", output_to_operand_aliasing={{0}: (7, {})} | custom-call | tf_op jit(solution)/shard_map/begin_update/pallas_call | solution.py:215
  17.2 0.0 collective-permute-done.1.refs_0_
  17.2 0.5 %collective-permute-done.10.refs_7_ = bf16[2,64,256]{2,1,0:T(8,128)(2,1)S(1)} collective-permute-done((bf16[2,64,256]{2,1,0:T(8,128)(2,1)S(1)}, bf16[2,64,256]{2,1,0:T(8,128)(2,1)S(1)}, u32[]{:S(2)}, u32[]{:S(2)}) %collective-permute-start.10) | collective-permute-done | bytes 65568 | tf_op jit(solution)/shard_map/ppermute | solution.py:103
  17.7 0.0 collective-permute-done.7.refs_3_
  17.7 0.0 collective-permute-done.5.refs_2_
  17.7 0.0 collective-permute-done.3.refs_1_
  17.7 1.7 %end_update.1 = (f32[4096,128]{1,0:T(8,128)}, f32[4104,128]{1,0:T(8,128)S(1)}) custom-call(bf16[2,64,256]{2,1,0:T(8,128)(2,1)S(1)} %collective-permute-done.1.refs_0_, bf16[2,64,256]{2,1,0:T(8,128)(2,1)S(1)} %collective-permute-done.3.refs_1_, bf16[2,64,256]{2,1,0:T(8,128)(2,1)S(1)} %collective-permute-done.5.refs_2_, ...), custom_call_target="tpu_custom_call", output_to_operand_aliasing={{1}: (9, {})} | custom-call | tf_op jit(solution)/shard_map/end_update/pallas_call | solution.py:280
  (2 shorter events, 0.0 us)
Async XLA Ops:
  1.4 8.5 %collective-permute-start = (bf16[2,64,256]{2,1,0:T(8,128)(2,1)S(1)}, bf16[2,64,256]{2,1,0:T(8,128)(2,1)S(1)}, u32[]{:S(2)}, u32[]{:S(2)}) collective-permute-start(bf16[2,64,256]{2,1,0:T(8,128)(2,1)S(1)} %factor.1.refs_0_.refs_4_), channel_id=1, source_target_pairs={{0,24},{2,0},{4,8},{6,16},{8,26},{10,2},{12,18},{14,10},{16,28},{1... | collective-permute-start | bytes 196616 | tf_op jit(solution)/shard_map/ppermute | solution.py:307
  6.9 6.4 %collective-permute-start.9 = (bf16[2,64,256]{2,1,0:T(8,128)(2,1)S(1)}, bf16[2,64,256]{2,1,0:T(8,128)(2,1)S(1)}, u32[]{:S(2)}, u32[]{:S(2)}) collective-permute-start(bf16[2,64,256]{2,1,0:T(8,128)(2,1)S(1)} %factor.1.refs_0_.refs_4_), channel_id=1, source_target_pairs={{8,0},{0,2},{6,4},{4,6},{10,8},{2,10},{14,12},{12,14},{18,16},{16,... | collective-permute-start | bytes 196616 | tf_op jit(solution)/shard_map/ppermute | solution.py:103
  7.0 6.4 %collective-permute-start.8 = (bf16[2,64,256]{2,1,0:T(8,128)(2,1)S(1)}, bf16[2,64,256]{2,1,0:T(8,128)(2,1)S(1)}, u32[]{:S(2)}, u32[]{:S(2)}) collective-permute-start(bf16[2,64,256]{2,1,0:T(8,128)(2,1)S(1)} %factor.1.refs_0_.refs_4_), channel_id=1, source_target_pairs={{4,0},{6,2},{0,4},{2,6},{12,8},{26,10},{8,12},{10,14},{20,16},{22,... | collective-permute-start | bytes 196616 | tf_op jit(solution)/shard_map/ppermute | solution.py:103
  9.9 4.3 %collective-permute-start.6 = (bf16[2,64,256]{2,1,0:T(8,128)(2,1)S(1)}, bf16[2,64,256]{2,1,0:T(8,128)(2,1)S(1)}, u32[]{:S(2)}, u32[]{:S(2)}) collective-permute-start(bf16[2,64,256]{2,1,0:T(8,128)(2,1)S(1)} %collective-permute-done.refs_0_), channel_id=1, source_target_pairs={{16,0},{26,2},{28,4},{30,6},{24,8},{18,10},{20,12},{22,14},{0,16},... | collective-permute-start | bytes 196616 | tf_op jit(solution)/shard_map/ppermute | solution.py:103
  11.3 4.3 %collective-permute-start.4 = (bf16[2,64,256]{2,1,0:T(8,128)(2,1)S(1)}, bf16[2,64,256]{2,1,0:T(8,128)(2,1)S(1)}, u32[]{:S(2)}, u32[]{:S(2)}) collective-permute-start(bf16[2,64,256]{2,1,0:T(8,128)(2,1)S(1)} %collective-permute-done.refs_0_), channel_id=1, source_target_pairs={{8,0},{18,2},{12,4},{14,6},{0,8},{26,10},{4,12},{6,14},{24,16},{2,... | collective-permute-start | bytes 196616 | tf_op jit(solution)/shard_map/ppermute | solution.py:103
  12.1 4.3 %collective-permute-start.2 = (bf16[2,64,256]{2,1,0:T(8,128)(2,1)S(1)}, bf16[2,64,256]{2,1,0:T(8,128)(2,1)S(1)}, u32[]{:S(2)}, u32[]{:S(2)}) collective-permute-start(bf16[2,64,256]{2,1,0:T(8,128)(2,1)S(1)} %collective-permute-done.refs_0_), channel_id=1, source_target_pairs={{2,0},{10,2},{20,4},{22,6},{16,8},{24,10},{28,12},{30,14},{8,16},{... | collective-permute-start | bytes 196616 | tf_op jit(solution)/shard_map/ppermute | solution.py:103
  13.4 4.3 %collective-permute-start.10 = (bf16[2,64,256]{2,1,0:T(8,128)(2,1)S(1)}, bf16[2,64,256]{2,1,0:T(8,128)(2,1)S(1)}, u32[]{:S(2)}, u32[]{:S(2)}) collective-permute-start(bf16[2,64,256]{2,1,0:T(8,128)(2,1)S(1)} %select_select_fusion), channel_id=1, source_target_pairs={{2,0},{0,2},{6,4},{4,6},{10,8},{8,10},{14,12},{12,14},{18,16},{16,... | collective-permute-start | bytes 196616 | tf_op jit(solution)/shard_map/ppermute | solution.py:103
  14.2 3.0 %collective-permute-start.1 = (bf16[2,64,256]{2,1,0:T(8,128)(2,1)S(1)}, bf16[2,64,256]{2,1,0:T(8,128)(2,1)S(1)}, u32[]{:S(2)}, u32[]{:S(2)}) collective-permute-start(bf16[2,64,256]{2,1,0:T(8,128)(2,1)S(1)} %collective-permute-done.refs_0_), channel_id=1, source_target_pairs={{1,0},{0,1},{3,2},{2,3},{5,4},{4,5},{7,6},{6,7},{9,8},{8,9},{11,10... | collective-permute-start | bytes 196616 | tf_op jit(solution)/shard_map/ppermute | solution.py:327
  14.2 3.5 %collective-permute-start.7 = (bf16[2,64,256]{2,1,0:T(8,128)(2,1)S(1)}, bf16[2,64,256]{2,1,0:T(8,128)(2,1)S(1)}, u32[]{:S(2)}, u32[]{:S(2)}) collective-permute-start(bf16[2,64,256]{2,1,0:T(8,128)(2,1)S(1)} %collective-permute-done.6.refs_3_), channel_id=1, source_target_pairs={{1,0},{0,1},{3,2},{2,3},{5,4},{4,5},{7,6},{6,7},{9,8},{8,9},{11,10... | collective-permute-start | bytes 196616 | tf_op jit(solution)/shard_map/ppermute | solution.py:327
  15.6 2.1 %collective-permute-start.5 = (bf16[2,64,256]{2,1,0:T(8,128)(2,1)S(1)}, bf16[2,64,256]{2,1,0:T(8,128)(2,1)S(1)}, u32[]{:S(2)}, u32[]{:S(2)}) collective-permute-start(bf16[2,64,256]{2,1,0:T(8,128)(2,1)S(1)} %collective-permute-done.4.refs_2_), channel_id=1, source_target_pairs={{1,0},{0,1},{3,2},{2,3},{5,4},{4,5},{7,6},{6,7},{9,8},{8,9},{11,10... | collective-permute-start | bytes 196616 | tf_op jit(solution)/shard_map/ppermute | solution.py:327
  16.4 1.4 %collective-permute-start.3 = (bf16[2,64,256]{2,1,0:T(8,128)(2,1)S(1)}, bf16[2,64,256]{2,1,0:T(8,128)(2,1)S(1)}, u32[]{:S(2)}, u32[]{:S(2)}) collective-permute-start(bf16[2,64,256]{2,1,0:T(8,128)(2,1)S(1)} %broadcast_select_fusion.refs_1_), channel_id=1, source_target_pairs={{1,0},{0,1},{3,2},{2,3},{5,4},{4,5},{7,6},{6,7},{9,8},{8,9},{11,10... | collective-permute-start | bytes 196616 | tf_op jit(solution)/shard_map/ppermute | solution.py:327

commit v28 on v27

--- a/solution.py
+++ b/solution.py
@@ -262,7 +262,7 @@
             store = pltpu.make_async_copy(
                 share_ref.at[pl.ds(start, lines)], out_ref.at[pl.ds(start, lines)], sems.at[at_row * half + k]
             )
-            store.start()
+            store.start(priority=k % 2)
             stores.append(store)
     for store in stores:
         store.wait()

time: 19.5 us -> 19.5 us (level)
  no operation moved by 1% of the time
where the time goes in v28:
time: 19.5 us; the launch traced here: 19.4 us
  starting transfers between devices  11.8 us (61%)
  Pallas kernels  5.36 us (27%)
  waiting for transfers between devices  2.14 us (11%)
    ppermute x6, starting transfers between devices, move(): lax.ppermute(x, ('row', 'col'), [(a * count + b, r * count + c) for (r, c...  7.25 us
    ppermute x1, starting transfers between devices, per_device(): lax.ppermute(factor, ('row', 'col'), [(a * count + b, slots[a][b] * count...  3.95 us
    ppermute x6, waiting for transfers between devices, move(): lax.ppermute(x, ('row', 'col'), [(a * count + b, r * count + c) for (r, c...  2.12 us
    pallas_call x1, Pallas kernels, end_update(): pl.pallas_call(body, out_shape=[jax.ShapeDtypeStruct((half * pieces * row...  1.66 us
    pallas_call x1, Pallas kernels, load_share(): pl.pallas_call(body, out_shape=jax.ShapeDtypeStruct((rows + per_row, LANE...  1.6 us
    pallas_call x1, Pallas kernels, make_factor(): pl.pallas_call(factor_kernel, out_shape=jax.ShapeDtypeStruct((half, tile_...  1.34 us
    pallas_call x1, Pallas kernels, begin_update(): pl.pallas_call(body, out_shape=[jax.ShapeDtypeStruct(share.shape, jnp.flo...  0.76 us
    ppermute x4, starting transfers between devices, per_device(): others += [lax.ppermute(piece, 'layer', pairs) for piece in plane]  0.58 us
  transfers between devices with their start and end apart: 11, of which 3 were waited for; matrix products, arithmetic and copies ran while one was open for 0% of the time, Pallas kernels for 12%

profile of v28, /device:TPU:0, one launch (start us, length us, event | category | flops | bytes accessed | tf_op | source)
XLA Modules:
  0.0 19.4 jit_solution(9769628208819897835)
XLA Ops:
  0.0 1.3 %factor.1.refs_0_.refs_4_ = bf16[2,64,256]{2,1,0:T(8,128)(2,1)S(1)} custom-call(f32[4,1,64,256]{3,2,1,0:T(8,128)} %panel_ref.1, f32[256,256]{1,0:T(8,128)} %inverse_ref.1), custom_call_target="tpu_custom_call" | custom-call | tf_op jit(solution)/shard_map/factor/pallas_call | solution.py:55
  1.4 3.9 %collective-permute-start = (bf16[2,64,256]{2,1,0:T(8,128)(2,1)S(1)}, bf16[2,64,256]{2,1,0:T(8,128)(2,1)S(1)}, u32[]{:S(2)}, u32[]{:S(2)}) collective-permute-start(bf16[2,64,256]{2,1,0:T(8,128)(2,1)S(1)} %factor.1.refs_0_.refs_4_), channel_id=1, source_target_pairs={{0,24},{2,0},{4,8},{6,16},{8,26},{10,2},{12,18},{14,10},{16,28},{1... | collective-permute-start | bytes 196616 | tf_op jit(solution)/shard_map/ppermute | solution.py:307
  5.3 1.6 %load_share.1.refs_7_ = f32[4104,128]{1,0:T(8,128)S(1)} custom-call(bf16[2,64,256]{2,1,0:T(8,128)(2,1)S(1)} %factor.1.refs_0_.refs_4_, f32[8192,128]{1,0:T(8,128)} %bitcast.2), custom_call_target="tpu_custom_call" | custom-call | bytes 4194304 | tf_op jit(solution)/shard_map/load_share/pallas_call | solution.py:135
  6.9 0.1 collective-permute-start.9
  7.0 2.9 %collective-permute-start.8 = (bf16[2,64,256]{2,1,0:T(8,128)(2,1)S(1)}, bf16[2,64,256]{2,1,0:T(8,128)(2,1)S(1)}, u32[]{:S(2)}, u32[]{:S(2)}) collective-permute-start(bf16[2,64,256]{2,1,0:T(8,128)(2,1)S(1)} %factor.1.refs_0_.refs_4_), channel_id=1, source_target_pairs={{4,0},{6,2},{0,4},{2,6},{12,8},{26,10},{8,12},{10,14},{20,16},{22,... | collective-permute-start | bytes 196616 | tf_op jit(solution)/shard_map/ppermute | solution.py:103
  9.8 0.0 collective-permute-done.refs_0_
  9.9 1.5 %collective-permute-start.6 = (bf16[2,64,256]{2,1,0:T(8,128)(2,1)S(1)}, bf16[2,64,256]{2,1,0:T(8,128)(2,1)S(1)}, u32[]{:S(2)}, u32[]{:S(2)}) collective-permute-start(bf16[2,64,256]{2,1,0:T(8,128)(2,1)S(1)} %collective-permute-done.refs_0_), channel_id=1, source_target_pairs={{16,0},{26,2},{28,4},{30,6},{24,8},{18,10},{20,12},{22,14},{0,16},... | collective-permute-start | bytes 196616 | tf_op jit(solution)/shard_map/ppermute | solution.py:103
  11.3 0.7 %collective-permute-start.4 = (bf16[2,64,256]{2,1,0:T(8,128)(2,1)S(1)}, bf16[2,64,256]{2,1,0:T(8,128)(2,1)S(1)}, u32[]{:S(2)}, u32[]{:S(2)}) collective-permute-start(bf16[2,64,256]{2,1,0:T(8,128)(2,1)S(1)} %collective-permute-done.refs_0_), channel_id=1, source_target_pairs={{8,0},{18,2},{12,4},{14,6},{0,8},{26,10},{4,12},{6,14},{24,16},{2,... | collective-permute-start | bytes 196616 | tf_op jit(solution)/shard_map/ppermute | solution.py:103
  12.1 1.3 %collective-permute-start.2 = (bf16[2,64,256]{2,1,0:T(8,128)(2,1)S(1)}, bf16[2,64,256]{2,1,0:T(8,128)(2,1)S(1)}, u32[]{:S(2)}, u32[]{:S(2)}) collective-permute-start(bf16[2,64,256]{2,1,0:T(8,128)(2,1)S(1)} %collective-permute-done.refs_0_), channel_id=1, source_target_pairs={{2,0},{10,2},{20,4},{22,6},{16,8},{24,10},{28,12},{30,14},{8,16},{... | collective-permute-start | bytes 196616 | tf_op jit(solution)/shard_map/ppermute | solution.py:103
  13.3 0.0 collective-permute-done.9.refs_6_
  13.3 0.0 collective-permute-done.8.refs_5_
  13.4 0.8 %collective-permute-start.10 = (bf16[2,64,256]{2,1,0:T(8,128)(2,1)S(1)}, bf16[2,64,256]{2,1,0:T(8,128)(2,1)S(1)}, u32[]{:S(2)}, u32[]{:S(2)}) collective-permute-start(bf16[2,64,256]{2,1,0:T(8,128)(2,1)S(1)} %select_select_fusion), channel_id=1, source_target_pairs={{2,0},{0,2},{6,4},{4,6},{10,8},{8,10},{14,12},{12,14},{18,16},{16,... | collective-permute-start | bytes 196616 | tf_op jit(solution)/shard_map/ppermute | solution.py:103
  14.2 0.0 collective-permute-start.1
  14.2 0.0 collective-permute-done.6.refs_3_
  14.2 0.5 %collective-permute-start.7 = (bf16[2,64,256]{2,1,0:T(8,128)(2,1)S(1)}, bf16[2,64,256]{2,1,0:T(8,128)(2,1)S(1)}, u32[]{:S(2)}, u32[]{:S(2)}) collective-permute-start(bf16[2,64,256]{2,1,0:T(8,128)(2,1)S(1)} %collective-permute-done.6.refs_3_), channel_id=1, source_target_pairs={{1,0},{0,1},{3,2},{2,3},{5,4},{4,5},{7,6},{6,7},{9,8},{8,9},{11,10... | collective-permute-start | bytes 196616 | tf_op jit(solution)/shard_map/ppermute | solution.py:327
  14.7 0.9 %collective-permute-done.4.refs_2_ = bf16[2,64,256]{2,1,0:T(8,128)(2,1)S(1)} collective-permute-done((bf16[2,64,256]{2,1,0:T(8,128)(2,1)S(1)}, bf16[2,64,256]{2,1,0:T(8,128)(2,1)S(1)}, u32[]{:S(2)}, u32[]{:S(2)}) %collective-permute-start.4) | collective-permute-done | bytes 65568 | tf_op jit(solution)/shard_map/ppermute | solution.py:103
  15.6 0.0 collective-permute-start.5
  15.6 0.7 %collective-permute-done.2 = bf16[2,64,256]{2,1,0:T(8,128)(2,1)S(1)} collective-permute-done((bf16[2,64,256]{2,1,0:T(8,128)(2,1)S(1)}, bf16[2,64,256]{2,1,0:T(8,128)(2,1)S(1)}, u32[]{:S(2)}, u32[]{:S(2)}) %collective-permute-start.2) | collective-permute-done | bytes 65568 | tf_op jit(solution)/shard_map/ppermute | solution.py:103
  16.4 0.1 collective-permute-start.3
  16.4 0.8 %begin_update.1 = (f32[4104,128]{1,0:T(8,128)S(1)}, bf16[512,256]{1,0:T(8,128)(2,1)S(1)}, bf16[2,64,256]{2,1,0:T(8,128)(2,1)S(1)}, bf16[2,64,256]{2,1,0:T(8,128)(2,1)S(1)}) custom-call(bf16[2,64,256]{2,1,0:T(8,128)(2,1)S(1)} %collective-permute-done.refs_0_, bf16[2,64,256]{2,1,0:T(8,128)(2,1)S(1)} %broadcast_select_fusion.refs_1_, ...), custom_call_target="tpu_custom_call", output_to_operand_aliasing={{0}: (7, {})} | custom-call | tf_op jit(solution)/shard_map/begin_update/pallas_call | solution.py:215
  17.2 0.0 collective-permute-done.1.refs_0_
  17.2 0.5 %collective-permute-done.10.refs_7_ = bf16[2,64,256]{2,1,0:T(8,128)(2,1)S(1)} collective-permute-done((bf16[2,64,256]{2,1,0:T(8,128)(2,1)S(1)}, bf16[2,64,256]{2,1,0:T(8,128)(2,1)S(1)}, u32[]{:S(2)}, u32[]{:S(2)}) %collective-permute-start.10) | collective-permute-done | bytes 65568 | tf_op jit(solution)/shard_map/ppermute | solution.py:103
  17.7 0.0 collective-permute-done.7.refs_3_
  17.7 0.0 collective-permute-done.5.refs_2_
  17.7 0.0 collective-permute-done.3.refs_1_
  17.7 1.7 %end_update.1 = (f32[4096,128]{1,0:T(8,128)}, f32[4104,128]{1,0:T(8,128)S(1)}) custom-call(bf16[2,64,256]{2,1,0:T(8,128)(2,1)S(1)} %collective-permute-done.1.refs_0_, bf16[2,64,256]{2,1,0:T(8,128)(2,1)S(1)} %collective-permute-done.3.refs_1_, bf16[2,64,256]{2,1,0:T(8,128)(2,1)S(1)} %collective-permute-done.5.refs_2_, ...), custom_call_target="tpu_custom_call", output_to_operand_aliasing={{1}: (9, {})} | custom-call | tf_op jit(solution)/shard_map/end_update/pallas_call | solution.py:280
  (2 shorter events, 0.0 us)
Async XLA Ops:
  1.4 8.5 %collective-permute-start = (bf16[2,64,256]{2,1,0:T(8,128)(2,1)S(1)}, bf16[2,64,256]{2,1,0:T(8,128)(2,1)S(1)}, u32[]{:S(2)}, u32[]{:S(2)}) collective-permute-start(bf16[2,64,256]{2,1,0:T(8,128)(2,1)S(1)} %factor.1.refs_0_.refs_4_), channel_id=1, source_target_pairs={{0,24},{2,0},{4,8},{6,16},{8,26},{10,2},{12,18},{14,10},{16,28},{1... | collective-permute-start | bytes 196616 | tf_op jit(solution)/shard_map/ppermute | solution.py:307
  6.9 6.4 %collective-permute-start.9 = (bf16[2,64,256]{2,1,0:T(8,128)(2,1)S(1)}, bf16[2,64,256]{2,1,0:T(8,128)(2,1)S(1)}, u32[]{:S(2)}, u32[]{:S(2)}) collective-permute-start(bf16[2,64,256]{2,1,0:T(8,128)(2,1)S(1)} %factor.1.refs_0_.refs_4_), channel_id=1, source_target_pairs={{8,0},{0,2},{6,4},{4,6},{10,8},{2,10},{14,12},{12,14},{18,16},{16,... | collective-permute-start | bytes 196616 | tf_op jit(solution)/shard_map/ppermute | solution.py:103
  7.0 6.4 %collective-permute-start.8 = (bf16[2,64,256]{2,1,0:T(8,128)(2,1)S(1)}, bf16[2,64,256]{2,1,0:T(8,128)(2,1)S(1)}, u32[]{:S(2)}, u32[]{:S(2)}) collective-permute-start(bf16[2,64,256]{2,1,0:T(8,128)(2,1)S(1)} %factor.1.refs_0_.refs_4_), channel_id=1, source_target_pairs={{4,0},{6,2},{0,4},{2,6},{12,8},{26,10},{8,12},{10,14},{20,16},{22,... | collective-permute-start | bytes 196616 | tf_op jit(solution)/shard_map/ppermute | solution.py:103
  9.9 4.3 %collective-permute-start.6 = (bf16[2,64,256]{2,1,0:T(8,128)(2,1)S(1)}, bf16[2,64,256]{2,1,0:T(8,128)(2,1)S(1)}, u32[]{:S(2)}, u32[]{:S(2)}) collective-permute-start(bf16[2,64,256]{2,1,0:T(8,128)(2,1)S(1)} %collective-permute-done.refs_0_), channel_id=1, source_target_pairs={{16,0},{26,2},{28,4},{30,6},{24,8},{18,10},{20,12},{22,14},{0,16},... | collective-permute-start | bytes 196616 | tf_op jit(solution)/shard_map/ppermute | solution.py:103
  11.3 4.3 %collective-permute-start.4 = (bf16[2,64,256]{2,1,0:T(8,128)(2,1)S(1)}, bf16[2,64,256]{2,1,0:T(8,128)(2,1)S(1)}, u32[]{:S(2)}, u32[]{:S(2)}) collective-permute-start(bf16[2,64,256]{2,1,0:T(8,128)(2,1)S(1)} %collective-permute-done.refs_0_), channel_id=1, source_target_pairs={{8,0},{18,2},{12,4},{14,6},{0,8},{26,10},{4,12},{6,14},{24,16},{2,... | collective-permute-start | bytes 196616 | tf_op jit(solution)/shard_map/ppermute | solution.py:103
  12.1 4.3 %collective-permute-start.2 = (bf16[2,64,256]{2,1,0:T(8,128)(2,1)S(1)}, bf16[2,64,256]{2,1,0:T(8,128)(2,1)S(1)}, u32[]{:S(2)}, u32[]{:S(2)}) collective-permute-start(bf16[2,64,256]{2,1,0:T(8,128)(2,1)S(1)} %collective-permute-done.refs_0_), channel_id=1, source_target_pairs={{2,0},{10,2},{20,4},{22,6},{16,8},{24,10},{28,12},{30,14},{8,16},{... | collective-permute-start | bytes 196616 | tf_op jit(solution)/shard_map/ppermute | solution.py:103
  13.4 4.3 %collective-permute-start.10 = (bf16[2,64,256]{2,1,0:T(8,128)(2,1)S(1)}, bf16[2,64,256]{2,1,0:T(8,128)(2,1)S(1)}, u32[]{:S(2)}, u32[]{:S(2)}) collective-permute-start(bf16[2,64,256]{2,1,0:T(8,128)(2,1)S(1)} %select_select_fusion), channel_id=1, source_target_pairs={{2,0},{0,2},{6,4},{4,6},{10,8},{8,10},{14,12},{12,14},{18,16},{16,... | collective-permute-start | bytes 196616 | tf_op jit(solution)/shard_map/ppermute | solution.py:103
  14.2 3.0 %collective-permute-start.1 = (bf16[2,64,256]{2,1,0:T(8,128)(2,1)S(1)}, bf16[2,64,256]{2,1,0:T(8,128)(2,1)S(1)}, u32[]{:S(2)}, u32[]{:S(2)}) collective-permute-start(bf16[2,64,256]{2,1,0:T(8,128)(2,1)S(1)} %collective-permute-done.refs_0_), channel_id=1, source_target_pairs={{1,0},{0,1},{3,2},{2,3},{5,4},{4,5},{7,6},{6,7},{9,8},{8,9},{11,10... | collective-permute-start | bytes 196616 | tf_op jit(solution)/shard_map/ppermute | solution.py:327
  14.2 3.5 %collective-permute-start.7 = (bf16[2,64,256]{2,1,0:T(8,128)(2,1)S(1)}, bf16[2,64,256]{2,1,0:T(8,128)(2,1)S(1)}, u32[]{:S(2)}, u32[]{:S(2)}) collective-permute-start(bf16[2,64,256]{2,1,0:T(8,128)(2,1)S(1)} %collective-permute-done.6.refs_3_), channel_id=1, source_target_pairs={{1,0},{0,1},{3,2},{2,3},{5,4},{4,5},{7,6},{6,7},{9,8},{8,9},{11,10... | collective-permute-start | bytes 196616 | tf_op jit(solution)/shard_map/ppermute | solution.py:327
  15.6 2.1 %collective-permute-start.5 = (bf16[2,64,256]{2,1,0:T(8,128)(2,1)S(1)}, bf16[2,64,256]{2,1,0:T(8,128)(2,1)S(1)}, u32[]{:S(2)}, u32[]{:S(2)}) collective-permute-start(bf16[2,64,256]{2,1,0:T(8,128)(2,1)S(1)} %collective-permute-done.4.refs_2_), channel_id=1, source_target_pairs={{1,0},{0,1},{3,2},{2,3},{5,4},{4,5},{7,6},{6,7},{9,8},{8,9},{11,10... | collective-permute-start | bytes 196616 | tf_op jit(solution)/shard_map/ppermute | solution.py:327
  16.4 1.4 %collective-permute-start.3 = (bf16[2,64,256]{2,1,0:T(8,128)(2,1)S(1)}, bf16[2,64,256]{2,1,0:T(8,128)(2,1)S(1)}, u32[]{:S(2)}, u32[]{:S(2)}) collective-permute-start(bf16[2,64,256]{2,1,0:T(8,128)(2,1)S(1)} %broadcast_select_fusion.refs_1_), channel_id=1, source_target_pairs={{1,0},{0,1},{3,2},{2,3},{5,4},{4,5},{7,6},{6,7},{9,8},{8,9},{11,10... | collective-permute-start | bytes 196616 | tf_op jit(solution)/shard_map/ppermute | solution.py:327

commit v29 on v27

--- a/solution.py
+++ b/solution.py
@@ -79,7 +79,7 @@
 
 def plane_mates(count, plane):
     if count == 4:
-        return ((0, 3, 1, 2), (0, 1, 2, 3), (0, 2, 1, 3), (0, 2, 1, 3))[plane]
+        return ((0, 3, 2, 1), (0, 1, 2, 3), (0, 2, 1, 3), (0, 2, 1, 3))[plane]
     return tuple(range(count))
 
 

time: 19.5 us -> 19.5 us (level)
  starting transfers between devices: 11.8 us -> 11.6 us
  transfers between devices with their start and end apart: 11 -> 11, of which waited for: 3 -> 4; matrix products, arithmetic and copies ran while one was open for 0% -> 0% of each run, Pallas kernels for 12% -> 12%
where the time goes in v29:
time: 19.5 us; the launch traced here: 19.4 us
  starting transfers between devices  11.6 us (59%)
  Pallas kernels  5.34 us (27%)
  waiting for transfers between devices  2.32 us (12%)
    ppermute x6, starting transfers between devices, move(): lax.ppermute(x, ('row', 'col'), [(a * count + b, r * count + c) for (r, c...  7.25 us
    ppermute x1, starting transfers between devices, per_device(): lax.ppermute(factor, ('row', 'col'), [(a * count + b, slots[a][b] * count...  3.95 us
    ppermute x6, waiting for transfers between devices, move(): lax.ppermute(x, ('row', 'col'), [(a * count + b, r * count + c) for (r, c...  2.31 us
    pallas_call x1, Pallas kernels, end_update(): pl.pallas_call(body, out_shape=[jax.ShapeDtypeStruct((half * pieces * row...  1.66 us
    pallas_call x1, Pallas kernels, load_share(): pl.pallas_call(body, out_shape=jax.ShapeDtypeStruct((rows + per_row, LANE...  1.6 us
    pallas_call x1, Pallas kernels, make_factor(): pl.pallas_call(factor_kernel, out_shape=jax.ShapeDtypeStruct((half, tile_...  1.34 us
    pallas_call x1, Pallas kernels, begin_update(): pl.pallas_call(body, out_shape=[jax.ShapeDtypeStruct(share.shape, jnp.flo...  0.75 us
    ppermute x4, starting transfers between devices, per_device(): others += [lax.ppermute(piece, 'layer', pairs) for piece in plane]  0.42 us
  transfers between devices with their start and end apart: 11, of which 4 were waited for; matrix products, arithmetic and copies ran while one was open for 0% of the time, Pallas kernels for 12%

profile of v29, /device:TPU:0, one launch (start us, length us, event | category | flops | bytes accessed | tf_op | source)
XLA Modules:
  0.0 19.4 jit_solution(9906088510778256287)
XLA Ops:
  0.0 1.3 %factor.1.refs_0_.refs_4_ = bf16[2,64,256]{2,1,0:T(8,128)(2,1)S(1)} custom-call(f32[4,1,64,256]{3,2,1,0:T(8,128)} %panel_ref.1, f32[256,256]{1,0:T(8,128)} %inverse_ref.1), custom_call_target="tpu_custom_call" | custom-call | tf_op jit(solution)/shard_map/factor/pallas_call | solution.py:55
  1.4 3.9 %collective-permute-start = (bf16[2,64,256]{2,1,0:T(8,128)(2,1)S(1)}, bf16[2,64,256]{2,1,0:T(8,128)(2,1)S(1)}, u32[]{:S(2)}, u32[]{:S(2)}) collective-permute-start(bf16[2,64,256]{2,1,0:T(8,128)(2,1)S(1)} %factor.1.refs_0_.refs_4_), channel_id=1, source_target_pairs={{0,24},{2,0},{4,8},{6,16},{8,26},{10,2},{12,18},{14,10},{16,28},{1... | collective-permute-start | bytes 196616 | tf_op jit(solution)/shard_map/ppermute | solution.py:307
  5.3 1.6 %load_share.1.refs_7_ = f32[4104,128]{1,0:T(8,128)S(1)} custom-call(bf16[2,64,256]{2,1,0:T(8,128)(2,1)S(1)} %factor.1.refs_0_.refs_4_, f32[8192,128]{1,0:T(8,128)} %bitcast.2), custom_call_target="tpu_custom_call" | custom-call | bytes 4194304 | tf_op jit(solution)/shard_map/load_share/pallas_call | solution.py:135
  6.9 0.1 collective-permute-start.9
  7.0 2.9 %collective-permute-start.8 = (bf16[2,64,256]{2,1,0:T(8,128)(2,1)S(1)}, bf16[2,64,256]{2,1,0:T(8,128)(2,1)S(1)}, u32[]{:S(2)}, u32[]{:S(2)}) collective-permute-start(bf16[2,64,256]{2,1,0:T(8,128)(2,1)S(1)} %factor.1.refs_0_.refs_4_), channel_id=1, source_target_pairs={{4,0},{6,2},{0,4},{2,6},{12,8},{26,10},{8,12},{10,14},{20,16},{22,... | collective-permute-start | bytes 196616 | tf_op jit(solution)/shard_map/ppermute | solution.py:103
  9.8 0.0 collective-permute-done.refs_0_
  9.9 1.8 %collective-permute-start.6 = (bf16[2,64,256]{2,1,0:T(8,128)(2,1)S(1)}, bf16[2,64,256]{2,1,0:T(8,128)(2,1)S(1)}, u32[]{:S(2)}, u32[]{:S(2)}) collective-permute-start(bf16[2,64,256]{2,1,0:T(8,128)(2,1)S(1)} %collective-permute-done.refs_0_), channel_id=1, source_target_pairs={{8,0},{26,2},{28,4},{30,6},{0,8},{18,10},{20,12},{22,14},{24,16},{... | collective-permute-start | bytes 196616 | tf_op jit(solution)/shard_map/ppermute | solution.py:103
  11.6 0.5 %collective-permute-start.4 = (bf16[2,64,256]{2,1,0:T(8,128)(2,1)S(1)}, bf16[2,64,256]{2,1,0:T(8,128)(2,1)S(1)}, u32[]{:S(2)}, u32[]{:S(2)}) collective-permute-start(bf16[2,64,256]{2,1,0:T(8,128)(2,1)S(1)} %collective-permute-done.refs_0_), channel_id=1, source_target_pairs={{16,0},{18,2},{12,4},{14,6},{24,8},{26,10},{4,12},{6,14},{0,16},{2... | collective-permute-start | bytes 196616 | tf_op jit(solution)/shard_map/ppermute | solution.py:103
  12.1 1.3 %collective-permute-start.2 = (bf16[2,64,256]{2,1,0:T(8,128)(2,1)S(1)}, bf16[2,64,256]{2,1,0:T(8,128)(2,1)S(1)}, u32[]{:S(2)}, u32[]{:S(2)}) collective-permute-start(bf16[2,64,256]{2,1,0:T(8,128)(2,1)S(1)} %collective-permute-done.refs_0_), channel_id=1, source_target_pairs={{2,0},{10,2},{20,4},{22,6},{16,8},{24,10},{28,12},{30,14},{8,16},{... | collective-permute-start | bytes 196616 | tf_op jit(solution)/shard_map/ppermute | solution.py:103
  13.3 0.0 collective-permute-done.9.refs_6_
  13.3 0.0 collective-permute-done.8.refs_5_
  13.4 0.8 %collective-permute-start.10 = (bf16[2,64,256]{2,1,0:T(8,128)(2,1)S(1)}, bf16[2,64,256]{2,1,0:T(8,128)(2,1)S(1)}, u32[]{:S(2)}, u32[]{:S(2)}) collective-permute-start(bf16[2,64,256]{2,1,0:T(8,128)(2,1)S(1)} %select_select_fusion), channel_id=1, source_target_pairs={{2,0},{0,2},{6,4},{4,6},{10,8},{8,10},{14,12},{12,14},{18,16},{16,... | collective-permute-start | bytes 196616 | tf_op jit(solution)/shard_map/ppermute | solution.py:103
  14.2 0.0 collective-permute-start.1
  14.2 0.2 %collective-permute-done.6.refs_3_ = bf16[2,64,256]{2,1,0:T(8,128)(2,1)S(1)} collective-permute-done((bf16[2,64,256]{2,1,0:T(8,128)(2,1)S(1)}, bf16[2,64,256]{2,1,0:T(8,128)(2,1)S(1)}, u32[]{:S(2)}, u32[]{:S(2)}) %collective-permute-start.6) | collective-permute-done | bytes 65568 | tf_op jit(solution)/shard_map/ppermute | solution.py:103
  14.4 0.3 %collective-permute-start.7 = (bf16[2,64,256]{2,1,0:T(8,128)(2,1)S(1)}, bf16[2,64,256]{2,1,0:T(8,128)(2,1)S(1)}, u32[]{:S(2)}, u32[]{:S(2)}) collective-permute-start(bf16[2,64,256]{2,1,0:T(8,128)(2,1)S(1)} %collective-permute-done.6.refs_3_), channel_id=1, source_target_pairs={{1,0},{0,1},{3,2},{2,3},{5,4},{4,5},{7,6},{6,7},{9,8},{8,9},{11,10... | collective-permute-start | bytes 196616 | tf_op jit(solution)/shard_map/ppermute | solution.py:327
  14.7 1.2 %collective-permute-done.4.refs_2_ = bf16[2,64,256]{2,1,0:T(8,128)(2,1)S(1)} collective-permute-done((bf16[2,64,256]{2,1,0:T(8,128)(2,1)S(1)}, bf16[2,64,256]{2,1,0:T(8,128)(2,1)S(1)}, u32[]{:S(2)}, u32[]{:S(2)}) %collective-permute-start.4) | collective-permute-done | bytes 65568 | tf_op jit(solution)/shard_map/ppermute | solution.py:103
  15.9 0.0 collective-permute-start.5
  15.9 0.5 %collective-permute-done.2 = bf16[2,64,256]{2,1,0:T(8,128)(2,1)S(1)} collective-permute-done((bf16[2,64,256]{2,1,0:T(8,128)(2,1)S(1)}, bf16[2,64,256]{2,1,0:T(8,128)(2,1)S(1)}, u32[]{:S(2)}, u32[]{:S(2)}) %collective-permute-start.2) | collective-permute-done | bytes 65568 | tf_op jit(solution)/shard_map/ppermute | solution.py:103
  16.4 0.1 collective-permute-start.3
  16.5 0.7 %begin_update.1 = (f32[4104,128]{1,0:T(8,128)S(1)}, bf16[512,256]{1,0:T(8,128)(2,1)S(1)}, bf16[2,64,256]{2,1,0:T(8,128)(2,1)S(1)}, bf16[2,64,256]{2,1,0:T(8,128)(2,1)S(1)}) custom-call(bf16[2,64,256]{2,1,0:T(8,128)(2,1)S(1)} %collective-permute-done.refs_0_, bf16[2,64,256]{2,1,0:T(8,128)(2,1)S(1)} %broadcast_select_fusion.refs_1_, ...), custom_call_target="tpu_custom_call", output_to_operand_aliasing={{0}: (7, {})} | custom-call | tf_op jit(solution)/shard_map/begin_update/pallas_call | solution.py:215
  17.2 0.0 collective-permute-done.1.refs_0_
  17.2 0.5 %collective-permute-done.10.refs_7_ = bf16[2,64,256]{2,1,0:T(8,128)(2,1)S(1)} collective-permute-done((bf16[2,64,256]{2,1,0:T(8,128)(2,1)S(1)}, bf16[2,64,256]{2,1,0:T(8,128)(2,1)S(1)}, u32[]{:S(2)}, u32[]{:S(2)}) %collective-permute-start.10) | collective-permute-done | bytes 65568 | tf_op jit(solution)/shard_map/ppermute | solution.py:103
  17.7 0.0 collective-permute-done.7.refs_3_
  17.7 0.0 collective-permute-done.5.refs_2_
  17.7 0.0 collective-permute-done.3.refs_1_
  17.7 1.7 %end_update.1 = (f32[4096,128]{1,0:T(8,128)}, f32[4104,128]{1,0:T(8,128)S(1)}) custom-call(bf16[2,64,256]{2,1,0:T(8,128)(2,1)S(1)} %collective-permute-done.1.refs_0_, bf16[2,64,256]{2,1,0:T(8,128)(2,1)S(1)} %collective-permute-done.3.refs_1_, bf16[2,64,256]{2,1,0:T(8,128)(2,1)S(1)} %collective-permute-done.5.refs_2_, ...), custom_call_target="tpu_custom_call", output_to_operand_aliasing={{1}: (9, {})} | custom-call | tf_op jit(solution)/shard_map/end_update/pallas_call | solution.py:280
  (2 shorter events, 0.0 us)
Async XLA Ops:
  1.4 8.5 %collective-permute-start = (bf16[2,64,256]{2,1,0:T(8,128)(2,1)S(1)}, bf16[2,64,256]{2,1,0:T(8,128)(2,1)S(1)}, u32[]{:S(2)}, u32[]{:S(2)}) collective-permute-start(bf16[2,64,256]{2,1,0:T(8,128)(2,1)S(1)} %factor.1.refs_0_.refs_4_), channel_id=1, source_target_pairs={{0,24},{2,0},{4,8},{6,16},{8,26},{10,2},{12,18},{14,10},{16,28},{1... | collective-permute-start | bytes 196616 | tf_op jit(solution)/shard_map/ppermute | solution.py:307
  6.9 6.4 %collective-permute-start.9 = (bf16[2,64,256]{2,1,0:T(8,128)(2,1)S(1)}, bf16[2,64,256]{2,1,0:T(8,128)(2,1)S(1)}, u32[]{:S(2)}, u32[]{:S(2)}) collective-permute-start(bf16[2,64,256]{2,1,0:T(8,128)(2,1)S(1)} %factor.1.refs_0_.refs_4_), channel_id=1, source_target_pairs={{8,0},{0,2},{6,4},{4,6},{10,8},{2,10},{14,12},{12,14},{18,16},{16,... | collective-permute-start | bytes 196616 | tf_op jit(solution)/shard_map/ppermute | solution.py:103
  7.0 6.4 %collective-permute-start.8 = (bf16[2,64,256]{2,1,0:T(8,128)(2,1)S(1)}, bf16[2,64,256]{2,1,0:T(8,128)(2,1)S(1)}, u32[]{:S(2)}, u32[]{:S(2)}) collective-permute-start(bf16[2,64,256]{2,1,0:T(8,128)(2,1)S(1)} %factor.1.refs_0_.refs_4_), channel_id=1, source_target_pairs={{4,0},{6,2},{0,4},{2,6},{12,8},{26,10},{8,12},{10,14},{20,16},{22,... | collective-permute-start | bytes 196616 | tf_op jit(solution)/shard_map/ppermute | solution.py:103
  9.9 4.5 %collective-permute-start.6 = (bf16[2,64,256]{2,1,0:T(8,128)(2,1)S(1)}, bf16[2,64,256]{2,1,0:T(8,128)(2,1)S(1)}, u32[]{:S(2)}, u32[]{:S(2)}) collective-permute-start(bf16[2,64,256]{2,1,0:T(8,128)(2,1)S(1)} %collective-permute-done.refs_0_), channel_id=1, source_target_pairs={{8,0},{26,2},{28,4},{30,6},{0,8},{18,10},{20,12},{22,14},{24,16},{... | collective-permute-start | bytes 196616 | tf_op jit(solution)/shard_map/ppermute | solution.py:103
  11.6 4.3 %collective-permute-start.4 = (bf16[2,64,256]{2,1,0:T(8,128)(2,1)S(1)}, bf16[2,64,256]{2,1,0:T(8,128)(2,1)S(1)}, u32[]{:S(2)}, u32[]{:S(2)}) collective-permute-start(bf16[2,64,256]{2,1,0:T(8,128)(2,1)S(1)} %collective-permute-done.refs_0_), channel_id=1, source_target_pairs={{16,0},{18,2},{12,4},{14,6},{24,8},{26,10},{4,12},{6,14},{0,16},{2... | collective-permute-start | bytes 196616 | tf_op jit(solution)/shard_map/ppermute | solution.py:103
  12.1 4.3 %collective-permute-start.2 = (bf16[2,64,256]{2,1,0:T(8,128)(2,1)S(1)}, bf16[2,64,256]{2,1,0:T(8,128)(2,1)S(1)}, u32[]{:S(2)}, u32[]{:S(2)}) collective-permute-start(bf16[2,64,256]{2,1,0:T(8,128)(2,1)S(1)} %collective-permute-done.refs_0_), channel_id=1, source_target_pairs={{2,0},{10,2},{20,4},{22,6},{16,8},{24,10},{28,12},{30,14},{8,16},{... | collective-permute-start | bytes 196616 | tf_op jit(solution)/shard_map/ppermute | solution.py:103
  13.4 4.3 %collective-permute-start.10 = (bf16[2,64,256]{2,1,0:T(8,128)(2,1)S(1)}, bf16[2,64,256]{2,1,0:T(8,128)(2,1)S(1)}, u32[]{:S(2)}, u32[]{:S(2)}) collective-permute-start(bf16[2,64,256]{2,1,0:T(8,128)(2,1)S(1)} %select_select_fusion), channel_id=1, source_target_pairs={{2,0},{0,2},{6,4},{4,6},{10,8},{8,10},{14,12},{12,14},{18,16},{16,... | collective-permute-start | bytes 196616 | tf_op jit(solution)/shard_map/ppermute | solution.py:103
  14.2 3.0 %collective-permute-start.1 = (bf16[2,64,256]{2,1,0:T(8,128)(2,1)S(1)}, bf16[2,64,256]{2,1,0:T(8,128)(2,1)S(1)}, u32[]{:S(2)}, u32[]{:S(2)}) collective-permute-start(bf16[2,64,256]{2,1,0:T(8,128)(2,1)S(1)} %collective-permute-done.refs_0_), channel_id=1, source_target_pairs={{1,0},{0,1},{3,2},{2,3},{5,4},{4,5},{7,6},{6,7},{9,8},{8,9},{11,10... | collective-permute-start | bytes 196616 | tf_op jit(solution)/shard_map/ppermute | solution.py:327
  14.4 3.3 %collective-permute-start.7 = (bf16[2,64,256]{2,1,0:T(8,128)(2,1)S(1)}, bf16[2,64,256]{2,1,0:T(8,128)(2,1)S(1)}, u32[]{:S(2)}, u32[]{:S(2)}) collective-permute-start(bf16[2,64,256]{2,1,0:T(8,128)(2,1)S(1)} %collective-permute-done.6.refs_3_), channel_id=1, source_target_pairs={{1,0},{0,1},{3,2},{2,3},{5,4},{4,5},{7,6},{6,7},{9,8},{8,9},{11,10... | collective-permute-start | bytes 196616 | tf_op jit(solution)/shard_map/ppermute | solution.py:327
  15.9 1.8 %collective-permute-start.5 = (bf16[2,64,256]{2,1,0:T(8,128)(2,1)S(1)}, bf16[2,64,256]{2,1,0:T(8,128)(2,1)S(1)}, u32[]{:S(2)}, u32[]{:S(2)}) collective-permute-start(bf16[2,64,256]{2,1,0:T(8,128)(2,1)S(1)} %collective-permute-done.4.refs_2_), channel_id=1, source_target_pairs={{1,0},{0,1},{3,2},{2,3},{5,4},{4,5},{7,6},{6,7},{9,8},{8,9},{11,10... | collective-permute-start | bytes 196616 | tf_op jit(solution)/shard_map/ppermute | solution.py:327
  16.4 1.4 %collective-permute-start.3 = (bf16[2,64,256]{2,1,0:T(8,128)(2,1)S(1)}, bf16[2,64,256]{2,1,0:T(8,128)(2,1)S(1)}, u32[]{:S(2)}, u32[]{:S(2)}) collective-permute-start(bf16[2,64,256]{2,1,0:T(8,128)(2,1)S(1)} %broadcast_select_fusion.refs_1_), channel_id=1, source_target_pairs={{1,0},{0,1},{3,2},{2,3},{5,4},{4,5},{7,6},{6,7},{9,8},{8,9},{11,10... | collective-permute-start | bytes 196616 | tf_op jit(solution)/shard_map/ppermute | solution.py:327

commit v30 on v27

--- a/solution.py
+++ b/solution.py
@@ -25,17 +25,15 @@
     tile_rows = factor_ref.shape[1]
     width = factor_ref.shape[2]
     layer = lax.axis_index("layer")
-    copies = [
-        pltpu.make_async_copy(panel_ref.at[pl.ds(layer * half, half), 0], panel_buf, sems.at[0]),
-        pltpu.make_async_copy(inverse_ref, inverse_buf, sems.at[1]),
-    ]
-    for copy in copies:
-        copy.start()
-    for copy in copies:
-        copy.wait()
+    panel_copy = pltpu.make_async_copy(panel_ref.at[pl.ds(layer * half, half), 0], panel_buf, sems.at[0])
+    inverse_copy = pltpu.make_async_copy(inverse_ref, inverse_buf, sems.at[1])
+    inverse_copy.start()
+    panel_copy.start()
+    inverse_copy.wait()
+    inverse = split(inverse_buf[...])
+    panel_copy.wait()
     rows = half * tile_rows
     panel = split(panel_buf[...].reshape(rows, width))
-    inverse = split(inverse_buf[...])
 
     def times(parts, part):
         return lax.dot_general(

time: 19.5 us -> 19.5 us (level)
  no operation moved by 1% of the time
where the time goes in v30:
time: 19.5 us; the launch traced here: 19.4 us
  starting transfers between devices  11.8 us (61%)
  Pallas kernels  5.36 us (27%)
  waiting for transfers between devices  2.14 us (11%)
    ppermute x6, starting transfers between devices, move(): lax.ppermute(x, ('row', 'col'), [(a * count + b, r * count + c) for (r, c...  7.26 us
    ppermute x1, starting transfers between devices, per_device(): lax.ppermute(factor, ('row', 'col'), [(a * count + b, slots[a][b] * count...  3.95 us
    ppermute x6, waiting for transfers between devices, move(): lax.ppermute(x, ('row', 'col'), [(a * count + b, r * count + c) for (r, c...  2.12 us
    pallas_call x1, Pallas kernels, end_update(): pl.pallas_call(body, out_shape=[jax.ShapeDtypeStruct((half * pieces * row...  1.66 us
    pallas_call x1, Pallas kernels, load_share(): pl.pallas_call(body, out_shape=jax.ShapeDtypeStruct((rows + per_row, LANE...  1.6 us
    pallas_call x1, Pallas kernels, make_factor(): pl.pallas_call(factor_kernel, out_shape=jax.ShapeDtypeStruct((half, tile_...  1.34 us
    pallas_call x1, Pallas kernels, begin_update(): pl.pallas_call(body, out_shape=[jax.ShapeDtypeStruct(share.shape, jnp.flo...  0.76 us
    ppermute x4, starting transfers between devices, per_device(): others += [lax.ppermute(piece, 'layer', pairs) for piece in plane]  0.58 us
  transfers between devices with their start and end apart: 11, of which 3 were waited for; matrix products, arithmetic and copies ran while one was open for 0% of the time, Pallas kernels for 12%

profile of v30, /device:TPU:0, one launch (start us, length us, event | category | flops | bytes accessed | tf_op | source)
XLA Modules:
  0.0 19.4 jit_solution(13812832223159328227)
XLA Ops:
  0.0 1.3 %factor.1.refs_0_.refs_4_ = bf16[2,64,256]{2,1,0:T(8,128)(2,1)S(1)} custom-call(f32[4,1,64,256]{3,2,1,0:T(8,128)} %panel_ref.1, f32[256,256]{1,0:T(8,128)} %inverse_ref.1), custom_call_target="tpu_custom_call" | custom-call | tf_op jit(solution)/shard_map/factor/pallas_call | solution.py:53
  1.3 3.9 %collective-permute-start = (bf16[2,64,256]{2,1,0:T(8,128)(2,1)S(1)}, bf16[2,64,256]{2,1,0:T(8,128)(2,1)S(1)}, u32[]{:S(2)}, u32[]{:S(2)}) collective-permute-start(bf16[2,64,256]{2,1,0:T(8,128)(2,1)S(1)} %factor.1.refs_0_.refs_4_), channel_id=1, source_target_pairs={{0,24},{2,0},{4,8},{6,16},{8,26},{10,2},{12,18},{14,10},{16,28},{1... | collective-permute-start | bytes 196616 | tf_op jit(solution)/shard_map/ppermute | solution.py:305
  5.3 1.6 %load_share.1.refs_7_ = f32[4104,128]{1,0:T(8,128)S(1)} custom-call(bf16[2,64,256]{2,1,0:T(8,128)(2,1)S(1)} %factor.1.refs_0_.refs_4_, f32[8192,128]{1,0:T(8,128)} %bitcast.2), custom_call_target="tpu_custom_call" | custom-call | bytes 4194304 | tf_op jit(solution)/shard_map/load_share/pallas_call | solution.py:133
  6.9 0.1 collective-permute-start.9
  7.0 2.9 %collective-permute-start.8 = (bf16[2,64,256]{2,1,0:T(8,128)(2,1)S(1)}, bf16[2,64,256]{2,1,0:T(8,128)(2,1)S(1)}, u32[]{:S(2)}, u32[]{:S(2)}) collective-permute-start(bf16[2,64,256]{2,1,0:T(8,128)(2,1)S(1)} %factor.1.refs_0_.refs_4_), channel_id=1, source_target_pairs={{4,0},{6,2},{0,4},{2,6},{12,8},{26,10},{8,12},{10,14},{20,16},{22,... | collective-permute-start | bytes 196616 | tf_op jit(solution)/shard_map/ppermute | solution.py:101
  9.8 0.0 collective-permute-done.refs_0_
  9.9 1.5 %collective-permute-start.6 = (bf16[2,64,256]{2,1,0:T(8,128)(2,1)S(1)}, bf16[2,64,256]{2,1,0:T(8,128)(2,1)S(1)}, u32[]{:S(2)}, u32[]{:S(2)}) collective-permute-start(bf16[2,64,256]{2,1,0:T(8,128)(2,1)S(1)} %collective-permute-done.refs_0_), channel_id=1, source_target_pairs={{16,0},{26,2},{28,4},{30,6},{24,8},{18,10},{20,12},{22,14},{0,16},... | collective-permute-start | bytes 196616 | tf_op jit(solution)/shard_map/ppermute | solution.py:101
  11.3 0.7 %collective-permute-start.4 = (bf16[2,64,256]{2,1,0:T(8,128)(2,1)S(1)}, bf16[2,64,256]{2,1,0:T(8,128)(2,1)S(1)}, u32[]{:S(2)}, u32[]{:S(2)}) collective-permute-start(bf16[2,64,256]{2,1,0:T(8,128)(2,1)S(1)} %collective-permute-done.refs_0_), channel_id=1, source_target_pairs={{8,0},{18,2},{12,4},{14,6},{0,8},{26,10},{4,12},{6,14},{24,16},{2,... | collective-permute-start | bytes 196616 | tf_op jit(solution)/shard_map/ppermute | solution.py:101
  12.1 1.3 %collective-permute-start.2 = (bf16[2,64,256]{2,1,0:T(8,128)(2,1)S(1)}, bf16[2,64,256]{2,1,0:T(8,128)(2,1)S(1)}, u32[]{:S(2)}, u32[]{:S(2)}) collective-permute-start(bf16[2,64,256]{2,1,0:T(8,128)(2,1)S(1)} %collective-permute-done.refs_0_), channel_id=1, source_target_pairs={{2,0},{10,2},{20,4},{22,6},{16,8},{24,10},{28,12},{30,14},{8,16},{... | collective-permute-start | bytes 196616 | tf_op jit(solution)/shard_map/ppermute | solution.py:101
  13.3 0.0 collective-permute-done.9.refs_6_
  13.3 0.0 collective-permute-done.8.refs_5_
  13.4 0.8 %collective-permute-start.10 = (bf16[2,64,256]{2,1,0:T(8,128)(2,1)S(1)}, bf16[2,64,256]{2,1,0:T(8,128)(2,1)S(1)}, u32[]{:S(2)}, u32[]{:S(2)}) collective-permute-start(bf16[2,64,256]{2,1,0:T(8,128)(2,1)S(1)} %select_select_fusion), channel_id=1, source_target_pairs={{2,0},{0,2},{6,4},{4,6},{10,8},{8,10},{14,12},{12,14},{18,16},{16,... | collective-permute-start | bytes 196616 | tf_op jit(solution)/shard_map/ppermute | solution.py:101
  14.2 0.0 collective-permute-start.1
  14.2 0.0 collective-permute-done.6.refs_3_
  14.2 0.5 %collective-permute-start.7 = (bf16[2,64,256]{2,1,0:T(8,128)(2,1)S(1)}, bf16[2,64,256]{2,1,0:T(8,128)(2,1)S(1)}, u32[]{:S(2)}, u32[]{:S(2)}) collective-permute-start(bf16[2,64,256]{2,1,0:T(8,128)(2,1)S(1)} %collective-permute-done.6.refs_3_), channel_id=1, source_target_pairs={{1,0},{0,1},{3,2},{2,3},{5,4},{4,5},{7,6},{6,7},{9,8},{8,9},{11,10... | collective-permute-start | bytes 196616 | tf_op jit(solution)/shard_map/ppermute | solution.py:325
  14.7 0.9 %collective-permute-done.4.refs_2_ = bf16[2,64,256]{2,1,0:T(8,128)(2,1)S(1)} collective-permute-done((bf16[2,64,256]{2,1,0:T(8,128)(2,1)S(1)}, bf16[2,64,256]{2,1,0:T(8,128)(2,1)S(1)}, u32[]{:S(2)}, u32[]{:S(2)}) %collective-permute-start.4) | collective-permute-done | bytes 65568 | tf_op jit(solution)/shard_map/ppermute | solution.py:101
  15.6 0.0 collective-permute-start.5
  15.6 0.7 %collective-permute-done.2 = bf16[2,64,256]{2,1,0:T(8,128)(2,1)S(1)} collective-permute-done((bf16[2,64,256]{2,1,0:T(8,128)(2,1)S(1)}, bf16[2,64,256]{2,1,0:T(8,128)(2,1)S(1)}, u32[]{:S(2)}, u32[]{:S(2)}) %collective-permute-start.2) | collective-permute-done | bytes 65568 | tf_op jit(solution)/shard_map/ppermute | solution.py:101
  16.4 0.1 collective-permute-start.3
  16.4 0.8 %begin_update.1 = (f32[4104,128]{1,0:T(8,128)S(1)}, bf16[512,256]{1,0:T(8,128)(2,1)S(1)}, bf16[2,64,256]{2,1,0:T(8,128)(2,1)S(1)}, bf16[2,64,256]{2,1,0:T(8,128)(2,1)S(1)}) custom-call(bf16[2,64,256]{2,1,0:T(8,128)(2,1)S(1)} %collective-permute-done.refs_0_, bf16[2,64,256]{2,1,0:T(8,128)(2,1)S(1)} %broadcast_select_fusion.refs_1_, ...), custom_call_target="tpu_custom_call", output_to_operand_aliasing={{0}: (7, {})} | custom-call | tf_op jit(solution)/shard_map/begin_update/pallas_call | solution.py:213
  17.2 0.0 collective-permute-done.1.refs_0_
  17.2 0.5 %collective-permute-done.10.refs_7_ = bf16[2,64,256]{2,1,0:T(8,128)(2,1)S(1)} collective-permute-done((bf16[2,64,256]{2,1,0:T(8,128)(2,1)S(1)}, bf16[2,64,256]{2,1,0:T(8,128)(2,1)S(1)}, u32[]{:S(2)}, u32[]{:S(2)}) %collective-permute-start.10) | collective-permute-done | bytes 65568 | tf_op jit(solution)/shard_map/ppermute | solution.py:101
  17.7 0.0 collective-permute-done.7.refs_3_
  17.7 0.0 collective-permute-done.5.refs_2_
  17.7 0.0 collective-permute-done.3.refs_1_
  17.7 1.7 %end_update.1 = (f32[4096,128]{1,0:T(8,128)}, f32[4104,128]{1,0:T(8,128)S(1)}) custom-call(bf16[2,64,256]{2,1,0:T(8,128)(2,1)S(1)} %collective-permute-done.1.refs_0_, bf16[2,64,256]{2,1,0:T(8,128)(2,1)S(1)} %collective-permute-done.3.refs_1_, bf16[2,64,256]{2,1,0:T(8,128)(2,1)S(1)} %collective-permute-done.5.refs_2_, ...), custom_call_target="tpu_custom_call", output_to_operand_aliasing={{1}: (9, {})} | custom-call | tf_op jit(solution)/shard_map/end_update/pallas_call | solution.py:278
  (2 shorter events, 0.0 us)
Async XLA Ops:
  1.3 8.5 %collective-permute-start = (bf16[2,64,256]{2,1,0:T(8,128)(2,1)S(1)}, bf16[2,64,256]{2,1,0:T(8,128)(2,1)S(1)}, u32[]{:S(2)}, u32[]{:S(2)}) collective-permute-start(bf16[2,64,256]{2,1,0:T(8,128)(2,1)S(1)} %factor.1.refs_0_.refs_4_), channel_id=1, source_target_pairs={{0,24},{2,0},{4,8},{6,16},{8,26},{10,2},{12,18},{14,10},{16,28},{1... | collective-permute-start | bytes 196616 | tf_op jit(solution)/shard_map/ppermute | solution.py:305
  6.9 6.4 %collective-permute-start.9 = (bf16[2,64,256]{2,1,0:T(8,128)(2,1)S(1)}, bf16[2,64,256]{2,1,0:T(8,128)(2,1)S(1)}, u32[]{:S(2)}, u32[]{:S(2)}) collective-permute-start(bf16[2,64,256]{2,1,0:T(8,128)(2,1)S(1)} %factor.1.refs_0_.refs_4_), channel_id=1, source_target_pairs={{8,0},{0,2},{6,4},{4,6},{10,8},{2,10},{14,12},{12,14},{18,16},{16,... | collective-permute-start | bytes 196616 | tf_op jit(solution)/shard_map/ppermute | solution.py:101
  7.0 6.4 %collective-permute-start.8 = (bf16[2,64,256]{2,1,0:T(8,128)(2,1)S(1)}, bf16[2,64,256]{2,1,0:T(8,128)(2,1)S(1)}, u32[]{:S(2)}, u32[]{:S(2)}) collective-permute-start(bf16[2,64,256]{2,1,0:T(8,128)(2,1)S(1)} %factor.1.refs_0_.refs_4_), channel_id=1, source_target_pairs={{4,0},{6,2},{0,4},{2,6},{12,8},{26,10},{8,12},{10,14},{20,16},{22,... | collective-permute-start | bytes 196616 | tf_op jit(solution)/shard_map/ppermute | solution.py:101
  9.9 4.3 %collective-permute-start.6 = (bf16[2,64,256]{2,1,0:T(8,128)(2,1)S(1)}, bf16[2,64,256]{2,1,0:T(8,128)(2,1)S(1)}, u32[]{:S(2)}, u32[]{:S(2)}) collective-permute-start(bf16[2,64,256]{2,1,0:T(8,128)(2,1)S(1)} %collective-permute-done.refs_0_), channel_id=1, source_target_pairs={{16,0},{26,2},{28,4},{30,6},{24,8},{18,10},{20,12},{22,14},{0,16},... | collective-permute-start | bytes 196616 | tf_op jit(solution)/shard_map/ppermute | solution.py:101
  11.3 4.3 %collective-permute-start.4 = (bf16[2,64,256]{2,1,0:T(8,128)(2,1)S(1)}, bf16[2,64,256]{2,1,0:T(8,128)(2,1)S(1)}, u32[]{:S(2)}, u32[]{:S(2)}) collective-permute-start(bf16[2,64,256]{2,1,0:T(8,128)(2,1)S(1)} %collective-permute-done.refs_0_), channel_id=1, source_target_pairs={{8,0},{18,2},{12,4},{14,6},{0,8},{26,10},{4,12},{6,14},{24,16},{2,... | collective-permute-start | bytes 196616 | tf_op jit(solution)/shard_map/ppermute | solution.py:101
  12.1 4.3 %collective-permute-start.2 = (bf16[2,64,256]{2,1,0:T(8,128)(2,1)S(1)}, bf16[2,64,256]{2,1,0:T(8,128)(2,1)S(1)}, u32[]{:S(2)}, u32[]{:S(2)}) collective-permute-start(bf16[2,64,256]{2,1,0:T(8,128)(2,1)S(1)} %collective-permute-done.refs_0_), channel_id=1, source_target_pairs={{2,0},{10,2},{20,4},{22,6},{16,8},{24,10},{28,12},{30,14},{8,16},{... | collective-permute-start | bytes 196616 | tf_op jit(solution)/shard_map/ppermute | solution.py:101
  13.4 4.3 %collective-permute-start.10 = (bf16[2,64,256]{2,1,0:T(8,128)(2,1)S(1)}, bf16[2,64,256]{2,1,0:T(8,128)(2,1)S(1)}, u32[]{:S(2)}, u32[]{:S(2)}) collective-permute-start(bf16[2,64,256]{2,1,0:T(8,128)(2,1)S(1)} %select_select_fusion), channel_id=1, source_target_pairs={{2,0},{0,2},{6,4},{4,6},{10,8},{8,10},{14,12},{12,14},{18,16},{16,... | collective-permute-start | bytes 196616 | tf_op jit(solution)/shard_map/ppermute | solution.py:101
  14.2 3.0 %collective-permute-start.1 = (bf16[2,64,256]{2,1,0:T(8,128)(2,1)S(1)}, bf16[2,64,256]{2,1,0:T(8,128)(2,1)S(1)}, u32[]{:S(2)}, u32[]{:S(2)}) collective-permute-start(bf16[2,64,256]{2,1,0:T(8,128)(2,1)S(1)} %collective-permute-done.refs_0_), channel_id=1, source_target_pairs={{1,0},{0,1},{3,2},{2,3},{5,4},{4,5},{7,6},{6,7},{9,8},{8,9},{11,10... | collective-permute-start | bytes 196616 | tf_op jit(solution)/shard_map/ppermute | solution.py:325
  14.2 3.5 %collective-permute-start.7 = (bf16[2,64,256]{2,1,0:T(8,128)(2,1)S(1)}, bf16[2,64,256]{2,1,0:T(8,128)(2,1)S(1)}, u32[]{:S(2)}, u32[]{:S(2)}) collective-permute-start(bf16[2,64,256]{2,1,0:T(8,128)(2,1)S(1)} %collective-permute-done.6.refs_3_), channel_id=1, source_target_pairs={{1,0},{0,1},{3,2},{2,3},{5,4},{4,5},{7,6},{6,7},{9,8},{8,9},{11,10... | collective-permute-start | bytes 196616 | tf_op jit(solution)/shard_map/ppermute | solution.py:325
  15.6 2.1 %collective-permute-start.5 = (bf16[2,64,256]{2,1,0:T(8,128)(2,1)S(1)}, bf16[2,64,256]{2,1,0:T(8,128)(2,1)S(1)}, u32[]{:S(2)}, u32[]{:S(2)}) collective-permute-start(bf16[2,64,256]{2,1,0:T(8,128)(2,1)S(1)} %collective-permute-done.4.refs_2_), channel_id=1, source_target_pairs={{1,0},{0,1},{3,2},{2,3},{5,4},{4,5},{7,6},{6,7},{9,8},{8,9},{11,10... | collective-permute-start | bytes 196616 | tf_op jit(solution)/shard_map/ppermute | solution.py:325
  16.4 1.3 %collective-permute-start.3 = (bf16[2,64,256]{2,1,0:T(8,128)(2,1)S(1)}, bf16[2,64,256]{2,1,0:T(8,128)(2,1)S(1)}, u32[]{:S(2)}, u32[]{:S(2)}) collective-permute-start(bf16[2,64,256]{2,1,0:T(8,128)(2,1)S(1)} %broadcast_select_fusion.refs_1_), channel_id=1, source_target_pairs={{1,0},{0,1},{3,2},{2,3},{5,4},{4,5},{7,6},{6,7},{9,8},{8,9},{11,10... | collective-permute-start | bytes 196616 | tf_op jit(solution)/shard_map/ppermute | solution.py:325

commit v31 on v27

--- a/solution.py
+++ b/solution.py
@@ -240,16 +240,17 @@
         fill_columns(
             columns_buf.at[at], column_refs[at * pieces : (at + 1) * pieces], plane_slots(pieces), r, c, owner
         )
-    last_buf[...] = row_refs[-1][...]
-    if pieces == 4:
-
-        @pl.when(r == c)
-        def _():
-            take_rows(last_buf, own_ref, c, line_steps(pieces)[-1], pieces)
-
     stores = []
     for at_row, row_ref in enumerate((*row_refs[:-1], last_buf)):
         first_row = partner(c, line_steps(pieces)[at_row], pieces) * tile_rows
+        if at_row == pieces - 1:
+            last_buf[...] = row_refs[-1][...]
+            if pieces == 4:
+
+                @pl.when(r == c)
+                def _(step=line_steps(pieces)[-1]):
+                    take_rows(last_buf, own_ref, c, step, pieces)
+
         rows = row_ref[...]
         products = [(product_of(rows, columns_buf[at]), owner) for at, owner in enumerate(owners)]
         if at_row == pieces - 1:

time: 19.5 us -> 19.5 us (level)
  no operation moved by 1% of the time
where the time goes in v31:
time: 19.5 us; the launch traced here: 19.4 us
  starting transfers between devices  11.8 us (61%)
  Pallas kernels  5.35 us (27%)
  waiting for transfers between devices  2.14 us (11%)
    ppermute x6, starting transfers between devices, move(): lax.ppermute(x, ('row', 'col'), [(a * count + b, r * count + c) for (r, c...  7.25 us
    ppermute x1, starting transfers between devices, per_device(): lax.ppermute(factor, ('row', 'col'), [(a * count + b, slots[a][b] * count...  3.95 us
    ppermute x6, waiting for transfers between devices, move(): lax.ppermute(x, ('row', 'col'), [(a * count + b, r * count + c) for (r, c...  2.12 us
    pallas_call x1, Pallas kernels, end_update(): pl.pallas_call(body, out_shape=[jax.ShapeDtypeStruct((half * pieces * row...  1.65 us
    pallas_call x1, Pallas kernels, load_share(): pl.pallas_call(body, out_shape=jax.ShapeDtypeStruct((rows + per_row, LANE...  1.6 us
    pallas_call x1, Pallas kernels, make_factor(): pl.pallas_call(factor_kernel, out_shape=jax.ShapeDtypeStruct((half, tile_...  1.34 us
    pallas_call x1, Pallas kernels, begin_update(): pl.pallas_call(body, out_shape=[jax.ShapeDtypeStruct(share.shape, jnp.flo...  0.76 us
    ppermute x4, starting transfers between devices, per_device(): others += [lax.ppermute(piece, 'layer', pairs) for piece in plane]  0.58 us
  transfers between devices with their start and end apart: 11, of which 3 were waited for; matrix products, arithmetic and copies ran while one was open for 0% of the time, Pallas kernels for 12%

profile of v31, /device:TPU:0, one launch (start us, length us, event | category | flops | bytes accessed | tf_op | source)
XLA Modules:
  0.0 19.4 jit_solution(10260855440723484269)
XLA Ops:
  0.0 1.3 %factor.1.refs_0_.refs_4_ = bf16[2,64,256]{2,1,0:T(8,128)(2,1)S(1)} custom-call(f32[4,1,64,256]{3,2,1,0:T(8,128)} %panel_ref.1, f32[256,256]{1,0:T(8,128)} %inverse_ref.1), custom_call_target="tpu_custom_call" | custom-call | tf_op jit(solution)/shard_map/factor/pallas_call | solution.py:55
  1.4 3.9 %collective-permute-start = (bf16[2,64,256]{2,1,0:T(8,128)(2,1)S(1)}, bf16[2,64,256]{2,1,0:T(8,128)(2,1)S(1)}, u32[]{:S(2)}, u32[]{:S(2)}) collective-permute-start(bf16[2,64,256]{2,1,0:T(8,128)(2,1)S(1)} %factor.1.refs_0_.refs_4_), channel_id=1, source_target_pairs={{0,24},{2,0},{4,8},{6,16},{8,26},{10,2},{12,18},{14,10},{16,28},{1... | collective-permute-start | bytes 196616 | tf_op jit(solution)/shard_map/ppermute | solution.py:308
  5.3 1.6 %load_share.1.refs_7_ = f32[4104,128]{1,0:T(8,128)S(1)} custom-call(bf16[2,64,256]{2,1,0:T(8,128)(2,1)S(1)} %factor.1.refs_0_.refs_4_, f32[8192,128]{1,0:T(8,128)} %bitcast.2), custom_call_target="tpu_custom_call" | custom-call | bytes 4194304 | tf_op jit(solution)/shard_map/load_share/pallas_call | solution.py:135
  6.9 0.1 collective-permute-start.9
  7.0 2.9 %collective-permute-start.8 = (bf16[2,64,256]{2,1,0:T(8,128)(2,1)S(1)}, bf16[2,64,256]{2,1,0:T(8,128)(2,1)S(1)}, u32[]{:S(2)}, u32[]{:S(2)}) collective-permute-start(bf16[2,64,256]{2,1,0:T(8,128)(2,1)S(1)} %factor.1.refs_0_.refs_4_), channel_id=1, source_target_pairs={{4,0},{6,2},{0,4},{2,6},{12,8},{26,10},{8,12},{10,14},{20,16},{22,... | collective-permute-start | bytes 196616 | tf_op jit(solution)/shard_map/ppermute | solution.py:103
  9.8 0.0 collective-permute-done.refs_0_
  9.9 1.5 %collective-permute-start.6 = (bf16[2,64,256]{2,1,0:T(8,128)(2,1)S(1)}, bf16[2,64,256]{2,1,0:T(8,128)(2,1)S(1)}, u32[]{:S(2)}, u32[]{:S(2)}) collective-permute-start(bf16[2,64,256]{2,1,0:T(8,128)(2,1)S(1)} %collective-permute-done.refs_0_), channel_id=1, source_target_pairs={{16,0},{26,2},{28,4},{30,6},{24,8},{18,10},{20,12},{22,14},{0,16},... | collective-permute-start | bytes 196616 | tf_op jit(solution)/shard_map/ppermute | solution.py:103
  11.3 0.7 %collective-permute-start.4 = (bf16[2,64,256]{2,1,0:T(8,128)(2,1)S(1)}, bf16[2,64,256]{2,1,0:T(8,128)(2,1)S(1)}, u32[]{:S(2)}, u32[]{:S(2)}) collective-permute-start(bf16[2,64,256]{2,1,0:T(8,128)(2,1)S(1)} %collective-permute-done.refs_0_), channel_id=1, source_target_pairs={{8,0},{18,2},{12,4},{14,6},{0,8},{26,10},{4,12},{6,14},{24,16},{2,... | collective-permute-start | bytes 196616 | tf_op jit(solution)/shard_map/ppermute | solution.py:103
  12.1 1.3 %collective-permute-start.2 = (bf16[2,64,256]{2,1,0:T(8,128)(2,1)S(1)}, bf16[2,64,256]{2,1,0:T(8,128)(2,1)S(1)}, u32[]{:S(2)}, u32[]{:S(2)}) collective-permute-start(bf16[2,64,256]{2,1,0:T(8,128)(2,1)S(1)} %collective-permute-done.refs_0_), channel_id=1, source_target_pairs={{2,0},{10,2},{20,4},{22,6},{16,8},{24,10},{28,12},{30,14},{8,16},{... | collective-permute-start | bytes 196616 | tf_op jit(solution)/shard_map/ppermute | solution.py:103
  13.3 0.0 collective-permute-done.9.refs_6_
  13.3 0.0 collective-permute-done.8.refs_5_
  13.4 0.8 %collective-permute-start.10 = (bf16[2,64,256]{2,1,0:T(8,128)(2,1)S(1)}, bf16[2,64,256]{2,1,0:T(8,128)(2,1)S(1)}, u32[]{:S(2)}, u32[]{:S(2)}) collective-permute-start(bf16[2,64,256]{2,1,0:T(8,128)(2,1)S(1)} %select_select_fusion), channel_id=1, source_target_pairs={{2,0},{0,2},{6,4},{4,6},{10,8},{8,10},{14,12},{12,14},{18,16},{16,... | collective-permute-start | bytes 196616 | tf_op jit(solution)/shard_map/ppermute | solution.py:103
  14.2 0.0 collective-permute-start.1
  14.2 0.0 collective-permute-done.6.refs_3_
  14.2 0.5 %collective-permute-start.7 = (bf16[2,64,256]{2,1,0:T(8,128)(2,1)S(1)}, bf16[2,64,256]{2,1,0:T(8,128)(2,1)S(1)}, u32[]{:S(2)}, u32[]{:S(2)}) collective-permute-start(bf16[2,64,256]{2,1,0:T(8,128)(2,1)S(1)} %collective-permute-done.6.refs_3_), channel_id=1, source_target_pairs={{1,0},{0,1},{3,2},{2,3},{5,4},{4,5},{7,6},{6,7},{9,8},{8,9},{11,10... | collective-permute-start | bytes 196616 | tf_op jit(solution)/shard_map/ppermute | solution.py:328
  14.7 0.9 %collective-permute-done.4.refs_2_ = bf16[2,64,256]{2,1,0:T(8,128)(2,1)S(1)} collective-permute-done((bf16[2,64,256]{2,1,0:T(8,128)(2,1)S(1)}, bf16[2,64,256]{2,1,0:T(8,128)(2,1)S(1)}, u32[]{:S(2)}, u32[]{:S(2)}) %collective-permute-start.4) | collective-permute-done | bytes 65568 | tf_op jit(solution)/shard_map/ppermute | solution.py:103
  15.6 0.0 collective-permute-start.5
  15.6 0.7 %collective-permute-done.2 = bf16[2,64,256]{2,1,0:T(8,128)(2,1)S(1)} collective-permute-done((bf16[2,64,256]{2,1,0:T(8,128)(2,1)S(1)}, bf16[2,64,256]{2,1,0:T(8,128)(2,1)S(1)}, u32[]{:S(2)}, u32[]{:S(2)}) %collective-permute-start.2) | collective-permute-done | bytes 65568 | tf_op jit(solution)/shard_map/ppermute | solution.py:103
  16.4 0.1 collective-permute-start.3
  16.4 0.8 %begin_update.1 = (f32[4104,128]{1,0:T(8,128)S(1)}, bf16[512,256]{1,0:T(8,128)(2,1)S(1)}, bf16[2,64,256]{2,1,0:T(8,128)(2,1)S(1)}, bf16[2,64,256]{2,1,0:T(8,128)(2,1)S(1)}) custom-call(bf16[2,64,256]{2,1,0:T(8,128)(2,1)S(1)} %collective-permute-done.refs_0_, bf16[2,64,256]{2,1,0:T(8,128)(2,1)S(1)} %broadcast_select_fusion.refs_1_, ...), custom_call_target="tpu_custom_call", output_to_operand_aliasing={{0}: (7, {})} | custom-call | tf_op jit(solution)/shard_map/begin_update/pallas_call | solution.py:215
  17.2 0.0 collective-permute-done.1.refs_0_
  17.2 0.5 %collective-permute-done.10.refs_7_ = bf16[2,64,256]{2,1,0:T(8,128)(2,1)S(1)} collective-permute-done((bf16[2,64,256]{2,1,0:T(8,128)(2,1)S(1)}, bf16[2,64,256]{2,1,0:T(8,128)(2,1)S(1)}, u32[]{:S(2)}, u32[]{:S(2)}) %collective-permute-start.10) | collective-permute-done | bytes 65568 | tf_op jit(solution)/shard_map/ppermute | solution.py:103
  17.7 0.0 collective-permute-done.7.refs_3_
  17.7 0.0 collective-permute-done.5.refs_2_
  17.7 0.0 collective-permute-done.3.refs_1_
  17.7 1.7 %end_update.1 = (f32[4096,128]{1,0:T(8,128)}, f32[4104,128]{1,0:T(8,128)S(1)}) custom-call(bf16[2,64,256]{2,1,0:T(8,128)(2,1)S(1)} %collective-permute-done.1.refs_0_, bf16[2,64,256]{2,1,0:T(8,128)(2,1)S(1)} %collective-permute-done.3.refs_1_, bf16[2,64,256]{2,1,0:T(8,128)(2,1)S(1)} %collective-permute-done.5.refs_2_, ...), custom_call_target="tpu_custom_call", output_to_operand_aliasing={{1}: (9, {})} | custom-call | tf_op jit(solution)/shard_map/end_update/pallas_call | solution.py:281
  (2 shorter events, 0.0 us)
Async XLA Ops:
  1.4 8.5 %collective-permute-start = (bf16[2,64,256]{2,1,0:T(8,128)(2,1)S(1)}, bf16[2,64,256]{2,1,0:T(8,128)(2,1)S(1)}, u32[]{:S(2)}, u32[]{:S(2)}) collective-permute-start(bf16[2,64,256]{2,1,0:T(8,128)(2,1)S(1)} %factor.1.refs_0_.refs_4_), channel_id=1, source_target_pairs={{0,24},{2,0},{4,8},{6,16},{8,26},{10,2},{12,18},{14,10},{16,28},{1... | collective-permute-start | bytes 196616 | tf_op jit(solution)/shard_map/ppermute | solution.py:308
  6.9 6.4 %collective-permute-start.9 = (bf16[2,64,256]{2,1,0:T(8,128)(2,1)S(1)}, bf16[2,64,256]{2,1,0:T(8,128)(2,1)S(1)}, u32[]{:S(2)}, u32[]{:S(2)}) collective-permute-start(bf16[2,64,256]{2,1,0:T(8,128)(2,1)S(1)} %factor.1.refs_0_.refs_4_), channel_id=1, source_target_pairs={{8,0},{0,2},{6,4},{4,6},{10,8},{2,10},{14,12},{12,14},{18,16},{16,... | collective-permute-start | bytes 196616 | tf_op jit(solution)/shard_map/ppermute | solution.py:103
  7.0 6.4 %collective-permute-start.8 = (bf16[2,64,256]{2,1,0:T(8,128)(2,1)S(1)}, bf16[2,64,256]{2,1,0:T(8,128)(2,1)S(1)}, u32[]{:S(2)}, u32[]{:S(2)}) collective-permute-start(bf16[2,64,256]{2,1,0:T(8,128)(2,1)S(1)} %factor.1.refs_0_.refs_4_), channel_id=1, source_target_pairs={{4,0},{6,2},{0,4},{2,6},{12,8},{26,10},{8,12},{10,14},{20,16},{22,... | collective-permute-start | bytes 196616 | tf_op jit(solution)/shard_map/ppermute | solution.py:103
  9.9 4.3 %collective-permute-start.6 = (bf16[2,64,256]{2,1,0:T(8,128)(2,1)S(1)}, bf16[2,64,256]{2,1,0:T(8,128)(2,1)S(1)}, u32[]{:S(2)}, u32[]{:S(2)}) collective-permute-start(bf16[2,64,256]{2,1,0:T(8,128)(2,1)S(1)} %collective-permute-done.refs_0_), channel_id=1, source_target_pairs={{16,0},{26,2},{28,4},{30,6},{24,8},{18,10},{20,12},{22,14},{0,16},... | collective-permute-start | bytes 196616 | tf_op jit(solution)/shard_map/ppermute | solution.py:103
  11.3 4.3 %collective-permute-start.4 = (bf16[2,64,256]{2,1,0:T(8,128)(2,1)S(1)}, bf16[2,64,256]{2,1,0:T(8,128)(2,1)S(1)}, u32[]{:S(2)}, u32[]{:S(2)}) collective-permute-start(bf16[2,64,256]{2,1,0:T(8,128)(2,1)S(1)} %collective-permute-done.refs_0_), channel_id=1, source_target_pairs={{8,0},{18,2},{12,4},{14,6},{0,8},{26,10},{4,12},{6,14},{24,16},{2,... | collective-permute-start | bytes 196616 | tf_op jit(solution)/shard_map/ppermute | solution.py:103
  12.1 4.3 %collective-permute-start.2 = (bf16[2,64,256]{2,1,0:T(8,128)(2,1)S(1)}, bf16[2,64,256]{2,1,0:T(8,128)(2,1)S(1)}, u32[]{:S(2)}, u32[]{:S(2)}) collective-permute-start(bf16[2,64,256]{2,1,0:T(8,128)(2,1)S(1)} %collective-permute-done.refs_0_), channel_id=1, source_target_pairs={{2,0},{10,2},{20,4},{22,6},{16,8},{24,10},{28,12},{30,14},{8,16},{... | collective-permute-start | bytes 196616 | tf_op jit(solution)/shard_map/ppermute | solution.py:103
  13.4 4.3 %collective-permute-start.10 = (bf16[2,64,256]{2,1,0:T(8,128)(2,1)S(1)}, bf16[2,64,256]{2,1,0:T(8,128)(2,1)S(1)}, u32[]{:S(2)}, u32[]{:S(2)}) collective-permute-start(bf16[2,64,256]{2,1,0:T(8,128)(2,1)S(1)} %select_select_fusion), channel_id=1, source_target_pairs={{2,0},{0,2},{6,4},{4,6},{10,8},{8,10},{14,12},{12,14},{18,16},{16,... | collective-permute-start | bytes 196616 | tf_op jit(solution)/shard_map/ppermute | solution.py:103
  14.2 3.0 %collective-permute-start.1 = (bf16[2,64,256]{2,1,0:T(8,128)(2,1)S(1)}, bf16[2,64,256]{2,1,0:T(8,128)(2,1)S(1)}, u32[]{:S(2)}, u32[]{:S(2)}) collective-permute-start(bf16[2,64,256]{2,1,0:T(8,128)(2,1)S(1)} %collective-permute-done.refs_0_), channel_id=1, source_target_pairs={{1,0},{0,1},{3,2},{2,3},{5,4},{4,5},{7,6},{6,7},{9,8},{8,9},{11,10... | collective-permute-start | bytes 196616 | tf_op jit(solution)/shard_map/ppermute | solution.py:328
  14.2 3.5 %collective-permute-start.7 = (bf16[2,64,256]{2,1,0:T(8,128)(2,1)S(1)}, bf16[2,64,256]{2,1,0:T(8,128)(2,1)S(1)}, u32[]{:S(2)}, u32[]{:S(2)}) collective-permute-start(bf16[2,64,256]{2,1,0:T(8,128)(2,1)S(1)} %collective-permute-done.6.refs_3_), channel_id=1, source_target_pairs={{1,0},{0,1},{3,2},{2,3},{5,4},{4,5},{7,6},{6,7},{9,8},{8,9},{11,10... | collective-permute-start | bytes 196616 | tf_op jit(solution)/shard_map/ppermute | solution.py:328
  15.6 2.1 %collective-permute-start.5 = (bf16[2,64,256]{2,1,0:T(8,128)(2,1)S(1)}, bf16[2,64,256]{2,1,0:T(8,128)(2,1)S(1)}, u32[]{:S(2)}, u32[]{:S(2)}) collective-permute-start(bf16[2,64,256]{2,1,0:T(8,128)(2,1)S(1)} %collective-permute-done.4.refs_2_), channel_id=1, source_target_pairs={{1,0},{0,1},{3,2},{2,3},{5,4},{4,5},{7,6},{6,7},{9,8},{8,9},{11,10... | collective-permute-start | bytes 196616 | tf_op jit(solution)/shard_map/ppermute | solution.py:328
  16.4 1.4 %collective-permute-start.3 = (bf16[2,64,256]{2,1,0:T(8,128)(2,1)S(1)}, bf16[2,64,256]{2,1,0:T(8,128)(2,1)S(1)}, u32[]{:S(2)}, u32[]{:S(2)}) collective-permute-start(bf16[2,64,256]{2,1,0:T(8,128)(2,1)S(1)} %broadcast_select_fusion.refs_1_), channel_id=1, source_target_pairs={{1,0},{0,1},{3,2},{2,3},{5,4},{4,5},{7,6},{6,7},{9,8},{8,9},{11,10... | collective-permute-start | bytes 196616 | tf_op jit(solution)/shard_map/ppermute | solution.py:328

commit v32 on v29

--- a/solution.py
+++ b/solution.py
@@ -73,7 +73,7 @@
 
 def plane_slots(count):
     if count == 4:
-        return ((3, 0, 1, 2), (3, 0, 2, 1), (3, 2, 1, 0), (2, 3, 1, 0))
+        return ((3, 0, 2, 1), (3, 0, 2, 1), (3, 2, 1, 0), (2, 3, 1, 0))
     return tuple(tuple(count - 1 - b for b in range(count)) for _ in range(count))
 
 

time: 19.5 us -> 19.5 us (level)
  starting transfers between devices: 11.6 us -> 11.4 us
    ppermute x4, starting transfers between devices: 0.42 us -> 0.19 us  [per_device(): others += [lax.ppermute(piece, 'layer', pairs) for piece in plane]]
where the time goes in v32:
time: 19.5 us; the launch traced here: 19.3 us
  starting transfers between devices  11.4 us (58%)
  Pallas kernels  5.36 us (27%)
  waiting for transfers between devices  2.51 us (13%)
    ppermute x6, starting transfers between devices, move(): lax.ppermute(x, ('row', 'col'), [(a * count + b, r * count + c) for (r, c...  7.25 us
    ppermute x1, starting transfers between devices, per_device(): lax.ppermute(factor, ('row', 'col'), [(a * count + b, slots[a][b] * count...  3.95 us
    ppermute x6, waiting for transfers between devices, move(): lax.ppermute(x, ('row', 'col'), [(a * count + b, r * count + c) for (r, c...  2.5 us
    pallas_call x1, Pallas kernels, end_update(): pl.pallas_call(body, out_shape=[jax.ShapeDtypeStruct((half * pieces * row...  1.66 us
    pallas_call x1, Pallas kernels, load_share(): pl.pallas_call(body, out_shape=jax.ShapeDtypeStruct((rows + per_row, LANE...  1.6 us
    pallas_call x1, Pallas kernels, make_factor(): pl.pallas_call(factor_kernel, out_shape=jax.ShapeDtypeStruct((half, tile_...  1.34 us
    pallas_call x1, Pallas kernels, begin_update(): pl.pallas_call(body, out_shape=[jax.ShapeDtypeStruct(share.shape, jnp.flo...  0.76 us
  transfers between devices with their start and end apart: 11, of which 4 were waited for; matrix products, arithmetic and copies ran while one was open for 0% of the time, Pallas kernels for 12%

profile of v32, /device:TPU:0, one launch (start us, length us, event | category | flops | bytes accessed | tf_op | source)
XLA Modules:
  0.0 19.3 jit_solution(6455958552985995535)
XLA Ops:
  0.0 1.3 %factor.1.refs_0_.refs_4_ = bf16[2,64,256]{2,1,0:T(8,128)(2,1)S(1)} custom-call(f32[4,1,64,256]{3,2,1,0:T(8,128)} %panel_ref.1, f32[256,256]{1,0:T(8,128)} %inverse_ref.1), custom_call_target="tpu_custom_call" | custom-call | tf_op jit(solution)/shard_map/factor/pallas_call | solution.py:55
  1.4 3.9 %collective-permute-start = (bf16[2,64,256]{2,1,0:T(8,128)(2,1)S(1)}, bf16[2,64,256]{2,1,0:T(8,128)(2,1)S(1)}, u32[]{:S(2)}, u32[]{:S(2)}) collective-permute-start(bf16[2,64,256]{2,1,0:T(8,128)(2,1)S(1)} %factor.1.refs_0_.refs_4_), channel_id=1, source_target_pairs={{0,24},{2,0},{4,16},{6,8},{8,26},{10,2},{12,18},{14,10},{16,28},{1... | collective-permute-start | bytes 196616 | tf_op jit(solution)/shard_map/ppermute | solution.py:307
  5.3 1.6 %load_share.1.refs_7_ = f32[4104,128]{1,0:T(8,128)S(1)} custom-call(bf16[2,64,256]{2,1,0:T(8,128)(2,1)S(1)} %factor.1.refs_0_.refs_4_, f32[8192,128]{1,0:T(8,128)} %bitcast.2), custom_call_target="tpu_custom_call" | custom-call | bytes 4194304 | tf_op jit(solution)/shard_map/load_share/pallas_call | solution.py:135
  6.9 0.1 collective-permute-start.9
  7.0 2.9 %collective-permute-start.8 = (bf16[2,64,256]{2,1,0:T(8,128)(2,1)S(1)}, bf16[2,64,256]{2,1,0:T(8,128)(2,1)S(1)}, u32[]{:S(2)}, u32[]{:S(2)}) collective-permute-start(bf16[2,64,256]{2,1,0:T(8,128)(2,1)S(1)} %factor.1.refs_0_.refs_4_), channel_id=1, source_target_pairs={{4,0},{6,2},{0,4},{2,6},{12,8},{26,10},{8,12},{10,14},{20,16},{22,... | collective-permute-start | bytes 196616 | tf_op jit(solution)/shard_map/ppermute | solution.py:103
  9.8 0.0 collective-permute-done.refs_0_
  9.8 1.5 %collective-permute-start.6 = (bf16[2,64,256]{2,1,0:T(8,128)(2,1)S(1)}, bf16[2,64,256]{2,1,0:T(8,128)(2,1)S(1)}, u32[]{:S(2)}, u32[]{:S(2)}) collective-permute-start(bf16[2,64,256]{2,1,0:T(8,128)(2,1)S(1)} %collective-permute-done.refs_0_), channel_id=1, source_target_pairs={{8,0},{26,2},{28,4},{30,6},{0,8},{18,10},{20,12},{22,14},{24,16},{... | collective-permute-start | bytes 196616 | tf_op jit(solution)/shard_map/ppermute | solution.py:103
  11.3 0.8 %collective-permute-start.4 = (bf16[2,64,256]{2,1,0:T(8,128)(2,1)S(1)}, bf16[2,64,256]{2,1,0:T(8,128)(2,1)S(1)}, u32[]{:S(2)}, u32[]{:S(2)}) collective-permute-start(bf16[2,64,256]{2,1,0:T(8,128)(2,1)S(1)} %collective-permute-done.refs_0_), channel_id=1, source_target_pairs={{16,0},{18,2},{12,4},{14,6},{24,8},{26,10},{4,12},{6,14},{0,16},{2... | collective-permute-start | bytes 196616 | tf_op jit(solution)/shard_map/ppermute | solution.py:103
  12.1 1.2 %collective-permute-start.2 = (bf16[2,64,256]{2,1,0:T(8,128)(2,1)S(1)}, bf16[2,64,256]{2,1,0:T(8,128)(2,1)S(1)}, u32[]{:S(2)}, u32[]{:S(2)}) collective-permute-start(bf16[2,64,256]{2,1,0:T(8,128)(2,1)S(1)} %collective-permute-done.refs_0_), channel_id=1, source_target_pairs={{2,0},{10,2},{20,4},{22,6},{16,8},{24,10},{28,12},{30,14},{8,16},{... | collective-permute-start | bytes 196616 | tf_op jit(solution)/shard_map/ppermute | solution.py:103
  13.3 0.0 collective-permute-done.9.refs_6_
  13.3 0.0 collective-permute-done.8.refs_5_
  13.3 0.9 %collective-permute-start.10 = (bf16[2,64,256]{2,1,0:T(8,128)(2,1)S(1)}, bf16[2,64,256]{2,1,0:T(8,128)(2,1)S(1)}, u32[]{:S(2)}, u32[]{:S(2)}) collective-permute-start(bf16[2,64,256]{2,1,0:T(8,128)(2,1)S(1)} %select_select_fusion), channel_id=1, source_target_pairs={{2,0},{0,2},{6,4},{4,6},{10,8},{8,10},{14,12},{12,14},{18,16},{16,... | collective-permute-start | bytes 196616 | tf_op jit(solution)/shard_map/ppermute | solution.py:103
  14.2 0.0 collective-permute-start.1
  14.2 0.4 %collective-permute-done.6.refs_3_ = bf16[2,64,256]{2,1,0:T(8,128)(2,1)S(1)} collective-permute-done((bf16[2,64,256]{2,1,0:T(8,128)(2,1)S(1)}, bf16[2,64,256]{2,1,0:T(8,128)(2,1)S(1)}, u32[]{:S(2)}, u32[]{:S(2)}) %collective-permute-start.6) | collective-permute-done | bytes 65568 | tf_op jit(solution)/shard_map/ppermute | solution.py:103
  14.6 0.1 collective-permute-start.7
  14.7 0.9 %collective-permute-done.4.refs_2_ = bf16[2,64,256]{2,1,0:T(8,128)(2,1)S(1)} collective-permute-done((bf16[2,64,256]{2,1,0:T(8,128)(2,1)S(1)}, bf16[2,64,256]{2,1,0:T(8,128)(2,1)S(1)}, u32[]{:S(2)}, u32[]{:S(2)}) %collective-permute-start.4) | collective-permute-done | bytes 65568 | tf_op jit(solution)/shard_map/ppermute | solution.py:103
  15.6 0.0 collective-permute-start.5
  15.6 0.8 %collective-permute-done.2 = bf16[2,64,256]{2,1,0:T(8,128)(2,1)S(1)} collective-permute-done((bf16[2,64,256]{2,1,0:T(8,128)(2,1)S(1)}, bf16[2,64,256]{2,1,0:T(8,128)(2,1)S(1)}, u32[]{:S(2)}, u32[]{:S(2)}) %collective-permute-start.2) | collective-permute-done | bytes 65568 | tf_op jit(solution)/shard_map/ppermute | solution.py:103
  16.4 0.1 collective-permute-start.3
  16.4 0.8 %begin_update.1 = (f32[4104,128]{1,0:T(8,128)S(1)}, bf16[512,256]{1,0:T(8,128)(2,1)S(1)}, bf16[2,64,256]{2,1,0:T(8,128)(2,1)S(1)}, bf16[2,64,256]{2,1,0:T(8,128)(2,1)S(1)}) custom-call(bf16[2,64,256]{2,1,0:T(8,128)(2,1)S(1)} %collective-permute-done.refs_0_, bf16[2,64,256]{2,1,0:T(8,128)(2,1)S(1)} %broadcast_select_fusion.refs_1_, ...), custom_call_target="tpu_custom_call", output_to_operand_aliasing={{0}: (7, {})} | custom-call | tf_op jit(solution)/shard_map/begin_update/pallas_call | solution.py:215
  17.2 0.0 collective-permute-done.1.refs_0_
  17.2 0.5 %collective-permute-done.10.refs_7_ = bf16[2,64,256]{2,1,0:T(8,128)(2,1)S(1)} collective-permute-done((bf16[2,64,256]{2,1,0:T(8,128)(2,1)S(1)}, bf16[2,64,256]{2,1,0:T(8,128)(2,1)S(1)}, u32[]{:S(2)}, u32[]{:S(2)}) %collective-permute-start.10) | collective-permute-done | bytes 65568 | tf_op jit(solution)/shard_map/ppermute | solution.py:103
  17.7 0.0 collective-permute-done.7.refs_3_
  17.7 0.0 collective-permute-done.5.refs_2_
  17.7 0.0 collective-permute-done.3.refs_1_
  17.7 1.7 %end_update.1 = (f32[4096,128]{1,0:T(8,128)}, f32[4104,128]{1,0:T(8,128)S(1)}) custom-call(bf16[2,64,256]{2,1,0:T(8,128)(2,1)S(1)} %collective-permute-done.1.refs_0_, bf16[2,64,256]{2,1,0:T(8,128)(2,1)S(1)} %collective-permute-done.3.refs_1_, bf16[2,64,256]{2,1,0:T(8,128)(2,1)S(1)} %collective-permute-done.5.refs_2_, ...), custom_call_target="tpu_custom_call", output_to_operand_aliasing={{1}: (9, {})} | custom-call | tf_op jit(solution)/shard_map/end_update/pallas_call | solution.py:280
  (2 shorter events, 0.0 us)
Async XLA Ops:
  1.4 8.5 %collective-permute-start = (bf16[2,64,256]{2,1,0:T(8,128)(2,1)S(1)}, bf16[2,64,256]{2,1,0:T(8,128)(2,1)S(1)}, u32[]{:S(2)}, u32[]{:S(2)}) collective-permute-start(bf16[2,64,256]{2,1,0:T(8,128)(2,1)S(1)} %factor.1.refs_0_.refs_4_), channel_id=1, source_target_pairs={{0,24},{2,0},{4,16},{6,8},{8,26},{10,2},{12,18},{14,10},{16,28},{1... | collective-permute-start | bytes 196616 | tf_op jit(solution)/shard_map/ppermute | solution.py:307
  6.9 6.4 %collective-permute-start.9 = (bf16[2,64,256]{2,1,0:T(8,128)(2,1)S(1)}, bf16[2,64,256]{2,1,0:T(8,128)(2,1)S(1)}, u32[]{:S(2)}, u32[]{:S(2)}) collective-permute-start(bf16[2,64,256]{2,1,0:T(8,128)(2,1)S(1)} %factor.1.refs_0_.refs_4_), channel_id=1, source_target_pairs={{8,0},{0,2},{6,4},{4,6},{10,8},{2,10},{14,12},{12,14},{18,16},{16,... | collective-permute-start | bytes 196616 | tf_op jit(solution)/shard_map/ppermute | solution.py:103
  7.0 6.4 %collective-permute-start.8 = (bf16[2,64,256]{2,1,0:T(8,128)(2,1)S(1)}, bf16[2,64,256]{2,1,0:T(8,128)(2,1)S(1)}, u32[]{:S(2)}, u32[]{:S(2)}) collective-permute-start(bf16[2,64,256]{2,1,0:T(8,128)(2,1)S(1)} %factor.1.refs_0_.refs_4_), channel_id=1, source_target_pairs={{4,0},{6,2},{0,4},{2,6},{12,8},{26,10},{8,12},{10,14},{20,16},{22,... | collective-permute-start | bytes 196616 | tf_op jit(solution)/shard_map/ppermute | solution.py:103
  9.8 4.8 %collective-permute-start.6 = (bf16[2,64,256]{2,1,0:T(8,128)(2,1)S(1)}, bf16[2,64,256]{2,1,0:T(8,128)(2,1)S(1)}, u32[]{:S(2)}, u32[]{:S(2)}) collective-permute-start(bf16[2,64,256]{2,1,0:T(8,128)(2,1)S(1)} %collective-permute-done.refs_0_), channel_id=1, source_target_pairs={{8,0},{26,2},{28,4},{30,6},{0,8},{18,10},{20,12},{22,14},{24,16},{... | collective-permute-start | bytes 196616 | tf_op jit(solution)/shard_map/ppermute | solution.py:103
  11.3 4.3 %collective-permute-start.4 = (bf16[2,64,256]{2,1,0:T(8,128)(2,1)S(1)}, bf16[2,64,256]{2,1,0:T(8,128)(2,1)S(1)}, u32[]{:S(2)}, u32[]{:S(2)}) collective-permute-start(bf16[2,64,256]{2,1,0:T(8,128)(2,1)S(1)} %collective-permute-done.refs_0_), channel_id=1, source_target_pairs={{16,0},{18,2},{12,4},{14,6},{24,8},{26,10},{4,12},{6,14},{0,16},{2... | collective-permute-start | bytes 196616 | tf_op jit(solution)/shard_map/ppermute | solution.py:103
  12.1 4.3 %collective-permute-start.2 = (bf16[2,64,256]{2,1,0:T(8,128)(2,1)S(1)}, bf16[2,64,256]{2,1,0:T(8,128)(2,1)S(1)}, u32[]{:S(2)}, u32[]{:S(2)}) collective-permute-start(bf16[2,64,256]{2,1,0:T(8,128)(2,1)S(1)} %collective-permute-done.refs_0_), channel_id=1, source_target_pairs={{2,0},{10,2},{20,4},{22,6},{16,8},{24,10},{28,12},{30,14},{8,16},{... | collective-permute-start | bytes 196616 | tf_op jit(solution)/shard_map/ppermute | solution.py:103
  13.3 4.3 %collective-permute-start.10 = (bf16[2,64,256]{2,1,0:T(8,128)(2,1)S(1)}, bf16[2,64,256]{2,1,0:T(8,128)(2,1)S(1)}, u32[]{:S(2)}, u32[]{:S(2)}) collective-permute-start(bf16[2,64,256]{2,1,0:T(8,128)(2,1)S(1)} %select_select_fusion), channel_id=1, source_target_pairs={{2,0},{0,2},{6,4},{4,6},{10,8},{8,10},{14,12},{12,14},{18,16},{16,... | collective-permute-start | bytes 196616 | tf_op jit(solution)/shard_map/ppermute | solution.py:103
  14.2 3.0 %collective-permute-start.1 = (bf16[2,64,256]{2,1,0:T(8,128)(2,1)S(1)}, bf16[2,64,256]{2,1,0:T(8,128)(2,1)S(1)}, u32[]{:S(2)}, u32[]{:S(2)}) collective-permute-start(bf16[2,64,256]{2,1,0:T(8,128)(2,1)S(1)} %collective-permute-done.refs_0_), channel_id=1, source_target_pairs={{1,0},{0,1},{3,2},{2,3},{5,4},{4,5},{7,6},{6,7},{9,8},{8,9},{11,10... | collective-permute-start | bytes 196616 | tf_op jit(solution)/shard_map/ppermute | solution.py:327
  14.6 3.1 %collective-permute-start.7 = (bf16[2,64,256]{2,1,0:T(8,128)(2,1)S(1)}, bf16[2,64,256]{2,1,0:T(8,128)(2,1)S(1)}, u32[]{:S(2)}, u32[]{:S(2)}) collective-permute-start(bf16[2,64,256]{2,1,0:T(8,128)(2,1)S(1)} %collective-permute-done.6.refs_3_), channel_id=1, source_target_pairs={{1,0},{0,1},{3,2},{2,3},{5,4},{4,5},{7,6},{6,7},{9,8},{8,9},{11,10... | collective-permute-start | bytes 196616 | tf_op jit(solution)/shard_map/ppermute | solution.py:327
  15.6 2.1 %collective-permute-start.5 = (bf16[2,64,256]{2,1,0:T(8,128)(2,1)S(1)}, bf16[2,64,256]{2,1,0:T(8,128)(2,1)S(1)}, u32[]{:S(2)}, u32[]{:S(2)}) collective-permute-start(bf16[2,64,256]{2,1,0:T(8,128)(2,1)S(1)} %collective-permute-done.4.refs_2_), channel_id=1, source_target_pairs={{1,0},{0,1},{3,2},{2,3},{5,4},{4,5},{7,6},{6,7},{9,8},{8,9},{11,10... | collective-permute-start | bytes 196616 | tf_op jit(solution)/shard_map/ppermute | solution.py:327
  16.4 1.3 %collective-permute-start.3 = (bf16[2,64,256]{2,1,0:T(8,128)(2,1)S(1)}, bf16[2,64,256]{2,1,0:T(8,128)(2,1)S(1)}, u32[]{:S(2)}, u32[]{:S(2)}) collective-permute-start(bf16[2,64,256]{2,1,0:T(8,128)(2,1)S(1)} %broadcast_select_fusion.refs_1_), channel_id=1, source_target_pairs={{1,0},{0,1},{3,2},{2,3},{5,4},{4,5},{7,6},{6,7},{9,8},{8,9},{11,10... | collective-permute-start | bytes 196616 | tf_op jit(solution)/shard_map/ppermute | solution.py:327

commit v33 on v32

--- a/solution.py
+++ b/solution.py
@@ -73,7 +73,7 @@
 
 def plane_slots(count):
     if count == 4:
-        return ((3, 0, 2, 1), (3, 0, 2, 1), (3, 2, 1, 0), (2, 3, 1, 0))
+        return ((3, 0, 2, 1), (2, 0, 3, 1), (3, 2, 1, 0), (2, 3, 1, 0))
     return tuple(tuple(count - 1 - b for b in range(count)) for _ in range(count))
 
 

time: 19.5 us -> 19.7 us (1.010); the launches traced: 19.3 us -> 19.3 us
  no operation moved by 1% of the time
where the time goes in v33:
time: 19.7 us; the launch traced here: 19.3 us
  starting transfers between devices  11.4 us (58%)
  Pallas kernels  5.36 us (27%)
  waiting for transfers between devices  2.51 us (13%)
    ppermute x6, starting transfers between devices, move(): lax.ppermute(x, ('row', 'col'), [(a * count + b, r * count + c) for (r, c...  7.25 us
    ppermute x1, starting transfers between devices, per_device(): lax.ppermute(factor, ('row', 'col'), [(a * count + b, slots[a][b] * count...  3.95 us
    ppermute x6, waiting for transfers between devices, move(): lax.ppermute(x, ('row', 'col'), [(a * count + b, r * count + c) for (r, c...  2.5 us
    pallas_call x1, Pallas kernels, end_update(): pl.pallas_call(body, out_shape=[jax.ShapeDtypeStruct((half * pieces * row...  1.66 us
    pallas_call x1, Pallas kernels, load_share(): pl.pallas_call(body, out_shape=jax.ShapeDtypeStruct((rows + per_row, LANE...  1.6 us
    pallas_call x1, Pallas kernels, make_factor(): pl.pallas_call(factor_kernel, out_shape=jax.ShapeDtypeStruct((half, tile_...  1.34 us
    pallas_call x1, Pallas kernels, begin_update(): pl.pallas_call(body, out_shape=[jax.ShapeDtypeStruct(share.shape, jnp.flo...  0.76 us
  transfers between devices with their start and end apart: 11, of which 4 were waited for; matrix products, arithmetic and copies ran while one was open for 0% of the time, Pallas kernels for 12%

profile of v33, /device:TPU:0, one launch (start us, length us, event | category | flops | bytes accessed | tf_op | source)
XLA Modules:
  0.0 19.3 jit_solution(2144536841483416721)
XLA Ops:
  0.0 1.3 %factor.1.refs_0_.refs_4_ = bf16[2,64,256]{2,1,0:T(8,128)(2,1)S(1)} custom-call(f32[4,1,64,256]{3,2,1,0:T(8,128)} %panel_ref.1, f32[256,256]{1,0:T(8,128)} %inverse_ref.1), custom_call_target="tpu_custom_call" | custom-call | tf_op jit(solution)/shard_map/factor/pallas_call | solution.py:55
  1.4 3.9 %collective-permute-start = (bf16[2,64,256]{2,1,0:T(8,128)(2,1)S(1)}, bf16[2,64,256]{2,1,0:T(8,128)(2,1)S(1)}, u32[]{:S(2)}, u32[]{:S(2)}) collective-permute-start(bf16[2,64,256]{2,1,0:T(8,128)(2,1)S(1)} %factor.1.refs_0_.refs_4_), channel_id=1, source_target_pairs={{0,24},{2,0},{4,16},{6,8},{8,18},{10,2},{12,26},{14,10},{16,28},{1... | collective-permute-start | bytes 196616 | tf_op jit(solution)/shard_map/ppermute | solution.py:307
  5.3 1.6 %load_share.1.refs_7_ = f32[4104,128]{1,0:T(8,128)S(1)} custom-call(bf16[2,64,256]{2,1,0:T(8,128)(2,1)S(1)} %factor.1.refs_0_.refs_4_, f32[8192,128]{1,0:T(8,128)} %bitcast.2), custom_call_target="tpu_custom_call" | custom-call | bytes 4194304 | tf_op jit(solution)/shard_map/load_share/pallas_call | solution.py:135
  6.9 0.1 collective-permute-start.9
  7.0 2.9 %collective-permute-start.8 = (bf16[2,64,256]{2,1,0:T(8,128)(2,1)S(1)}, bf16[2,64,256]{2,1,0:T(8,128)(2,1)S(1)}, u32[]{:S(2)}, u32[]{:S(2)}) collective-permute-start(bf16[2,64,256]{2,1,0:T(8,128)(2,1)S(1)} %factor.1.refs_0_.refs_4_), channel_id=1, source_target_pairs={{4,0},{6,2},{0,4},{2,6},{12,8},{26,10},{8,12},{10,14},{20,16},{22,... | collective-permute-start | bytes 196616 | tf_op jit(solution)/shard_map/ppermute | solution.py:103
  9.8 0.0 collective-permute-done.refs_0_
  9.8 1.5 %collective-permute-start.6 = (bf16[2,64,256]{2,1,0:T(8,128)(2,1)S(1)}, bf16[2,64,256]{2,1,0:T(8,128)(2,1)S(1)}, u32[]{:S(2)}, u32[]{:S(2)}) collective-permute-start(bf16[2,64,256]{2,1,0:T(8,128)(2,1)S(1)} %collective-permute-done.refs_0_), channel_id=1, source_target_pairs={{8,0},{26,2},{28,4},{30,6},{0,8},{18,10},{20,12},{22,14},{24,16},{... | collective-permute-start | bytes 196616 | tf_op jit(solution)/shard_map/ppermute | solution.py:103
  11.3 0.8 %collective-permute-start.4 = (bf16[2,64,256]{2,1,0:T(8,128)(2,1)S(1)}, bf16[2,64,256]{2,1,0:T(8,128)(2,1)S(1)}, u32[]{:S(2)}, u32[]{:S(2)}) collective-permute-start(bf16[2,64,256]{2,1,0:T(8,128)(2,1)S(1)} %collective-permute-done.refs_0_), channel_id=1, source_target_pairs={{16,0},{18,2},{12,4},{14,6},{24,8},{26,10},{4,12},{6,14},{0,16},{2... | collective-permute-start | bytes 196616 | tf_op jit(solution)/shard_map/ppermute | solution.py:103
  12.1 1.2 %collective-permute-start.2 = (bf16[2,64,256]{2,1,0:T(8,128)(2,1)S(1)}, bf16[2,64,256]{2,1,0:T(8,128)(2,1)S(1)}, u32[]{:S(2)}, u32[]{:S(2)}) collective-permute-start(bf16[2,64,256]{2,1,0:T(8,128)(2,1)S(1)} %collective-permute-done.refs_0_), channel_id=1, source_target_pairs={{2,0},{10,2},{20,4},{22,6},{16,8},{24,10},{28,12},{30,14},{8,16},{... | collective-permute-start | bytes 196616 | tf_op jit(solution)/shard_map/ppermute | solution.py:103
  13.3 0.0 collective-permute-done.9.refs_6_
  13.3 0.0 collective-permute-done.8.refs_5_
  13.3 0.9 %collective-permute-start.10 = (bf16[2,64,256]{2,1,0:T(8,128)(2,1)S(1)}, bf16[2,64,256]{2,1,0:T(8,128)(2,1)S(1)}, u32[]{:S(2)}, u32[]{:S(2)}) collective-permute-start(bf16[2,64,256]{2,1,0:T(8,128)(2,1)S(1)} %select_select_fusion), channel_id=1, source_target_pairs={{2,0},{0,2},{6,4},{4,6},{10,8},{8,10},{14,12},{12,14},{18,16},{16,... | collective-permute-start | bytes 196616 | tf_op jit(solution)/shard_map/ppermute | solution.py:103
  14.2 0.0 collective-permute-start.1
  14.2 0.4 %collective-permute-done.6.refs_3_ = bf16[2,64,256]{2,1,0:T(8,128)(2,1)S(1)} collective-permute-done((bf16[2,64,256]{2,1,0:T(8,128)(2,1)S(1)}, bf16[2,64,256]{2,1,0:T(8,128)(2,1)S(1)}, u32[]{:S(2)}, u32[]{:S(2)}) %collective-permute-start.6) | collective-permute-done | bytes 65568 | tf_op jit(solution)/shard_map/ppermute | solution.py:103
  14.6 0.1 collective-permute-start.7
  14.7 0.9 %collective-permute-done.4.refs_2_ = bf16[2,64,256]{2,1,0:T(8,128)(2,1)S(1)} collective-permute-done((bf16[2,64,256]{2,1,0:T(8,128)(2,1)S(1)}, bf16[2,64,256]{2,1,0:T(8,128)(2,1)S(1)}, u32[]{:S(2)}, u32[]{:S(2)}) %collective-permute-start.4) | collective-permute-done | bytes 65568 | tf_op jit(solution)/shard_map/ppermute | solution.py:103
  15.6 0.0 collective-permute-start.5
  15.6 0.8 %collective-permute-done.2 = bf16[2,64,256]{2,1,0:T(8,128)(2,1)S(1)} collective-permute-done((bf16[2,64,256]{2,1,0:T(8,128)(2,1)S(1)}, bf16[2,64,256]{2,1,0:T(8,128)(2,1)S(1)}, u32[]{:S(2)}, u32[]{:S(2)}) %collective-permute-start.2) | collective-permute-done | bytes 65568 | tf_op jit(solution)/shard_map/ppermute | solution.py:103
  16.4 0.1 collective-permute-start.3
  16.4 0.8 %begin_update.1 = (f32[4104,128]{1,0:T(8,128)S(1)}, bf16[512,256]{1,0:T(8,128)(2,1)S(1)}, bf16[2,64,256]{2,1,0:T(8,128)(2,1)S(1)}, bf16[2,64,256]{2,1,0:T(8,128)(2,1)S(1)}) custom-call(bf16[2,64,256]{2,1,0:T(8,128)(2,1)S(1)} %collective-permute-done.refs_0_, bf16[2,64,256]{2,1,0:T(8,128)(2,1)S(1)} %broadcast_select_fusion.refs_1_, ...), custom_call_target="tpu_custom_call", output_to_operand_aliasing={{0}: (7, {})} | custom-call | tf_op jit(solution)/shard_map/begin_update/pallas_call | solution.py:215
  17.2 0.0 collective-permute-done.1.refs_0_
  17.2 0.5 %collective-permute-done.10.refs_7_ = bf16[2,64,256]{2,1,0:T(8,128)(2,1)S(1)} collective-permute-done((bf16[2,64,256]{2,1,0:T(8,128)(2,1)S(1)}, bf16[2,64,256]{2,1,0:T(8,128)(2,1)S(1)}, u32[]{:S(2)}, u32[]{:S(2)}) %collective-permute-start.10) | collective-permute-done | bytes 65568 | tf_op jit(solution)/shard_map/ppermute | solution.py:103
  17.7 0.0 collective-permute-done.7.refs_3_
  17.7 0.0 collective-permute-done.5.refs_2_
  17.7 0.0 collective-permute-done.3.refs_1_
  17.7 1.7 %end_update.1 = (f32[4096,128]{1,0:T(8,128)}, f32[4104,128]{1,0:T(8,128)S(1)}) custom-call(bf16[2,64,256]{2,1,0:T(8,128)(2,1)S(1)} %collective-permute-done.1.refs_0_, bf16[2,64,256]{2,1,0:T(8,128)(2,1)S(1)} %collective-permute-done.3.refs_1_, bf16[2,64,256]{2,1,0:T(8,128)(2,1)S(1)} %collective-permute-done.5.refs_2_, ...), custom_call_target="tpu_custom_call", output_to_operand_aliasing={{1}: (9, {})} | custom-call | tf_op jit(solution)/shard_map/end_update/pallas_call | solution.py:280
  (2 shorter events, 0.0 us)
Async XLA Ops:
  1.4 8.5 %collective-permute-start = (bf16[2,64,256]{2,1,0:T(8,128)(2,1)S(1)}, bf16[2,64,256]{2,1,0:T(8,128)(2,1)S(1)}, u32[]{:S(2)}, u32[]{:S(2)}) collective-permute-start(bf16[2,64,256]{2,1,0:T(8,128)(2,1)S(1)} %factor.1.refs_0_.refs_4_), channel_id=1, source_target_pairs={{0,24},{2,0},{4,16},{6,8},{8,18},{10,2},{12,26},{14,10},{16,28},{1... | collective-permute-start | bytes 196616 | tf_op jit(solution)/shard_map/ppermute | solution.py:307
  6.9 6.4 %collective-permute-start.9 = (bf16[2,64,256]{2,1,0:T(8,128)(2,1)S(1)}, bf16[2,64,256]{2,1,0:T(8,128)(2,1)S(1)}, u32[]{:S(2)}, u32[]{:S(2)}) collective-permute-start(bf16[2,64,256]{2,1,0:T(8,128)(2,1)S(1)} %factor.1.refs_0_.refs_4_), channel_id=1, source_target_pairs={{8,0},{0,2},{6,4},{4,6},{10,8},{2,10},{14,12},{12,14},{18,16},{16,... | collective-permute-start | bytes 196616 | tf_op jit(solution)/shard_map/ppermute | solution.py:103
  7.0 6.4 %collective-permute-start.8 = (bf16[2,64,256]{2,1,0:T(8,128)(2,1)S(1)}, bf16[2,64,256]{2,1,0:T(8,128)(2,1)S(1)}, u32[]{:S(2)}, u32[]{:S(2)}) collective-permute-start(bf16[2,64,256]{2,1,0:T(8,128)(2,1)S(1)} %factor.1.refs_0_.refs_4_), channel_id=1, source_target_pairs={{4,0},{6,2},{0,4},{2,6},{12,8},{26,10},{8,12},{10,14},{20,16},{22,... | collective-permute-start | bytes 196616 | tf_op jit(solution)/shard_map/ppermute | solution.py:103
  9.8 4.8 %collective-permute-start.6 = (bf16[2,64,256]{2,1,0:T(8,128)(2,1)S(1)}, bf16[2,64,256]{2,1,0:T(8,128)(2,1)S(1)}, u32[]{:S(2)}, u32[]{:S(2)}) collective-permute-start(bf16[2,64,256]{2,1,0:T(8,128)(2,1)S(1)} %collective-permute-done.refs_0_), channel_id=1, source_target_pairs={{8,0},{26,2},{28,4},{30,6},{0,8},{18,10},{20,12},{22,14},{24,16},{... | collective-permute-start | bytes 196616 | tf_op jit(solution)/shard_map/ppermute | solution.py:103
  11.3 4.3 %collective-permute-start.4 = (bf16[2,64,256]{2,1,0:T(8,128)(2,1)S(1)}, bf16[2,64,256]{2,1,0:T(8,128)(2,1)S(1)}, u32[]{:S(2)}, u32[]{:S(2)}) collective-permute-start(bf16[2,64,256]{2,1,0:T(8,128)(2,1)S(1)} %collective-permute-done.refs_0_), channel_id=1, source_target_pairs={{16,0},{18,2},{12,4},{14,6},{24,8},{26,10},{4,12},{6,14},{0,16},{2... | collective-permute-start | bytes 196616 | tf_op jit(solution)/shard_map/ppermute | solution.py:103
  12.1 4.3 %collective-permute-start.2 = (bf16[2,64,256]{2,1,0:T(8,128)(2,1)S(1)}, bf16[2,64,256]{2,1,0:T(8,128)(2,1)S(1)}, u32[]{:S(2)}, u32[]{:S(2)}) collective-permute-start(bf16[2,64,256]{2,1,0:T(8,128)(2,1)S(1)} %collective-permute-done.refs_0_), channel_id=1, source_target_pairs={{2,0},{10,2},{20,4},{22,6},{16,8},{24,10},{28,12},{30,14},{8,16},{... | collective-permute-start | bytes 196616 | tf_op jit(solution)/shard_map/ppermute | solution.py:103
  13.3 4.3 %collective-permute-start.10 = (bf16[2,64,256]{2,1,0:T(8,128)(2,1)S(1)}, bf16[2,64,256]{2,1,0:T(8,128)(2,1)S(1)}, u32[]{:S(2)}, u32[]{:S(2)}) collective-permute-start(bf16[2,64,256]{2,1,0:T(8,128)(2,1)S(1)} %select_select_fusion), channel_id=1, source_target_pairs={{2,0},{0,2},{6,4},{4,6},{10,8},{8,10},{14,12},{12,14},{18,16},{16,... | collective-permute-start | bytes 196616 | tf_op jit(solution)/shard_map/ppermute | solution.py:103
  14.2 3.0 %collective-permute-start.1 = (bf16[2,64,256]{2,1,0:T(8,128)(2,1)S(1)}, bf16[2,64,256]{2,1,0:T(8,128)(2,1)S(1)}, u32[]{:S(2)}, u32[]{:S(2)}) collective-permute-start(bf16[2,64,256]{2,1,0:T(8,128)(2,1)S(1)} %collective-permute-done.refs_0_), channel_id=1, source_target_pairs={{1,0},{0,1},{3,2},{2,3},{5,4},{4,5},{7,6},{6,7},{9,8},{8,9},{11,10... | collective-permute-start | bytes 196616 | tf_op jit(solution)/shard_map/ppermute | solution.py:327
  14.6 3.1 %collective-permute-start.7 = (bf16[2,64,256]{2,1,0:T(8,128)(2,1)S(1)}, bf16[2,64,256]{2,1,0:T(8,128)(2,1)S(1)}, u32[]{:S(2)}, u32[]{:S(2)}) collective-permute-start(bf16[2,64,256]{2,1,0:T(8,128)(2,1)S(1)} %collective-permute-done.6.refs_3_), channel_id=1, source_target_pairs={{1,0},{0,1},{3,2},{2,3},{5,4},{4,5},{7,6},{6,7},{9,8},{8,9},{11,10... | collective-permute-start | bytes 196616 | tf_op jit(solution)/shard_map/ppermute | solution.py:327
  15.6 2.1 %collective-permute-start.5 = (bf16[2,64,256]{2,1,0:T(8,128)(2,1)S(1)}, bf16[2,64,256]{2,1,0:T(8,128)(2,1)S(1)}, u32[]{:S(2)}, u32[]{:S(2)}) collective-permute-start(bf16[2,64,256]{2,1,0:T(8,128)(2,1)S(1)} %collective-permute-done.4.refs_2_), channel_id=1, source_target_pairs={{1,0},{0,1},{3,2},{2,3},{5,4},{4,5},{7,6},{6,7},{9,8},{8,9},{11,10... | collective-permute-start | bytes 196616 | tf_op jit(solution)/shard_map/ppermute | solution.py:327
  16.4 1.3 %collective-permute-start.3 = (bf16[2,64,256]{2,1,0:T(8,128)(2,1)S(1)}, bf16[2,64,256]{2,1,0:T(8,128)(2,1)S(1)}, u32[]{:S(2)}, u32[]{:S(2)}) collective-permute-start(bf16[2,64,256]{2,1,0:T(8,128)(2,1)S(1)} %broadcast_select_fusion.refs_1_), channel_id=1, source_target_pairs={{1,0},{0,1},{3,2},{2,3},{5,4},{4,5},{7,6},{6,7},{9,8},{8,9},{11,10... | collective-permute-start | bytes 196616 | tf_op jit(solution)/shard_map/ppermute | solution.py:327
